TPU v7x, 32 devices: a whole 2x2x4 slice. The times are simulated.
32 devices in a mesh: group: 2 (over y), expert: 4 (over z), tensor: 4 (over x, core).
Axes of the slice: x: 2, y: 2, z: 4, core: 2. Of those that a mesh axis runs over, the one named last changes fastest.
Arguments:
- inputs: bfloat16 [1024, 1024], P(('group', 'expert')), parts along dimension 0, may hold values from -6 to 6
- cotangent: bfloat16 [1024, 1024], P(('group', 'expert')), parts along dimension 0, may hold values from -6 to 6
- gate_values: float32 [1024, 2], P(('group', 'expert')), parts along dimension 0, may hold values from 0.25 to 1
- routes: int32 [1024, 2], P(('group', 'expert')), parts along dimension 0, may hold values from 0 to 7, all different within a row; in each aligned block of 128 rows (0 to 127, 128 to 255, ...) at most 64 rows name the same one
- pair_weight: bfloat16 [8, 256, 1024], P('expert', None, 'tensor'), may hold values from -1.5 to 1.5
- up_weight: bfloat16 [8, 1024, 2048], P('expert', None, 'tensor'), may hold values from -0.1875 to 0.1875
- down_weight: bfloat16 [8, 2048, 1024], P('expert', 'tensor'), may hold values from -0.125 to 0.125
Outputs:
- mixed: bfloat16 [1024, 1024], P(('group', 'expert'), 'tensor'), parts along dimension 0
- grad_input: bfloat16 [1024, 1024], P(('group', 'expert'), 'tensor'), parts along dimension 0
- grad_pair: bfloat16 [16, 256, 1024], P(('group', 'expert'), None, 'tensor'), parts along dimension 0
- grad_up: bfloat16 [16, 1024, 2048], P(('group', 'expert'), None, 'tensor'), parts along dimension 0
- grad_down: bfloat16 [16, 2048, 1024], P(('group', 'expert'), 'tensor'), parts along dimension 0
There are 2 independent parts, one for each index of `group`. A program takes and returns all parts, laid end to end along the dimension named above; an argument that names none is the same for every part. Nothing has to cross between parts.
Inputs may be any that keep to these rules, and one draw needn't show every extreme that they name: `routes`: the 2 experts of one example differ. Among the rows of one device (aligned blocks of 128 examples) no expert is named more than 64 times, and in every draw some expert is named exactly 64 times in some block.
All inputs are finite; a program needn't handle non-finite values.
Results may differ from a plain program's by a relative error of at most 0.011.
Values may be sent and summed in bfloat16 or wider, within the bound.
No kernel may reach another device: no remote copies, remote signals or barrier semaphores. Data moves between devices by JAX's collectives and lax.ppermute only.
A program may use at most 64 MiB of HBM per device.

v0:
```python
import jax
import jax.numpy as jnp
from jax import lax
from jax.sharding import PartitionSpec as P

NF = 16
DE = 64


def dispatch_tables(routes, expert_total, capacity):
    row_count, pick_count = routes.shape
    flat_ids = routes.reshape(-1)
    onehot = (flat_ids[:, None] == jnp.arange(expert_total, dtype=jnp.int32)[None, :]).astype(
        jnp.int32
    )
    before = jnp.cumsum(onehot, axis=0) - onehot
    position = jnp.sum(before * onehot, axis=1)
    slot_index = flat_ids * capacity + position
    slot_count = expert_total * capacity
    tables = slot_index[:, None] == jnp.arange(slot_count, dtype=jnp.int32)[None, :]
    tables = tables.reshape(row_count, pick_count, slot_count)
    return jnp.transpose(tables, (1, 2, 0)).astype(jnp.bfloat16)


def body(inputs, cotangent, gate_values, routes, pair_weight, up_weight, down_weight):
    local_count = up_weight.shape[0]
    expert_count = lax.axis_size("expert")
    tensor_count = lax.axis_size("tensor")
    expert_total = local_count * expert_count
    row_count, pick_count = routes.shape
    feature_width = inputs.shape[1]
    capacity = 2 * row_count * pick_count // expert_total
    expert_rows = expert_count * capacity
    part_width = feature_width // tensor_count
    tensor_index = lax.axis_index("tensor")
    feature_start = tensor_index * part_width
    tables = dispatch_tables(routes, expert_total, capacity)
    any_table = jnp.sum(tables, axis=0)
    scaled = (gate_values[:, :, None] * cotangent[:, None, :].astype(jnp.float32)).astype(
        jnp.bfloat16
    )
    input_slice = lax.dynamic_slice_in_dim(inputs, feature_start, part_width, 1)
    cotangent_slice = lax.dynamic_slice_in_dim(cotangent, feature_start, part_width, 1)
    input_slots = jnp.dot(any_table, inputs, preferred_element_type=jnp.float32).astype(
        jnp.bfloat16
    )
    grad_slots = jnp.einsum(
        "ksr,rkd->sd", tables, scaled, preferred_element_type=jnp.float32
    ).astype(jnp.bfloat16)
    send_shape = (expert_count, local_count, capacity, feature_width)
    input_homes, grad_homes = (
        lax.all_to_all(
            input_slots.reshape(send_shape), "expert", split_axis=0, concat_axis=2, tiled=True
        ),
        lax.all_to_all(
            grad_slots.reshape(send_shape), "expert", split_axis=0, concat_axis=2, tiled=True
        ),
    )
    input_rows = input_homes.reshape(local_count, expert_rows, feature_width)
    grad_rows = grad_homes.reshape(local_count, expert_rows, feature_width)
    cells = jnp.transpose(input_rows.reshape(local_count, expert_rows, NF, DE), (0, 2, 3, 1))
    gram = jnp.einsum("eidr,ejdr->eijr", cells, cells, preferred_element_type=jnp.float32) / DE
    gram_flat = gram.reshape(local_count, NF * NF, expert_rows).astype(jnp.bfloat16)
    input_mine = lax.dynamic_slice_in_dim(input_rows, feature_start, part_width, 2)
    cross_sum = input_mine.astype(jnp.float32) + jnp.einsum(
        "epr,epd->erd", gram_flat, pair_weight, preferred_element_type=jnp.float32
    )
    cross_part = cross_sum.astype(jnp.bfloat16)
    cross_whole = lax.all_gather(cross_part, "tensor", axis=2, tiled=True)
    hidden_pre = jnp.einsum(
        "erd,edh->erh", cross_whole, up_weight, preferred_element_type=jnp.float32
    )
    hidden_act = jax.nn.silu(hidden_pre).astype(jnp.bfloat16)
    out_terms = jnp.einsum(
        "erh,ehd->erd", hidden_act, down_weight, preferred_element_type=jnp.float32
    )
    out_mine = lax.psum_scatter(
        out_terms.astype(jnp.bfloat16), "tensor", scatter_dimension=2, tiled=True
    )
    grad_act = jnp.einsum(
        "erd,ehd->erh", grad_rows, down_weight, preferred_element_type=jnp.float32
    )
    sigmoid_pre = jax.nn.sigmoid(hidden_pre)
    grad_pre = (grad_act * sigmoid_pre * (1.0 + hidden_pre * (1.0 - sigmoid_pre))).astype(
        jnp.bfloat16
    )
    grad_down = jnp.einsum(
        "erh,erd->ehd", hidden_act, grad_rows, preferred_element_type=jnp.float32
    ).astype(jnp.bfloat16)
    grad_up = jnp.einsum(
        "erd,erh->edh", cross_whole, grad_pre, preferred_element_type=jnp.float32
    ).astype(jnp.bfloat16)
    cross_terms = jnp.einsum(
        "erh,edh->erd", grad_pre, up_weight, preferred_element_type=jnp.float32
    )
    grad_cross = lax.psum_scatter(
        cross_terms.astype(jnp.bfloat16), "tensor", scatter_dimension=2, tiled=True
    )
    grad_pair = jnp.einsum(
        "epr,erd->epd", gram_flat, grad_cross, preferred_element_type=jnp.float32
    ).astype(jnp.bfloat16)
    pair_terms = jnp.einsum(
        "erd,epd->epr", grad_cross, pair_weight, preferred_element_type=jnp.float32
    )
    grad_gram = (
        lax.psum(pair_terms.astype(jnp.bfloat16), "tensor")
        .astype(jnp.float32)
        .reshape(local_count, NF, NF, expert_rows)
    )
    symmetric = grad_gram + jnp.swapaxes(grad_gram, 1, 2)
    field_count = part_width // DE
    symmetric_mine = lax.dynamic_slice_in_dim(symmetric, tensor_index * field_count, field_count, 1)
    gram_back = (
        jnp.einsum(
            "eijr,ejdr->eidr",
            symmetric_mine,
            cells.astype(jnp.float32),
            precision=lax.Precision.HIGHEST,
        )
        / DE
    )
    gram_back = jnp.transpose(gram_back, (0, 3, 1, 2)).reshape(local_count, expert_rows, part_width)
    grad_mine = (grad_cross.astype(jnp.float32) + gram_back).astype(jnp.bfloat16)
    back_shape = (1, local_count, expert_rows, part_width)
    out_back, grad_back = (
        lax.all_to_all(
            out_mine.reshape(back_shape), "expert", split_axis=2, concat_axis=0, tiled=True
        ),
        lax.all_to_all(
            grad_mine.reshape(back_shape), "expert", split_axis=2, concat_axis=0, tiled=True
        ),
    )
    out_back = out_back.reshape(expert_total * capacity, part_width)
    grad_back = grad_back.reshape(expert_total * capacity, part_width)
    picked = jnp.einsum("ksr,sd->rkd", tables, out_back, preferred_element_type=jnp.float32)
    mixed = (
        input_slice.astype(jnp.float32) + jnp.sum(gate_values[:, :, None] * picked, axis=1)
    ).astype(jnp.bfloat16)
    grad_input = (
        cotangent_slice.astype(jnp.float32)
        + jnp.dot(any_table.T, grad_back, preferred_element_type=jnp.float32)
    ).astype(jnp.bfloat16)
    return (mixed, grad_input, grad_pair, grad_up, grad_down)


def solution(mesh):
    placed = (
        P(("group", "expert"), None),
        P(("group", "expert"), None),
        P(("group", "expert"), None),
        P(("group", "expert"), None),
        P("expert", None, "tensor"),
        P("expert", None, "tensor"),
        P("expert", "tensor", None),
    )
    return jax.shard_map(
        body,
        mesh=mesh,
        in_specs=placed,
        out_specs=(
            P(("group", "expert"), "tensor"),
            P(("group", "expert"), "tensor"),
            P(("group", "expert"), None, "tensor"),
            P(("group", "expert"), None, "tensor"),
            P(("group", "expert"), "tensor", None),
        ),
        check_vma=False,
    )
```

profile of v0, /device:TPU:0, one launch (start us, length us, event | category | flops | bytes accessed | tf_op | source)
XLA Modules:
  0.0 236.6 jit_solution(314568766993111018)
XLA Ops:
  10.4 2.3 convolution_convert_fusion.4
  12.7 6.3 %all-to-all-start = ((bf16[4,2,64,1024]{3,2,1,0:T(8,128)(2,1)}), bf16[4,2,64,1024]{3,2,1,0:T(8,128)(2,1)S(1)}, u32[]{:S(2)}, u32[]{:S(2)}) async-start(bf16[4,2,64,1024]{3,2,1,0:T(8,128)(2,1)} %bitcast.85), calls=%async_computation | async-start | bytes 2097152 | tf_op jit(solution)/shard_map/all_to_all | solution.py:52
  19.9 2.5 %bitcast_convert_fusion = bf16[512,1024]{1,0:T(8,128)(2,1)} fusion(f32[128,1024]{1,0:T(8,128)} %convert_element_type.101, f32[128,2]{0,1:T(2,128)S(1)} %copy-done.7, s32[2,128]{1,0:T(2,128)S(1)} %add_bitcast_fusion), kind=kOutput, calls=%fused_computation.1 | convolution fusion | flops 269615104 | bytes 1574912 | tf_op jit(solution)/shard_map/ksr,rkd->sd/dot_general | solution.py:47
  22.4 22.3 %all-to-all-done = bf16[4,2,64,1024]{3,2,1,0:T(8,128)(2,1)S(1)} async-done(((bf16[4,2,64,1024]{3,2,1,0:T(8,128)(2,1)}), bf16[4,2,64,1024]{3,2,1,0:T(8,128)(2,1)S(1)}, u32[]{:S(2)}, u32[]{:S(2)}) %all-to-all-start) | async-done | bytes 1048608 | tf_op jit(solution)/shard_map/all_to_all | solution.py:52
  44.8 4.2 %all-to-all-start.2 = ((bf16[4,2,64,1024]{3,2,1,0:T(8,128)(2,1)}), bf16[4,2,64,1024]{3,2,1,0:T(8,128)(2,1)}, u32[]{:S(2)}, u32[]{:S(2)}) async-start(bf16[4,2,64,1024]{3,2,1,0:T(8,128)(2,1)} %bitcast.84), calls=%async_computation.3 | async-start | bytes 2097152 | tf_op jit(solution)/shard_map/all_to_all | solution.py:55
  50.4 2.3 reshape_reshape.3
  52.7 4.7 %fusion.3 = bf16[2,16,16,256]{1,2,3,0:T(8,128)(2,1)} fusion(bf16[2,256,16,64]{3,2,1,0:T(8,128)(2,1)} %reshape_reshape.3), kind=kOutput, calls=%fused_computation.7 | convolution fusion | flops 17039360 | bytes 1310720 | tf_op jit(solution)/shard_map/eidr,ejdr->eijr/dot_general | solution.py:62
  57.4 3.4 %copy.91 = bf16[2,16,16,256]{3,2,1,0:T(8,128)(2,1)S(1)} copy(bf16[2,16,16,256]{1,2,3,0:T(8,128)(2,1)} %fusion.3) | data formatting | bytes 524288 | tf_op jit(solution)/shard_map/convert_element_type | solution.py:63
  62.9 11.4 %all-to-all-done.2 = bf16[4,2,64,1024]{3,2,1,0:T(8,128)(2,1)} async-done(((bf16[4,2,64,1024]{3,2,1,0:T(8,128)(2,1)}), bf16[4,2,64,1024]{3,2,1,0:T(8,128)(2,1)}, u32[]{:S(2)}, u32[]{:S(2)}) %all-to-all-start.2) | async-done | bytes 1048608 | tf_op jit(solution)/shard_map/all_to_all | solution.py:55
  75.6 5.6 %all-gather.2.cloned.1.call-done = bf16[2,256,1024]{2,1,0:T(8,128)(2,1)} async-done(((bf16[2,256,256]{2,1,0:T(8,128)(2,1)}), bf16[2,256,1024]{2,1,0:T(8,128)(2,1)}) %all-gather.2.cloned.1.call-update) | async-done | bytes 1048592 | tf_op jit(solution)/shard_map/all_gather | solution.py:69
  86.9 3.7 %convolution_convert_fusion.3 = bf16[2,256,1024]{2,1,0:T(8,128)(2,1)} fusion(bf16[2,512,1024]{2,1,0:T(8,128)(2,1)} %param.13, f32[2,256,512]{2,1,0:T(8,128)} %copy-done.5), kind=kOutput, calls=%fused_computation.9 | convolution fusion | flops 538705920 | bytes 4194304 | tf_op jit(solution)/shard_map/erh,ehd->erd/dot_general | solution.py:74
  93.7 3.4 %convolution_convert_fusion = bf16[2,512,1024]{2,1,0:T(8,128)(2,1)} fusion(bf16[2,256,1024]{2,1,0:T(8,128)(2,1)S(1)} %bitcast.92, f32[2,256,512]{2,1,0:T(8,128)} %copy-done.5), kind=kOutput, calls=%fused_computation.5 | convolution fusion | flops 539230208 | bytes 4194304 | tf_op jit(solution)/shard_map/erh,erd->ehd/dot_general | solution.py:87
  97.1 14.8 %reduce-scatter.5.cloned.1.call-done = bf16[2,256,256]{2,1,0:T(8,128)(2,1)} async-done(((bf16[2,256,1024]{2,1,0:T(8,128)(2,1)}), bf16[2,256,256]{2,1,0:T(8,128)(2,1)}) %reduce-scatter.5.cloned.1.call-update) | async-done | bytes 262160 | tf_op jit(solution)/shard_map/reduce_scatter | solution.py:96
  113.9 4.6 %copy.98 = bf16[2,16,16,256]{1,2,3,0:T(8,128)(2,1)} copy(bf16[2,16,16,256]{3,2,1,0:T(8,128)(2,1)} %bitcast.89) | data formatting | bytes 524288 | tf_op jit(solution)/shard_map/reshape | solution.py:108
  118.5 3.1 %convolution_convert_fusion.1 = bf16[2,1024,512]{2,1,0:T(8,128)(2,1)} fusion(bf16[2,256,1024]{2,1,0:T(8,128)(2,1)S(1)} %copy-done.1, bf16[2,256,512]{2,1,0:T(8,128)(2,1)} %copy-done.4), kind=kOutput, calls=%fused_computation.6 | convolution fusion | flops 537919488 | bytes 3670016 | tf_op jit(solution)/shard_map/erd,erh->edh/dot_general | solution.py:90
  121.6 17.9 %reduce-scatter.3.cloned.1.call-done = bf16[2,256,256]{2,1,0:T(8,128)(2,1)} async-done(((bf16[2,256,1024]{2,1,0:T(8,128)(2,1)}), bf16[2,256,256]{2,1,0:T(8,128)(2,1)}) %reduce-scatter.3.cloned.1.call-update) | async-done | bytes 262160 | tf_op jit(solution)/shard_map/reduce_scatter | solution.py:77
  141.4 4.6 %all-to-all-start.1 = ((bf16[1,2,256,256]{3,1,0,2:T(2,128)(2,1)}), bf16[1,2,256,256]{3,1,0,2:T(2,128)(2,1)}, u32[]{:S(2)}, u32[]{:S(2)}) async-start(bf16[1,2,256,256]{3,1,0,2:T(2,128)(2,1)} %copy.93), calls=%async_computation.2 | async-start | bytes 524288 | tf_op jit(solution)/shard_map/all_to_all | solution.py:126
  146.0 47.1 %all-reduce.2.cloned.1.call-done = bf16[2,16,16,256]{1,2,3,0:T(8,128)(2,1)} async-done(((bf16[2,16,16,256]{1,2,3,0:T(8,128)(2,1)}), bf16[2,16,16,256]{1,2,3,0:T(8,128)(2,1)}) %all-reduce.2.cloned.1.call-update) | async-done | bytes 262160 | tf_op jit(solution)/shard_map/psum | solution.py:106
  193.1 4.1 %convert_bitcast_fusion = (f32[2,16,16,256]{2,1,3,0:T(8,128)}, f32[2,16,16,256]{1,2,3,0:T(8,128)S(1)}) fusion(bf16[2,16,16,256]{1,2,3,0:T(8,128)(2,1)} %all-reduce.2.cloned.1.call-done), kind=kLoop, calls=%fused_computation.25 | loop fusion | flops 131072 | bytes 1310720 | tf_op jit(solution)/shard_map/transpose | solution.py:110
  197.2 3.1 %constant_dynamic-slice_fusion = f32[2,4,16,256]{1,2,3,0:T(8,128)} fusion(f32[2,16,16,256]{1,2,3,0:T(8,128)S(1)} %get-tuple-element.21, s32[]{:T(128)S(6)} %select_n.9), kind=kLoop, calls=%fused_computation.47 | loop fusion | bytes 262148 | tf_op jit(solution)/shard_map/dynamic_slice | solution.py:112
  200.3 4.8 %copy.114 = f32[2,4,16,256]{2,1,3,0:T(4,128)S(1)} copy(f32[2,4,16,256]{1,2,3,0:T(8,128)} %constant_dynamic-slice_fusion) | data formatting | bytes 262144
  205.1 5.1 %fusion.6 = f32[2,256,4,64]{3,2,1,0:T(4,128)} fusion(bf16[2,256,16,64]{3,2,1,0:T(8,128)(2,1)} %reshape_reshape.3, f32[2,4,16,256]{2,1,3,0:T(4,128)S(1)} %copy.114, f32[2,16,16,256]{2,1,3,0:T(8,128)} %get-tuple-element.20, s32[]{:T(128)S(6)} %select_n.9), kind=kOutput, calls=%fused_computation.11 | convolution fusion | flops 25329664 | bytes 3801092 | tf_op jit(solution)/shard_map/eijr,ejdr->eidr/dot_general | solution.py:114
  214.9 4.6 %all-to-all-start.3 = ((bf16[1,2,256,256]{3,1,0,2:T(2,128)(2,1)}), bf16[1,2,256,256]{3,1,0,2:T(2,128)(2,1)S(1)}, u32[]{:S(2)}, u32[]{:S(2)}) async-start(bf16[1,2,256,256]{3,1,0,2:T(2,128)(2,1)} %copy.102), calls=%async_computation.5 | async-start | bytes 524288 | tf_op jit(solution)/shard_map/all_to_all | solution.py:129
  223.3 5.0 %all-to-all-done.3 = bf16[1,2,256,256]{3,1,0,2:T(2,128)(2,1)S(1)} async-done(((bf16[1,2,256,256]{3,1,0,2:T(2,128)(2,1)}), bf16[1,2,256,256]{3,1,0,2:T(2,128)(2,1)S(1)}, u32[]{:S(2)}, u32[]{:S(2)}) %all-to-all-start.3) | async-done | bytes 262176 | tf_op jit(solution)/shard_map/all_to_all | solution.py:129
  (64 shorter events, 31.6 us)
Async XLA Ops:
  7.2 74.0 %copy-start = (bf16[2,1024,512]{2,1,0:T(8,128)(2,1)S(1)}, bf16[2,1024,512]{2,1,0:T(8,128)(2,1)}, u32[]{:S(2)}) copy-start(bf16[2,1024,512]{2,1,0:T(8,128)(2,1)} %param.12) | copy-start | bytes 6291460
  7.2 11.9 %copy-start.6 = (bf16[128,1024]{1,0:T(8,128)(2,1)S(1)}, bf16[128,1024]{1,0:T(8,128)(2,1)}, u32[]{:S(2)}) copy-start(bf16[128,1024]{1,0:T(8,128)(2,1)} %param.8) | copy-start | bytes 786436
  10.3 9.5 %copy-start.7 = (f32[128,2]{0,1:T(2,128)S(1)}, f32[128,2]{0,1:T(2,128)}, u32[]{:S(2)}) copy-start(f32[128,2]{0,1:T(2,128)} %param.9) | copy-start | bytes 3076
  12.7 32.0 %all-to-all-start = ((bf16[4,2,64,1024]{3,2,1,0:T(8,128)(2,1)}), bf16[4,2,64,1024]{3,2,1,0:T(8,128)(2,1)S(1)}, u32[]{:S(2)}, u32[]{:S(2)}) async-start(bf16[4,2,64,1024]{3,2,1,0:T(8,128)(2,1)} %bitcast.85), calls=%async_computation | async-start | bytes 2097152 | tf_op jit(solution)/shard_map/all_to_all | solution.py:52
  44.8 4.3 %copy-start.2 = (bf16[4,2,64,1024]{3,2,1,0:T(8,128)(2,1)}, bf16[4,2,64,1024]{3,2,1,0:T(8,128)(2,1)S(1)}, u32[]{:S(2)}) copy-start(bf16[4,2,64,1024]{3,2,1,0:T(8,128)(2,1)S(1)} %all-to-all-done) | copy-start | bytes 3145732
  44.8 29.5 %all-to-all-start.2 = ((bf16[4,2,64,1024]{3,2,1,0:T(8,128)(2,1)}), bf16[4,2,64,1024]{3,2,1,0:T(8,128)(2,1)}, u32[]{:S(2)}, u32[]{:S(2)}) async-start(bf16[4,2,64,1024]{3,2,1,0:T(8,128)(2,1)} %bitcast.84), calls=%async_computation.3 | async-start | bytes 2097152 | tf_op jit(solution)/shard_map/all_to_all | solution.py:55
  49.0 32.2 %all-gather.2.cloned.1.call-start = ((), (), s32[]{:S(2)}) async-start(), calls=%async_computation.6 | async-start | bytes 1310720 | tf_op jit(solution)/shard_map/all_gather | solution.py:69
  62.8 49.0 %reduce-scatter.5.cloned.1.call-start = ((), (), s32[]{:S(2)}) async-start(), calls=%async_computation.8 | async-start | bytes 1310720 | tf_op jit(solution)/shard_map/reduce_scatter | solution.py:96
  81.2 2.1 copy-start.8
  83.3 1.0 copy-start.5
  84.3 0.8 copy-start.4
  86.8 52.7 %reduce-scatter.3.cloned.1.call-start = ((), (), s32[]{:S(2)}) async-start(), calls=%async_computation.7 | async-start | bytes 1310720 | tf_op jit(solution)/shard_map/reduce_scatter | solution.py:77
  90.6 102.5 %all-reduce.2.cloned.1.call-start = ((), (), s32[]{:S(2)}) async-start(), calls=%async_computation.9 | async-start | bytes 4194304 | tf_op jit(solution)/shard_map/psum | solution.py:106
  113.9 4.6 %copy-start.1 = (bf16[2,256,1024]{2,1,0:T(8,128)(2,1)S(1)}, bf16[2,256,1024]{2,1,0:T(8,128)(2,1)}, u32[]{:S(2)}) copy-start(bf16[2,256,1024]{2,1,0:T(8,128)(2,1)} %all-gather.2.cloned.1.call-done) | copy-start | bytes 3145732
  141.4 73.5 %all-to-all-start.1 = ((bf16[1,2,256,256]{3,1,0,2:T(2,128)(2,1)}), bf16[1,2,256,256]{3,1,0,2:T(2,128)(2,1)}, u32[]{:S(2)}, u32[]{:S(2)}) async-start(bf16[1,2,256,256]{3,1,0,2:T(2,128)(2,1)} %copy.93), calls=%async_computation.2 | async-start | bytes 524288 | tf_op jit(solution)/shard_map/all_to_all | solution.py:126
  210.2 2.6 %copy-start.3 = (bf16[2,256,256]{2,1,0:T(8,128)(2,1)S(1)}, bf16[2,256,256]{2,1,0:T(8,128)(2,1)}, u32[]{:S(2)}) copy-start(bf16[2,256,256]{2,1,0:T(8,128)(2,1)} %reduce-scatter.5.cloned.1.call-done) | copy-start | bytes 786436
  214.9 13.4 %all-to-all-start.3 = ((bf16[1,2,256,256]{3,1,0,2:T(2,128)(2,1)}), bf16[1,2,256,256]{3,1,0,2:T(2,128)(2,1)S(1)}, u32[]{:S(2)}, u32[]{:S(2)}) async-start(bf16[1,2,256,256]{3,1,0,2:T(2,128)(2,1)} %copy.102), calls=%async_computation.5 | async-start | bytes 524288 | tf_op jit(solution)/shard_map/all_to_all | solution.py:129
Sparse Core Ops, SparseCore 0:
  63.0 18.1 all-gather.1
  86.9 24.8 reduce-scatter.4
  114.6 24.8 reduce-scatter.2
  141.7 51.3 all-reduce.1
where the time goes:
time: 238 us; the launch traced here: 237 us
  waiting for transfers between devices  124 us (52%)
  matrix products  36.6 us (15%)
  local copies, waits for them, and re-layouts  33.6 us (14%)
  starting transfers between devices  19.9 us (8%)
  between operations  14 us (6%)
  other arithmetic  8.36 us (4%)
    psum x1, waiting for transfers between devices, body(): lax.psum(pair_terms.astype(jnp.bfloat16), 'tensor').astype(jnp.float32)  47.1 us
    all_to_all x1, waiting for transfers between devices, body(): lax.all_to_all(input_slots.reshape(send_shape), 'expert', split_axis=0, c...  22.3 us
    reduce_scatter x1, waiting for transfers between devices, body(): lax.psum_scatter(out_terms.astype(jnp.bfloat16), 'tensor', scatter_dimens...  17.9 us
    reduce_scatter x1, waiting for transfers between devices, body(): lax.psum_scatter(cross_terms.astype(jnp.bfloat16), 'tensor', scatter_dime...  14.8 us
    all_to_all x1, waiting for transfers between devices, body(): lax.all_to_all(grad_slots.reshape(send_shape), 'expert', split_axis=0, co...  11.4 us
    unnamed x22, local copies, waits for them, and re-layouts  8.91 us
    all_to_all x1, starting transfers between devices, body(): lax.all_to_all(input_slots.reshape(send_shape), 'expert', split_axis=0, c...  6.32 us
    all_gather x1, waiting for transfers between devices, body(): cross_whole = lax.all_gather(cross_part, 'tensor', axis=2, tiled=True)  5.57 us
  transfers between devices with their start and end apart: 8, of which 7 were waited for; matrix products, arithmetic and copies ran while one was open for 28% of the time, Pallas kernels for 0%

commit v1 on v0

--- a/solution.py
+++ b/solution.py
@@ -1,6 +1,10 @@
+import functools
+
 import jax
 import jax.numpy as jnp
 from jax import lax
+from jax.experimental import pallas as pl
+from jax.experimental.pallas import tpu as pltpu
 from jax.sharding import PartitionSpec as P
 
 NF = 16
@@ -143,6 +147,320 @@
     return (mixed, grad_input, grad_pair, grad_up, grad_down)
 
 
+F32 = jnp.float32
+BF16 = jnp.bfloat16
+NT = (((1,), (1,)), ((), ()))
+TN = (((0,), (0,)), ((), ()))
+
+
+def mm(a, b, dims=None):
+    if dims is None:
+        return jnp.dot(a, b, preferred_element_type=F32)
+    return lax.dot_general(a, b, dims, preferred_element_type=F32)
+
+
+def kernel_call(kernel, out_shape, scratch=(), flops=0, nbytes=0):
+    return pl.pallas_call(
+        kernel,
+        out_shape=out_shape,
+        scratch_shapes=list(scratch),
+        compiler_params=pltpu.CompilerParams(vmem_limit_bytes=48 * 1024 * 1024),
+        cost_estimate=pl.CostEstimate(flops=flops, bytes_accessed=nbytes, transcendentals=0),
+    )
+
+
+def shape(dims, dtype=BF16):
+    return jax.ShapeDtypeStruct(dims, dtype)
+
+
+def meta_kernel(gates_ref, routes_ref, meta_ref):
+    rows = gates_ref.shape[0]
+    eye = lax.broadcasted_iota(jnp.int32, (rows, rows), 0) == lax.broadcasted_iota(
+        jnp.int32, (rows, rows), 1
+    )
+
+    def row_of(column):
+        return jnp.sum(jnp.where(eye, column, 0.0), axis=0, keepdims=True)
+
+    routes = routes_ref[...].astype(F32)
+    gates = gates_ref[...]
+    for k in range(2):
+        meta_ref[k : k + 1, :] = row_of(routes[:, k : k + 1])
+        meta_ref[2 + k : 3 + k, :] = row_of(gates[:, k : k + 1])
+    meta_ref[4:8, :] = jnp.zeros((4, rows), F32)
+
+
+def gather_rows(whole, own_ref, near, far, core):
+    half = own_ref.shape[0] // 2
+    whole[0 : 2 * half, :] = own_ref[...]
+    for r in range(3):
+        start = 2 * half * (r + 1)
+        whole[pl.ds(pl.multiple_of(start + core * half, half), half), :] = near[r][...]
+        whole[pl.ds(pl.multiple_of(start + (1 - core) * half, half), half), :] = far[r][...]
+
+
+def forward_kernel(*refs):
+    (xo, x1, x2, x3, y1, y2, y3, m0, m1, m2, m3, p0, p1, p2, p3, up, down) = refs[:17]
+    keep, send, cross_o, act_o, dfac_o, gram_o, pick_o, gate_o, pair_o = refs[17:26]
+    whole, flipped = refs[26:]
+    j = lax.axis_index("tensor")
+    core = lax.rem(j, 2)
+    xi = j // 2
+    first = lax.axis_index("expert") * 2
+    gather_rows(whole, xo, (x1, x2, x3), (y1, y2, y3), core)
+    for k, piece in enumerate((p0, p1, p2, p3)):
+        at = pl.multiple_of((j ^ k) * 256, 256)
+        for e in range(2):
+            pair_o[e, :, pl.ds(at, 256)] = piece[e]
+    meta = jnp.concatenate([m0[...], m1[...], m2[...], m3[...]], axis=1)
+    tokens = meta.shape[1]
+    before = (
+        lax.broadcasted_iota(jnp.int32, (tokens, tokens), 0)
+        < lax.broadcasted_iota(jnp.int32, (tokens, tokens), 1)
+    ).astype(F32).astype(BF16)
+    for e in range(2):
+        mine = (first + e).astype(F32)
+        s0 = meta[0:1, :] == mine
+        s1 = meta[1:2, :] == mine
+        named = jnp.where(s0, 1.0, 0.0) + jnp.where(s1, 1.0, 0.0)
+        gate = jnp.where(s0, meta[2:3, :], 0.0) + jnp.where(s1, meta[3:4, :], 0.0)
+        place = mm(jnp.broadcast_to(named, (8, tokens)).astype(BF16), before)[0:1, :]
+        place = jnp.where(named > 0.5, place, -1.0)
+        slot = lax.broadcasted_iota(jnp.int32, (256, tokens), 0).astype(F32)
+        hit = slot == place
+        pick = jnp.where(hit, 1.0, 0.0).astype(BF16)
+        gate_o[e] = jnp.broadcast_to(
+            jnp.sum(jnp.where(hit, gate, 0.0), axis=1, keepdims=True), (256, 128)
+        )
+        pick_o[e] = pick
+        rows = mm(pick, whole[...])
+        flipped[...] = rows.T
+
+        def gram_step(i, carry):
+            left = flipped[pl.ds(pl.multiple_of(i * 64, 64), 64), :]
+            out = []
+            for q in range(16):
+                prod = left * flipped[q * 64 : q * 64 + 64, :]
+                out.append(jnp.sum(prod, axis=0, keepdims=True))
+            block = jnp.concatenate(out, axis=0) * (1.0 / DE)
+            gram_o[e, pl.ds(pl.multiple_of(i * 16, 16), 16), :] = block.astype(BF16)
+            return carry
+
+        lax.fori_loop(0, 16, gram_step, 0)
+        cross = (rows + mm(gram_o[e], pair_o[e], TN)).astype(BF16)
+        cross_o[e] = cross
+        pre = mm(cross, up[e])
+        sig = jax.nn.sigmoid(pre)
+        act = (pre * sig).astype(BF16)
+        act_o[e] = act
+        dfac_o[e] = sig * (1.0 + pre * (1.0 - sig))
+        for xr in range(2):
+            for part in range(2):
+                block = 2 * (xi ^ xr) + (core ^ part)
+                at = pl.multiple_of(block * 256, 256)
+                term = mm(act, down[e, :, pl.ds(at, 256)]).astype(BF16)
+                (keep, send)[part][xr, e * 256 : e * 256 + 256, :] = term
+
+
+def backward_kernel(*refs):
+    (co, c1, c2, c3, d1, d2, d3, pick, gate, dfac, pair, up, down) = refs[:13]
+    keep, send, grad_o, pre_o = refs[13:17]
+    whole, terms = refs[17:]
+    j = lax.axis_index("tensor")
+    core = lax.rem(j, 2)
+    xi = j // 2
+    gather_rows(whole, co, (c1, c2, c3), (d1, d2, d3), core)
+    a = lax.broadcasted_iota(jnp.int32, (256, 256), 0)
+    b = lax.broadcasted_iota(jnp.int32, (256, 256), 1)
+    swapped = (a % 16) * 16 + a // 16
+    both = (jnp.where(a == b, 1.0, 0.0) + jnp.where(swapped == b, 1.0, 0.0)).astype(BF16)
+    for e in range(2):
+        grad = (gate[e][:, 0:1] * mm(pick[e], whole[...])).astype(BF16)
+        grad_o[e] = grad
+        grad_act = mm(grad, down[e], NT)
+        pre = (grad_act * dfac[e]).astype(BF16)
+        pre_o[e] = pre
+        terms[...] = mm(pre, up[e], NT).astype(BF16)
+        back = mm(pair[e], terms[...], NT).astype(BF16)
+        back = mm(both, back).astype(BF16)
+        wide = back.reshape(4, 64, 256)
+        for xr in range(2):
+            for part in range(2):
+                block = 2 * (xi ^ xr) + (core ^ part)
+                at = pl.multiple_of(block * 256, 256)
+                dst = (keep, send)[part]
+                dst[xr, e * 256 : e * 256 + 256, :] = terms[:, pl.ds(at, 256)]
+        for q in range(4):
+            rel = q ^ j
+
+            for xr in range(2):
+                for part in range(2):
+                    @pl.when(rel == 2 * xr + part)
+                    def _():
+                        dst = (keep, send)[part]
+                        dst[xr, 512 + e * 64 : 512 + e * 64 + 64, :] = wide[q]
+
+
+def weights_kernel(act, grad, cross, pre, down_o, up_o):
+    for e in range(2):
+        down_o[e] = mm(act[e], grad[e], TN).astype(BF16)
+        up_o[e] = mm(cross[e], pre[e], TN).astype(BF16)
+
+
+def add2(a, b):
+    return (a.astype(F32) + b.astype(F32)).astype(BF16)
+
+
+def mixed_kernel(mine, theirs, pick, gate, out_o):
+    total = jnp.zeros((512, 256), F32)
+    for e in range(2):
+        at = slice(e * 256, e * 256 + 256)
+        rows = add2(mine[at, :], theirs[at, :]).astype(F32)
+        rows = (rows * gate[e][:, 0:1]).astype(BF16)
+        total = total + mm(pick[e], rows, TN)
+    total = total.astype(BF16)
+    for r in range(4):
+        out_o[r] = total[r * 128 : r * 128 + 128, :]
+
+
+def combine_kernel(mine, theirs, pick, out_o, rows_o):
+    total = jnp.zeros((512, 256), F32)
+    back = jnp.zeros((64, 512), F32)
+    for e in range(2):
+        at = slice(e * 256, e * 256 + 256)
+        rows = add2(mine[at, :], theirs[at, :])
+        rows_o[e] = rows
+        total = total + mm(pick[e], rows, TN)
+        sat = slice(512 + e * 64, 512 + e * 64 + 64)
+        back = back + mm(add2(mine[sat, :], theirs[sat, :]), pick[e])
+    total = total.astype(BF16)
+    back = back.astype(BF16)
+    for r in range(4):
+        out_o[r, 0:128, :] = total[r * 128 : r * 128 + 128, :]
+        part = back[:, r * 128 : r * 128 + 128]
+        out_o[r, 128:160, 0:128] = part[0:32]
+        out_o[r, 128:160, 128:256] = part[32:64]
+
+
+def pair_kernel(gram, rows, out_o):
+    for e in range(2):
+        out_o[e] = mm(gram[e], rows[e]).astype(BF16)
+
+
+def final_kernel(x, c, n0, n1, n2, n3, g0, g1, g2, g3, mixed_o, grad_o, flipped):
+    j = lax.axis_index("tensor")
+    at = pl.multiple_of(j * 256, 256)
+    total = x[:, pl.ds(at, 256)].astype(F32)
+    for n in (n0, n1, n2, n3):
+        total = total + n[...].astype(F32)
+    mixed_o[...] = total.astype(BF16)
+    flipped[...] = x[...].astype(F32).T
+    total = c[:, pl.ds(at, 256)].astype(F32)
+    back = jnp.zeros((32, 256), F32)
+    for g in (g0, g1, g2, g3):
+        total = total + g[0:128, :].astype(F32)
+        back = back + g[128:160, :].astype(F32)
+    back = jnp.concatenate([back[:, 0:128], back[:, 128:256]], axis=0)
+    pieces = []
+    for i in range(4):
+        acc = jnp.zeros((64, 128), F32)
+        for q in range(16):
+            acc = acc + back[i * 16 + q : i * 16 + q + 1, :] * flipped[q * 64 : q * 64 + 64, :]
+        pieces.append(acc)
+    gram_back = jnp.concatenate(pieces, axis=0) * (1.0 / DE)
+    grad_o[...] = (total + gram_back.T).astype(BF16)
+
+
+def swap(value, axis, mask):
+    size = lax.axis_size(axis)
+    return lax.ppermute(value, axis, [(i, i ^ mask) for i in range(size)])
+
+
+def gathered_body(inputs, cotangent, gate_values, routes, pair_weight, up_weight, down_weight):
+    core = lax.axis_index("tensor") % 2
+    half = inputs.shape[0] // 2
+    x_half = lax.dynamic_slice_in_dim(inputs, core * half, half, 0)
+    c_half = lax.dynamic_slice_in_dim(cotangent, core * half, half, 0)
+    meta = kernel_call(meta_kernel, shape((8, 128), F32))(gate_values, routes)
+    x_near = [swap(x_half, "expert", r) for r in (1, 2, 3)]
+    metas = [meta] + [swap(meta, "expert", r) for r in (1, 2, 3)]
+    c_near = [swap(c_half, "expert", r) for r in (1, 2, 3)]
+    pair_x = swap(pair_weight, "tensor", 2)
+    pair_c = swap(pair_weight, "tensor", 1)
+    x_far = [swap(v, "tensor", 1) for v in x_near]
+    pair_d = swap(pair_x, "tensor", 1)
+    forward = kernel_call(
+        forward_kernel,
+        (
+            shape((2, 512, 256)),
+            shape((2, 512, 256)),
+            shape((2, 256, 1024)),
+            shape((2, 256, 512)),
+            shape((2, 256, 512), F32),
+            shape((2, 256, 256)),
+            shape((2, 256, 512)),
+            shape((2, 256, 128), F32),
+            shape((2, 256, 1024)),
+        ),
+        scratch=[pltpu.VMEM((512, 1024), BF16), pltpu.VMEM((1024, 256), F32)],
+        flops=4_000_000_000,
+        nbytes=10_000_000,
+    )
+    keep, send, cross, act, dfac, gram, pick, gate, pair_all = forward(
+        inputs, *x_near, *x_far, *metas, pair_weight, pair_c, pair_x, pair_d, up_weight, down_weight
+    )
+    got = swap(send, "tensor", 1)
+    out_there = swap(add2(keep[1], got[1]), "tensor", 2)
+    out_here = add2(keep[0], got[0])
+    c_far = [swap(v, "tensor", 1) for v in c_near]
+    backward = kernel_call(
+        backward_kernel,
+        (
+            shape((2, 640, 256)),
+            shape((2, 640, 256)),
+            shape((2, 256, 1024)),
+            shape((2, 256, 512)),
+        ),
+        scratch=[pltpu.VMEM((512, 1024), BF16), pltpu.VMEM((256, 1024), BF16)],
+        flops=2_000_000_000,
+        nbytes=10_000_000,
+    )
+    bkeep, bsend, grad, pre = backward(
+        cotangent, *c_near, *c_far, pick, gate, dfac, pair_all, up_weight, down_weight
+    )
+    bgot = swap(bsend, "tensor", 1)
+    back_there = swap(add2(bkeep[1], bgot[1]), "tensor", 2)
+    back_here = add2(bkeep[0], bgot[0])
+    mixed_parts = kernel_call(
+        mixed_kernel, shape((4, 128, 256)), flops=300_000_000, nbytes=2_000_000
+    )(out_here, out_there, pick, gate)
+    mixed_got = [mixed_parts[0]] + [swap(mixed_parts[r], "expert", r) for r in (1, 2, 3)]
+    grad_down, grad_up = kernel_call(
+        weights_kernel,
+        (shape((2, 512, 1024)), shape((2, 1024, 512))),
+        flops=3_000_000_000,
+        nbytes=8_000_000,
+    )(act, grad, cross, pre)
+    grad_parts, rows = kernel_call(
+        combine_kernel,
+        (shape((4, 160, 256)), shape((2, 256, 256))),
+        flops=300_000_000,
+        nbytes=2_000_000,
+    )(back_here, back_there, pick)
+    grad_got = [grad_parts[0]] + [swap(grad_parts[r], "expert", r) for r in (1, 2, 3)]
+    grad_pair = kernel_call(
+        pair_kernel, shape((2, 256, 256)), flops=300_000_000, nbytes=2_000_000
+    )(gram, rows)
+    mixed, grad_input = kernel_call(
+        final_kernel,
+        (shape((128, 256)), shape((128, 256))),
+        scratch=[pltpu.VMEM((1024, 128), F32)],
+        flops=100_000_000,
+        nbytes=1_000_000,
+    )(inputs, cotangent, *mixed_got, *grad_got)
+    return mixed, grad_input, grad_pair, grad_up, grad_down
+
+
 def solution(mesh):
     placed = (
         P(("group", "expert"), None),
@@ -153,8 +471,9 @@
         P("expert", None, "tensor"),
         P("expert", "tensor", None),
     )
+    small = mesh.shape["expert"] == 4 and mesh.shape["tensor"] == 4
     return jax.shard_map(
-        body,
+        gathered_body if small else body,
         mesh=mesh,
         in_specs=placed,
         out_specs=(

time: 238 us -> 86.1 us (0.36)
  waiting for transfers between devices: 124 us -> 23.1 us
  matrix products: 36.6 us -> 0 us
  local copies, waits for them, and re-layouts: 33.6 us -> 6.57 us
  Pallas kernels: 0 us -> 22 us
  between operations: 14 us -> 0.75 us
  starting transfers between devices: 19.9 us -> 33.1 us
  other arithmetic: 8.36 us -> 0.28 us
    psum x1 -> x0, waiting for transfers between devices: 47.1 us -> none  [body(): lax.psum(pair_terms.astype(jnp.bfloat16), 'tensor').astype(jnp.float32)]
    all_to_all x4 -> x0, waiting for transfers between devices: 38.8 us -> none  [the longest x1 22.3 us: body(): lax.all_to_all(input_slots.reshape(send_shape), 'expert', split_axis=0, c...]
    dot_general x15 -> x0, matrix products: 36.6 us -> none  [the longest x1 5.1 us: body(): jnp.einsum('eijr,ejdr->eidr', symmetric_mine, cells.astype(jnp.float32),...]
    ppermute x0 -> x28, starting transfers between devices: none -> 33.1 us  [swap(): return lax.ppermute(value, axis, [(i, i ^ mask) for i in range(size)])]
    reduce_scatter x2 -> x0, waiting for transfers between devices: 32.7 us -> none  [the longest x1 17.9 us: body(): lax.psum_scatter(out_terms.astype(jnp.bfloat16), 'tensor', scatter_dimens...]
    ppermute x0 -> x28, waiting for transfers between devices: none -> 23.1 us  [swap(): return lax.ppermute(value, axis, [(i, i ^ mask) for i in range(size)])]
    pallas_call x0 -> x8, Pallas kernels: none -> 22 us  [the longest x1 10.1 us: gathered_body(): forward(inputs, *x_near, *x_far, *metas, pair_weight, pair_c, pair_x, pai...]
    all_to_all x4 -> x0, starting transfers between devices: 19.8 us -> none  [the longest x1 6.32 us: body(): lax.all_to_all(input_slots.reshape(send_shape), 'expert', split_axis=0, c...]
  transfers between devices with their start and end apart: 8 -> 28, of which waited for: 7 -> 10; matrix products, arithmetic and copies ran while one was open for 28% -> 4% of each run, Pallas kernels for 0% -> 24%
where the time goes in v1:
time: 86.1 us; the launch traced here: 85.8 us
  starting transfers between devices  33.1 us (38%)
  waiting for transfers between devices  23.1 us (27%)
  Pallas kernels  22 us (26%)
  local copies, waits for them, and re-layouts  6.57 us (8%)
    ppermute x28, starting transfers between devices, swap(): return lax.ppermute(value, axis, [(i, i ^ mask) for i in range(size)])  33.1 us
    ppermute x28, waiting for transfers between devices, swap(): return lax.ppermute(value, axis, [(i, i ^ mask) for i in range(size)])  23.1 us
    pallas_call x1, Pallas kernels, gathered_body(): forward(inputs, *x_near, *x_far, *metas, pair_weight, pair_c, pair_x, pai...  10.1 us
    pallas_call x1, Pallas kernels, gathered_body(): backward(cotangent, *c_near, *c_far, pick, gate, dfac, pair_all, up_weigh...  5.94 us
    unnamed x12, local copies, waits for them, and re-layouts  4.7 us
    pallas_call x1, Pallas kernels, gathered_body(): kernel_call(weights_kernel, (shape((2, 512, 1024)), shape((2, 1024, 512))...  3.02 us
  transfers between devices with their start and end apart: 28, of which 10 were waited for; matrix products, arithmetic and copies ran while one was open for 4% of the time, Pallas kernels for 24%

profile of v1, /device:TPU:0, one launch (start us, length us, event | category | flops | bytes accessed | tf_op | source)
XLA Modules:
  0.0 85.8 jit_solution(8582540248111358947)
XLA Ops:
  0.6 3.0 %collective-permute-start.10 = (bf16[2,256,256]{2,1,0:T(8,128)(2,1)}, bf16[2,256,256]{2,1,0:T(8,128)(2,1)S(1)}, u32[]{:S(2)}, u32[]{:S(2)}) collective-permute-start(bf16[2,256,256]{2,1,0:T(8,128)(2,1)} %refs_11_.2), channel_id=1, source_target_pairs={{0,2},{1,3},{2,0},{3,1},{4,6},{5,7},{6,4},{7,5},{8,10},{9,11},{10,... | collective-permute-start | bytes 786440 | tf_op jit(solution)/shard_map/ppermute | solution.py:376
  4.5 3.7 %collective-permute-start.19 = (bf16[64,1024]{1,0:T(8,128)(2,1)S(1)}, bf16[64,1024]{1,0:T(8,128)(2,1)S(1)}, u32[]{:S(2)}, u32[]{:S(2)}) collective-permute-start(bf16[64,1024]{1,0:T(8,128)(2,1)S(1)} %constant_dynamic-slice_fusion), channel_id=1, source_target_pairs={{0,12},{4,8},{8,4},{12,0},{1,13},{5,9},{9,5},{13,1},{2,14},{6,10},... | collective-permute-start | bytes 393224 | tf_op jit(solution)/shard_map/ppermute | solution.py:376
  10.7 3.7 %collective-permute-start.8 = (f32[8,128]{1,0:T(8,128)S(1)}, f32[8,128]{1,0:T(8,128)S(1)}, u32[]{:S(2)}, u32[]{:S(2)}) collective-permute-start(f32[8,128]{1,0:T(8,128)S(1)} %shard_map.110.refs_7_), channel_id=1, source_target_pairs={{0,12},{4,8},{8,4},{12,0},{1,13},{5,9},{9,5},{13,1},{2,14},{6,10},... | collective-permute-start | bytes 12296 | tf_op jit(solution)/shard_map/ppermute | solution.py:376
  14.4 2.9 %collective-permute-done.8.refs_10_ = f32[8,128]{1,0:T(8,128)S(1)} collective-permute-done((f32[8,128]{1,0:T(8,128)S(1)}, f32[8,128]{1,0:T(8,128)S(1)}, u32[]{:S(2)}, u32[]{:S(2)}) %collective-permute-start.8) | collective-permute-done | bytes 4128 | tf_op jit(solution)/shard_map/ppermute | solution.py:376
  17.3 3.5 %collective-permute-start.7 = (f32[8,128]{1,0:T(8,128)S(1)}, f32[8,128]{1,0:T(8,128)S(1)}, u32[]{:S(2)}, u32[]{:S(2)}) collective-permute-start(f32[8,128]{1,0:T(8,128)S(1)} %shard_map.110.refs_7_), channel_id=1, source_target_pairs={{0,8},{4,12},{8,0},{12,4},{1,9},{5,13},{9,1},{13,5},{2,10},{6,14},... | collective-permute-start | bytes 12296 | tf_op jit(solution)/shard_map/ppermute | solution.py:376
  20.8 1.6 %collective-permute-done.7.refs_9_ = f32[8,128]{1,0:T(8,128)S(1)} collective-permute-done((f32[8,128]{1,0:T(8,128)S(1)}, f32[8,128]{1,0:T(8,128)S(1)}, u32[]{:S(2)}, u32[]{:S(2)}) %collective-permute-start.7) | collective-permute-done | bytes 4128 | tf_op jit(solution)/shard_map/ppermute | solution.py:376
  22.3 1.9 %collective-permute-start.6 = (f32[8,128]{1,0:T(8,128)S(1)}, f32[8,128]{1,0:T(8,128)S(1)}, u32[]{:S(2)}, u32[]{:S(2)}) collective-permute-start(f32[8,128]{1,0:T(8,128)S(1)} %shard_map.110.refs_7_), channel_id=1, source_target_pairs={{0,4},{4,0},{8,12},{12,8},{1,5},{5,1},{9,13},{13,9},{2,6},{6,2},{1... | collective-permute-start | bytes 12296 | tf_op jit(solution)/shard_map/ppermute | solution.py:376
  26.0 3.0 %collective-permute-start.2 = (bf16[64,1024]{1,0:T(8,128)(2,1)S(1)}, bf16[64,1024]{1,0:T(8,128)(2,1)S(1)}, u32[]{:S(2)}, u32[]{:S(2)}) collective-permute-start(bf16[64,1024]{1,0:T(8,128)(2,1)S(1)} %constant_dynamic-slice_fusion.1), channel_id=1, source_target_pairs={{0,12},{4,8},{8,4},{12,0},{1,13},{5,9},{9,5},{13,1},{2,14},{6,10},... | collective-permute-start | bytes 393224 | tf_op jit(solution)/shard_map/ppermute | solution.py:376
  29.4 1.0 %collective-permute-start = (bf16[64,1024]{1,0:T(8,128)(2,1)S(1)}, bf16[64,1024]{1,0:T(8,128)(2,1)S(1)}, u32[]{:S(2)}, u32[]{:S(2)}) collective-permute-start(bf16[64,1024]{1,0:T(8,128)(2,1)S(1)} %constant_dynamic-slice_fusion.1), channel_id=1, source_target_pairs={{0,4},{4,0},{8,12},{12,8},{1,5},{5,1},{9,13},{13,9},{2,6},{6,2},{1... | collective-permute-start | bytes 393224 | tf_op jit(solution)/shard_map/ppermute | solution.py:376
  30.9 2.2 %collective-permute-done.2.refs_3_ = bf16[64,1024]{1,0:T(8,128)(2,1)S(1)} collective-permute-done((bf16[64,1024]{1,0:T(8,128)(2,1)S(1)}, bf16[64,1024]{1,0:T(8,128)(2,1)S(1)}, u32[]{:S(2)}, u32[]{:S(2)}) %collective-permute-start.2) | collective-permute-done | bytes 131104 | tf_op jit(solution)/shard_map/ppermute | solution.py:376
  33.1 4.8 %collective-permute-done.1.refs_2_ = bf16[64,1024]{1,0:T(8,128)(2,1)S(1)} collective-permute-done((bf16[64,1024]{1,0:T(8,128)(2,1)S(1)}, bf16[64,1024]{1,0:T(8,128)(2,1)S(1)}, u32[]{:S(2)}, u32[]{:S(2)}) %collective-permute-start.1) | collective-permute-done | bytes 131104 | tf_op jit(solution)/shard_map/ppermute | solution.py:376
  40.8 0.9 %copy-done.4 = bf16[2,256,256]{2,1,0:T(8,128)(2,1)S(1)} copy-done((bf16[2,256,256]{2,1,0:T(8,128)(2,1)S(1)}, bf16[2,256,256]{2,1,0:T(8,128)(2,1)}, u32[]{:S(2)}) %copy-start.4) | copy-done | bytes 262168
  41.7 10.1 %shard_map.111 = (bf16[2,512,256]{2,1,0:T(8,128)(2,1)S(1)}, bf16[2,512,256]{2,1,0:T(8,128)(2,1)S(1)}, bf16[2,256,1024]{2,1,0:T(8,128)(2,1)S(1)}, bf16[2,256,512]...) custom-call(bf16[128,1024]{1,0:T(8,128)(2,1)S(1)} %copy-done.2, ...), custom_call_target="tpu_custom_call" | custom-call | flops 4000000000 | bytes 10000000 | tf_op jit(solution)/shard_map/pallas_call | solution.py:409
  52.1 1.2 %copy-done.1 = f32[2,256,512]{2,1,0:T(8,128)S(1)} copy-done((f32[2,256,512]{2,1,0:T(8,128)S(1)}, f32[2,256,512]{2,1,0:T(8,128)}, u32[]{:S(2)}) %copy-start.1) | copy-done | bytes 1048600
  53.3 5.9 %shard_map.113 = (bf16[2,640,256]{2,1,0:T(8,128)(2,1)S(1)}, bf16[2,640,256]{2,1,0:T(8,128)(2,1)S(1)}, bf16[2,256,1024]{2,1,0:T(8,128)(2,1)S(1)}, bf16[2,256,512]{2,1,0:T(8,128)(2,1)S(1)}) custom-call(bf16[128,1024]{1,0:T(8,128)(2,1)S(1)} %copy-done, bf16[64,1024]{1,0:T(8,128)(2,1)S(1)} %collective-permute-done.17.refs_1_, ...), custom_call_target="tpu_custom_call" | custom-call | flops 2000000000 | bytes 10000000 | tf_op jit(solution)/shard_map/pallas_call | solution.py:428
  60.3 1.1 %collective-permute-done.23 = bf16[2,640,256]{2,1,0:T(8,128)(2,1)S(1)} collective-permute-done((bf16[2,640,256]{2,1,0:T(8,128)(2,1)S(1)}, bf16[2,640,256]{2,1,0:T(8,128)(2,1)S(1)}, u32[]{:S(2)}, u32[]{:S(2)}) %collective-permute-start.23) | collective-permute-done | bytes 655392 | tf_op jit(solution)/shard_map/ppermute | solution.py:376
  62.1 6.8 %collective-permute-done.13.theirs = bf16[512,256]{1,0:T(8,128)(2,1)S(1)} collective-permute-done((bf16[512,256]{1,0:T(8,128)(2,1)S(1)}, bf16[512,256]{1,0:T(8,128)(2,1)S(1)}, u32[]{:S(2)}, u32[]{:S(2)}) %collective-permute-start.13) | collective-permute-done | bytes 262176 | tf_op jit(solution)/shard_map/ppermute | solution.py:376
  69.4 2.2 %collective-permute-start.16 = (bf16[128,256]{1,0:T(8,128)(2,1)S(1)}, bf16[128,256]{1,0:T(8,128)(2,1)S(1)}, u32[]{:S(2)}, u32[]{:S(2)}) collective-permute-start(bf16[128,256]{1,0:T(8,128)(2,1)S(1)} %get-tuple-element.51), channel_id=1, source_target_pairs={{0,12},{4,8},{8,4},{12,0},{1,13},{5,9},{9,5},{13,1},{2,14},{6,10},... | collective-permute-start | bytes 196616 | tf_op jit(solution)/shard_map/ppermute | solution.py:376
  71.7 2.2 %collective-permute-start.14 = (bf16[128,256]{1,0:T(8,128)(2,1)S(1)}, bf16[128,256]{1,0:T(8,128)(2,1)S(1)}, u32[]{:S(2)}, u32[]{:S(2)}) collective-permute-start(bf16[128,256]{1,0:T(8,128)(2,1)S(1)} %get-tuple-element.53), channel_id=1, source_target_pairs={{0,4},{4,0},{8,12},{12,8},{1,5},{5,1},{9,13},{13,9},{2,6},{6,2},{1... | collective-permute-start | bytes 196616 | tf_op jit(solution)/shard_map/ppermute | solution.py:376
  73.9 1.4 %collective-permute-done.24.theirs = bf16[640,256]{1,0:T(8,128)(2,1)S(1)} collective-permute-done((bf16[640,256]{1,0:T(8,128)(2,1)S(1)}, bf16[640,256]{1,0:T(8,128)(2,1)S(1)}, u32[]{:S(2)}, u32[]{:S(2)}) %collective-permute-start.24) | collective-permute-done | bytes 327712 | tf_op jit(solution)/shard_map/ppermute | solution.py:376
  75.7 2.2 %collective-permute-start.27 = (bf16[160,256]{1,0:T(8,128)(2,1)S(1)}, bf16[160,256]{1,0:T(8,128)(2,1)S(1)}, u32[]{:S(2)}, u32[]{:S(2)}) collective-permute-start(bf16[160,256]{1,0:T(8,128)(2,1)S(1)} %get-tuple-element.47), channel_id=1, source_target_pairs={{0,12},{4,8},{8,4},{12,0},{1,13},{5,9},{9,5},{13,1},{2,14},{6,10},... | collective-permute-start | bytes 245768 | tf_op jit(solution)/shard_map/ppermute | solution.py:376
  77.9 2.2 %collective-permute-start.25 = (bf16[160,256]{1,0:T(8,128)(2,1)S(1)}, bf16[160,256]{1,0:T(8,128)(2,1)S(1)}, u32[]{:S(2)}, u32[]{:S(2)}) collective-permute-start(bf16[160,256]{1,0:T(8,128)(2,1)S(1)} %get-tuple-element.49), channel_id=1, source_target_pairs={{0,4},{4,0},{8,12},{12,8},{1,5},{5,1},{9,13},{13,9},{2,6},{6,2},{1... | collective-permute-start | bytes 245768 | tf_op jit(solution)/shard_map/ppermute | solution.py:376
  80.2 3.0 %shard_map.117 = (bf16[2,512,1024]{2,1,0:T(8,128)(2,1)}, bf16[2,1024,512]{2,1,0:T(8,128)(2,1)}) custom-call(bf16[2,256,512]{2,1,0:T(8,128)(2,1)S(1)} %get-tuple-element.37.act, bf16[2,256,1024]{2,1,0:T(8,128)(2,1)S(1)} %get-tuple-element.38.grad, bf16[2,256,1024]{2,1,0:T(8,128)(2,1)S(1)} %get-tuple-element.39.cross, ...), custom_call_target="tpu_custom_call" | custom-call | flops 3000000000 | bytes 8000000 | tf_op jit(solution)/shard_map/pallas_call | solution.py:438
  84.8 1.0 %shard_map.115 = (bf16[128,256]{1,0:T(8,128)(2,1)}, bf16[128,256]{1,0:T(8,128)(2,1)}) custom-call(bf16[128,1024]{1,0:T(8,128)(2,1)S(1)} %copy-done.3, bf16[128,1024]{1,0:T(8,128)(2,1)S(1)} %copy-done, bf16[128,256]{1,0:T(8,128)(2,1)S(1)} %get-tuple-element.54.n0, bf16[128,256]{1,0:T(8,128)(2,1)S(1)} %collective-permute-done.14.n1, ...), custom_call_target="tpu_custom_call" | custom-call | flops 100000000 | bytes 1000000 | tf_op jit(solution)/shard_map/pallas_call | solution.py:454
  (58 shorter events, 13.4 us)
Async XLA Ops:
  0.6 29.7 %collective-permute-start.10 = (bf16[2,256,256]{2,1,0:T(8,128)(2,1)}, bf16[2,256,256]{2,1,0:T(8,128)(2,1)S(1)}, u32[]{:S(2)}, u32[]{:S(2)}) collective-permute-start(bf16[2,256,256]{2,1,0:T(8,128)(2,1)} %refs_11_.2), channel_id=1, source_target_pairs={{0,2},{1,3},{2,0},{3,1},{4,6},{5,7},{6,4},{7,5},{8,10},{9,11},{10,... | collective-permute-start | bytes 786440 | tf_op jit(solution)/shard_map/ppermute | solution.py:376
  4.5 24.4 %collective-permute-start.19 = (bf16[64,1024]{1,0:T(8,128)(2,1)S(1)}, bf16[64,1024]{1,0:T(8,128)(2,1)S(1)}, u32[]{:S(2)}, u32[]{:S(2)}) collective-permute-start(bf16[64,1024]{1,0:T(8,128)(2,1)S(1)} %constant_dynamic-slice_fusion), channel_id=1, source_target_pairs={{0,12},{4,8},{8,4},{12,0},{1,13},{5,9},{9,5},{13,1},{2,14},{6,10},... | collective-permute-start | bytes 393224 | tf_op jit(solution)/shard_map/ppermute | solution.py:376
  8.2 21.2 %collective-permute-start.18 = (bf16[64,1024]{1,0:T(8,128)(2,1)S(1)}, bf16[64,1024]{1,0:T(8,128)(2,1)S(1)}, u32[]{:S(2)}, u32[]{:S(2)}) collective-permute-start(bf16[64,1024]{1,0:T(8,128)(2,1)S(1)} %constant_dynamic-slice_fusion), channel_id=1, source_target_pairs={{0,8},{4,12},{8,0},{12,4},{1,9},{5,13},{9,1},{13,5},{2,10},{6,14},... | collective-permute-start | bytes 393224 | tf_op jit(solution)/shard_map/ppermute | solution.py:376
  8.2 22.1 %collective-permute-start.17 = (bf16[64,1024]{1,0:T(8,128)(2,1)S(1)}, bf16[64,1024]{1,0:T(8,128)(2,1)S(1)}, u32[]{:S(2)}, u32[]{:S(2)}) collective-permute-start(bf16[64,1024]{1,0:T(8,128)(2,1)S(1)} %constant_dynamic-slice_fusion), channel_id=1, source_target_pairs={{0,4},{4,0},{8,12},{12,8},{1,5},{5,1},{9,13},{13,9},{2,6},{6,2},{1... | collective-permute-start | bytes 393224 | tf_op jit(solution)/shard_map/ppermute | solution.py:376
  10.7 6.6 %collective-permute-start.8 = (f32[8,128]{1,0:T(8,128)S(1)}, f32[8,128]{1,0:T(8,128)S(1)}, u32[]{:S(2)}, u32[]{:S(2)}) collective-permute-start(f32[8,128]{1,0:T(8,128)S(1)} %shard_map.110.refs_7_), channel_id=1, source_target_pairs={{0,12},{4,8},{8,4},{12,0},{1,13},{5,9},{9,5},{13,1},{2,14},{6,10},... | collective-permute-start | bytes 12296 | tf_op jit(solution)/shard_map/ppermute | solution.py:376
  17.3 5.1 %collective-permute-start.7 = (f32[8,128]{1,0:T(8,128)S(1)}, f32[8,128]{1,0:T(8,128)S(1)}, u32[]{:S(2)}, u32[]{:S(2)}) collective-permute-start(f32[8,128]{1,0:T(8,128)S(1)} %shard_map.110.refs_7_), channel_id=1, source_target_pairs={{0,8},{4,12},{8,0},{12,4},{1,9},{5,13},{9,1},{13,5},{2,10},{6,14},... | collective-permute-start | bytes 12296 | tf_op jit(solution)/shard_map/ppermute | solution.py:376
  26.0 7.2 %collective-permute-start.2 = (bf16[64,1024]{1,0:T(8,128)(2,1)S(1)}, bf16[64,1024]{1,0:T(8,128)(2,1)S(1)}, u32[]{:S(2)}, u32[]{:S(2)}) collective-permute-start(bf16[64,1024]{1,0:T(8,128)(2,1)S(1)} %constant_dynamic-slice_fusion.1), channel_id=1, source_target_pairs={{0,12},{4,8},{8,4},{12,0},{1,13},{5,9},{9,5},{13,1},{2,14},{6,10},... | collective-permute-start | bytes 393224 | tf_op jit(solution)/shard_map/ppermute | solution.py:376
  28.9 9.0 %collective-permute-start.1 = (bf16[64,1024]{1,0:T(8,128)(2,1)S(1)}, bf16[64,1024]{1,0:T(8,128)(2,1)S(1)}, u32[]{:S(2)}, u32[]{:S(2)}) collective-permute-start(bf16[64,1024]{1,0:T(8,128)(2,1)S(1)} %constant_dynamic-slice_fusion.1), channel_id=1, source_target_pairs={{0,8},{4,12},{8,0},{12,4},{1,9},{5,13},{9,1},{13,5},{2,10},{6,14},... | collective-permute-start | bytes 393224 | tf_op jit(solution)/shard_map/ppermute | solution.py:376
  29.4 8.6 %collective-permute-start = (bf16[64,1024]{1,0:T(8,128)(2,1)S(1)}, bf16[64,1024]{1,0:T(8,128)(2,1)S(1)}, u32[]{:S(2)}, u32[]{:S(2)}) collective-permute-start(bf16[64,1024]{1,0:T(8,128)(2,1)S(1)} %constant_dynamic-slice_fusion.1), channel_id=1, source_target_pairs={{0,4},{4,0},{8,12},{12,8},{1,5},{5,1},{9,13},{13,9},{2,6},{6,2},{1... | collective-permute-start | bytes 393224 | tf_op jit(solution)/shard_map/ppermute | solution.py:376
  30.4 9.5 %collective-permute-start.9 = (bf16[2,256,256]{2,1,0:T(8,128)(2,1)}, bf16[2,256,256]{2,1,0:T(8,128)(2,1)S(1)}, u32[]{:S(2)}, u32[]{:S(2)}) collective-permute-start(bf16[2,256,256]{2,1,0:T(8,128)(2,1)} %refs_11_.2), channel_id=1, source_target_pairs={{0,1},{1,0},{2,3},{3,2},{4,5},{5,4},{6,7},{7,6},{8,9},{9,8},{10,11... | collective-permute-start | bytes 786440 | tf_op jit(solution)/shard_map/ppermute | solution.py:376
  30.4 9.4 %collective-permute-start.11 = (bf16[2,256,256]{2,1,0:T(8,128)(2,1)S(1)}, bf16[2,256,256]{2,1,0:T(8,128)(2,1)S(1)}, u32[]{:S(2)}, u32[]{:S(2)}) collective-permute-start(bf16[2,256,256]{2,1,0:T(8,128)(2,1)S(1)} %collective-permute-done.10.refs_13_), channel_id=1, source_target_pairs={{0,1},{1,0},{2,3},{3,2},{4,5},{5,4},{6,7},{7,6},{8,9},{9,8},{10,11... | collective-permute-start | bytes 786440 | tf_op jit(solution)/shard_map/ppermute | solution.py:376
  33.1 5.3 %collective-permute-start.5 = (bf16[64,1024]{1,0:T(8,128)(2,1)S(1)}, bf16[64,1024]{1,0:T(8,128)(2,1)S(1)}, u32[]{:S(2)}, u32[]{:S(2)}) collective-permute-start(bf16[64,1024]{1,0:T(8,128)(2,1)S(1)} %collective-permute-done.2.refs_3_), channel_id=1, source_target_pairs={{0,1},{1,0},{2,3},{3,2},{4,5},{5,4},{6,7},{7,6},{8,9},{9,8},{10,11... | collective-permute-start | bytes 393224 | tf_op jit(solution)/shard_map/ppermute | solution.py:376
  38.5 13.6 %collective-permute-start.22 = (bf16[64,1024]{1,0:T(8,128)(2,1)S(1)}, bf16[64,1024]{1,0:T(8,128)(2,1)S(1)}, u32[]{:S(2)}, u32[]{:S(2)}) collective-permute-start(bf16[64,1024]{1,0:T(8,128)(2,1)S(1)} %collective-permute-done.19.refs_3_), channel_id=1, source_target_pairs={{0,1},{1,0},{2,3},{3,2},{4,5},{5,4},{6,7},{7,6},{8,9},{9,8},{10,11... | collective-permute-start | bytes 393224 | tf_op jit(solution)/shard_map/ppermute | solution.py:376
  39.3 12.8 %collective-permute-start.21 = (bf16[64,1024]{1,0:T(8,128)(2,1)S(1)}, bf16[64,1024]{1,0:T(8,128)(2,1)S(1)}, u32[]{:S(2)}, u32[]{:S(2)}) collective-permute-start(bf16[64,1024]{1,0:T(8,128)(2,1)S(1)} %collective-permute-done.18.refs_2_), channel_id=1, source_target_pairs={{0,1},{1,0},{2,3},{3,2},{4,5},{5,4},{6,7},{7,6},{8,9},{9,8},{10,11... | collective-permute-start | bytes 393224 | tf_op jit(solution)/shard_map/ppermute | solution.py:376
  39.5 12.6 %collective-permute-start.20 = (bf16[64,1024]{1,0:T(8,128)(2,1)S(1)}, bf16[64,1024]{1,0:T(8,128)(2,1)S(1)}, u32[]{:S(2)}, u32[]{:S(2)}) collective-permute-start(bf16[64,1024]{1,0:T(8,128)(2,1)S(1)} %collective-permute-done.17.refs_1_), channel_id=1, source_target_pairs={{0,1},{1,0},{2,3},{3,2},{4,5},{5,4},{6,7},{7,6},{8,9},{9,8},{10,11... | collective-permute-start | bytes 393224 | tf_op jit(solution)/shard_map/ppermute | solution.py:376
  51.8 7.8 %collective-permute-start.12 = (bf16[2,512,256]{2,1,0:T(8,128)(2,1)S(1)}, bf16[2,512,256]{2,1,0:T(8,128)(2,1)S(1)}, u32[]{:S(2)}, u32[]{:S(2)}) collective-permute-start(bf16[2,512,256]{2,1,0:T(8,128)(2,1)S(1)} %get-tuple-element.25), channel_id=1, source_target_pairs={{0,1},{1,0},{2,3},{3,2},{4,5},{5,4},{6,7},{7,6},{8,9},{9,8},{10,11... | collective-permute-start | bytes 1572872 | tf_op jit(solution)/shard_map/ppermute | solution.py:376
  59.7 9.2 %collective-permute-start.13 = (bf16[512,256]{1,0:T(8,128)(2,1)S(1)}, bf16[512,256]{1,0:T(8,128)(2,1)S(1)}, u32[]{:S(2)}, u32[]{:S(2)}) collective-permute-start(bf16[512,256]{1,0:T(8,128)(2,1)S(1)} %get-tuple-element.45), channel_id=1, source_target_pairs={{0,2},{1,3},{2,0},{3,1},{4,6},{5,7},{6,4},{7,5},{8,10},{9,11},{10,... | collective-permute-start | bytes 786440 | tf_op jit(solution)/shard_map/ppermute | solution.py:376
  61.6 13.7 %collective-permute-start.24 = (bf16[640,256]{1,0:T(8,128)(2,1)S(1)}, bf16[640,256]{1,0:T(8,128)(2,1)S(1)}, u32[]{:S(2)}, u32[]{:S(2)}) collective-permute-start(bf16[640,256]{1,0:T(8,128)(2,1)S(1)} %get-tuple-element.43), channel_id=1, source_target_pairs={{0,2},{1,3},{2,0},{3,1},{4,6},{5,7},{6,4},{7,5},{8,10},{9,11},{10,... | collective-permute-start | bytes 983048 | tf_op jit(solution)/shard_map/ppermute | solution.py:376
  69.4 8.5 %collective-permute-start.16 = (bf16[128,256]{1,0:T(8,128)(2,1)S(1)}, bf16[128,256]{1,0:T(8,128)(2,1)S(1)}, u32[]{:S(2)}, u32[]{:S(2)}) collective-permute-start(bf16[128,256]{1,0:T(8,128)(2,1)S(1)} %get-tuple-element.51), channel_id=1, source_target_pairs={{0,12},{4,8},{8,4},{12,0},{1,13},{5,9},{9,5},{13,1},{2,14},{6,10},... | collective-permute-start | bytes 196616 | tf_op jit(solution)/shard_map/ppermute | solution.py:376
  71.7 12.5 %collective-permute-start.15 = (bf16[128,256]{1,0:T(8,128)(2,1)S(1)}, bf16[128,256]{1,0:T(8,128)(2,1)S(1)}, u32[]{:S(2)}, u32[]{:S(2)}) collective-permute-start(bf16[128,256]{1,0:T(8,128)(2,1)S(1)} %get-tuple-element.52), channel_id=1, source_target_pairs={{0,8},{4,12},{8,0},{12,4},{1,9},{5,13},{9,1},{13,5},{2,10},{6,14},... | collective-permute-start | bytes 196616 | tf_op jit(solution)/shard_map/ppermute | solution.py:376
  71.7 12.5 %collective-permute-start.14 = (bf16[128,256]{1,0:T(8,128)(2,1)S(1)}, bf16[128,256]{1,0:T(8,128)(2,1)S(1)}, u32[]{:S(2)}, u32[]{:S(2)}) collective-permute-start(bf16[128,256]{1,0:T(8,128)(2,1)S(1)} %get-tuple-element.53), channel_id=1, source_target_pairs={{0,4},{4,0},{8,12},{12,8},{1,5},{5,1},{9,13},{13,9},{2,6},{6,2},{1... | collective-permute-start | bytes 196616 | tf_op jit(solution)/shard_map/ppermute | solution.py:376
  75.7 8.4 %collective-permute-start.27 = (bf16[160,256]{1,0:T(8,128)(2,1)S(1)}, bf16[160,256]{1,0:T(8,128)(2,1)S(1)}, u32[]{:S(2)}, u32[]{:S(2)}) collective-permute-start(bf16[160,256]{1,0:T(8,128)(2,1)S(1)} %get-tuple-element.47), channel_id=1, source_target_pairs={{0,12},{4,8},{8,4},{12,0},{1,13},{5,9},{9,5},{13,1},{2,14},{6,10},... | collective-permute-start | bytes 245768 | tf_op jit(solution)/shard_map/ppermute | solution.py:376
  77.9 6.9 %collective-permute-start.26 = (bf16[160,256]{1,0:T(8,128)(2,1)S(1)}, bf16[160,256]{1,0:T(8,128)(2,1)S(1)}, u32[]{:S(2)}, u32[]{:S(2)}) collective-permute-start(bf16[160,256]{1,0:T(8,128)(2,1)S(1)} %get-tuple-element.48), channel_id=1, source_target_pairs={{0,8},{4,12},{8,0},{12,4},{1,9},{5,13},{9,1},{13,5},{2,10},{6,14},... | collective-permute-start | bytes 245768 | tf_op jit(solution)/shard_map/ppermute | solution.py:376
  77.9 6.9 %collective-permute-start.25 = (bf16[160,256]{1,0:T(8,128)(2,1)S(1)}, bf16[160,256]{1,0:T(8,128)(2,1)S(1)}, u32[]{:S(2)}, u32[]{:S(2)}) collective-permute-start(bf16[160,256]{1,0:T(8,128)(2,1)S(1)} %get-tuple-element.49), channel_id=1, source_target_pairs={{0,4},{4,0},{8,12},{12,8},{1,5},{5,1},{9,13},{13,9},{2,6},{6,2},{1... | collective-permute-start | bytes 245768 | tf_op jit(solution)/shard_map/ppermute | solution.py:376
  (9 other events, 43.3 us)

commit v2 on v1

--- a/solution.py
+++ b/solution.py
@@ -159,13 +159,19 @@
     return lax.dot_general(a, b, dims, preferred_element_type=F32)
 
 
-def kernel_call(kernel, out_shape, scratch=(), flops=0, nbytes=0):
+def kernel_call(kernel, out_shape, scratch=(), flops=0, nbytes=0, waits=0, operands=0, vmem=20):
+    specs = {}
+    if waits:
+        specs["in_specs"] = [pl.BlockSpec(memory_space=pltpu.VMEM)] * (operands - waits) + [
+            pl.BlockSpec(memory_space=pl.ANY)
+        ] * waits
     return pl.pallas_call(
         kernel,
         out_shape=out_shape,
         scratch_shapes=list(scratch),
-        compiler_params=pltpu.CompilerParams(vmem_limit_bytes=48 * 1024 * 1024),
+        compiler_params=pltpu.CompilerParams(vmem_limit_bytes=vmem * 1024 * 1024),
         cost_estimate=pl.CostEstimate(flops=flops, bytes_accessed=nbytes, transcendentals=0),
+        **specs,
     )
 
 
@@ -173,21 +179,25 @@
     return jax.ShapeDtypeStruct(dims, dtype)
 
 
-def meta_kernel(gates_ref, routes_ref, meta_ref):
-    rows = gates_ref.shape[0]
-    eye = lax.broadcasted_iota(jnp.int32, (rows, rows), 0) == lax.broadcasted_iota(
-        jnp.int32, (rows, rows), 1
-    )
-
-    def row_of(column):
-        return jnp.sum(jnp.where(eye, column, 0.0), axis=0, keepdims=True)
-
-    routes = routes_ref[...].astype(F32)
-    gates = gates_ref[...]
-    for k in range(2):
-        meta_ref[k : k + 1, :] = row_of(routes[:, k : k + 1])
-        meta_ref[2 + k : 3 + k, :] = row_of(gates[:, k : k + 1])
-    meta_ref[4:8, :] = jnp.zeros((4, rows), F32)
+def input_kernel(x, gates, routes, out_o):
+    rows, width = x.shape
+    half = rows // 2
+    core = lax.rem(lax.axis_index("tensor"), 2)
+    start = pl.multiple_of(core * half, half)
+    high = gates[...].astype(BF16).astype(F32)
+    low = gates[...] - high
+    meta = jnp.concatenate(
+        [routes[...].astype(F32), high, low, jnp.zeros((rows - 6, rows), F32)], axis=0
+    )
+    out_o[:, 0:width] = x[pl.ds(start, half), :]
+    columns = meta.T
+    out_o[:, width:] = jnp.where(core == 0, columns[0:half], columns[half:]).astype(BF16)
+
+
+def cotangent_kernel(c, after, out_o):
+    half = c.shape[0] // 2
+    core = lax.rem(lax.axis_index("tensor"), 2)
+    out_o[...] = c[pl.ds(pl.multiple_of(core * half, half), half), :]
 
 
 def gather_rows(whole, own_ref, near, far, core):
@@ -195,29 +205,43 @@
     whole[0 : 2 * half, :] = own_ref[...]
     for r in range(3):
         start = 2 * half * (r + 1)
-        whole[pl.ds(pl.multiple_of(start + core * half, half), half), :] = near[r][...]
-        whole[pl.ds(pl.multiple_of(start + (1 - core) * half, half), half), :] = far[r][...]
+        whole[pl.ds(pl.multiple_of(start + core * half, half), half), :] = near[r][:, 0:1024]
+        whole[pl.ds(pl.multiple_of(start + (1 - core) * half, half), half), :] = far[r][:, 0:1024]
 
 
 def forward_kernel(*refs):
-    (xo, x1, x2, x3, y1, y2, y3, m0, m1, m2, m3, p0, p1, p2, p3, up, down) = refs[:17]
-    keep, send, cross_o, act_o, dfac_o, gram_o, pick_o, gate_o, pair_o = refs[17:26]
-    whole, flipped = refs[26:]
+    (xo, x1, x2, x3, y1, y2, y3, gates, routes, p0, p1, p2, p3, up, down) = refs[:15]
+    keep, send0, send1, send2, cross_o, act_o, dfac_o, gram_o, pick_o, gate_o, pair_o = refs[15:26]
+    whole, flipped, info, partial, half_gram = refs[26:]
     j = lax.axis_index("tensor")
     core = lax.rem(j, 2)
     xi = j // 2
     first = lax.axis_index("expert") * 2
-    gather_rows(whole, xo, (x1, x2, x3), (y1, y2, y3), core)
+    near, far = (x1, x2, x3), (y1, y2, y3)
+    gather_rows(whole, xo, near, far, core)
+    for r in range(3):
+        start = 128 * r
+        info[pl.ds(pl.multiple_of(start + core * 64, 64), 64), :] = near[r][:, 1024:]
+        info[pl.ds(pl.multiple_of(start + (1 - core) * 64, 64), 64), :] = far[r][:, 1024:]
     for k, piece in enumerate((p0, p1, p2, p3)):
         at = pl.multiple_of((j ^ k) * 256, 256)
         for e in range(2):
             pair_o[e, :, pl.ds(at, 256)] = piece[e]
-    meta = jnp.concatenate([m0[...], m1[...], m2[...], m3[...]], axis=1)
+    others = info[...].astype(F32).T
+    mine_info = jnp.concatenate([routes[...].astype(F32), gates[...]], axis=0)
+    there = jnp.concatenate([others[0:2], others[2:4] + others[4:6]], axis=0)
+    meta = jnp.concatenate([mine_info, there], axis=1)
     tokens = meta.shape[1]
     before = (
         lax.broadcasted_iota(jnp.int32, (tokens, tokens), 0)
         < lax.broadcasted_iota(jnp.int32, (tokens, tokens), 1)
     ).astype(F32).astype(BF16)
+    a = lax.broadcasted_iota(jnp.int32, (256, 144), 0)
+    n = lax.broadcasted_iota(jnp.int32, (256, 144), 1)
+    low = jnp.minimum(a // 16, a % 16)
+    high = jnp.maximum(a // 16, a % 16)
+    spread = jnp.where(low * 16 - low * (low - 1) // 2 + high - low == n, 1.0, 0.0).astype(BF16)
+    half_gram[136:144, :] = jnp.zeros((8, 256), F32)
     for e in range(2):
         mine = (first + e).astype(F32)
         s0 = meta[0:1, :] == mine
@@ -236,17 +260,22 @@
         rows = mm(pick, whole[...])
         flipped[...] = rows.T
 
-        def gram_step(i, carry):
-            left = flipped[pl.ds(pl.multiple_of(i * 64, 64), 64), :]
-            out = []
-            for q in range(16):
+        at = 0
+        for i in range(16):
+            left = flipped[i * 64 : i * 64 + 64, :]
+            for q in range(i, 16):
                 prod = left * flipped[q * 64 : q * 64 + 64, :]
-                out.append(jnp.sum(prod, axis=0, keepdims=True))
-            block = jnp.concatenate(out, axis=0) * (1.0 / DE)
-            gram_o[e, pl.ds(pl.multiple_of(i * 16, 16), 16), :] = block.astype(BF16)
-            return carry
-
-        lax.fori_loop(0, 16, gram_step, 0)
+                part = jnp.sum(prod.reshape(8, 8, 256), axis=0)
+                for lane in range(2):
+                    partial[lane, at * 8 : at * 8 + 8, :] = part[:, lane * 128 : lane * 128 + 128]
+                at += 1
+        for g in range(17):
+            for lane in range(2):
+                acc = partial[lane, pl.ds(g * 64, 8, stride=8), :]
+                for q in range(1, 8):
+                    acc = acc + partial[lane, pl.ds(g * 64 + q, 8, stride=8), :]
+                half_gram[g * 8 : g * 8 + 8, lane * 128 : lane * 128 + 128] = acc * (1.0 / DE)
+        gram_o[e] = mm(spread, half_gram[...].astype(BF16)).astype(BF16)
         cross = (rows + mm(gram_o[e], pair_o[e], TN)).astype(BF16)
         cross_o[e] = cross
         pre = mm(cross, up[e])
@@ -259,13 +288,16 @@
                 block = 2 * (xi ^ xr) + (core ^ part)
                 at = pl.multiple_of(block * 256, 256)
                 term = mm(act, down[e, :, pl.ds(at, 256)]).astype(BF16)
-                (keep, send)[part][xr, e * 256 : e * 256 + 256, :] = term
+                if part == 1 and xr == 1:
+                    (send1, send2)[e][...] = term
+                else:
+                    (keep.at[xr], send0)[part][e * 256 : e * 256 + 256, :] = term
 
 
 def backward_kernel(*refs):
-    (co, c1, c2, c3, d1, d2, d3, pick, gate, dfac, pair, up, down) = refs[:13]
-    keep, send, grad_o, pre_o = refs[13:17]
-    whole, terms = refs[17:]
+    (co, c1, c2, c3, d1, d2, d3, pick, gate, dfac, pair, up, down, after) = refs[:14]
+    keep, send0, send1, send2, grad_o, pre_o = refs[14:20]
+    whole, terms = refs[20:]
     j = lax.axis_index("tensor")
     core = lax.rem(j, 2)
     xi = j // 2
@@ -288,17 +320,16 @@
             for part in range(2):
                 block = 2 * (xi ^ xr) + (core ^ part)
                 at = pl.multiple_of(block * 256, 256)
-                dst = (keep, send)[part]
-                dst[xr, e * 256 : e * 256 + 256, :] = terms[:, pl.ds(at, 256)]
-        for q in range(4):
-            rel = q ^ j
-
-            for xr in range(2):
-                for part in range(2):
-                    @pl.when(rel == 2 * xr + part)
-                    def _():
-                        dst = (keep, send)[part]
-                        dst[xr, 512 + e * 64 : 512 + e * 64 + 64, :] = wide[q]
+                if part == 1 and xr == 1:
+                    dst, row = (send1, send2)[e], 0
+                else:
+                    dst, row = (keep.at[xr], send0)[part], e * 320
+                dst[row : row + 256, :] = terms[:, pl.ds(at, 256)]
+                for q in range(4):
+                    def put(dst=dst, row=row, q=q):
+                        dst[row + 256 : row + 320, :] = wide[q]
+
+                    pl.when(block == q)(put)
 
 
 def weights_kernel(act, grad, cross, pre, down_o, up_o):
@@ -311,11 +342,11 @@
     return (a.astype(F32) + b.astype(F32)).astype(BF16)
 
 
-def mixed_kernel(mine, theirs, pick, gate, out_o):
+def mixed_kernel(mine, other, theirs, pick, gate, out_o):
     total = jnp.zeros((512, 256), F32)
     for e in range(2):
         at = slice(e * 256, e * 256 + 256)
-        rows = add2(mine[at, :], theirs[at, :]).astype(F32)
+        rows = add2(add2(mine[0, at, :], other[at, :]), theirs[at, :]).astype(F32)
         rows = (rows * gate[e][:, 0:1]).astype(BF16)
         total = total + mm(pick[e], rows, TN)
     total = total.astype(BF16)
@@ -323,16 +354,16 @@
         out_o[r] = total[r * 128 : r * 128 + 128, :]
 
 
-def combine_kernel(mine, theirs, pick, out_o, rows_o):
+def combine_kernel(mine, other, theirs, pick, out_o, rows_o):
     total = jnp.zeros((512, 256), F32)
     back = jnp.zeros((64, 512), F32)
     for e in range(2):
-        at = slice(e * 256, e * 256 + 256)
-        rows = add2(mine[at, :], theirs[at, :])
+        at = slice(e * 320, e * 320 + 320)
+        both = add2(add2(mine[0, at, :], other[at, :]), theirs[at, :])
+        rows = both[0:256]
         rows_o[e] = rows
         total = total + mm(pick[e], rows, TN)
-        sat = slice(512 + e * 64, 512 + e * 64 + 64)
-        back = back + mm(add2(mine[sat, :], theirs[sat, :]), pick[e])
+        back = back + mm(both[256:320], pick[e])
     total = total.astype(BF16)
     back = back.astype(BF16)
     for r in range(4):
@@ -377,23 +408,24 @@
 
 
 def gathered_body(inputs, cotangent, gate_values, routes, pair_weight, up_weight, down_weight):
-    core = lax.axis_index("tensor") % 2
     half = inputs.shape[0] // 2
-    x_half = lax.dynamic_slice_in_dim(inputs, core * half, half, 0)
-    c_half = lax.dynamic_slice_in_dim(cotangent, core * half, half, 0)
-    meta = kernel_call(meta_kernel, shape((8, 128), F32))(gate_values, routes)
+    width = inputs.shape[1]
+    gates, choices = gate_values.T, routes.T
+    x_half = kernel_call(input_kernel, shape((half, width + 128)))(inputs, gates, choices)
     x_near = [swap(x_half, "expert", r) for r in (1, 2, 3)]
-    metas = [meta] + [swap(meta, "expert", r) for r in (1, 2, 3)]
-    c_near = [swap(c_half, "expert", r) for r in (1, 2, 3)]
     pair_x = swap(pair_weight, "tensor", 2)
     pair_c = swap(pair_weight, "tensor", 1)
     x_far = [swap(v, "tensor", 1) for v in x_near]
     pair_d = swap(pair_x, "tensor", 1)
+    c_half = kernel_call(cotangent_kernel, shape((half, width)), waits=1, operands=2)(cotangent, x_near[0])
+    c_near = [swap(c_half, "expert", r) for r in (1, 2, 3)]
     forward = kernel_call(
         forward_kernel,
         (
             shape((2, 512, 256)),
-            shape((2, 512, 256)),
+            shape((512, 256)),
+            shape((256, 256)),
+            shape((256, 256)),
             shape((2, 256, 1024)),
             shape((2, 256, 512)),
             shape((2, 256, 512), F32),
@@ -402,38 +434,49 @@
             shape((2, 256, 128), F32),
             shape((2, 256, 1024)),
         ),
-        scratch=[pltpu.VMEM((512, 1024), BF16), pltpu.VMEM((1024, 256), F32)],
+        scratch=[
+            pltpu.VMEM((512, 1024), BF16),
+            pltpu.VMEM((1024, 256), F32),
+            pltpu.VMEM((384, 128), BF16),
+            pltpu.VMEM((2, 1088, 128), F32),
+            pltpu.VMEM((144, 256), F32),
+        ],
         flops=4_000_000_000,
         nbytes=10_000_000,
     )
-    keep, send, cross, act, dfac, gram, pick, gate, pair_all = forward(
-        inputs, *x_near, *x_far, *metas, pair_weight, pair_c, pair_x, pair_d, up_weight, down_weight
-    )
-    got = swap(send, "tensor", 1)
-    out_there = swap(add2(keep[1], got[1]), "tensor", 2)
-    out_here = add2(keep[0], got[0])
+    keep, send0, send1, send2, cross, act, dfac, gram, pick, gate, pair_all = forward(
+        inputs, *x_near, *x_far, gates, choices, pair_weight, pair_c, pair_x, pair_d, up_weight, down_weight
+    )
+    got_here = swap(send0, "tensor", 1)
+    got_away = [swap(v, "tensor", 1) for v in (send1, send2)]
+    out_away = add2(keep[1], jnp.concatenate(got_away, axis=0))
+    out_there = swap(out_away, "tensor", 2)
     c_far = [swap(v, "tensor", 1) for v in c_near]
     backward = kernel_call(
         backward_kernel,
         (
             shape((2, 640, 256)),
-            shape((2, 640, 256)),
+            shape((640, 256)),
+            shape((320, 256)),
+            shape((320, 256)),
             shape((2, 256, 1024)),
             shape((2, 256, 512)),
         ),
         scratch=[pltpu.VMEM((512, 1024), BF16), pltpu.VMEM((256, 1024), BF16)],
+        waits=1,
+        operands=14,
         flops=2_000_000_000,
         nbytes=10_000_000,
     )
-    bkeep, bsend, grad, pre = backward(
-        cotangent, *c_near, *c_far, pick, gate, dfac, pair_all, up_weight, down_weight
-    )
-    bgot = swap(bsend, "tensor", 1)
-    back_there = swap(add2(bkeep[1], bgot[1]), "tensor", 2)
-    back_here = add2(bkeep[0], bgot[0])
+    bkeep, bsend0, bsend1, bsend2, grad, pre = backward(
+        cotangent, *c_near, *c_far, pick, gate, dfac, pair_all, up_weight, down_weight, out_away
+    )
+    bgot_here = swap(bsend0, "tensor", 1)
+    bgot_away = [swap(v, "tensor", 1) for v in (bsend1, bsend2)]
+    back_there = swap(add2(bkeep[1], jnp.concatenate(bgot_away, axis=0)), "tensor", 2)
     mixed_parts = kernel_call(
         mixed_kernel, shape((4, 128, 256)), flops=300_000_000, nbytes=2_000_000
-    )(out_here, out_there, pick, gate)
+    )(keep, got_here, out_there, pick, gate)
     mixed_got = [mixed_parts[0]] + [swap(mixed_parts[r], "expert", r) for r in (1, 2, 3)]
     grad_down, grad_up = kernel_call(
         weights_kernel,
@@ -446,7 +489,7 @@
         (shape((4, 160, 256)), shape((2, 256, 256))),
         flops=300_000_000,
         nbytes=2_000_000,
-    )(back_here, back_there, pick)
+    )(bkeep, bgot_here, back_there, pick)
     grad_got = [grad_parts[0]] + [swap(grad_parts[r], "expert", r) for r in (1, 2, 3)]
     grad_pair = kernel_call(
         pair_kernel, shape((2, 256, 256)), flops=300_000_000, nbytes=2_000_000

time: 86.1 us -> 72.8 us (0.85)
  starting transfers between devices: 33.1 us -> 25.5 us
  Pallas kernels: 22 us -> 14.5 us
  local copies, waits for them, and re-layouts: 6.57 us -> 9.75 us
  waiting for transfers between devices: 23.1 us -> 21.8 us
    ppermute x28 -> x29, starting transfers between devices: 33.1 us -> 25.5 us  [swap(): return lax.ppermute(value, axis, [(i, i ^ mask) for i in range(size)])]
    pallas_call x2 -> x3, Pallas kernels: 10.3 us -> 5.01 us  [the longest x1 4.9 us: gathered_body(): forward(inputs, *x_near, *x_far, gates, choices, pair_weight, pair_c, pai...]
    unnamed x12 -> x28, local copies, waits for them, and re-layouts: 4.7 us -> 9.71 us
    pallas_call x1, Pallas kernels: 5.94 us -> 3.63 us  [gathered_body(): backward(cotangent, *c_near, *c_far, pick, gate, dfac, pair_all, up_weigh...]
    dynamic_slice x2 -> x0, local copies, waits for them, and re-layouts: 1.83 us -> none  [the longest x1 0.91 us: gathered_body(): x_half = lax.dynamic_slice_in_dim(inputs, core * half, half, 0)]
    ppermute x28 -> x29, waiting for transfers between devices: 23.1 us -> 21.8 us  [swap(): return lax.ppermute(value, axis, [(i, i ^ mask) for i in range(size)])]
  transfers between devices with their start and end apart: 28 -> 29, of which waited for: 10 -> 12; matrix products, arithmetic and copies ran while one was open for 4% -> 0% of each run, Pallas kernels for 24% -> 14%
where the time goes in v2:
time: 72.8 us; the launch traced here: 72.5 us
  starting transfers between devices  25.5 us (35%)
  waiting for transfers between devices  21.8 us (30%)
  Pallas kernels  14.5 us (20%)
  local copies, waits for them, and re-layouts  9.75 us (13%)
  between operations  0.77 us (1%)
    ppermute x29, starting transfers between devices, swap(): return lax.ppermute(value, axis, [(i, i ^ mask) for i in range(size)])  25.5 us
    ppermute x29, waiting for transfers between devices, swap(): return lax.ppermute(value, axis, [(i, i ^ mask) for i in range(size)])  21.8 us
    unnamed x28, local copies, waits for them, and re-layouts  9.71 us
    pallas_call x1, Pallas kernels, gathered_body(): forward(inputs, *x_near, *x_far, gates, choices, pair_weight, pair_c, pai...  4.9 us
    pallas_call x1, Pallas kernels, gathered_body(): backward(cotangent, *c_near, *c_far, pick, gate, dfac, pair_all, up_weigh...  3.63 us
    pallas_call x1, Pallas kernels, gathered_body(): kernel_call(weights_kernel, (shape((2, 512, 1024)), shape((2, 1024, 512))...  3.02 us
  transfers between devices with their start and end apart: 29, of which 12 were waited for; matrix products, arithmetic and copies ran while one was open for 0% of the time, Pallas kernels for 14%

profile of v2, /device:TPU:0, one launch (start us, length us, event | category | flops | bytes accessed | tf_op | source)
XLA Modules:
  0.0 72.5 jit_solution(16200726251444888561)
XLA Ops:
  0.6 3.0 %collective-permute-start.7 = (bf16[2,256,256]{2,1,0:T(8,128)(2,1)}, bf16[2,256,256]{2,1,0:T(8,128)(2,1)S(1)}, u32[]{:S(2)}, u32[]{:S(2)}) collective-permute-start(bf16[2,256,256]{2,1,0:T(8,128)(2,1)} %refs_9_.1), channel_id=1, source_target_pairs={{0,2},{1,3},{2,0},{3,1},{4,6},{5,7},{6,4},{7,5},{8,10},{9,11},{10,... | collective-permute-start | bytes 786440 | tf_op jit(solution)/shard_map/ppermute | solution.py:407
  3.6 0.9 %copy-done.6 = bf16[128,1024]{1,0:T(8,128)(2,1)S(1)} copy-done((bf16[128,1024]{1,0:T(8,128)(2,1)S(1)}, bf16[128,1024]{1,0:T(8,128)(2,1)}, u32[]{:S(2)}) %copy-start.6) | copy-done | bytes 262168
  6.1 1.6 %collective-permute-start = (bf16[64,1152]{1,0:T(8,128)(2,1)S(1)}, bf16[64,1152]{1,0:T(8,128)(2,1)S(1)}, u32[]{:S(2)}, u32[]{:S(2)}) collective-permute-start(bf16[64,1152]{1,0:T(8,128)(2,1)S(1)} %shard_map.110), channel_id=1, source_target_pairs={{0,4},{4,0},{8,12},{12,8},{1,5},{5,1},{9,13},{13,9},{2,6},{6,2},{1... | collective-permute-start | bytes 442376 | tf_op jit(solution)/shard_map/ppermute | solution.py:407
  7.7 2.6 %collective-permute-start.1 = (bf16[64,1152]{1,0:T(8,128)(2,1)S(1)}, bf16[64,1152]{1,0:T(8,128)(2,1)S(1)}, u32[]{:S(2)}, u32[]{:S(2)}) collective-permute-start(bf16[64,1152]{1,0:T(8,128)(2,1)S(1)} %shard_map.110), channel_id=1, source_target_pairs={{0,8},{4,12},{8,0},{12,4},{1,9},{5,13},{9,1},{13,5},{2,10},{6,14},... | collective-permute-start | bytes 442376 | tf_op jit(solution)/shard_map/ppermute | solution.py:407
  11.0 2.2 %collective-permute-done.refs_1_.after = bf16[64,1152]{1,0:T(8,128)(2,1)S(1)} collective-permute-done((bf16[64,1152]{1,0:T(8,128)(2,1)S(1)}, bf16[64,1152]{1,0:T(8,128)(2,1)S(1)}, u32[]{:S(2)}, u32[]{:S(2)}) %collective-permute-start) | collective-permute-done | bytes 147488 | tf_op jit(solution)/shard_map/ppermute | solution.py:407
  13.2 8.3 %collective-permute-done.1.refs_2_ = bf16[64,1152]{1,0:T(8,128)(2,1)S(1)} collective-permute-done((bf16[64,1152]{1,0:T(8,128)(2,1)S(1)}, bf16[64,1152]{1,0:T(8,128)(2,1)S(1)}, u32[]{:S(2)}, u32[]{:S(2)}) %collective-permute-start.1) | collective-permute-done | bytes 147488 | tf_op jit(solution)/shard_map/ppermute | solution.py:407
  22.1 0.9 %copy-done = bf16[128,1024]{1,0:T(8,128)(2,1)S(1)} copy-done((bf16[128,1024]{1,0:T(8,128)(2,1)S(1)}, bf16[128,1024]{1,0:T(8,128)(2,1)}, u32[]{:S(2)}) %copy-start) | copy-done | bytes 262168
  23.1 1.7 %collective-permute-start.16 = (bf16[64,1024]{1,0:T(8,128)(2,1)S(1)}, bf16[64,1024]{1,0:T(8,128)(2,1)S(1)}, u32[]{:S(2)}, u32[]{:S(2)}) collective-permute-start(bf16[64,1024]{1,0:T(8,128)(2,1)S(1)} %shard_map.113), channel_id=1, source_target_pairs={{0,4},{4,0},{8,12},{12,8},{1,5},{5,1},{9,13},{13,9},{2,6},{6,2},{1... | collective-permute-start | bytes 393224 | tf_op jit(solution)/shard_map/ppermute | solution.py:407
  24.8 1.2 %collective-permute-start.17 = (bf16[64,1024]{1,0:T(8,128)(2,1)S(1)}, bf16[64,1024]{1,0:T(8,128)(2,1)S(1)}, u32[]{:S(2)}, u32[]{:S(2)}) collective-permute-start(bf16[64,1024]{1,0:T(8,128)(2,1)S(1)} %shard_map.113), channel_id=1, source_target_pairs={{0,8},{4,12},{8,0},{12,4},{1,9},{5,13},{9,1},{13,5},{2,10},{6,14},... | collective-permute-start | bytes 393224 | tf_op jit(solution)/shard_map/ppermute | solution.py:407
  26.0 1.6 %collective-permute-start.18 = (bf16[64,1024]{1,0:T(8,128)(2,1)S(1)}, bf16[64,1024]{1,0:T(8,128)(2,1)S(1)}, u32[]{:S(2)}, u32[]{:S(2)}) collective-permute-start(bf16[64,1024]{1,0:T(8,128)(2,1)S(1)} %shard_map.113), channel_id=1, source_target_pairs={{0,12},{4,8},{8,4},{12,0},{1,13},{5,9},{9,5},{13,1},{2,14},{6,10},... | collective-permute-start | bytes 393224 | tf_op jit(solution)/shard_map/ppermute | solution.py:407
  27.5 1.6 %copy-done.2 = bf16[2,1024,512]{2,1,0:T(8,128)(2,1)S(1)} copy-done((bf16[2,1024,512]{2,1,0:T(8,128)(2,1)S(1)}, bf16[2,1024,512]{2,1,0:T(8,128)(2,1)}, u32[]{:S(2)}) %copy-start.2) | copy-done | bytes 2097176
  29.1 1.6 %copy-done.4 = bf16[2,512,1024]{2,1,0:T(8,128)(2,1)S(1)} copy-done((bf16[2,512,1024]{2,1,0:T(8,128)(2,1)S(1)}, bf16[2,512,1024]{2,1,0:T(8,128)(2,1)}, u32[]{:S(2)}) %copy-start.4) | copy-done | bytes 2097176
  34.0 4.9 %shard_map.111 = (bf16[2,512,256]{2,1,0:T(8,128)(2,1)S(1)}, bf16[512,256]{1,0:T(8,128)(2,1)S(1)}, bf16[256,256]{1,0:T(8,128)(2,1)S(1)}, bf16[256,256]{1,0:T(8,12...) custom-call(bf16[128,1024]{1,0:T(8,128)(2,1)S(1)} %copy-done.7, ...), custom_call_target="tpu_custom_call" | custom-call | flops 4000000000 | bytes 10000000 | tf_op jit(solution)/shard_map/pallas_call | solution.py:447
  41.4 3.6 %shard_map.114 = (bf16[2,640,256]{2,1,0:T(8,128)(2,1)S(1)}, bf16[640,256]{1,0:T(8,128)(2,1)S(1)}, bf16[320,256]{1,0:T(8,128)(2,1)S(1)}, bf16[320,256]{1,0:T(8,12...) custom-call(bf16[128,1024]{1,0:T(8,128)(2,1)S(1)} %copy-done.1, ...), custom_call_target="tpu_custom_call" | custom-call | flops 2000000000 | bytes 10000000 | tf_op jit(solution)/shard_map/pallas_call | solution.py:471
  46.8 1.2 %collective-permute-start.25 = (bf16[640,256]{1,0:T(8,128)(2,1)S(1)}, bf16[640,256]{1,0:T(8,128)(2,1)S(1)}, u32[]{:S(2)}, u32[]{:S(2)}) collective-permute-start(bf16[640,256]{1,0:T(8,128)(2,1)S(1)} %fusion), channel_id=1, source_target_pairs={{0,2},{1,3},{2,0},{3,1},{4,6},{5,7},{6,4},{7,5},{8,10},{9,11},{10,... | collective-permute-start | bytes 983048 | tf_op jit(solution)/shard_map/ppermute | solution.py:407
  48.0 6.9 %collective-permute-done.12.theirs = bf16[512,256]{1,0:T(8,128)(2,1)S(1)} collective-permute-done((bf16[512,256]{1,0:T(8,128)(2,1)S(1)}, bf16[512,256]{1,0:T(8,128)(2,1)S(1)}, u32[]{:S(2)}, u32[]{:S(2)}) %collective-permute-start.12) | collective-permute-done | bytes 262176 | tf_op jit(solution)/shard_map/ppermute | solution.py:407
  56.1 2.1 %collective-permute-start.14 = (bf16[128,256]{1,0:T(8,128)(2,1)S(1)}, bf16[128,256]{1,0:T(8,128)(2,1)S(1)}, u32[]{:S(2)}, u32[]{:S(2)}) collective-permute-start(bf16[128,256]{1,0:T(8,128)(2,1)S(1)} %get-tuple-element.56), channel_id=1, source_target_pairs={{0,8},{4,12},{8,0},{12,4},{1,9},{5,13},{9,1},{13,5},{2,10},{6,14},... | collective-permute-start | bytes 196616 | tf_op jit(solution)/shard_map/ppermute | solution.py:407
  58.2 1.6 %collective-permute-start.15 = (bf16[128,256]{1,0:T(8,128)(2,1)S(1)}, bf16[128,256]{1,0:T(8,128)(2,1)S(1)}, u32[]{:S(2)}, u32[]{:S(2)}) collective-permute-start(bf16[128,256]{1,0:T(8,128)(2,1)S(1)} %get-tuple-element.55), channel_id=1, source_target_pairs={{0,12},{4,8},{8,4},{12,0},{1,13},{5,9},{9,5},{13,1},{2,14},{6,10},... | collective-permute-start | bytes 196616 | tf_op jit(solution)/shard_map/ppermute | solution.py:407
  59.8 1.5 %collective-permute-done.25.theirs = bf16[640,256]{1,0:T(8,128)(2,1)S(1)} collective-permute-done((bf16[640,256]{1,0:T(8,128)(2,1)S(1)}, bf16[640,256]{1,0:T(8,128)(2,1)S(1)}, u32[]{:S(2)}, u32[]{:S(2)}) %collective-permute-start.25) | collective-permute-done | bytes 327712 | tf_op jit(solution)/shard_map/ppermute | solution.py:407
  62.6 2.1 %collective-permute-start.27 = (bf16[160,256]{1,0:T(8,128)(2,1)S(1)}, bf16[160,256]{1,0:T(8,128)(2,1)S(1)}, u32[]{:S(2)}, u32[]{:S(2)}) collective-permute-start(bf16[160,256]{1,0:T(8,128)(2,1)S(1)} %get-tuple-element.52), channel_id=1, source_target_pairs={{0,8},{4,12},{8,0},{12,4},{1,9},{5,13},{9,1},{13,5},{2,10},{6,14},... | collective-permute-start | bytes 245768 | tf_op jit(solution)/shard_map/ppermute | solution.py:407
  64.7 1.6 %collective-permute-start.28 = (bf16[160,256]{1,0:T(8,128)(2,1)S(1)}, bf16[160,256]{1,0:T(8,128)(2,1)S(1)}, u32[]{:S(2)}, u32[]{:S(2)}) collective-permute-start(bf16[160,256]{1,0:T(8,128)(2,1)S(1)} %get-tuple-element.51), channel_id=1, source_target_pairs={{0,12},{4,8},{8,4},{12,0},{1,13},{5,9},{9,5},{13,1},{2,14},{6,10},... | collective-permute-start | bytes 245768 | tf_op jit(solution)/shard_map/ppermute | solution.py:407
  66.2 3.0 %shard_map.118 = (bf16[2,512,1024]{2,1,0:T(8,128)(2,1)}, bf16[2,1024,512]{2,1,0:T(8,128)(2,1)}) custom-call(bf16[2,256,512]{2,1,0:T(8,128)(2,1)S(1)} %get-tuple-element.45.act, bf16[2,256,1024]{2,1,0:T(8,128)(2,1)S(1)} %get-tuple-element.46.grad, bf16[2,256,1024]{2,1,0:T(8,128)(2,1)S(1)} %get-tuple-element.47.cross, ...), custom_call_target="tpu_custom_call" | custom-call | flops 3000000000 | bytes 8000000 | tf_op jit(solution)/shard_map/pallas_call | solution.py:481
  70.2 1.3 %collective-permute-done.27.g2 = bf16[160,256]{1,0:T(8,128)(2,1)S(1)} collective-permute-done((bf16[160,256]{1,0:T(8,128)(2,1)S(1)}, bf16[160,256]{1,0:T(8,128)(2,1)S(1)}, u32[]{:S(2)}, u32[]{:S(2)}) %collective-permute-start.27) | collective-permute-done | bytes 81952 | tf_op jit(solution)/shard_map/ppermute | solution.py:407
  71.5 1.0 %shard_map.116 = (bf16[128,256]{1,0:T(8,128)(2,1)}, bf16[128,256]{1,0:T(8,128)(2,1)}) custom-call(bf16[128,1024]{1,0:T(8,128)(2,1)S(1)} %copy-done.8, bf16[128,1024]{1,0:T(8,128)(2,1)S(1)} %copy-done.1, bf16[128,256]{1,0:T(8,128)(2,1)S(1)} %get-tuple-element.58.n0, bf16[128,256]{1,0:T(8,128)(2,1)S(1)} %collective-permute-done.13.n1, ...), custom_call_target="tpu_custom_call" | custom-call | flops 100000000 | bytes 1000000 | tf_op jit(solution)/shard_map/pallas_call | solution.py:497
  (75 shorter events, 13.7 us)
Async XLA Ops:
  0.6 9.9 %collective-permute-start.7 = (bf16[2,256,256]{2,1,0:T(8,128)(2,1)}, bf16[2,256,256]{2,1,0:T(8,128)(2,1)S(1)}, u32[]{:S(2)}, u32[]{:S(2)}) collective-permute-start(bf16[2,256,256]{2,1,0:T(8,128)(2,1)} %refs_9_.1), channel_id=1, source_target_pairs={{0,2},{1,3},{2,0},{3,1},{4,6},{5,7},{6,4},{7,5},{8,10},{9,11},{10,... | collective-permute-start | bytes 786440 | tf_op jit(solution)/shard_map/ppermute | solution.py:407
  6.1 7.2 %collective-permute-start = (bf16[64,1152]{1,0:T(8,128)(2,1)S(1)}, bf16[64,1152]{1,0:T(8,128)(2,1)S(1)}, u32[]{:S(2)}, u32[]{:S(2)}) collective-permute-start(bf16[64,1152]{1,0:T(8,128)(2,1)S(1)} %shard_map.110), channel_id=1, source_target_pairs={{0,4},{4,0},{8,12},{12,8},{1,5},{5,1},{9,13},{13,9},{2,6},{6,2},{1... | collective-permute-start | bytes 442376 | tf_op jit(solution)/shard_map/ppermute | solution.py:407
  7.7 13.9 %collective-permute-start.1 = (bf16[64,1152]{1,0:T(8,128)(2,1)S(1)}, bf16[64,1152]{1,0:T(8,128)(2,1)S(1)}, u32[]{:S(2)}, u32[]{:S(2)}) collective-permute-start(bf16[64,1152]{1,0:T(8,128)(2,1)S(1)} %shard_map.110), channel_id=1, source_target_pairs={{0,8},{4,12},{8,0},{12,4},{1,9},{5,13},{9,1},{13,5},{2,10},{6,14},... | collective-permute-start | bytes 442376 | tf_op jit(solution)/shard_map/ppermute | solution.py:407
  10.3 11.3 %collective-permute-start.2 = (bf16[64,1152]{1,0:T(8,128)(2,1)S(1)}, bf16[64,1152]{1,0:T(8,128)(2,1)S(1)}, u32[]{:S(2)}, u32[]{:S(2)}) collective-permute-start(bf16[64,1152]{1,0:T(8,128)(2,1)S(1)} %shard_map.110), channel_id=1, source_target_pairs={{0,12},{4,8},{8,4},{12,0},{1,13},{5,9},{9,5},{13,1},{2,14},{6,10},... | collective-permute-start | bytes 442376 | tf_op jit(solution)/shard_map/ppermute | solution.py:407
  10.5 12.6 %collective-permute-start.6 = (bf16[2,256,256]{2,1,0:T(8,128)(2,1)}, bf16[2,256,256]{2,1,0:T(8,128)(2,1)S(1)}, u32[]{:S(2)}, u32[]{:S(2)}) collective-permute-start(bf16[2,256,256]{2,1,0:T(8,128)(2,1)} %refs_9_.1), channel_id=1, source_target_pairs={{0,1},{1,0},{2,3},{3,2},{4,5},{5,4},{6,7},{7,6},{8,9},{9,8},{10,11... | collective-permute-start | bytes 786440 | tf_op jit(solution)/shard_map/ppermute | solution.py:407
  10.5 17.0 %collective-permute-start.8 = (bf16[2,256,256]{2,1,0:T(8,128)(2,1)S(1)}, bf16[2,256,256]{2,1,0:T(8,128)(2,1)S(1)}, u32[]{:S(2)}, u32[]{:S(2)}) collective-permute-start(bf16[2,256,256]{2,1,0:T(8,128)(2,1)S(1)} %collective-permute-done.7.refs_11_), channel_id=1, source_target_pairs={{0,1},{1,0},{2,3},{3,2},{4,5},{5,4},{6,7},{7,6},{8,9},{9,8},{10,11... | collective-permute-start | bytes 786440 | tf_op jit(solution)/shard_map/ppermute | solution.py:407
  13.2 11.5 %collective-permute-start.3 = (bf16[64,1152]{1,0:T(8,128)(2,1)S(1)}, bf16[64,1152]{1,0:T(8,128)(2,1)S(1)}, u32[]{:S(2)}, u32[]{:S(2)}) collective-permute-start(bf16[64,1152]{1,0:T(8,128)(2,1)S(1)} %collective-permute-done.refs_1_.after), channel_id=1, source_target_pairs={{0,1},{1,0},{2,3},{3,2},{4,5},{5,4},{6,7},{7,6},{8,9},{9,8},{10,11... | collective-permute-start | bytes 442376 | tf_op jit(solution)/shard_map/ppermute | solution.py:407
  21.6 4.4 %collective-permute-start.4 = (bf16[64,1152]{1,0:T(8,128)(2,1)S(1)}, bf16[64,1152]{1,0:T(8,128)(2,1)S(1)}, u32[]{:S(2)}, u32[]{:S(2)}) collective-permute-start(bf16[64,1152]{1,0:T(8,128)(2,1)S(1)} %collective-permute-done.1.refs_2_), channel_id=1, source_target_pairs={{0,1},{1,0},{2,3},{3,2},{4,5},{5,4},{6,7},{7,6},{8,9},{9,8},{10,11... | collective-permute-start | bytes 442376 | tf_op jit(solution)/shard_map/ppermute | solution.py:407
  21.6 6.0 %collective-permute-start.5 = (bf16[64,1152]{1,0:T(8,128)(2,1)S(1)}, bf16[64,1152]{1,0:T(8,128)(2,1)S(1)}, u32[]{:S(2)}, u32[]{:S(2)}) collective-permute-start(bf16[64,1152]{1,0:T(8,128)(2,1)S(1)} %collective-permute-done.2.refs_3_), channel_id=1, source_target_pairs={{0,1},{1,0},{2,3},{3,2},{4,5},{5,4},{6,7},{7,6},{8,9},{9,8},{10,11... | collective-permute-start | bytes 442376 | tf_op jit(solution)/shard_map/ppermute | solution.py:407
  23.1 16.4 %collective-permute-start.16 = (bf16[64,1024]{1,0:T(8,128)(2,1)S(1)}, bf16[64,1024]{1,0:T(8,128)(2,1)S(1)}, u32[]{:S(2)}, u32[]{:S(2)}) collective-permute-start(bf16[64,1024]{1,0:T(8,128)(2,1)S(1)} %shard_map.113), channel_id=1, source_target_pairs={{0,4},{4,0},{8,12},{12,8},{1,5},{5,1},{9,13},{13,9},{2,6},{6,2},{1... | collective-permute-start | bytes 393224 | tf_op jit(solution)/shard_map/ppermute | solution.py:407
  24.8 14.8 %collective-permute-start.17 = (bf16[64,1024]{1,0:T(8,128)(2,1)S(1)}, bf16[64,1024]{1,0:T(8,128)(2,1)S(1)}, u32[]{:S(2)}, u32[]{:S(2)}) collective-permute-start(bf16[64,1024]{1,0:T(8,128)(2,1)S(1)} %shard_map.113), channel_id=1, source_target_pairs={{0,8},{4,12},{8,0},{12,4},{1,9},{5,13},{9,1},{13,5},{2,10},{6,14},... | collective-permute-start | bytes 393224 | tf_op jit(solution)/shard_map/ppermute | solution.py:407
  26.0 14.0 %collective-permute-start.18 = (bf16[64,1024]{1,0:T(8,128)(2,1)S(1)}, bf16[64,1024]{1,0:T(8,128)(2,1)S(1)}, u32[]{:S(2)}, u32[]{:S(2)}) collective-permute-start(bf16[64,1024]{1,0:T(8,128)(2,1)S(1)} %shard_map.113), channel_id=1, source_target_pairs={{0,12},{4,8},{8,4},{12,0},{1,13},{5,9},{9,5},{13,1},{2,14},{6,10},... | collective-permute-start | bytes 393224 | tf_op jit(solution)/shard_map/ppermute | solution.py:407
  39.0 1.5 %collective-permute-start.10 = (bf16[256,256]{1,0:T(8,128)(2,1)S(1)}, bf16[256,256]{1,0:T(8,128)(2,1)S(1)}, u32[]{:S(2)}, u32[]{:S(2)}) collective-permute-start(bf16[256,256]{1,0:T(8,128)(2,1)S(1)} %get-tuple-element.30), channel_id=1, source_target_pairs={{0,1},{1,0},{2,3},{3,2},{4,5},{5,4},{6,7},{7,6},{8,9},{9,8},{10,11... | collective-permute-start | bytes 393224 | tf_op jit(solution)/shard_map/ppermute | solution.py:407
  45.2 1.5 %collective-permute-start.23 = (bf16[320,256]{1,0:T(8,128)(2,1)S(1)}, bf16[320,256]{1,0:T(8,128)(2,1)S(1)}, u32[]{:S(2)}, u32[]{:S(2)}) collective-permute-start(bf16[320,256]{1,0:T(8,128)(2,1)S(1)} %get-tuple-element.38), channel_id=1, source_target_pairs={{0,1},{1,0},{2,3},{3,2},{4,5},{5,4},{6,7},{7,6},{8,9},{9,8},{10,11... | collective-permute-start | bytes 491528 | tf_op jit(solution)/shard_map/ppermute | solution.py:407
  45.6 2.4 %collective-permute-start.9 = (bf16[512,256]{1,0:T(8,128)(2,1)S(1)}, bf16[512,256]{1,0:T(8,128)(2,1)S(1)}, u32[]{:S(2)}, u32[]{:S(2)}) collective-permute-start(bf16[512,256]{1,0:T(8,128)(2,1)S(1)} %get-tuple-element.29), channel_id=1, source_target_pairs={{0,1},{1,0},{2,3},{3,2},{4,5},{5,4},{6,7},{7,6},{8,9},{9,8},{10,11... | collective-permute-start | bytes 786440 | tf_op jit(solution)/shard_map/ppermute | solution.py:407
  45.7 9.1 %collective-permute-start.12 = (bf16[512,256]{1,0:T(8,128)(2,1)S(1)}, bf16[512,256]{1,0:T(8,128)(2,1)S(1)}, u32[]{:S(2)}, u32[]{:S(2)}) collective-permute-start(bf16[512,256]{1,0:T(8,128)(2,1)S(1)} %fusion.1.refs_13_), channel_id=1, source_target_pairs={{0,2},{1,3},{2,0},{3,1},{4,6},{5,7},{6,4},{7,5},{8,10},{9,11},{10,... | collective-permute-start | bytes 786440 | tf_op jit(solution)/shard_map/ppermute | solution.py:407
  46.3 13.5 %collective-permute-start.22 = (bf16[640,256]{1,0:T(8,128)(2,1)S(1)}, bf16[640,256]{1,0:T(8,128)(2,1)S(1)}, u32[]{:S(2)}, u32[]{:S(2)}) collective-permute-start(bf16[640,256]{1,0:T(8,128)(2,1)S(1)} %get-tuple-element.37), channel_id=1, source_target_pairs={{0,1},{1,0},{2,3},{3,2},{4,5},{5,4},{6,7},{7,6},{8,9},{9,8},{10,11... | collective-permute-start | bytes 983048 | tf_op jit(solution)/shard_map/ppermute | solution.py:407
  46.8 14.5 %collective-permute-start.25 = (bf16[640,256]{1,0:T(8,128)(2,1)S(1)}, bf16[640,256]{1,0:T(8,128)(2,1)S(1)}, u32[]{:S(2)}, u32[]{:S(2)}) collective-permute-start(bf16[640,256]{1,0:T(8,128)(2,1)S(1)} %fusion), channel_id=1, source_target_pairs={{0,2},{1,3},{2,0},{3,1},{4,6},{5,7},{6,4},{7,5},{8,10},{9,11},{10,... | collective-permute-start | bytes 983048 | tf_op jit(solution)/shard_map/ppermute | solution.py:407
  55.3 9.3 %collective-permute-start.13 = (bf16[128,256]{1,0:T(8,128)(2,1)S(1)}, bf16[128,256]{1,0:T(8,128)(2,1)S(1)}, u32[]{:S(2)}, u32[]{:S(2)}) collective-permute-start(bf16[128,256]{1,0:T(8,128)(2,1)S(1)} %get-tuple-element.57), channel_id=1, source_target_pairs={{0,4},{4,0},{8,12},{12,8},{1,5},{5,1},{9,13},{13,9},{2,6},{6,2},{1... | collective-permute-start | bytes 196616 | tf_op jit(solution)/shard_map/ppermute | solution.py:407
  56.1 14.1 %collective-permute-start.14 = (bf16[128,256]{1,0:T(8,128)(2,1)S(1)}, bf16[128,256]{1,0:T(8,128)(2,1)S(1)}, u32[]{:S(2)}, u32[]{:S(2)}) collective-permute-start(bf16[128,256]{1,0:T(8,128)(2,1)S(1)} %get-tuple-element.56), channel_id=1, source_target_pairs={{0,8},{4,12},{8,0},{12,4},{1,9},{5,13},{9,1},{13,5},{2,10},{6,14},... | collective-permute-start | bytes 196616 | tf_op jit(solution)/shard_map/ppermute | solution.py:407
  58.2 12.0 %collective-permute-start.15 = (bf16[128,256]{1,0:T(8,128)(2,1)S(1)}, bf16[128,256]{1,0:T(8,128)(2,1)S(1)}, u32[]{:S(2)}, u32[]{:S(2)}) collective-permute-start(bf16[128,256]{1,0:T(8,128)(2,1)S(1)} %get-tuple-element.55), channel_id=1, source_target_pairs={{0,12},{4,8},{8,4},{12,0},{1,13},{5,9},{9,5},{13,1},{2,14},{6,10},... | collective-permute-start | bytes 196616 | tf_op jit(solution)/shard_map/ppermute | solution.py:407
  61.8 8.4 %collective-permute-start.26 = (bf16[160,256]{1,0:T(8,128)(2,1)S(1)}, bf16[160,256]{1,0:T(8,128)(2,1)S(1)}, u32[]{:S(2)}, u32[]{:S(2)}) collective-permute-start(bf16[160,256]{1,0:T(8,128)(2,1)S(1)} %get-tuple-element.53), channel_id=1, source_target_pairs={{0,4},{4,0},{8,12},{12,8},{1,5},{5,1},{9,13},{13,9},{2,6},{6,2},{1... | collective-permute-start | bytes 245768 | tf_op jit(solution)/shard_map/ppermute | solution.py:407
  62.6 8.9 %collective-permute-start.27 = (bf16[160,256]{1,0:T(8,128)(2,1)S(1)}, bf16[160,256]{1,0:T(8,128)(2,1)S(1)}, u32[]{:S(2)}, u32[]{:S(2)}) collective-permute-start(bf16[160,256]{1,0:T(8,128)(2,1)S(1)} %get-tuple-element.52), channel_id=1, source_target_pairs={{0,8},{4,12},{8,0},{12,4},{1,9},{5,13},{9,1},{13,5},{2,10},{6,14},... | collective-permute-start | bytes 245768 | tf_op jit(solution)/shard_map/ppermute | solution.py:407
  64.7 6.8 %collective-permute-start.28 = (bf16[160,256]{1,0:T(8,128)(2,1)S(1)}, bf16[160,256]{1,0:T(8,128)(2,1)S(1)}, u32[]{:S(2)}, u32[]{:S(2)}) collective-permute-start(bf16[160,256]{1,0:T(8,128)(2,1)S(1)} %get-tuple-element.51), channel_id=1, source_target_pairs={{0,12},{4,8},{8,4},{12,0},{1,13},{5,9},{9,5},{13,1},{2,14},{6,10},... | collective-permute-start | bytes 245768 | tf_op jit(solution)/shard_map/ppermute | solution.py:407
  (19 other events, 55.0 us)

commit v3 on v0

--- a/solution.py
+++ b/solution.py
@@ -1,6 +1,10 @@
+import functools
+
 import jax
 import jax.numpy as jnp
 from jax import lax
+from jax.experimental import pallas as pl
+from jax.experimental.pallas import tpu as pltpu
 from jax.sharding import PartitionSpec as P
 
 NF = 16
@@ -143,6 +147,421 @@
     return (mixed, grad_input, grad_pair, grad_up, grad_down)
 
 
+F32 = jnp.float32
+BF16 = jnp.bfloat16
+NT = (((1,), (1,)), ((), ()))
+TN = (((0,), (0,)), ((), ()))
+WIDTH = 1024
+HALF = 64
+
+
+def mm(a, b, dims=None):
+    if dims is None:
+        return jnp.dot(a, b, preferred_element_type=F32)
+    return lax.dot_general(a, b, dims, preferred_element_type=F32)
+
+
+def kernel_call(kernel, out_shape, where, scratch=(), flops=0, nbytes=0, vmem=48):
+    kinds = {"v": pltpu.VMEM, "a": pl.ANY, "h": pltpu.HBM}
+    return pl.pallas_call(
+        kernel,
+        out_shape=out_shape,
+        in_specs=[pl.BlockSpec(memory_space=kinds[w]) for w in where],
+        scratch_shapes=list(scratch),
+        compiler_params=pltpu.CompilerParams(vmem_limit_bytes=vmem * 1024 * 1024),
+        cost_estimate=pl.CostEstimate(flops=flops, bytes_accessed=nbytes, transcendentals=0),
+    )
+
+
+def shape(dims, dtype=BF16):
+    return jax.ShapeDtypeStruct(dims, dtype)
+
+
+def load(pairs, sems):
+    copies = [pltpu.make_async_copy(a, b, sems.at[n]) for n, (a, b) in enumerate(pairs)]
+    for copy in copies:
+        copy.start()
+    return copies
+
+
+def payload_kernel(x, c, gates_in, routes_in, pair_in, out_o, pair_o, gates, routes, sems):
+    core = lax.rem(lax.axis_index("tensor"), 2)
+    mine = pl.ds(pl.multiple_of(core * HALF, HALF), HALF)
+    copies = load(
+        [
+            (gates_in, gates),
+            (routes_in, routes),
+            (x.at[mine, :], out_o.at[:, 0:WIDTH]),
+            (c.at[mine, :], out_o.at[:, WIDTH : 2 * WIDTH]),
+            (pair_in, pair_o),
+        ],
+        sems,
+    )
+    copies[0].wait()
+    copies[1].wait()
+    high = gates[...].astype(BF16).astype(F32)
+    low = gates[...] - high
+    meta = jnp.concatenate(
+        [routes[...].astype(F32), high, low, jnp.zeros((122, 128), F32)], axis=0
+    )
+    columns = meta.T
+    out_o[:, 2 * WIDTH :] = jnp.where(core == 0, columns[0:HALF], columns[HALF:]).astype(BF16)
+    for copy in copies[2:]:
+        copy.wait()
+
+
+def join_kernel(a, b, after, out_o):
+    out_o[0:HALF, :] = a[...]
+    out_o[HALF : 2 * HALF, :] = b[...]
+
+
+def place_rows(whole, info, block, core, near, far):
+    for at, piece in ((core, near), (1 - core, far)):
+        rows = pl.ds(pl.multiple_of(block * 128 + at * HALF, HALF), HALF)
+        whole[rows, :] = piece[:, 0 : 2 * WIDTH]
+        info[rows, :] = piece[:, 2 * WIDTH :]
+
+
+def towers(meta, whole, up, down, ready, pair, outs, scratch):
+    keep, send_here, send_away, send_last, cross_o, act_o, grad_o, pre_o, gram_o, pick_o, gate_o = outs
+    flipped, partial, half_gram, terms = scratch
+    j = lax.axis_index("tensor")
+    core = lax.rem(j, 2)
+    xi = j // 2
+    first = lax.axis_index("expert") * 2
+    tokens = meta.shape[1]
+    before = (
+        lax.broadcasted_iota(jnp.int32, (tokens, tokens), 0)
+        < lax.broadcasted_iota(jnp.int32, (tokens, tokens), 1)
+    ).astype(F32).astype(BF16)
+    a = lax.broadcasted_iota(jnp.int32, (256, 144), 0)
+    n = lax.broadcasted_iota(jnp.int32, (256, 144), 1)
+    low = jnp.minimum(a // 16, a % 16)
+    high = jnp.maximum(a // 16, a % 16)
+    spread = jnp.where(low * 16 - low * (low - 1) // 2 + high - low == n, 1.0, 0.0).astype(BF16)
+    a = lax.broadcasted_iota(jnp.int32, (256, 256), 0)
+    b = lax.broadcasted_iota(jnp.int32, (256, 256), 1)
+    swapped = (a % 16) * 16 + a // 16
+    both = (jnp.where(a == b, 1.0, 0.0) + jnp.where(swapped == b, 1.0, 0.0)).astype(BF16)
+    half_gram[136:144, :] = jnp.zeros((8, 128), F32)
+    for e in range(2):
+        mine = (first + e).astype(F32)
+        s0 = meta[0:1, :] == mine
+        s1 = meta[1:2, :] == mine
+        named = jnp.where(s0, 1.0, 0.0) + jnp.where(s1, 1.0, 0.0)
+        gate = jnp.where(s0, meta[2:3, :], 0.0) + jnp.where(s1, meta[3:4, :], 0.0)
+        place = mm(jnp.broadcast_to(named, (8, tokens)).astype(BF16), before)[0:1, :]
+        place = jnp.where(named > 0.5, place, -1.0)
+        hit = lax.broadcasted_iota(jnp.int32, (128, tokens), 0).astype(F32) == place
+        pick = jnp.where(hit, 1.0, 0.0).astype(BF16)
+        weight = jnp.sum(jnp.where(hit, gate, 0.0), axis=1, keepdims=True)
+        gate_o[e] = jnp.broadcast_to(weight, (128, 128))
+        pick_o[e] = pick
+        rows = mm(pick, whole[:, 0:WIDTH])
+        grad = (weight * mm(pick, whole[:, WIDTH : 2 * WIDTH])).astype(BF16)
+        grad_o[e] = grad
+        flipped[...] = rows.T
+        at = 0
+        for i in range(16):
+            left = flipped[i * 64 : i * 64 + 64, :]
+            for q in range(i, 16):
+                prod = left * flipped[q * 64 : q * 64 + 64, :]
+                partial[at * 8 : at * 8 + 8, :] = jnp.sum(prod.reshape(8, 8, 128), axis=0)
+                at += 1
+        for g in range(17):
+            acc = partial[pl.ds(g * 64, 8, stride=8), :]
+            for q in range(1, 8):
+                acc = acc + partial[pl.ds(g * 64 + q, 8, stride=8), :]
+            half_gram[g * 8 : g * 8 + 8, :] = acc * (1.0 / DE)
+        gram = mm(spread, half_gram[...].astype(BF16)).astype(BF16)
+        gram_o[e] = gram
+        cross = (rows + mm(gram, pair[e], TN)).astype(BF16)
+        cross_o[e] = cross
+        if e == 0:
+            for copy in ready:
+                copy.wait()
+        pre = mm(cross, up[e])
+        sig = jax.nn.sigmoid(pre)
+        act = (pre * sig).astype(BF16)
+        act_o[e] = act
+        slope = sig * (1.0 + pre * (1.0 - sig))
+        dpre = (mm(grad, down[e], NT) * slope).astype(BF16)
+        pre_o[e] = dpre
+        terms[...] = mm(dpre, up[e], NT).astype(BF16)
+        back = mm(both, mm(pair[e], terms[...], NT).astype(BF16)).astype(BF16)
+        for xr in (1, 0):
+            for part in (1, 0):
+                block = 2 * (xi ^ xr) + (core ^ part)
+                cols = pl.ds(pl.multiple_of(block * 256, 256), 256)
+                if part == 0:
+                    low, high = keep.at[xr, 0:320], keep.at[xr, 320:576]
+                elif xr == 0:
+                    low, high = send_here.at[0:320], send_here.at[320:576]
+                else:
+                    low, high = send_away, send_last
+                low[e * 128 : e * 128 + 128, :] = terms[:, cols]
+                high[e * 128 : e * 128 + 128, :] = mm(act, down[e, :, cols]).astype(BF16)
+                for q in range(4):
+                    def put(low=low, q=q):
+                        low[256:320, e * 128 : e * 128 + 128] = back[q * 64 : q * 64 + 64, :]
+
+                    pl.when(block == q)(put)
+
+
+def own_chunk_kernel(*refs):
+    x, c, gates_in, routes_in, near, far, p0, p1, p2, p3, up_in, down_in = refs[:12]
+    outs, pair_o = refs[12:23], refs[23]
+    whole, info, gates, routes, up, down, sems = refs[24:31]
+    j = lax.axis_index("tensor")
+    copies = load(
+        [
+            (gates_in, gates),
+            (routes_in, routes),
+            (x, whole.at[0:128, 0:WIDTH]),
+            (c, whole.at[0:128, WIDTH : 2 * WIDTH]),
+            (up_in, up),
+            (down_in, down),
+        ],
+        sems,
+    )
+    place_rows(whole, info, 1, lax.rem(j, 2), near, far)
+    for k, piece in enumerate((p0, p1, p2, p3)):
+        cols = pl.ds(pl.multiple_of((j ^ k) * 256, 256), 256)
+        for e in range(2):
+            pair_o[e, :, cols] = piece[e]
+    for copy in copies[:4]:
+        copy.wait()
+    other = info[128:256, :].astype(F32).T
+    meta = jnp.concatenate(
+        [
+            jnp.concatenate([routes[...].astype(F32), other[0:2]], axis=1),
+            jnp.concatenate([gates[...], other[2:4] + other[4:6]], axis=1),
+        ],
+        axis=0,
+    )
+    towers(meta, whole, up, down, copies[4:], pair_o, outs, refs[31:])
+
+
+def far_chunk_kernel(*refs):
+    near, far, pair, up_in, down_in = refs[:5]
+    outs = refs[5:16]
+    whole, info, up, down, sems = refs[16:21]
+    core = lax.rem(lax.axis_index("tensor"), 2)
+    copies = load([(up_in, up), (down_in, down)], sems)
+    for r in range(2):
+        rows = slice(r * HALF, r * HALF + HALF)
+        place_rows(whole, info, r, core, near.at[rows, :], far.at[rows, :])
+    other = info[...].astype(F32).T
+    meta = jnp.concatenate([other[0:2], other[2:4] + other[4:6]], axis=0)
+    towers(meta, whole, up, down, copies, pair, outs, refs[21:])
+
+
+def weights_kernel(act0, grad0, cross0, pre0, act1, grad1, cross1, pre1, down_o, up_o):
+    def stack(a, b):
+        return jnp.concatenate([a, b], axis=0)
+
+    for e in range(2):
+        down_o[e] = mm(stack(act0[e], act1[e]), stack(grad0[e], grad1[e]), TN).astype(BF16)
+        up_o[e] = mm(stack(cross0[e], cross1[e]), stack(pre0[e], pre1[e]), TN).astype(BF16)
+
+
+def add2(a, b):
+    return (a.astype(F32) + b.astype(F32)).astype(BF16)
+
+
+def combine_kernel(mine, other, theirs, pick, gate, first_o, second_o, rows_o):
+    both = add2(add2(mine[0], other[...]), theirs[...])
+    grads = jnp.zeros((256, 256), F32)
+    mixed = jnp.zeros((256, 256), F32)
+    back = jnp.zeros((64, 256), F32)
+    for e in range(2):
+        rows = both[e * 128 : e * 128 + 128]
+        rows_o[e] = rows
+        grads = grads + mm(pick[e], rows, TN)
+        back = back + mm(both[256:320, e * 128 : e * 128 + 128], pick[e])
+        out = both[320 + e * 128 : 448 + e * 128].astype(F32) * gate[e][:, 0:1]
+        mixed = mixed + mm(pick[e], out.astype(BF16), TN)
+    for p, dst in enumerate((first_o, second_o)):
+        rows = slice(p * 128, p * 128 + 128)
+        dst[0:128, :] = grads[rows].astype(BF16)
+        part = back[:, rows].astype(BF16)
+        dst[128:160, 0:128] = part[0:32]
+        dst[128:160, 128:256] = part[32:64]
+        dst[160:288, :] = mixed[rows].astype(BF16)
+
+
+def pair_kernel(gram0, rows0, gram1, rows1, out_o):
+    for e in range(2):
+        out_o[e] = (mm(gram0[e], rows0[e]) + mm(gram1[e], rows1[e])).astype(BF16)
+
+
+def final_kernel(x_in, c_in, g0, g1, g2, g3, mixed_o, grad_o, x, c, flipped, sems):
+    copies = load([(x_in, x), (c_in, c)], sems)
+    for copy in copies:
+        copy.wait()
+    cols = pl.ds(pl.multiple_of(lax.axis_index("tensor") * 256, 256), 256)
+    mixed = x[:, cols].astype(F32)
+    total = c[:, cols].astype(F32)
+    back = jnp.zeros((32, 256), F32)
+    for g in (g0, g1, g2, g3):
+        total = total + g[0:128, :].astype(F32)
+        back = back + g[128:160, :].astype(F32)
+        mixed = mixed + g[160:288, :].astype(F32)
+    mixed_o[...] = mixed.astype(BF16)
+    flipped[...] = x[...].astype(F32).T
+    back = jnp.concatenate([back[:, 0:128], back[:, 128:256]], axis=0)
+    pieces = []
+    for i in range(4):
+        acc = jnp.zeros((64, 128), F32)
+        for q in range(16):
+            acc = acc + back[i * 16 + q : i * 16 + q + 1, :] * flipped[q * 64 : q * 64 + 64, :]
+        pieces.append(acc)
+    gram_back = jnp.concatenate(pieces, axis=0) * (1.0 / DE)
+    grad_o[...] = (total + gram_back.T).astype(BF16)
+
+
+def swap(value, axis, mask):
+    size = lax.axis_size(axis)
+    return lax.ppermute(value, axis, [(i, i ^ mask) for i in range(size)])
+
+
+def chunk_outs():
+    return (
+        shape((2, 576, 256)),
+        shape((576, 256)),
+        shape((320, 256)),
+        shape((256, 256)),
+        shape((2, 128, 1024)),
+        shape((2, 128, 512)),
+        shape((2, 128, 1024)),
+        shape((2, 128, 512)),
+        shape((2, 256, 128)),
+        shape((2, 128, 256)),
+        shape((2, 128, 128), F32),
+    )
+
+
+def chunk_scratch():
+    return [
+        pltpu.VMEM((1024, 128), F32),
+        pltpu.VMEM((1088, 128), F32),
+        pltpu.VMEM((144, 128), F32),
+        pltpu.VMEM((128, 1024), BF16),
+    ]
+
+
+def weight_scratch():
+    return [pltpu.VMEM((2, 1024, 512), BF16), pltpu.VMEM((2, 512, 1024), BF16)]
+
+
+def away_kernel(keep, low, high, *rest):
+    out_o = rest[-1]
+    rows = low.shape[0]
+    out_o[0:rows, :] = add2(keep[1, 0:rows], low[...])
+    out_o[rows:, :] = add2(keep[1, rows:], high[...])
+
+
+def sums_over_tensor(keep, send_here, send_away, send_last, after=()):
+    got = (swap(send_away, "tensor", 1), swap(send_last, "tensor", 1))
+    add = kernel_call(away_kernel, shape((576, 256)), "vvv" + "a" * len(after))
+    there = swap(add(keep, *got, *after), "tensor", 2)
+    return swap(send_here, "tensor", 1), there
+
+
+def gathered_body(inputs, cotangent, gate_values, routes, pair_weight, up_weight, down_weight):
+    gates, choices = gate_values.T, routes.T
+    payload, pair_own = kernel_call(
+        payload_kernel,
+        (shape((HALF, 2 * WIDTH + 128)), shape((2, 256, 256))),
+        "hhhhh",
+        scratch=[
+            pltpu.VMEM((2, 128), F32),
+            pltpu.VMEM((2, 128), jnp.int32),
+            pltpu.SemaphoreType.DMA((5,)),
+        ],
+    )(inputs, cotangent, gates, choices, pair_weight)
+    got = [swap(payload, "expert", 1), swap(payload, "expert", 2)]
+    got.append(swap(got[1], "expert", 1))
+    pair_x = swap(pair_own, "tensor", 2)
+    pair_c = swap(pair_own, "tensor", 1)
+    pair_d = swap(pair_x, "tensor", 1)
+    near_other = swap(got[0], "tensor", 1)
+    chunk = kernel_call(
+        own_chunk_kernel,
+        chunk_outs() + (shape((2, 256, 1024)),),
+        "hhhhvvvvvvhh",
+        scratch=[
+            pltpu.VMEM((256, 2048), BF16),
+            pltpu.VMEM((256, 128), BF16),
+            pltpu.VMEM((2, 128), F32),
+            pltpu.VMEM((2, 128), jnp.int32),
+        ]
+        + weight_scratch()
+        + [pltpu.SemaphoreType.DMA((6,))]
+        + chunk_scratch(),
+        flops=4_000_000_000,
+        nbytes=10_000_000,
+    )(
+        inputs, cotangent, gates, choices, got[0], near_other,
+        pair_own, pair_c, pair_x, pair_d, up_weight, down_weight,
+    )
+    keep, here, away, last, cross, act, grad, pre, gram, pick, gate, pair_all = chunk
+    other, theirs = sums_over_tensor(keep, here, away, last)
+    part = shape((288, 256))
+    combine = kernel_call(
+        combine_kernel,
+        (part, part, shape((2, 128, 256))),
+        "vvvvv",
+        flops=300_000_000,
+        nbytes=2_000_000,
+    )
+    own_part, near_part, rows = combine(keep, other, theirs, pick, gate)
+    far_mine = kernel_call(join_kernel, shape((2 * HALF, 2 * WIDTH + 128)), "vva")(
+        got[1], got[2], gate
+    )
+    far_other = swap(far_mine, "tensor", 1)
+    chunk = kernel_call(
+        far_chunk_kernel,
+        chunk_outs(),
+        "vvvhh",
+        scratch=[pltpu.VMEM((256, 2048), BF16), pltpu.VMEM((256, 128), BF16)]
+        + weight_scratch()
+        + [pltpu.SemaphoreType.DMA((2,))]
+        + chunk_scratch(),
+        flops=4_000_000_000,
+        nbytes=10_000_000,
+    )(far_mine, far_other, pair_all, up_weight, down_weight)
+    fkeep, fhere, faway, flast, fcross, fact, fgrad, fpre, fgram, fpick, fgate = chunk
+    fother, ftheirs = sums_over_tensor(fkeep, fhere, faway, flast, after=(theirs,))
+    near_got = swap(near_part, "expert", 1)
+    part2, part3, frows = combine(fkeep, fother, ftheirs, fpick, fgate)
+    got2, got3 = swap(part2, "expert", 2), swap(part3, "expert", 3)
+    grad_down, grad_up = kernel_call(
+        weights_kernel,
+        (shape((2, 512, 1024)), shape((2, 1024, 512))),
+        "vvvvvvvv",
+        flops=3_000_000_000,
+        nbytes=8_000_000,
+    )(act, grad, cross, pre, fact, fgrad, fcross, fpre)
+    grad_pair = kernel_call(
+        pair_kernel, shape((2, 256, 256)), "vvvv", flops=300_000_000, nbytes=2_000_000
+    )(gram, rows, fgram, frows)
+    mixed, grad_input = kernel_call(
+        final_kernel,
+        (shape((128, 256)), shape((128, 256))),
+        "hhvvvv",
+        scratch=[
+            pltpu.VMEM((128, 1024), BF16),
+            pltpu.VMEM((128, 1024), BF16),
+            pltpu.VMEM((1024, 128), F32),
+            pltpu.SemaphoreType.DMA((2,)),
+        ],
+        flops=100_000_000,
+        nbytes=1_000_000,
+    )(inputs, cotangent, own_part, near_got, got2, got3)
+    return mixed, grad_input, grad_pair, grad_up, grad_down
+
+
 def solution(mesh):
     placed = (
         P(("group", "expert"), None),
@@ -153,8 +572,9 @@
         P("expert", None, "tensor"),
         P("expert", "tensor", None),
     )
+    small = mesh.shape["expert"] == 4 and mesh.shape["tensor"] == 4
     return jax.shard_map(
-        body,
+        gathered_body if small else body,
         mesh=mesh,
         in_specs=placed,
         out_specs=(

time: 238 us -> 71.6 us (0.30)
  waiting for transfers between devices: 124 us -> 25.1 us
  matrix products: 36.6 us -> 0 us
  local copies, waits for them, and re-layouts: 33.6 us -> 4.21 us
  Pallas kernels: 0 us -> 23.3 us
  between operations: 14 us -> 0.93 us
  other arithmetic: 8.36 us -> 0 us
    psum x1 -> x0, waiting for transfers between devices: 47.1 us -> none  [body(): lax.psum(pair_terms.astype(jnp.bfloat16), 'tensor').astype(jnp.float32)]
    all_to_all x4 -> x0, waiting for transfers between devices: 38.8 us -> none  [the longest x1 22.3 us: body(): lax.all_to_all(input_slots.reshape(send_shape), 'expert', split_axis=0, c...]
    dot_general x15 -> x0, matrix products: 36.6 us -> none  [the longest x1 5.1 us: body(): jnp.einsum('eijr,ejdr->eidr', symmetric_mine, cells.astype(jnp.float32),...]
    reduce_scatter x2 -> x0, waiting for transfers between devices: 32.7 us -> none  [the longest x1 17.9 us: body(): lax.psum_scatter(out_terms.astype(jnp.bfloat16), 'tensor', scatter_dimens...]
    ppermute x0 -> x19, waiting for transfers between devices: none -> 25.1 us  [swap(): return lax.ppermute(value, axis, [(i, i ^ mask) for i in range(size)])]
    pallas_call x0 -> x11, Pallas kernels: none -> 23.3 us  [the longest x1 8.97 us: gathered_body(): kernel_call(own_chunk_kernel, chunk_outs() + (shape((2, 256, 1024)),), 'h...]
    all_to_all x4 -> x0, starting transfers between devices: 19.8 us -> none  [the longest x1 6.32 us: body(): lax.all_to_all(input_slots.reshape(send_shape), 'expert', split_axis=0, c...]
    ppermute x0 -> x19, starting transfers between devices: none -> 17.9 us  [swap(): return lax.ppermute(value, axis, [(i, i ^ mask) for i in range(size)])]
  transfers between devices with their start and end apart: 8 -> 19, of which waited for: 7 -> 6; matrix products, arithmetic and copies ran while one was open for 28% -> 0% of each run, Pallas kernels for 0% -> 31%
where the time goes in v3:
time: 71.6 us; the launch traced here: 71.4 us
  waiting for transfers between devices  25.1 us (35%)
  Pallas kernels  23.3 us (33%)
  starting transfers between devices  17.9 us (25%)
  local copies, waits for them, and re-layouts  4.21 us (6%)
  between operations  0.93 us (1%)
    ppermute x19, waiting for transfers between devices, swap(): return lax.ppermute(value, axis, [(i, i ^ mask) for i in range(size)])  25.1 us
    ppermute x19, starting transfers between devices, swap(): return lax.ppermute(value, axis, [(i, i ^ mask) for i in range(size)])  17.9 us
    pallas_call x1, Pallas kernels, gathered_body(): kernel_call(own_chunk_kernel, chunk_outs() + (shape((2, 256, 1024)),), 'h...  8.97 us
    pallas_call x1, Pallas kernels, gathered_body(): kernel_call(far_chunk_kernel, chunk_outs(), 'vvvhh', scratch=[pltpu.VMEM(...  8.09 us
    unnamed x16, local copies, waits for them, and re-layouts  4.21 us
    pallas_call x1, Pallas kernels, gathered_body(): kernel_call(weights_kernel, (shape((2, 512, 1024)), shape((2, 1024, 512))...  3.02 us
  transfers between devices with their start and end apart: 19, of which 6 were waited for; matrix products, arithmetic and copies ran while one was open for 0% of the time, Pallas kernels for 31%

profile of v3, /device:TPU:0, one launch (start us, length us, event | category | flops | bytes accessed | tf_op | source)
XLA Modules:
  0.0 71.4 jit_solution(14171168378471032384)
XLA Ops:
  0.6 0.9 %copy-done = bf16[128,1024]{1,0:T(8,128)(2,1)S(1)} copy-done((bf16[128,1024]{1,0:T(8,128)(2,1)S(1)}, bf16[128,1024]{1,0:T(8,128)(2,1)}, u32[]{:S(2)}) %copy-start) | copy-done | bytes 262168
  1.6 0.9 %copy-done.2 = bf16[128,1024]{1,0:T(8,128)(2,1)S(1)} copy-done((bf16[128,1024]{1,0:T(8,128)(2,1)S(1)}, bf16[128,1024]{1,0:T(8,128)(2,1)}, u32[]{:S(2)}) %copy-start.2) | copy-done | bytes 262168
  2.5 0.9 %copy-done.4 = bf16[2,256,256]{2,1,0:T(8,128)(2,1)S(1)} copy-done((bf16[2,256,256]{2,1,0:T(8,128)(2,1)S(1)}, bf16[2,256,256]{2,1,0:T(8,128)(2,1)}, u32[]{:S(2)}) %copy-start.4) | copy-done | bytes 262168
  3.5 0.7 copy-done.5
  4.2 0.7 copy-done.6
  5.1 3.1 %collective-permute-start = (bf16[64,2176]{1,0:T(8,128)(2,1)S(1)}, bf16[64,2176]{1,0:T(8,128)(2,1)S(1)}, u32[]{:S(2)}, u32[]{:S(2)}) collective-permute-start(bf16[64,2176]{1,0:T(8,128)(2,1)S(1)} %get-tuple-element.40), channel_id=1, source_target_pairs={{0,4},{4,0},{8,12},{12,8},{1,5},{5,1},{9,13},{13,9},{2,6},{6,2},{1... | collective-permute-start | bytes 835592 | tf_op jit(solution)/shard_map/ppermute | solution.py:425
  8.2 1.5 %collective-permute-start.3 = (bf16[2,256,256]{2,1,0:T(8,128)(2,1)S(1)}, bf16[2,256,256]{2,1,0:T(8,128)(2,1)S(1)}, u32[]{:S(2)}, u32[]{:S(2)}) collective-permute-start(bf16[2,256,256]{2,1,0:T(8,128)(2,1)S(1)} %get-tuple-element.41.refs_6_), channel_id=1, source_target_pairs={{0,2},{1,3},{2,0},{3,1},{4,6},{5,7},{6,4},{7,5},{8,10},{9,11},{10,... | collective-permute-start | bytes 786440 | tf_op jit(solution)/shard_map/ppermute | solution.py:425
  9.7 2.6 %collective-permute-start.10 = (bf16[64,2176]{1,0:T(8,128)(2,1)S(1)}, bf16[64,2176]{1,0:T(8,128)(2,1)S(1)}, u32[]{:S(2)}, u32[]{:S(2)}) collective-permute-start(bf16[64,2176]{1,0:T(8,128)(2,1)S(1)} %get-tuple-element.40), channel_id=1, source_target_pairs={{0,8},{4,12},{8,0},{12,4},{1,9},{5,13},{9,1},{13,5},{2,10},{6,14},... | collective-permute-start | bytes 835592 | tf_op jit(solution)/shard_map/ppermute | solution.py:425
  12.2 7.2 %collective-permute-done.refs_4_ = bf16[64,2176]{1,0:T(8,128)(2,1)S(1)} collective-permute-done((bf16[64,2176]{1,0:T(8,128)(2,1)S(1)}, bf16[64,2176]{1,0:T(8,128)(2,1)S(1)}, u32[]{:S(2)}, u32[]{:S(2)}) %collective-permute-start) | collective-permute-done | bytes 278560 | tf_op jit(solution)/shard_map/ppermute | solution.py:425
  20.0 4.5 %collective-permute-done.10.a = bf16[64,2176]{1,0:T(8,128)(2,1)S(1)} collective-permute-done((bf16[64,2176]{1,0:T(8,128)(2,1)S(1)}, bf16[64,2176]{1,0:T(8,128)(2,1)S(1)}, u32[]{:S(2)}, u32[]{:S(2)}) %collective-permute-start.10) | collective-permute-done | bytes 278560 | tf_op jit(solution)/shard_map/ppermute | solution.py:425
  24.5 9.0 %shard_map.111 = (bf16[2,576,256]{2,1,0:T(8,128)(2,1)S(1)}, bf16[576,256]{1,0:T(8,128)(2,1)S(1)}, bf16[320,256]{1,0:T(8,128)(2,1)S(1)}, bf16[256,256]{1,0:T(8,12...) custom-call(bf16[128,1024]{1,0:T(8,128)(2,1)S(1)} %copy-done, ...), custom_call_target="tpu_custom_call" | custom-call | flops 4000000000 | bytes 10000000 | tf_op jit(solution)/shard_map/pallas_call | solution.py:489
  34.2 1.8 %collective-permute-done.7.high = bf16[256,256]{1,0:T(8,128)(2,1)S(1)} collective-permute-done((bf16[256,256]{1,0:T(8,128)(2,1)S(1)}, bf16[256,256]{1,0:T(8,128)(2,1)S(1)}, u32[]{:S(2)}, u32[]{:S(2)}) %collective-permute-start.7) | collective-permute-done | bytes 131104 | tf_op jit(solution)/shard_map/ppermute | solution.py:425
  36.1 0.7 collective-permute-start.8
  36.8 8.1 %shard_map.115 = (bf16[2,576,256]{2,1,0:T(8,128)(2,1)S(1)}, bf16[576,256]{1,0:T(8,128)(2,1)S(1)}, bf16[320,256]{1,0:T(8,128)(2,1)S(1)}, bf16[256,256]{1,0:T(8,12...) custom-call(bf16[128,2176]{1,0:T(8,128)(2,1)S(1)} %shard_map.114.ref, ...), custom_call_target="tpu_custom_call" | custom-call | flops 4000000000 | bytes 10000000 | tf_op jit(solution)/shard_map/pallas_call | solution.py:523
  46.0 0.6 collective-permute-done.15.high
  46.6 1.5 %collective-permute-start.16 = (bf16[576,256]{1,0:T(8,128)(2,1)S(1)}, bf16[576,256]{1,0:T(8,128)(2,1)S(1)}, u32[]{:S(2)}, u32[]{:S(2)}) collective-permute-start(bf16[576,256]{1,0:T(8,128)(2,1)S(1)} %shard_map.116), channel_id=1, source_target_pairs={{0,2},{1,3},{2,0},{3,1},{4,6},{5,7},{6,4},{7,5},{8,10},{9,11},{10,... | collective-permute-start | bytes 884744 | tf_op jit(solution)/shard_map/ppermute | solution.py:425
  48.5 2.1 %collective-permute-start.9 = (bf16[288,256]{1,0:T(8,128)(2,1)S(1)}, bf16[288,256]{1,0:T(8,128)(2,1)S(1)}, u32[]{:S(2)}, u32[]{:S(2)}) collective-permute-start(bf16[288,256]{1,0:T(8,128)(2,1)S(1)} %get-tuple-element.49), channel_id=1, source_target_pairs={{0,4},{4,0},{8,12},{12,8},{1,5},{5,1},{9,13},{13,9},{2,6},{6,2},{1... | collective-permute-start | bytes 442376 | tf_op jit(solution)/shard_map/ppermute | solution.py:425
  50.6 5.3 %collective-permute-done.16.theirs = bf16[576,256]{1,0:T(8,128)(2,1)S(1)} collective-permute-done((bf16[576,256]{1,0:T(8,128)(2,1)S(1)}, bf16[576,256]{1,0:T(8,128)(2,1)S(1)}, u32[]{:S(2)}, u32[]{:S(2)}) %collective-permute-start.16) | collective-permute-done | bytes 294944 | tf_op jit(solution)/shard_map/ppermute | solution.py:425
  56.3 2.9 %collective-permute-start.17 = (bf16[288,256]{1,0:T(8,128)(2,1)S(1)}, bf16[288,256]{1,0:T(8,128)(2,1)S(1)}, u32[]{:S(2)}, u32[]{:S(2)}) collective-permute-start(bf16[288,256]{1,0:T(8,128)(2,1)S(1)} %get-tuple-element.57), channel_id=1, source_target_pairs={{0,8},{4,12},{8,0},{12,4},{1,9},{5,13},{9,1},{13,5},{2,10},{6,14},... | collective-permute-start | bytes 442376 | tf_op jit(solution)/shard_map/ppermute | solution.py:425
  59.2 1.4 %collective-permute-start.18 = (bf16[288,256]{1,0:T(8,128)(2,1)S(1)}, bf16[288,256]{1,0:T(8,128)(2,1)S(1)}, u32[]{:S(2)}, u32[]{:S(2)}) collective-permute-start(bf16[288,256]{1,0:T(8,128)(2,1)S(1)} %get-tuple-element.58), channel_id=1, source_target_pairs={{0,12},{4,8},{8,4},{12,0},{1,13},{5,9},{9,5},{13,1},{2,14},{6,10},... | collective-permute-start | bytes 442376 | tf_op jit(solution)/shard_map/ppermute | solution.py:425
  60.5 3.0 %shard_map.120 = (bf16[2,512,1024]{2,1,0:T(8,128)(2,1)}, bf16[2,1024,512]{2,1,0:T(8,128)(2,1)}) custom-call(bf16[2,128,512]{2,1,0:T(8,128)(2,1)S(1)} %get-tuple-element.65.act0, bf16[2,128,1024]{2,1,0:T(8,128)(2,1)S(1)} %get-tuple-element.66.grad0, bf16[2,128,1024]{2,1,0:T(8,128)(2,1)S(1)} %get-tuple-element.67.cross0, ...), custom_call_target="tpu_custom_call" | custom-call | flops 3000000000 | bytes 8000000 | tf_op jit(solution)/shard_map/pallas_call | solution.py:539
  63.6 1.0 %shard_map.119 = bf16[2,256,256]{2,1,0:T(8,128)(2,1)} custom-call(bf16[2,256,128]{2,1,0:T(8,128)(2,1)S(1)} %get-tuple-element.61.gram0, bf16[2,128,256]{2,1,0:T(8,128)(2,1)S(1)} %get-tuple-element.62.rows0, bf16[2,256,128]{2,1,0:T(8,128)(2,1)S(1)} %get-tuple-element.63.gram1, bf16[2,128,256]{2,1,0:T(8,128)(2,1)S(1)} %get-tuple-element.64.rows1), custom_call_target="tpu_custom_call" | custom-call | flops 300000000 | bytes 2000000 | tf_op jit(solution)/shard_map/pallas_call | solution.py:546
  64.6 5.6 %collective-permute-done.17.g2 = bf16[288,256]{1,0:T(8,128)(2,1)S(1)} collective-permute-done((bf16[288,256]{1,0:T(8,128)(2,1)S(1)}, bf16[288,256]{1,0:T(8,128)(2,1)S(1)}, u32[]{:S(2)}, u32[]{:S(2)}) %collective-permute-start.17) | collective-permute-done | bytes 147488 | tf_op jit(solution)/shard_map/ppermute | solution.py:425
  70.2 1.0 %shard_map.118 = (bf16[128,256]{1,0:T(8,128)(2,1)}, bf16[128,256]{1,0:T(8,128)(2,1)}) custom-call(bf16[128,1024]{1,0:T(8,128)(2,1)S(1)} %copy-done.1, bf16[128,1024]{1,0:T(8,128)(2,1)S(1)} %copy-done.3, bf16[288,256]{1,0:T(8,128)(2,1)S(1)} %get-tuple-element.48.g0, bf16[288,256]{1,0:T(8,128)(2,1)S(1)} %collective-permute-done.9.g1, ...), custom_call_target="tpu_custom_call" | custom-call | flops 100000000 | bytes 1000000 | tf_op jit(solution)/shard_map/pallas_call | solution.py:549
  (41 shorter events, 3.5 us)
Async XLA Ops:
  0.6 1.0 %copy-start = (bf16[128,1024]{1,0:T(8,128)(2,1)S(1)}, bf16[128,1024]{1,0:T(8,128)(2,1)}, u32[]{:S(2)}) copy-start(bf16[128,1024]{1,0:T(8,128)(2,1)} %x_in.1) | copy-start | bytes 786436
  1.6 0.9 %copy-start.2 = (bf16[128,1024]{1,0:T(8,128)(2,1)S(1)}, bf16[128,1024]{1,0:T(8,128)(2,1)}, u32[]{:S(2)}) copy-start(bf16[128,1024]{1,0:T(8,128)(2,1)} %c_in.1) | copy-start | bytes 786436
  5.1 14.4 %collective-permute-start = (bf16[64,2176]{1,0:T(8,128)(2,1)S(1)}, bf16[64,2176]{1,0:T(8,128)(2,1)S(1)}, u32[]{:S(2)}, u32[]{:S(2)}) collective-permute-start(bf16[64,2176]{1,0:T(8,128)(2,1)S(1)} %get-tuple-element.40), channel_id=1, source_target_pairs={{0,4},{4,0},{8,12},{12,8},{1,5},{5,1},{9,13},{13,9},{2,6},{6,2},{1... | collective-permute-start | bytes 835592 | tf_op jit(solution)/shard_map/ppermute | solution.py:425
  8.2 11.8 %collective-permute-start.3 = (bf16[2,256,256]{2,1,0:T(8,128)(2,1)S(1)}, bf16[2,256,256]{2,1,0:T(8,128)(2,1)S(1)}, u32[]{:S(2)}, u32[]{:S(2)}) collective-permute-start(bf16[2,256,256]{2,1,0:T(8,128)(2,1)S(1)} %get-tuple-element.41.refs_6_), channel_id=1, source_target_pairs={{0,2},{1,3},{2,0},{3,1},{4,6},{5,7},{6,4},{7,5},{8,10},{9,11},{10,... | collective-permute-start | bytes 786440 | tf_op jit(solution)/shard_map/ppermute | solution.py:425
  9.7 14.9 %collective-permute-start.10 = (bf16[64,2176]{1,0:T(8,128)(2,1)S(1)}, bf16[64,2176]{1,0:T(8,128)(2,1)S(1)}, u32[]{:S(2)}, u32[]{:S(2)}) collective-permute-start(bf16[64,2176]{1,0:T(8,128)(2,1)S(1)} %get-tuple-element.40), channel_id=1, source_target_pairs={{0,8},{4,12},{8,0},{12,4},{1,9},{5,13},{9,1},{13,5},{2,10},{6,14},... | collective-permute-start | bytes 835592 | tf_op jit(solution)/shard_map/ppermute | solution.py:425
  19.5 5.1 %collective-permute-start.1 = (bf16[64,2176]{1,0:T(8,128)(2,1)S(1)}, bf16[64,2176]{1,0:T(8,128)(2,1)S(1)}, u32[]{:S(2)}, u32[]{:S(2)}) collective-permute-start(bf16[64,2176]{1,0:T(8,128)(2,1)S(1)} %collective-permute-done.refs_4_), channel_id=1, source_target_pairs={{0,1},{1,0},{2,3},{3,2},{4,5},{5,4},{6,7},{7,6},{8,9},{9,8},{10,11... | collective-permute-start | bytes 835592 | tf_op jit(solution)/shard_map/ppermute | solution.py:425
  19.5 5.0 %collective-permute-start.2 = (bf16[2,256,256]{2,1,0:T(8,128)(2,1)S(1)}, bf16[2,256,256]{2,1,0:T(8,128)(2,1)S(1)}, u32[]{:S(2)}, u32[]{:S(2)}) collective-permute-start(bf16[2,256,256]{2,1,0:T(8,128)(2,1)S(1)} %get-tuple-element.41.refs_6_), channel_id=1, source_target_pairs={{0,1},{1,0},{2,3},{3,2},{4,5},{5,4},{6,7},{7,6},{8,9},{9,8},{10,11... | collective-permute-start | bytes 786440 | tf_op jit(solution)/shard_map/ppermute | solution.py:425
  20.0 4.5 %collective-permute-start.4 = (bf16[2,256,256]{2,1,0:T(8,128)(2,1)S(1)}, bf16[2,256,256]{2,1,0:T(8,128)(2,1)S(1)}, u32[]{:S(2)}, u32[]{:S(2)}) collective-permute-start(bf16[2,256,256]{2,1,0:T(8,128)(2,1)S(1)} %collective-permute-done.3.refs_8_), channel_id=1, source_target_pairs={{0,1},{1,0},{2,3},{3,2},{4,5},{5,4},{6,7},{7,6},{8,9},{9,8},{10,11... | collective-permute-start | bytes 786440 | tf_op jit(solution)/shard_map/ppermute | solution.py:425
  24.5 9.0 %collective-permute-start.11 = (bf16[64,2176]{1,0:T(8,128)(2,1)S(1)}, bf16[64,2176]{1,0:T(8,128)(2,1)S(1)}, u32[]{:S(2)}, u32[]{:S(2)}) collective-permute-start(bf16[64,2176]{1,0:T(8,128)(2,1)S(1)} %collective-permute-done.10.a), channel_id=1, source_target_pairs={{0,4},{4,0},{8,12},{12,8},{1,5},{5,1},{9,13},{13,9},{2,6},{6,2},{1... | collective-permute-start | bytes 835592 | tf_op jit(solution)/shard_map/ppermute | solution.py:425
  33.5 3.3 %copy-start.7 = (bf16[2,256,1024]{2,1,0:T(8,128)(2,1)S(1)}, bf16[2,256,1024]{2,1,0:T(8,128)(2,1)}, u32[]{:S(2)}) copy-start(bf16[2,256,1024]{2,1,0:T(8,128)(2,1)} %get-tuple-element.50.refs_2_) | copy-start | bytes 3145732
  33.6 3.2 %collective-permute-start.12 = (bf16[128,2176]{1,0:T(8,128)(2,1)S(1)}, bf16[128,2176]{1,0:T(8,128)(2,1)S(1)}, u32[]{:S(2)}, u32[]{:S(2)}) collective-permute-start(bf16[128,2176]{1,0:T(8,128)(2,1)S(1)} %shard_map.114.refs_0_), channel_id=1, source_target_pairs={{0,1},{1,0},{2,3},{3,2},{4,5},{5,4},{6,7},{7,6},{8,9},{9,8},{10,11... | collective-permute-start | bytes 1671176 | tf_op jit(solution)/shard_map/ppermute | solution.py:425
  33.7 2.4 %collective-permute-start.6 = (bf16[320,256]{1,0:T(8,128)(2,1)S(1)}, bf16[320,256]{1,0:T(8,128)(2,1)S(1)}, u32[]{:S(2)}, u32[]{:S(2)}) collective-permute-start(bf16[320,256]{1,0:T(8,128)(2,1)S(1)} %get-tuple-element.44), channel_id=1, source_target_pairs={{0,1},{1,0},{2,3},{3,2},{4,5},{5,4},{6,7},{7,6},{8,9},{9,8},{10,11... | collective-permute-start | bytes 491528 | tf_op jit(solution)/shard_map/ppermute | solution.py:425
  34.2 1.9 %collective-permute-start.7 = (bf16[256,256]{1,0:T(8,128)(2,1)S(1)}, bf16[256,256]{1,0:T(8,128)(2,1)S(1)}, u32[]{:S(2)}, u32[]{:S(2)}) collective-permute-start(bf16[256,256]{1,0:T(8,128)(2,1)S(1)} %get-tuple-element.45), channel_id=1, source_target_pairs={{0,1},{1,0},{2,3},{3,2},{4,5},{5,4},{6,7},{7,6},{8,9},{9,8},{10,11... | collective-permute-start | bytes 393224 | tf_op jit(solution)/shard_map/ppermute | solution.py:425
  36.1 9.9 %collective-permute-start.8 = (bf16[576,256]{1,0:T(8,128)(2,1)S(1)}, bf16[576,256]{1,0:T(8,128)(2,1)S(1)}, u32[]{:S(2)}, u32[]{:S(2)}) collective-permute-start(bf16[576,256]{1,0:T(8,128)(2,1)S(1)} %shard_map.112), channel_id=1, source_target_pairs={{0,2},{1,3},{2,0},{3,1},{4,6},{5,7},{6,4},{7,5},{8,10},{9,11},{10,... | collective-permute-start | bytes 884744 | tf_op jit(solution)/shard_map/ppermute | solution.py:425
  44.9 1.7 %collective-permute-start.14 = (bf16[320,256]{1,0:T(8,128)(2,1)S(1)}, bf16[320,256]{1,0:T(8,128)(2,1)S(1)}, u32[]{:S(2)}, u32[]{:S(2)}) collective-permute-start(bf16[320,256]{1,0:T(8,128)(2,1)S(1)} %get-tuple-element.53), channel_id=1, source_target_pairs={{0,1},{1,0},{2,3},{3,2},{4,5},{5,4},{6,7},{7,6},{8,9},{9,8},{10,11... | collective-permute-start | bytes 491528 | tf_op jit(solution)/shard_map/ppermute | solution.py:425
  45.0 1.6 %collective-permute-start.15 = (bf16[256,256]{1,0:T(8,128)(2,1)S(1)}, bf16[256,256]{1,0:T(8,128)(2,1)S(1)}, u32[]{:S(2)}, u32[]{:S(2)}) collective-permute-start(bf16[256,256]{1,0:T(8,128)(2,1)S(1)} %get-tuple-element.54), channel_id=1, source_target_pairs={{0,1},{1,0},{2,3},{3,2},{4,5},{5,4},{6,7},{7,6},{8,9},{9,8},{10,11... | collective-permute-start | bytes 393224 | tf_op jit(solution)/shard_map/ppermute | solution.py:425
  45.5 2.6 %collective-permute-start.5 = (bf16[576,256]{1,0:T(8,128)(2,1)S(1)}, bf16[576,256]{1,0:T(8,128)(2,1)S(1)}, u32[]{:S(2)}, u32[]{:S(2)}) collective-permute-start(bf16[576,256]{1,0:T(8,128)(2,1)S(1)} %get-tuple-element.43), channel_id=1, source_target_pairs={{0,1},{1,0},{2,3},{3,2},{4,5},{5,4},{6,7},{7,6},{8,9},{9,8},{10,11... | collective-permute-start | bytes 884744 | tf_op jit(solution)/shard_map/ppermute | solution.py:425
  45.5 5.0 %collective-permute-start.13 = (bf16[576,256]{1,0:T(8,128)(2,1)S(1)}, bf16[576,256]{1,0:T(8,128)(2,1)S(1)}, u32[]{:S(2)}, u32[]{:S(2)}) collective-permute-start(bf16[576,256]{1,0:T(8,128)(2,1)S(1)} %get-tuple-element.52), channel_id=1, source_target_pairs={{0,1},{1,0},{2,3},{3,2},{4,5},{5,4},{6,7},{7,6},{8,9},{9,8},{10,11... | collective-permute-start | bytes 884744 | tf_op jit(solution)/shard_map/ppermute | solution.py:425
  46.6 9.3 %collective-permute-start.16 = (bf16[576,256]{1,0:T(8,128)(2,1)S(1)}, bf16[576,256]{1,0:T(8,128)(2,1)S(1)}, u32[]{:S(2)}, u32[]{:S(2)}) collective-permute-start(bf16[576,256]{1,0:T(8,128)(2,1)S(1)} %shard_map.116), channel_id=1, source_target_pairs={{0,2},{1,3},{2,0},{3,1},{4,6},{5,7},{6,4},{7,5},{8,10},{9,11},{10,... | collective-permute-start | bytes 884744 | tf_op jit(solution)/shard_map/ppermute | solution.py:425
  48.5 16.1 %collective-permute-start.9 = (bf16[288,256]{1,0:T(8,128)(2,1)S(1)}, bf16[288,256]{1,0:T(8,128)(2,1)S(1)}, u32[]{:S(2)}, u32[]{:S(2)}) collective-permute-start(bf16[288,256]{1,0:T(8,128)(2,1)S(1)} %get-tuple-element.49), channel_id=1, source_target_pairs={{0,4},{4,0},{8,12},{12,8},{1,5},{5,1},{9,13},{13,9},{2,6},{6,2},{1... | collective-permute-start | bytes 442376 | tf_op jit(solution)/shard_map/ppermute | solution.py:425
  56.3 13.9 %collective-permute-start.17 = (bf16[288,256]{1,0:T(8,128)(2,1)S(1)}, bf16[288,256]{1,0:T(8,128)(2,1)S(1)}, u32[]{:S(2)}, u32[]{:S(2)}) collective-permute-start(bf16[288,256]{1,0:T(8,128)(2,1)S(1)} %get-tuple-element.57), channel_id=1, source_target_pairs={{0,8},{4,12},{8,0},{12,4},{1,9},{5,13},{9,1},{13,5},{2,10},{6,14},... | collective-permute-start | bytes 442376 | tf_op jit(solution)/shard_map/ppermute | solution.py:425
  59.2 11.0 %collective-permute-start.18 = (bf16[288,256]{1,0:T(8,128)(2,1)S(1)}, bf16[288,256]{1,0:T(8,128)(2,1)S(1)}, u32[]{:S(2)}, u32[]{:S(2)}) collective-permute-start(bf16[288,256]{1,0:T(8,128)(2,1)S(1)} %get-tuple-element.58), channel_id=1, source_target_pairs={{0,12},{4,8},{8,4},{12,0},{1,13},{5,9},{9,5},{13,1},{2,14},{6,10},... | collective-permute-start | bytes 442376 | tf_op jit(solution)/shard_map/ppermute | solution.py:425
  60.5 9.7 %copy-start.1 = (bf16[128,1024]{1,0:T(8,128)(2,1)S(1)}, bf16[128,1024]{1,0:T(8,128)(2,1)}, u32[]{:S(2)}) copy-start(bf16[128,1024]{1,0:T(8,128)(2,1)} %x_in.1) | copy-start | bytes 786436
  60.5 9.7 %copy-start.3 = (bf16[128,1024]{1,0:T(8,128)(2,1)S(1)}, bf16[128,1024]{1,0:T(8,128)(2,1)}, u32[]{:S(2)}) copy-start(bf16[128,1024]{1,0:T(8,128)(2,1)} %c_in.1) | copy-start | bytes 786436
  (3 other events, 2.3 us)

commit v4 on v3

--- a/solution.py
+++ b/solution.py
@@ -184,7 +184,7 @@
     return copies
 
 
-def payload_kernel(x, c, gates_in, routes_in, pair_in, out_o, pair_o, gates, routes, sems):
+def payload_kernel(x, c, gates_in, routes_in, pair_in, out_o, own_o, pair_o, gates, routes, sems):
     core = lax.rem(lax.axis_index("tensor"), 2)
     mine = pl.ds(pl.multiple_of(core * HALF, HALF), HALF)
     copies = load(
@@ -193,6 +193,8 @@
             (routes_in, routes),
             (x.at[mine, :], out_o.at[:, 0:WIDTH]),
             (c.at[mine, :], out_o.at[:, WIDTH : 2 * WIDTH]),
+            (x, own_o.at[:, 0:WIDTH]),
+            (c, own_o.at[:, WIDTH : 2 * WIDTH]),
             (pair_in, pair_o),
         ],
         sems,
@@ -205,6 +207,7 @@
         [routes[...].astype(F32), high, low, jnp.zeros((122, 128), F32)], axis=0
     )
     columns = meta.T
+    own_o[:, 2 * WIDTH :] = columns.astype(BF16)
     out_o[:, 2 * WIDTH :] = jnp.where(core == 0, columns[0:HALF], columns[HALF:]).astype(BF16)
     for copy in copies[2:]:
         copy.wait()
@@ -224,7 +227,7 @@
 
 def towers(meta, whole, up, down, ready, pair, outs, scratch):
     keep, send_here, send_away, send_last, cross_o, act_o, grad_o, pre_o, gram_o, pick_o, gate_o = outs
-    flipped, partial, half_gram, terms = scratch
+    flipped, partial, half_gram, terms, rows, slope, outs_s, backs = scratch
     j = lax.axis_index("tensor")
     core = lax.rem(j, 2)
     xi = j // 2
@@ -243,8 +246,9 @@
     b = lax.broadcasted_iota(jnp.int32, (256, 256), 1)
     swapped = (a % 16) * 16 + a // 16
     both = (jnp.where(a == b, 1.0, 0.0) + jnp.where(swapped == b, 1.0, 0.0)).astype(BF16)
-    half_gram[136:144, :] = jnp.zeros((8, 128), F32)
-    for e in range(2):
+    slots = lax.broadcasted_iota(jnp.int32, (128, tokens), 0).astype(F32)
+    both_e = range(2)
+    for e in both_e:
         mine = (first + e).astype(F32)
         s0 = meta[0:1, :] == mine
         s1 = meta[1:2, :] == mine
@@ -252,94 +256,87 @@
         gate = jnp.where(s0, meta[2:3, :], 0.0) + jnp.where(s1, meta[3:4, :], 0.0)
         place = mm(jnp.broadcast_to(named, (8, tokens)).astype(BF16), before)[0:1, :]
         place = jnp.where(named > 0.5, place, -1.0)
-        hit = lax.broadcasted_iota(jnp.int32, (128, tokens), 0).astype(F32) == place
-        pick = jnp.where(hit, 1.0, 0.0).astype(BF16)
+        hit = slots == place
+        pick_o[e] = jnp.where(hit, 1.0, 0.0).astype(BF16)
         weight = jnp.sum(jnp.where(hit, gate, 0.0), axis=1, keepdims=True)
         gate_o[e] = jnp.broadcast_to(weight, (128, 128))
-        pick_o[e] = pick
-        rows = mm(pick, whole[:, 0:WIDTH])
-        grad = (weight * mm(pick, whole[:, WIDTH : 2 * WIDTH])).astype(BF16)
-        grad_o[e] = grad
-        flipped[...] = rows.T
+    for e in both_e:
+        rows[e] = mm(pick_o[e], whole[:, 0:WIDTH])
+    for e in both_e:
+        flipped[e] = rows[e].T
+    for e in both_e:
+        grad = mm(pick_o[e], whole[:, WIDTH : 2 * WIDTH])
+        grad_o[e] = (gate_o[e][:, 0:1] * grad).astype(BF16)
+    for e in both_e:
+        half_gram[e, 136:144, :] = jnp.zeros((8, 128), F32)
         at = 0
         for i in range(16):
-            left = flipped[i * 64 : i * 64 + 64, :]
+            left = flipped[e, i * 64 : i * 64 + 64, :]
             for q in range(i, 16):
-                prod = left * flipped[q * 64 : q * 64 + 64, :]
-                partial[at * 8 : at * 8 + 8, :] = jnp.sum(prod.reshape(8, 8, 128), axis=0)
+                prod = left * flipped[e, q * 64 : q * 64 + 64, :]
+                partial[e, at * 8 : at * 8 + 8, :] = jnp.sum(prod.reshape(8, 8, 128), axis=0)
                 at += 1
         for g in range(17):
-            acc = partial[pl.ds(g * 64, 8, stride=8), :]
+            acc = partial[e, pl.ds(g * 64, 8, stride=8), :]
             for q in range(1, 8):
-                acc = acc + partial[pl.ds(g * 64 + q, 8, stride=8), :]
-            half_gram[g * 8 : g * 8 + 8, :] = acc * (1.0 / DE)
-        gram = mm(spread, half_gram[...].astype(BF16)).astype(BF16)
-        gram_o[e] = gram
-        cross = (rows + mm(gram, pair[e], TN)).astype(BF16)
-        cross_o[e] = cross
-        if e == 0:
-            for copy in ready:
-                copy.wait()
-        pre = mm(cross, up[e])
+                acc = acc + partial[e, pl.ds(g * 64 + q, 8, stride=8), :]
+            half_gram[e, g * 8 : g * 8 + 8, :] = acc * (1.0 / DE)
+        gram_o[e] = mm(spread, half_gram[e].astype(BF16)).astype(BF16)
+    for e in both_e:
+        cross_o[e] = (rows[e] + mm(gram_o[e], pair[e], TN)).astype(BF16)
+    for copy in ready:
+        copy.wait()
+    for e in both_e:
+        slope[e] = mm(grad_o[e], down[e], NT)
+    for e in both_e:
+        pre = mm(cross_o[e], up[e])
         sig = jax.nn.sigmoid(pre)
-        act = (pre * sig).astype(BF16)
-        act_o[e] = act
-        slope = sig * (1.0 + pre * (1.0 - sig))
-        dpre = (mm(grad, down[e], NT) * slope).astype(BF16)
-        pre_o[e] = dpre
-        terms[...] = mm(dpre, up[e], NT).astype(BF16)
-        back = mm(both, mm(pair[e], terms[...], NT).astype(BF16)).astype(BF16)
-        for xr in (1, 0):
-            for part in (1, 0):
-                block = 2 * (xi ^ xr) + (core ^ part)
-                cols = pl.ds(pl.multiple_of(block * 256, 256), 256)
-                if part == 0:
-                    low, high = keep.at[xr, 0:320], keep.at[xr, 320:576]
-                elif xr == 0:
-                    low, high = send_here.at[0:320], send_here.at[320:576]
-                else:
-                    low, high = send_away, send_last
-                low[e * 128 : e * 128 + 128, :] = terms[:, cols]
-                high[e * 128 : e * 128 + 128, :] = mm(act, down[e, :, cols]).astype(BF16)
-                for q in range(4):
-                    def put(low=low, q=q):
-                        low[256:320, e * 128 : e * 128 + 128] = back[q * 64 : q * 64 + 64, :]
-
-                    pl.when(block == q)(put)
+        act_o[e] = (pre * sig).astype(BF16)
+        pre_o[e] = (slope[e] * sig * (1.0 + pre * (1.0 - sig))).astype(BF16)
+    for e in both_e:
+        terms[e] = mm(pre_o[e], up[e], NT).astype(BF16)
+    for e in both_e:
+        outs_s[e] = mm(act_o[e], down[e]).astype(BF16)
+    for e in both_e:
+        back = mm(pair[e], terms[e], NT).astype(BF16)
+        backs[e] = mm(both, back).astype(BF16)
+    for xr in (1, 0):
+        for part in (1, 0):
+            block = 2 * (xi ^ xr) + (core ^ part)
+            cols = pl.ds(pl.multiple_of(block * 256, 256), 256)
+            if part == 0:
+                low, high = keep.at[xr, 0:320], keep.at[xr, 320:576]
+            elif xr == 0:
+                low, high = send_here.at[0:320], send_here.at[320:576]
+            else:
+                low, high = send_away, send_last
+            for e in both_e:
+                mine = slice(e * 128, e * 128 + 128)
+                low[mine, :] = terms[e, :, cols]
+                high[mine, :] = outs_s[e, :, cols]
+                rows64 = pl.ds(pl.multiple_of(block * 64, 64), 64)
+                low[256:320, mine] = backs[e, rows64, :]
+
+
+def read_meta(info):
+    rows = info[...].astype(F32).T
+    return jnp.concatenate([rows[0:2], rows[2:4] + rows[4:6]], axis=0)
 
 
 def own_chunk_kernel(*refs):
-    x, c, gates_in, routes_in, near, far, p0, p1, p2, p3, up_in, down_in = refs[:12]
-    outs, pair_o = refs[12:23], refs[23]
-    whole, info, gates, routes, up, down, sems = refs[24:31]
+    own, near, far, p0, p1, x0, x1, d0, d1, up_in, down_in = refs[:11]
+    outs, pair_o = refs[11:22], refs[22]
+    whole, info, up, down, sems = refs[23:28]
     j = lax.axis_index("tensor")
-    copies = load(
-        [
-            (gates_in, gates),
-            (routes_in, routes),
-            (x, whole.at[0:128, 0:WIDTH]),
-            (c, whole.at[0:128, WIDTH : 2 * WIDTH]),
-            (up_in, up),
-            (down_in, down),
-        ],
-        sems,
-    )
+    copies = load([(up_in, up), (down_in, down)], sems)
+    whole[0:128, :] = own[:, 0 : 2 * WIDTH]
+    info[0:128, :] = own[:, 2 * WIDTH :]
     place_rows(whole, info, 1, lax.rem(j, 2), near, far)
-    for k, piece in enumerate((p0, p1, p2, p3)):
+    for k, piece in enumerate((p0, p1, (x0, x1), (d0, d1))):
         cols = pl.ds(pl.multiple_of((j ^ k) * 256, 256), 256)
         for e in range(2):
-            pair_o[e, :, cols] = piece[e]
-    for copy in copies[:4]:
-        copy.wait()
-    other = info[128:256, :].astype(F32).T
-    meta = jnp.concatenate(
-        [
-            jnp.concatenate([routes[...].astype(F32), other[0:2]], axis=1),
-            jnp.concatenate([gates[...], other[2:4] + other[4:6]], axis=1),
-        ],
-        axis=0,
-    )
-    towers(meta, whole, up, down, copies[4:], pair_o, outs, refs[31:])
+            pair_o[e, :, cols] = piece[e][...]
+    towers(read_meta(info), whole, up, down, copies, pair_o, outs, refs[28:])
 
 
 def far_chunk_kernel(*refs):
@@ -351,12 +348,12 @@
     for r in range(2):
         rows = slice(r * HALF, r * HALF + HALF)
         place_rows(whole, info, r, core, near.at[rows, :], far.at[rows, :])
-    other = info[...].astype(F32).T
-    meta = jnp.concatenate([other[0:2], other[2:4] + other[4:6]], axis=0)
-    towers(meta, whole, up, down, copies, pair, outs, refs[21:])
-
-
-def weights_kernel(act0, grad0, cross0, pre0, act1, grad1, cross1, pre1, down_o, up_o):
+    towers(read_meta(info), whole, up, down, copies, pair, outs, refs[21:])
+
+
+def weights_kernel(act0, grad0, cross0, pre0, act1, grad1, cross1, pre1, down_o, up_o, done_o):
+    done_o[...] = jnp.zeros((8, 128), F32)
+
     def stack(a, b):
         return jnp.concatenate([a, b], axis=0)
 
@@ -369,7 +366,8 @@
     return (a.astype(F32) + b.astype(F32)).astype(BF16)
 
 
-def combine_kernel(mine, other, theirs, pick, gate, first_o, second_o, rows_o):
+def combine_kernel(mine, other, theirs, pick, gate, *rest):
+    first_o, second_o, rows_o = rest[-3:]
     both = add2(add2(mine[0], other[...]), theirs[...])
     grads = jnp.zeros((256, 256), F32)
     mixed = jnp.zeros((256, 256), F32)
@@ -395,20 +393,17 @@
         out_o[e] = (mm(gram0[e], rows0[e]) + mm(gram1[e], rows1[e])).astype(BF16)
 
 
-def final_kernel(x_in, c_in, g0, g1, g2, g3, mixed_o, grad_o, x, c, flipped, sems):
-    copies = load([(x_in, x), (c_in, c)], sems)
-    for copy in copies:
-        copy.wait()
-    cols = pl.ds(pl.multiple_of(lax.axis_index("tensor") * 256, 256), 256)
-    mixed = x[:, cols].astype(F32)
-    total = c[:, cols].astype(F32)
+def final_kernel(own, g0, g1, g2, g3, mixed_o, grad_o, flipped):
+    column = pl.multiple_of(lax.axis_index("tensor") * 256, 256)
+    mixed = own[:, pl.ds(column, 256)].astype(F32)
+    total = own[:, pl.ds(WIDTH + column, 256)].astype(F32)
     back = jnp.zeros((32, 256), F32)
     for g in (g0, g1, g2, g3):
         total = total + g[0:128, :].astype(F32)
         back = back + g[128:160, :].astype(F32)
         mixed = mixed + g[160:288, :].astype(F32)
     mixed_o[...] = mixed.astype(BF16)
-    flipped[...] = x[...].astype(F32).T
+    flipped[...] = own[:, 0:WIDTH].astype(F32).T
     back = jnp.concatenate([back[:, 0:128], back[:, 128:256]], axis=0)
     pieces = []
     for i in range(4):
@@ -443,10 +438,14 @@
 
 def chunk_scratch():
     return [
-        pltpu.VMEM((1024, 128), F32),
-        pltpu.VMEM((1088, 128), F32),
-        pltpu.VMEM((144, 128), F32),
-        pltpu.VMEM((128, 1024), BF16),
+        pltpu.VMEM((2, 1024, 128), F32),
+        pltpu.VMEM((2, 1088, 128), F32),
+        pltpu.VMEM((2, 144, 128), F32),
+        pltpu.VMEM((2, 128, 1024), BF16),
+        pltpu.VMEM((2, 128, 1024), F32),
+        pltpu.VMEM((2, 128, 512), F32),
+        pltpu.VMEM((2, 128, 1024), BF16),
+        pltpu.VMEM((2, 256, 128), BF16),
     ]
 
 
@@ -470,51 +469,53 @@
 
 def gathered_body(inputs, cotangent, gate_values, routes, pair_weight, up_weight, down_weight):
     gates, choices = gate_values.T, routes.T
-    payload, pair_own = kernel_call(
+    width = 2 * WIDTH + 128
+    payload, own, pair_own = kernel_call(
         payload_kernel,
-        (shape((HALF, 2 * WIDTH + 128)), shape((2, 256, 256))),
+        (shape((HALF, width)), shape((2 * HALF, width)), shape((2, 256, 256))),
         "hhhhh",
         scratch=[
             pltpu.VMEM((2, 128), F32),
             pltpu.VMEM((2, 128), jnp.int32),
-            pltpu.SemaphoreType.DMA((5,)),
+            pltpu.SemaphoreType.DMA((7,)),
         ],
+        vmem=60,
     )(inputs, cotangent, gates, choices, pair_weight)
     got = [swap(payload, "expert", 1), swap(payload, "expert", 2)]
     got.append(swap(got[1], "expert", 1))
-    pair_x = swap(pair_own, "tensor", 2)
+    pair_x = [swap(pair_own[e], "tensor", 2) for e in range(2)]
     pair_c = swap(pair_own, "tensor", 1)
-    pair_d = swap(pair_x, "tensor", 1)
+    pair_d = [swap(v, "tensor", 1) for v in pair_x]
     near_other = swap(got[0], "tensor", 1)
     chunk = kernel_call(
         own_chunk_kernel,
         chunk_outs() + (shape((2, 256, 1024)),),
-        "hhhhvvvvvvhh",
+        "vvvvvvvvvhh",
         scratch=[
             pltpu.VMEM((256, 2048), BF16),
             pltpu.VMEM((256, 128), BF16),
-            pltpu.VMEM((2, 128), F32),
-            pltpu.VMEM((2, 128), jnp.int32),
         ]
         + weight_scratch()
-        + [pltpu.SemaphoreType.DMA((6,))]
+        + [pltpu.SemaphoreType.DMA((2,))]
         + chunk_scratch(),
         flops=4_000_000_000,
         nbytes=10_000_000,
     )(
-        inputs, cotangent, gates, choices, got[0], near_other,
-        pair_own, pair_c, pair_x, pair_d, up_weight, down_weight,
+        own, got[0], near_other,
+        pair_own, pair_c, *pair_x, *pair_d, up_weight, down_weight,
     )
     keep, here, away, last, cross, act, grad, pre, gram, pick, gate, pair_all = chunk
     other, theirs = sums_over_tensor(keep, here, away, last)
     part = shape((288, 256))
-    combine = kernel_call(
-        combine_kernel,
-        (part, part, shape((2, 128, 256))),
-        "vvvvv",
-        flops=300_000_000,
-        nbytes=2_000_000,
-    )
+    def combine(*operands):
+        return kernel_call(
+            combine_kernel,
+            (part, part, shape((2, 128, 256))),
+            "vvvvva"[: len(operands)],
+            flops=300_000_000,
+            nbytes=2_000_000,
+        )(*operands)
+
     own_part, near_part, rows = combine(keep, other, theirs, pick, gate)
     far_mine = kernel_call(join_kernel, shape((2 * HALF, 2 * WIDTH + 128)), "vva")(
         got[1], got[2], gate
@@ -534,31 +535,28 @@
     fkeep, fhere, faway, flast, fcross, fact, fgrad, fpre, fgram, fpick, fgate = chunk
     fother, ftheirs = sums_over_tensor(fkeep, fhere, faway, flast, after=(theirs,))
     near_got = swap(near_part, "expert", 1)
-    part2, part3, frows = combine(fkeep, fother, ftheirs, fpick, fgate)
-    got2, got3 = swap(part2, "expert", 2), swap(part3, "expert", 3)
-    grad_down, grad_up = kernel_call(
+    grad_down, grad_up, weights_done = kernel_call(
         weights_kernel,
-        (shape((2, 512, 1024)), shape((2, 1024, 512))),
+        (shape((2, 512, 1024)), shape((2, 1024, 512)), shape((8, 128), F32)),
         "vvvvvvvv",
         flops=3_000_000_000,
         nbytes=8_000_000,
     )(act, grad, cross, pre, fact, fgrad, fcross, fpre)
+    part2, part3, frows = combine(
+        fkeep, fother, ftheirs, fpick, fgate, weights_done
+    )
+    got2, got3 = swap(part2, "expert", 2), swap(part3, "expert", 3)
     grad_pair = kernel_call(
         pair_kernel, shape((2, 256, 256)), "vvvv", flops=300_000_000, nbytes=2_000_000
     )(gram, rows, fgram, frows)
     mixed, grad_input = kernel_call(
         final_kernel,
         (shape((128, 256)), shape((128, 256))),
-        "hhvvvv",
-        scratch=[
-            pltpu.VMEM((128, 1024), BF16),
-            pltpu.VMEM((128, 1024), BF16),
-            pltpu.VMEM((1024, 128), F32),
-            pltpu.SemaphoreType.DMA((2,)),
-        ],
+        "vvvvv",
+        scratch=[pltpu.VMEM((1024, 128), F32)],
         flops=100_000_000,
         nbytes=1_000_000,
-    )(inputs, cotangent, own_part, near_got, got2, got3)
+    )(own, own_part, near_got, got2, got3)
     return mixed, grad_input, grad_pair, grad_up, grad_down
 
 

time: 71.6 us -> 74.5 us (1.041)
  waiting for transfers between devices: 25.1 us -> 32.1 us
  Pallas kernels: 23.3 us -> 20.8 us
  local copies, waits for them, and re-layouts: 4.21 us -> 3 us
  starting transfers between devices: 17.9 us -> 16.9 us
    ppermute x19 -> x21, waiting for transfers between devices: 25.1 us -> 32.1 us  [swap(): return lax.ppermute(value, axis, [(i, i ^ mask) for i in range(size)])]
    pallas_call x1, Pallas kernels: 8.09 us -> 5.53 us  [gathered_body(): kernel_call(far_chunk_kernel, chunk_outs(), 'vvvhh', scratch=[pltpu.VMEM(...]
    unnamed x16 -> x8, local copies, waits for them, and re-layouts: 4.21 us -> 2.01 us
    squeeze x0 -> x1, local copies, waits for them, and re-layouts: none -> 0.99 us  [gathered_body(): pair_x = [swap(pair_own[e], 'tensor', 2) for e in range(2)]]
    ppermute x19 -> x21, starting transfers between devices: 17.9 us -> 16.9 us  [swap(): return lax.ppermute(value, axis, [(i, i ^ mask) for i in range(size)])]
  transfers between devices with their start and end apart: 19 -> 21, of which waited for: 6 -> 8; matrix products, arithmetic and copies ran while one was open for 0% -> 1% of each run, Pallas kernels for 31% -> 24%
where the time goes in v4:
time: 74.5 us; the launch traced here: 73.6 us
  waiting for transfers between devices  32.1 us (43%)
  Pallas kernels  20.8 us (28%)
  starting transfers between devices  16.9 us (23%)
  local copies, waits for them, and re-layouts  3 us (4%)
  between operations  0.76 us (1%)
    ppermute x21, waiting for transfers between devices, swap(): return lax.ppermute(value, axis, [(i, i ^ mask) for i in range(size)])  32.1 us
    ppermute x21, starting transfers between devices, swap(): return lax.ppermute(value, axis, [(i, i ^ mask) for i in range(size)])  16.9 us
    pallas_call x1, Pallas kernels, gathered_body(): kernel_call(own_chunk_kernel, chunk_outs() + (shape((2, 256, 1024)),), 'v...  7.02 us
    pallas_call x1, Pallas kernels, gathered_body(): kernel_call(far_chunk_kernel, chunk_outs(), 'vvvhh', scratch=[pltpu.VMEM(...  5.53 us
    pallas_call x1, Pallas kernels, gathered_body(): kernel_call(weights_kernel, (shape((2, 512, 1024)), shape((2, 1024, 512))...  3.02 us
    pallas_call x1, Pallas kernels, gathered_body(): kernel_call(payload_kernel, (shape((HALF, width)), shape((2 * HALF, width...  2.31 us
    unnamed x8, local copies, waits for them, and re-layouts  2.01 us
  transfers between devices with their start and end apart: 21, of which 8 were waited for; matrix products, arithmetic and copies ran while one was open for 1% of the time, Pallas kernels for 24%

profile of v4, /device:TPU:0, one launch (start us, length us, event | category | flops | bytes accessed | tf_op | source)
XLA Modules:
  0.0 73.6 jit_solution(12693089230128435749)
XLA Ops:
  0.6 2.3 %shard_map.110 = (bf16[64,2176]{1,0:T(8,128)(2,1)}, bf16[128,2176]{1,0:T(8,128)(2,1)}, bf16[2,256,256]{2,1,0:T(8,128)(2,1)}) custom-call(bf16[128,1024]{1,0:T(8,128)(2,1)} %x.1, bf16[128,1024]{1,0:T(8,128)(2,1)} %c.1, f32[2,128]{1,0:T(2,128)} %bitcast.6, s32[2,128]{1,0:T(2,128)} %bitcast.7, bf16[2,256,256]{2,1,0:T(8,128)(2,1)} %pair_in.1), custom_call_target="tpu_custom_call" | custom-call | tf_op jit(solution)/shard_map/pallas_call | solution.py:473
  2.9 3.1 %collective-permute-start = (bf16[64,2176]{1,0:T(8,128)(2,1)}, bf16[64,2176]{1,0:T(8,128)(2,1)S(1)}, u32[]{:S(2)}, u32[]{:S(2)}) collective-permute-start(bf16[64,2176]{1,0:T(8,128)(2,1)} %get-tuple-element.43), channel_id=1, source_target_pairs={{0,4},{4,0},{8,12},{12,8},{1,5},{5,1},{9,13},{13,9},{2,6},{6,2},{1... | collective-permute-start | bytes 835592 | tf_op jit(solution)/shard_map/ppermute | solution.py:420
  6.0 2.6 %collective-permute-start.12 = (bf16[64,2176]{1,0:T(8,128)(2,1)}, bf16[64,2176]{1,0:T(8,128)(2,1)S(1)}, u32[]{:S(2)}, u32[]{:S(2)}) collective-permute-start(bf16[64,2176]{1,0:T(8,128)(2,1)} %get-tuple-element.43), channel_id=1, source_target_pairs={{0,8},{4,12},{8,0},{12,4},{1,9},{5,13},{9,1},{13,5},{2,10},{6,14},... | collective-permute-start | bytes 835592 | tf_op jit(solution)/shard_map/ppermute | solution.py:420
  8.6 10.1 %collective-permute-done.refs_1_ = bf16[64,2176]{1,0:T(8,128)(2,1)S(1)} collective-permute-done((bf16[64,2176]{1,0:T(8,128)(2,1)}, bf16[64,2176]{1,0:T(8,128)(2,1)S(1)}, u32[]{:S(2)}, u32[]{:S(2)}) %collective-permute-start) | collective-permute-done | bytes 278560 | tf_op jit(solution)/shard_map/ppermute | solution.py:420
  18.7 1.0 %slice_bitcast_fusion = (bf16[256,256]{1,0:T(8,128)(2,1)S(1)}, bf16[256,256]{1,0:T(8,128)(2,1)S(1)}) fusion(bf16[2,256,256]{2,1,0:T(8,128)(2,1)} %get-tuple-element.44.refs_3_), kind=kLoop, calls=%fused_computation | loop fusion | bytes 524288 | tf_op jit(solution)/shard_map/squeeze | solution.py:486
  19.7 1.7 %collective-permute-start.4 = (bf16[256,256]{1,0:T(8,128)(2,1)S(1)}, bf16[256,256]{1,0:T(8,128)(2,1)S(1)}, u32[]{:S(2)}, u32[]{:S(2)}) collective-permute-start(bf16[256,256]{1,0:T(8,128)(2,1)S(1)} %get-tuple-element.79), channel_id=1, source_target_pairs={{0,2},{1,3},{2,0},{3,1},{4,6},{5,7},{6,4},{7,5},{8,10},{9,11},{10,... | collective-permute-start | bytes 393224 | tf_op jit(solution)/shard_map/ppermute | solution.py:420
  21.8 4.3 %collective-permute-done.4.refs_6_ = bf16[256,256]{1,0:T(8,128)(2,1)S(1)} collective-permute-done((bf16[256,256]{1,0:T(8,128)(2,1)S(1)}, bf16[256,256]{1,0:T(8,128)(2,1)S(1)}, u32[]{:S(2)}, u32[]{:S(2)}) %collective-permute-start.4) | collective-permute-done | bytes 131104 | tf_op jit(solution)/shard_map/ppermute | solution.py:420
  26.1 2.4 %collective-permute-done.3.refs_5_ = bf16[256,256]{1,0:T(8,128)(2,1)S(1)} collective-permute-done((bf16[256,256]{1,0:T(8,128)(2,1)S(1)}, bf16[256,256]{1,0:T(8,128)(2,1)S(1)}, u32[]{:S(2)}, u32[]{:S(2)}) %collective-permute-start.3) | collective-permute-done | bytes 131104 | tf_op jit(solution)/shard_map/ppermute | solution.py:420
  28.5 1.3 %collective-permute-done.5.refs_7_ = bf16[256,256]{1,0:T(8,128)(2,1)S(1)} collective-permute-done((bf16[256,256]{1,0:T(8,128)(2,1)S(1)}, bf16[256,256]{1,0:T(8,128)(2,1)S(1)}, u32[]{:S(2)}, u32[]{:S(2)}) %collective-permute-start.5) | collective-permute-done | bytes 131104 | tf_op jit(solution)/shard_map/ppermute | solution.py:420
  29.9 1.1 %copy-done = bf16[128,2176]{1,0:T(8,128)(2,1)S(1)} copy-done((bf16[128,2176]{1,0:T(8,128)(2,1)S(1)}, bf16[128,2176]{1,0:T(8,128)(2,1)}, u32[]{:S(2)}) %copy-start) | copy-done | bytes 557080
  30.9 0.9 %copy-done.2 = bf16[2,256,256]{2,1,0:T(8,128)(2,1)S(1)} copy-done((bf16[2,256,256]{2,1,0:T(8,128)(2,1)S(1)}, bf16[2,256,256]{2,1,0:T(8,128)(2,1)}, u32[]{:S(2)}) %copy-start.2) | copy-done | bytes 262168
  31.9 7.0 %shard_map.111 = (bf16[2,576,256]{2,1,0:T(8,128)(2,1)S(1)}, bf16[576,256]{1,0:T(8,128)(2,1)S(1)}, bf16[320,256]{1,0:T(8,128)(2,1)S(1)}, bf16[256,256]{1,0:T(8,12...) custom-call(bf16[128,2176]{1,0:T(8,128)(2,1)S(1)} %copy-done, ...), custom_call_target="tpu_custom_call" | custom-call | flops 4000000000 | bytes 10000000 | tf_op jit(solution)/shard_map/pallas_call | solution.py:490
  40.1 1.4 %collective-permute-done.9.high = bf16[256,256]{1,0:T(8,128)(2,1)S(1)} collective-permute-done((bf16[256,256]{1,0:T(8,128)(2,1)S(1)}, bf16[256,256]{1,0:T(8,128)(2,1)S(1)}, u32[]{:S(2)}, u32[]{:S(2)}) %collective-permute-start.9) | collective-permute-done | bytes 131104 | tf_op jit(solution)/shard_map/ppermute | solution.py:420
  41.5 1.7 %collective-permute-start.10 = (bf16[576,256]{1,0:T(8,128)(2,1)S(1)}, bf16[576,256]{1,0:T(8,128)(2,1)S(1)}, u32[]{:S(2)}, u32[]{:S(2)}) collective-permute-start(bf16[576,256]{1,0:T(8,128)(2,1)S(1)} %shard_map.112), channel_id=1, source_target_pairs={{0,2},{1,3},{2,0},{3,1},{4,6},{5,7},{6,4},{7,5},{8,10},{9,11},{10,... | collective-permute-start | bytes 884744 | tf_op jit(solution)/shard_map/ppermute | solution.py:420
  43.2 5.5 %shard_map.115 = (bf16[2,576,256]{2,1,0:T(8,128)(2,1)S(1)}, bf16[576,256]{1,0:T(8,128)(2,1)S(1)}, bf16[320,256]{1,0:T(8,128)(2,1)S(1)}, bf16[256,256]{1,0:T(8,12...) custom-call(bf16[128,2176]{1,0:T(8,128)(2,1)S(1)} %shard_map.114.ref, ...), custom_call_target="tpu_custom_call" | custom-call | flops 4000000000 | bytes 10000000 | tf_op jit(solution)/shard_map/pallas_call | solution.py:524
  49.4 1.2 %collective-permute-done.10.theirs.rest_0_ = bf16[576,256]{1,0:T(8,128)(2,1)S(1)} collective-permute-done((bf16[576,256]{1,0:T(8,128)(2,1)S(1)}, bf16[576,256]{1,0:T(8,128)(2,1)S(1)}, u32[]{:S(2)}, u32[]{:S(2)}) %collective-permute-start.10) | collective-permute-done | bytes 294944 | tf_op jit(solution)/shard_map/ppermute | solution.py:420
  50.7 1.7 %collective-permute-start.18 = (bf16[576,256]{1,0:T(8,128)(2,1)S(1)}, bf16[576,256]{1,0:T(8,128)(2,1)S(1)}, u32[]{:S(2)}, u32[]{:S(2)}) collective-permute-start(bf16[576,256]{1,0:T(8,128)(2,1)S(1)} %shard_map.116), channel_id=1, source_target_pairs={{0,2},{1,3},{2,0},{3,1},{4,6},{5,7},{6,4},{7,5},{8,10},{9,11},{10,... | collective-permute-start | bytes 884744 | tf_op jit(solution)/shard_map/ppermute | solution.py:420
  53.7 3.0 %shard_map.117 = (bf16[2,512,1024]{2,1,0:T(8,128)(2,1)}, bf16[2,1024,512]{2,1,0:T(8,128)(2,1)}, f32[8,128]{1,0:T(8,128)S(1)}) custom-call(bf16[2,128,512]{2,1,0:T(8,128)(2,1)S(1)} %get-tuple-element.60.act0, bf16[2,128,1024]{2,1,0:T(8,128)(2,1)S(1)} %get-tuple-element.61.grad0, bf16[2,128,1024]{2,1,0:T(8,128)(2,1)S(1)} %get-tuple-element.62.cross0, ...), custom_call_target="tpu_custom_call" | custom-call | flops 3000000000 | bytes 8000000 | tf_op jit(solution)/shard_map/pallas_call | solution.py:538
  56.7 3.0 %collective-permute-done.18.theirs = bf16[576,256]{1,0:T(8,128)(2,1)S(1)} collective-permute-done((bf16[576,256]{1,0:T(8,128)(2,1)S(1)}, bf16[576,256]{1,0:T(8,128)(2,1)S(1)}, u32[]{:S(2)}, u32[]{:S(2)}) %collective-permute-start.18) | collective-permute-done | bytes 294944 | tf_op jit(solution)/shard_map/ppermute | solution.py:420
  60.2 1.8 %collective-permute-start.19 = (bf16[288,256]{1,0:T(8,128)(2,1)S(1)}, bf16[288,256]{1,0:T(8,128)(2,1)S(1)}, u32[]{:S(2)}, u32[]{:S(2)}) collective-permute-start(bf16[288,256]{1,0:T(8,128)(2,1)S(1)} %get-tuple-element.69), channel_id=1, source_target_pairs={{0,8},{4,12},{8,0},{12,4},{1,9},{5,13},{9,1},{13,5},{2,10},{6,14},... | collective-permute-start | bytes 442376 | tf_op jit(solution)/shard_map/ppermute | solution.py:420
  62.0 1.3 %collective-permute-start.20 = (bf16[288,256]{1,0:T(8,128)(2,1)S(1)}, bf16[288,256]{1,0:T(8,128)(2,1)S(1)}, u32[]{:S(2)}, u32[]{:S(2)}) collective-permute-start(bf16[288,256]{1,0:T(8,128)(2,1)S(1)} %get-tuple-element.70), channel_id=1, source_target_pairs={{0,12},{4,8},{8,4},{12,0},{1,13},{5,9},{9,5},{13,1},{2,14},{6,10},... | collective-permute-start | bytes 442376 | tf_op jit(solution)/shard_map/ppermute | solution.py:420
  63.3 1.0 %shard_map.120 = bf16[2,256,256]{2,1,0:T(8,128)(2,1)} custom-call(bf16[2,256,128]{2,1,0:T(8,128)(2,1)S(1)} %get-tuple-element.73.gram0, bf16[2,128,256]{2,1,0:T(8,128)(2,1)S(1)} %get-tuple-element.74.rows0, bf16[2,256,128]{2,1,0:T(8,128)(2,1)S(1)} %get-tuple-element.75.gram1, bf16[2,128,256]{2,1,0:T(8,128)(2,1)S(1)} %get-tuple-element.76.rows1), custom_call_target="tpu_custom_call" | custom-call | flops 300000000 | bytes 2000000 | tf_op jit(solution)/shard_map/pallas_call | solution.py:549
  64.3 8.3 %collective-permute-done.19.g2 = bf16[288,256]{1,0:T(8,128)(2,1)S(1)} collective-permute-done((bf16[288,256]{1,0:T(8,128)(2,1)S(1)}, bf16[288,256]{1,0:T(8,128)(2,1)S(1)}, u32[]{:S(2)}, u32[]{:S(2)}) %collective-permute-start.19) | collective-permute-done | bytes 147488 | tf_op jit(solution)/shard_map/ppermute | solution.py:420
  72.6 1.0 %shard_map.119 = (bf16[128,256]{1,0:T(8,128)(2,1)}, bf16[128,256]{1,0:T(8,128)(2,1)}) custom-call(bf16[128,2176]{1,0:T(8,128)(2,1)S(1)} %copy-done.1, bf16[288,256]{1,0:T(8,128)(2,1)S(1)} %get-tuple-element.51.g0, bf16[288,256]{1,0:T(8,128)(2,1)S(1)} %collective-permute-done.11.g1, bf16[288,256]{1,0:T(8,128)(2,1)S(1)} %collective-permute-done.19.g2, ...), custom_call_target="tpu_custom_call" | custom-call | flops 100000000 | bytes 1000000 | tf_op jit(solution)/shard_map/pallas_call | solution.py:552
  (38 shorter events, 4.0 us)
Async XLA Ops:
  2.9 15.8 %collective-permute-start = (bf16[64,2176]{1,0:T(8,128)(2,1)}, bf16[64,2176]{1,0:T(8,128)(2,1)S(1)}, u32[]{:S(2)}, u32[]{:S(2)}) collective-permute-start(bf16[64,2176]{1,0:T(8,128)(2,1)} %get-tuple-element.43), channel_id=1, source_target_pairs={{0,4},{4,0},{8,12},{12,8},{1,5},{5,1},{9,13},{13,9},{2,6},{6,2},{1... | collective-permute-start | bytes 835592 | tf_op jit(solution)/shard_map/ppermute | solution.py:420
  6.0 22.5 %collective-permute-start.12 = (bf16[64,2176]{1,0:T(8,128)(2,1)}, bf16[64,2176]{1,0:T(8,128)(2,1)S(1)}, u32[]{:S(2)}, u32[]{:S(2)}) collective-permute-start(bf16[64,2176]{1,0:T(8,128)(2,1)} %get-tuple-element.43), channel_id=1, source_target_pairs={{0,8},{4,12},{8,0},{12,4},{1,9},{5,13},{9,1},{13,5},{2,10},{6,14},... | collective-permute-start | bytes 835592 | tf_op jit(solution)/shard_map/ppermute | solution.py:420
  18.7 11.1 %collective-permute-start.1 = (bf16[64,2176]{1,0:T(8,128)(2,1)S(1)}, bf16[64,2176]{1,0:T(8,128)(2,1)S(1)}, u32[]{:S(2)}, u32[]{:S(2)}) collective-permute-start(bf16[64,2176]{1,0:T(8,128)(2,1)S(1)} %collective-permute-done.refs_1_), channel_id=1, source_target_pairs={{0,1},{1,0},{2,3},{3,2},{4,5},{5,4},{6,7},{7,6},{8,9},{9,8},{10,11... | collective-permute-start | bytes 835592 | tf_op jit(solution)/shard_map/ppermute | solution.py:420
  19.7 6.4 %collective-permute-start.4 = (bf16[256,256]{1,0:T(8,128)(2,1)S(1)}, bf16[256,256]{1,0:T(8,128)(2,1)S(1)}, u32[]{:S(2)}, u32[]{:S(2)}) collective-permute-start(bf16[256,256]{1,0:T(8,128)(2,1)S(1)} %get-tuple-element.79), channel_id=1, source_target_pairs={{0,2},{1,3},{2,0},{3,1},{4,6},{5,7},{6,4},{7,5},{8,10},{9,11},{10,... | collective-permute-start | bytes 393224 | tf_op jit(solution)/shard_map/ppermute | solution.py:420
  21.5 7.1 %collective-permute-start.3 = (bf16[256,256]{1,0:T(8,128)(2,1)S(1)}, bf16[256,256]{1,0:T(8,128)(2,1)S(1)}, u32[]{:S(2)}, u32[]{:S(2)}) collective-permute-start(bf16[256,256]{1,0:T(8,128)(2,1)S(1)} %get-tuple-element.80), channel_id=1, source_target_pairs={{0,2},{1,3},{2,0},{3,1},{4,6},{5,7},{6,4},{7,5},{8,10},{9,11},{10,... | collective-permute-start | bytes 393224 | tf_op jit(solution)/shard_map/ppermute | solution.py:420
  21.8 8.0 %collective-permute-start.2 = (bf16[2,256,256]{2,1,0:T(8,128)(2,1)}, bf16[2,256,256]{2,1,0:T(8,128)(2,1)S(1)}, u32[]{:S(2)}, u32[]{:S(2)}) collective-permute-start(bf16[2,256,256]{2,1,0:T(8,128)(2,1)} %get-tuple-element.44.refs_3_), channel_id=1, source_target_pairs={{0,1},{1,0},{2,3},{3,2},{4,5},{5,4},{6,7},{7,6},{8,9},{9,8},{10,11... | collective-permute-start | bytes 786440 | tf_op jit(solution)/shard_map/ppermute | solution.py:420
  26.1 2.4 %collective-permute-start.6 = (bf16[256,256]{1,0:T(8,128)(2,1)S(1)}, bf16[256,256]{1,0:T(8,128)(2,1)S(1)}, u32[]{:S(2)}, u32[]{:S(2)}) collective-permute-start(bf16[256,256]{1,0:T(8,128)(2,1)S(1)} %collective-permute-done.4.refs_6_), channel_id=1, source_target_pairs={{0,1},{1,0},{2,3},{3,2},{4,5},{5,4},{6,7},{7,6},{8,9},{9,8},{10,11... | collective-permute-start | bytes 393224 | tf_op jit(solution)/shard_map/ppermute | solution.py:420
  28.5 1.3 %collective-permute-start.5 = (bf16[256,256]{1,0:T(8,128)(2,1)S(1)}, bf16[256,256]{1,0:T(8,128)(2,1)S(1)}, u32[]{:S(2)}, u32[]{:S(2)}) collective-permute-start(bf16[256,256]{1,0:T(8,128)(2,1)S(1)} %collective-permute-done.3.refs_5_), channel_id=1, source_target_pairs={{0,1},{1,0},{2,3},{3,2},{4,5},{5,4},{6,7},{7,6},{8,9},{9,8},{10,11... | collective-permute-start | bytes 393224 | tf_op jit(solution)/shard_map/ppermute | solution.py:420
  28.5 10.4 %collective-permute-start.13 = (bf16[64,2176]{1,0:T(8,128)(2,1)S(1)}, bf16[64,2176]{1,0:T(8,128)(2,1)S(1)}, u32[]{:S(2)}, u32[]{:S(2)}) collective-permute-start(bf16[64,2176]{1,0:T(8,128)(2,1)S(1)} %collective-permute-done.12.a), channel_id=1, source_target_pairs={{0,4},{4,0},{8,12},{12,8},{1,5},{5,1},{9,13},{13,9},{2,6},{6,2},{1... | collective-permute-start | bytes 835592 | tf_op jit(solution)/shard_map/ppermute | solution.py:420
  29.9 1.1 %copy-start = (bf16[128,2176]{1,0:T(8,128)(2,1)S(1)}, bf16[128,2176]{1,0:T(8,128)(2,1)}, u32[]{:S(2)}) copy-start(bf16[128,2176]{1,0:T(8,128)(2,1)} %get-tuple-element.42.refs_0_.own) | copy-start | bytes 1671172
  38.9 4.3 %copy-start.3 = (bf16[2,256,1024]{2,1,0:T(8,128)(2,1)S(1)}, bf16[2,256,1024]{2,1,0:T(8,128)(2,1)}, u32[]{:S(2)}) copy-start(bf16[2,256,1024]{2,1,0:T(8,128)(2,1)} %get-tuple-element.53.refs_2_) | copy-start | bytes 3145732
  39.0 4.2 %collective-permute-start.14 = (bf16[128,2176]{1,0:T(8,128)(2,1)S(1)}, bf16[128,2176]{1,0:T(8,128)(2,1)S(1)}, u32[]{:S(2)}, u32[]{:S(2)}) collective-permute-start(bf16[128,2176]{1,0:T(8,128)(2,1)S(1)} %shard_map.114.refs_0_), channel_id=1, source_target_pairs={{0,1},{1,0},{2,3},{3,2},{4,5},{5,4},{6,7},{7,6},{8,9},{9,8},{10,11... | collective-permute-start | bytes 1671176 | tf_op jit(solution)/shard_map/ppermute | solution.py:420
  39.2 2.2 %collective-permute-start.8 = (bf16[320,256]{1,0:T(8,128)(2,1)S(1)}, bf16[320,256]{1,0:T(8,128)(2,1)S(1)}, u32[]{:S(2)}, u32[]{:S(2)}) collective-permute-start(bf16[320,256]{1,0:T(8,128)(2,1)S(1)} %get-tuple-element.47), channel_id=1, source_target_pairs={{0,1},{1,0},{2,3},{3,2},{4,5},{5,4},{6,7},{7,6},{8,9},{9,8},{10,11... | collective-permute-start | bytes 491528 | tf_op jit(solution)/shard_map/ppermute | solution.py:420
  39.6 1.9 %collective-permute-start.9 = (bf16[256,256]{1,0:T(8,128)(2,1)S(1)}, bf16[256,256]{1,0:T(8,128)(2,1)S(1)}, u32[]{:S(2)}, u32[]{:S(2)}) collective-permute-start(bf16[256,256]{1,0:T(8,128)(2,1)S(1)} %get-tuple-element.48), channel_id=1, source_target_pairs={{0,1},{1,0},{2,3},{3,2},{4,5},{5,4},{6,7},{7,6},{8,9},{9,8},{10,11... | collective-permute-start | bytes 393224 | tf_op jit(solution)/shard_map/ppermute | solution.py:420
  39.7 12.7 %collective-permute-start.7 = (bf16[576,256]{1,0:T(8,128)(2,1)S(1)}, bf16[576,256]{1,0:T(8,128)(2,1)S(1)}, u32[]{:S(2)}, u32[]{:S(2)}) collective-permute-start(bf16[576,256]{1,0:T(8,128)(2,1)S(1)} %get-tuple-element.46), channel_id=1, source_target_pairs={{0,1},{1,0},{2,3},{3,2},{4,5},{5,4},{6,7},{7,6},{8,9},{9,8},{10,11... | collective-permute-start | bytes 884744 | tf_op jit(solution)/shard_map/ppermute | solution.py:420
  41.5 9.1 %collective-permute-start.10 = (bf16[576,256]{1,0:T(8,128)(2,1)S(1)}, bf16[576,256]{1,0:T(8,128)(2,1)S(1)}, u32[]{:S(2)}, u32[]{:S(2)}) collective-permute-start(bf16[576,256]{1,0:T(8,128)(2,1)S(1)} %shard_map.112), channel_id=1, source_target_pairs={{0,2},{1,3},{2,0},{3,1},{4,6},{5,7},{6,4},{7,5},{8,10},{9,11},{10,... | collective-permute-start | bytes 884744 | tf_op jit(solution)/shard_map/ppermute | solution.py:420
  48.8 1.9 %collective-permute-start.16 = (bf16[320,256]{1,0:T(8,128)(2,1)S(1)}, bf16[320,256]{1,0:T(8,128)(2,1)S(1)}, u32[]{:S(2)}, u32[]{:S(2)}) collective-permute-start(bf16[320,256]{1,0:T(8,128)(2,1)S(1)} %get-tuple-element.56), channel_id=1, source_target_pairs={{0,1},{1,0},{2,3},{3,2},{4,5},{5,4},{6,7},{7,6},{8,9},{9,8},{10,11... | collective-permute-start | bytes 491528 | tf_op jit(solution)/shard_map/ppermute | solution.py:420
  48.8 1.8 %collective-permute-start.17 = (bf16[256,256]{1,0:T(8,128)(2,1)S(1)}, bf16[256,256]{1,0:T(8,128)(2,1)S(1)}, u32[]{:S(2)}, u32[]{:S(2)}) collective-permute-start(bf16[256,256]{1,0:T(8,128)(2,1)S(1)} %get-tuple-element.57), channel_id=1, source_target_pairs={{0,1},{1,0},{2,3},{3,2},{4,5},{5,4},{6,7},{7,6},{8,9},{9,8},{10,11... | collective-permute-start | bytes 393224 | tf_op jit(solution)/shard_map/ppermute | solution.py:420
  49.3 7.4 %collective-permute-start.15 = (bf16[576,256]{1,0:T(8,128)(2,1)S(1)}, bf16[576,256]{1,0:T(8,128)(2,1)S(1)}, u32[]{:S(2)}, u32[]{:S(2)}) collective-permute-start(bf16[576,256]{1,0:T(8,128)(2,1)S(1)} %get-tuple-element.55), channel_id=1, source_target_pairs={{0,1},{1,0},{2,3},{3,2},{4,5},{5,4},{6,7},{7,6},{8,9},{9,8},{10,11... | collective-permute-start | bytes 884744 | tf_op jit(solution)/shard_map/ppermute | solution.py:420
  50.7 9.0 %collective-permute-start.18 = (bf16[576,256]{1,0:T(8,128)(2,1)S(1)}, bf16[576,256]{1,0:T(8,128)(2,1)S(1)}, u32[]{:S(2)}, u32[]{:S(2)}) collective-permute-start(bf16[576,256]{1,0:T(8,128)(2,1)S(1)} %shard_map.116), channel_id=1, source_target_pairs={{0,2},{1,3},{2,0},{3,1},{4,6},{5,7},{6,4},{7,5},{8,10},{9,11},{10,... | collective-permute-start | bytes 884744 | tf_op jit(solution)/shard_map/ppermute | solution.py:420
  52.8 11.4 %collective-permute-start.11 = (bf16[288,256]{1,0:T(8,128)(2,1)S(1)}, bf16[288,256]{1,0:T(8,128)(2,1)S(1)}, u32[]{:S(2)}, u32[]{:S(2)}) collective-permute-start(bf16[288,256]{1,0:T(8,128)(2,1)S(1)} %get-tuple-element.52), channel_id=1, source_target_pairs={{0,4},{4,0},{8,12},{12,8},{1,5},{5,1},{9,13},{13,9},{2,6},{6,2},{1... | collective-permute-start | bytes 442376 | tf_op jit(solution)/shard_map/ppermute | solution.py:420
  56.7 15.9 %copy-start.1 = (bf16[128,2176]{1,0:T(8,128)(2,1)S(1)}, bf16[128,2176]{1,0:T(8,128)(2,1)}, u32[]{:S(2)}) copy-start(bf16[128,2176]{1,0:T(8,128)(2,1)} %get-tuple-element.42.refs_0_.own) | copy-start | bytes 1671172
  60.2 12.4 %collective-permute-start.19 = (bf16[288,256]{1,0:T(8,128)(2,1)S(1)}, bf16[288,256]{1,0:T(8,128)(2,1)S(1)}, u32[]{:S(2)}, u32[]{:S(2)}) collective-permute-start(bf16[288,256]{1,0:T(8,128)(2,1)S(1)} %get-tuple-element.69), channel_id=1, source_target_pairs={{0,8},{4,12},{8,0},{12,4},{1,9},{5,13},{9,1},{13,5},{2,10},{6,14},... | collective-permute-start | bytes 442376 | tf_op jit(solution)/shard_map/ppermute | solution.py:420
  62.0 10.6 %collective-permute-start.20 = (bf16[288,256]{1,0:T(8,128)(2,1)S(1)}, bf16[288,256]{1,0:T(8,128)(2,1)S(1)}, u32[]{:S(2)}, u32[]{:S(2)}) collective-permute-start(bf16[288,256]{1,0:T(8,128)(2,1)S(1)} %get-tuple-element.70), channel_id=1, source_target_pairs={{0,12},{4,8},{8,4},{12,0},{1,13},{5,9},{9,5},{13,1},{2,14},{6,10},... | collective-permute-start | bytes 442376 | tf_op jit(solution)/shard_map/ppermute | solution.py:420
  (1 other events, 0.9 us)

commit v5 on v4

--- a/solution.py
+++ b/solution.py
@@ -211,6 +211,12 @@
     out_o[:, 2 * WIDTH :] = jnp.where(core == 0, columns[0:HALF], columns[HALF:]).astype(BF16)
     for copy in copies[2:]:
         copy.wait()
+
+
+def stage_kernel(pair_x, own, pair, pair_x_o, own_o, pair_o):
+    pair_x_o[...] = pair_x[...]
+    own_o[...] = own[...]
+    pair_o[...] = pair[...]
 
 
 def join_kernel(a, b, after, out_o):
@@ -324,19 +330,19 @@
 
 
 def own_chunk_kernel(*refs):
-    own, near, far, p0, p1, x0, x1, d0, d1, up_in, down_in = refs[:11]
-    outs, pair_o = refs[11:22], refs[22]
-    whole, info, up, down, sems = refs[23:28]
+    own, p0, near, far, p1, p2, p3, up_in, down_in = refs[:9]
+    outs, pair_o = refs[9:20], refs[20]
+    whole, info, up, down, sems = refs[21:26]
     j = lax.axis_index("tensor")
     copies = load([(up_in, up), (down_in, down)], sems)
     whole[0:128, :] = own[:, 0 : 2 * WIDTH]
     info[0:128, :] = own[:, 2 * WIDTH :]
     place_rows(whole, info, 1, lax.rem(j, 2), near, far)
-    for k, piece in enumerate((p0, p1, (x0, x1), (d0, d1))):
+    for k, piece in enumerate((p0, p1, p2, p3)):
         cols = pl.ds(pl.multiple_of((j ^ k) * 256, 256), 256)
         for e in range(2):
-            pair_o[e, :, cols] = piece[e][...]
-    towers(read_meta(info), whole, up, down, copies, pair_o, outs, refs[28:])
+            pair_o[e, :, cols] = piece[e]
+    towers(read_meta(info), whole, up, down, copies, pair_o, outs, refs[26:])
 
 
 def far_chunk_kernel(*refs):
@@ -366,26 +372,57 @@
     return (a.astype(F32) + b.astype(F32)).astype(BF16)
 
 
-def combine_kernel(mine, other, theirs, pick, gate, *rest):
-    first_o, second_o, rows_o = rest[-3:]
-    both = add2(add2(mine[0], other[...]), theirs[...])
+def combine_grads(both, picks, rows_o):
     grads = jnp.zeros((256, 256), F32)
-    mixed = jnp.zeros((256, 256), F32)
     back = jnp.zeros((64, 256), F32)
     for e in range(2):
         rows = both[e * 128 : e * 128 + 128]
         rows_o[e] = rows
-        grads = grads + mm(pick[e], rows, TN)
-        back = back + mm(both[256:320, e * 128 : e * 128 + 128], pick[e])
-        out = both[320 + e * 128 : 448 + e * 128].astype(F32) * gate[e][:, 0:1]
-        mixed = mixed + mm(pick[e], out.astype(BF16), TN)
+        grads = grads + mm(picks[e], rows, TN)
+        back = back + mm(both[256:320, e * 128 : e * 128 + 128], picks[e])
+    return grads.astype(BF16), back.astype(BF16)
+
+
+def put_grads(dst, grads, back, p):
+    rows = slice(p * 128, p * 128 + 128)
+    dst[0:128, :] = grads[rows]
+    dst[128:160, 0:128] = back[0:32, rows]
+    dst[128:160, 128:256] = back[32:64, rows]
+
+
+def combine_outs(both, picks, gates):
+    mixed = jnp.zeros((256, 256), F32)
+    for e in range(2):
+        out = both[e * 128 : e * 128 + 128].astype(F32) * gates[e][:, 0:1]
+        mixed = mixed + mm(picks[e], out.astype(BF16), TN)
+    return mixed.astype(BF16)
+
+
+def combine_kernel(mine, other, theirs, pick, gate, first_o, second_o, rows_o):
+    both = add2(add2(mine[0], other[...]), theirs[...])
+    grads, back = combine_grads(both[0:320], pick, rows_o)
+    mixed = combine_outs(both[320:576], pick, gate)
     for p, dst in enumerate((first_o, second_o)):
-        rows = slice(p * 128, p * 128 + 128)
-        dst[0:128, :] = grads[rows].astype(BF16)
-        part = back[:, rows].astype(BF16)
-        dst[128:160, 0:128] = part[0:32]
-        dst[128:160, 128:256] = part[32:64]
-        dst[160:288, :] = mixed[rows].astype(BF16)
+        put_grads(dst, grads, back, p)
+        dst[160:288, :] = mixed[p * 128 : p * 128 + 128]
+
+
+def far_grads_kernel(mine, other, theirs, pick, after, first_o, second_o, rows_o):
+    both = add2(add2(mine[0, 0:320], other[0:320]), theirs[...])
+    grads, back = combine_grads(both, pick, rows_o)
+    for p, dst in enumerate((first_o, second_o)):
+        put_grads(dst, grads, back, p)
+
+
+def far_outs_kernel(mine, other, theirs, pick, gate, first_o, second_o):
+    both = add2(add2(mine[0, 320:576], other[320:576]), theirs[...])
+    mixed = combine_outs(both, pick, gate)
+    first_o[...] = mixed[0:128]
+    second_o[...] = mixed[128:256]
+
+
+def sum_kernel(a, b, out_o):
+    out_o[...] = add2(a[...], b[...])
 
 
 def pair_kernel(gram0, rows0, gram1, rows1, out_o):
@@ -393,14 +430,15 @@
         out_o[e] = (mm(gram0[e], rows0[e]) + mm(gram1[e], rows1[e])).astype(BF16)
 
 
-def final_kernel(own, g0, g1, g2, g3, mixed_o, grad_o, flipped):
+def final_kernel(own, g0, g1, far_grads, far_outs, mixed_o, grad_o, flipped):
     column = pl.multiple_of(lax.axis_index("tensor") * 256, 256)
-    mixed = own[:, pl.ds(column, 256)].astype(F32)
+    mixed = own[:, pl.ds(column, 256)].astype(F32) + far_outs[...].astype(F32)
     total = own[:, pl.ds(WIDTH + column, 256)].astype(F32)
     back = jnp.zeros((32, 256), F32)
-    for g in (g0, g1, g2, g3):
+    for g in (g0, g1, far_grads):
         total = total + g[0:128, :].astype(F32)
         back = back + g[128:160, :].astype(F32)
+    for g in (g0, g1):
         mixed = mixed + g[160:288, :].astype(F32)
     mixed_o[...] = mixed.astype(BF16)
     flipped[...] = own[:, 0:WIDTH].astype(F32).T
@@ -453,18 +491,17 @@
     return [pltpu.VMEM((2, 1024, 512), BF16), pltpu.VMEM((2, 512, 1024), BF16)]
 
 
-def away_kernel(keep, low, high, *rest):
-    out_o = rest[-1]
-    rows = low.shape[0]
-    out_o[0:rows, :] = add2(keep[1, 0:rows], low[...])
-    out_o[rows:, :] = add2(keep[1, rows:], high[...])
-
-
-def sums_over_tensor(keep, send_here, send_away, send_last, after=()):
-    got = (swap(send_away, "tensor", 1), swap(send_last, "tensor", 1))
-    add = kernel_call(away_kernel, shape((576, 256)), "vvv" + "a" * len(after))
-    there = swap(add(keep, *got, *after), "tensor", 2)
-    return swap(send_here, "tensor", 1), there
+def away_kernel(keep, low, high, out_o):
+    out_o[0:320, :] = add2(keep[1, 0:320], low[...])
+    out_o[320:576, :] = add2(keep[1, 320:576], high[...])
+
+
+def away_grads_kernel(keep, low, after, out_o):
+    out_o[...] = add2(keep[1, 0:320], low[...])
+
+
+def away_outs_kernel(keep, high, after, out_o):
+    out_o[...] = add2(keep[1, 320:576], high[...])
 
 
 def gathered_body(inputs, cotangent, gate_values, routes, pair_weight, up_weight, down_weight):
@@ -472,7 +509,11 @@
     width = 2 * WIDTH + 128
     payload, own, pair_own = kernel_call(
         payload_kernel,
-        (shape((HALF, width)), shape((2 * HALF, width)), shape((2, 256, 256))),
+        (
+            shape((HALF, width)),
+            shape((2 * HALF, width)),
+            shape((2, 256, 256)),
+        ),
         "hhhhh",
         scratch=[
             pltpu.VMEM((2, 128), F32),
@@ -483,14 +524,17 @@
     )(inputs, cotangent, gates, choices, pair_weight)
     got = [swap(payload, "expert", 1), swap(payload, "expert", 2)]
     got.append(swap(got[1], "expert", 1))
-    pair_x = [swap(pair_own[e], "tensor", 2) for e in range(2)]
+    both = shape((2, 256, 256))
+    pair_x, own, pair_own = kernel_call(
+        stage_kernel, (both, shape((2 * HALF, width)), both), "vvv"
+    )(swap(pair_own, "tensor", 2), own, pair_own)
     pair_c = swap(pair_own, "tensor", 1)
-    pair_d = [swap(v, "tensor", 1) for v in pair_x]
+    pair_d = swap(pair_x, "tensor", 1)
     near_other = swap(got[0], "tensor", 1)
     chunk = kernel_call(
         own_chunk_kernel,
         chunk_outs() + (shape((2, 256, 1024)),),
-        "vvvvvvvvvhh",
+        "vvvvvvvhh",
         scratch=[
             pltpu.VMEM((256, 2048), BF16),
             pltpu.VMEM((256, 128), BF16),
@@ -501,21 +545,23 @@
         flops=4_000_000_000,
         nbytes=10_000_000,
     )(
-        own, got[0], near_other,
-        pair_own, pair_c, *pair_x, *pair_d, up_weight, down_weight,
+        own, pair_own, got[0], near_other,
+        pair_c, pair_x, pair_d, up_weight, down_weight,
     )
     keep, here, away, last, cross, act, grad, pre, gram, pick, gate, pair_all = chunk
-    other, theirs = sums_over_tensor(keep, here, away, last)
+    away = kernel_call(away_kernel, shape((576, 256)), "vvv")(
+        keep, swap(away, "tensor", 1), swap(last, "tensor", 1)
+    )
+    theirs = swap(away, "tensor", 2)
+    other = swap(here, "tensor", 1)
     part = shape((288, 256))
-    def combine(*operands):
-        return kernel_call(
-            combine_kernel,
-            (part, part, shape((2, 128, 256))),
-            "vvvvva"[: len(operands)],
-            flops=300_000_000,
-            nbytes=2_000_000,
-        )(*operands)
-
+    combine = kernel_call(
+        combine_kernel,
+        (part, part, shape((2, 128, 256))),
+        "vvvvv",
+        flops=300_000_000,
+        nbytes=2_000_000,
+    )
     own_part, near_part, rows = combine(keep, other, theirs, pick, gate)
     far_mine = kernel_call(join_kernel, shape((2 * HALF, 2 * WIDTH + 128)), "vva")(
         got[1], got[2], gate
@@ -533,7 +579,15 @@
         nbytes=10_000_000,
     )(far_mine, far_other, pair_all, up_weight, down_weight)
     fkeep, fhere, faway, flast, fcross, fact, fgrad, fpre, fgram, fpick, fgate = chunk
-    fother, ftheirs = sums_over_tensor(fkeep, fhere, faway, flast, after=(theirs,))
+    fother = swap(fhere, "tensor", 1)
+    fgrads = kernel_call(away_grads_kernel, shape((320, 256)), "vva")(
+        fkeep, swap(faway, "tensor", 1), theirs
+    )
+    fouts = kernel_call(away_outs_kernel, shape((256, 256)), "vva")(
+        fkeep, swap(flast, "tensor", 1), fgrads
+    )
+    fgrads = swap(fgrads, "tensor", 2)
+    fouts = swap(fouts, "tensor", 2)
     near_got = swap(near_part, "expert", 1)
     grad_down, grad_up, weights_done = kernel_call(
         weights_kernel,
@@ -542,10 +596,18 @@
         flops=3_000_000_000,
         nbytes=8_000_000,
     )(act, grad, cross, pre, fact, fgrad, fcross, fpre)
-    part2, part3, frows = combine(
-        fkeep, fother, ftheirs, fpick, fgate, weights_done
-    )
-    got2, got3 = swap(part2, "expert", 2), swap(part3, "expert", 3)
+    part = shape((160, 256))
+    grads2, grads3, frows = kernel_call(
+        far_grads_kernel, (part, part, shape((2, 128, 256))), "vvvva"
+    )(fkeep, fother, fgrads, fpick, weights_done)
+    grads2 = kernel_call(sum_kernel, part, "vv")(grads2, swap(grads3, "expert", 1))
+    far_grads = swap(grads2, "expert", 2)
+    part = shape((128, 256))
+    outs2, outs3 = kernel_call(far_outs_kernel, (part, part), "vvvvv")(
+        fkeep, fother, fouts, fpick, fgate
+    )
+    outs2 = kernel_call(sum_kernel, part, "vv")(outs2, swap(outs3, "expert", 1))
+    far_outs = swap(outs2, "expert", 2)
     grad_pair = kernel_call(
         pair_kernel, shape((2, 256, 256)), "vvvv", flops=300_000_000, nbytes=2_000_000
     )(gram, rows, fgram, frows)
@@ -556,7 +618,7 @@
         scratch=[pltpu.VMEM((1024, 128), F32)],
         flops=100_000_000,
         nbytes=1_000_000,
-    )(own, own_part, near_got, got2, got3)
+    )(own, own_part, near_got, far_grads, far_outs)
     return mixed, grad_input, grad_pair, grad_up, grad_down
 
 

time: 74.5 us -> 64.1 us (0.86)
  waiting for transfers between devices: 32.1 us -> 17.2 us
  starting transfers between devices: 16.9 us -> 22.7 us
  local copies, waits for them, and re-layouts: 3 us -> 2.01 us
    ppermute x21 -> x22, waiting for transfers between devices: 32.1 us -> 17.2 us  [swap(): return lax.ppermute(value, axis, [(i, i ^ mask) for i in range(size)])]
    ppermute x21 -> x22, starting transfers between devices: 16.9 us -> 22.7 us  [swap(): return lax.ppermute(value, axis, [(i, i ^ mask) for i in range(size)])]
    squeeze x1 -> x0, local copies, waits for them, and re-layouts: 0.99 us -> none  [gathered_body(): pair_x = [swap(pair_own[e], 'tensor', 2) for e in range(2)]]
    unnamed x8 -> x6, local copies, waits for them, and re-layouts: 2.01 us -> 2.01 us
  transfers between devices with their start and end apart: 21 -> 22, of which waited for: 8 -> 8; matrix products, arithmetic and copies ran while one was open for 1% -> 0% of each run, Pallas kernels for 24% -> 28%
where the time goes in v5:
time: 64.1 us; the launch traced here: 63.8 us
  starting transfers between devices  22.7 us (35%)
  Pallas kernels  21.1 us (33%)
  waiting for transfers between devices  17.2 us (27%)
  local copies, waits for them, and re-layouts  2.01 us (3%)
  between operations  0.78 us (1%)
    ppermute x22, starting transfers between devices, swap(): return lax.ppermute(value, axis, [(i, i ^ mask) for i in range(size)])  22.7 us
    ppermute x22, waiting for transfers between devices, swap(): return lax.ppermute(value, axis, [(i, i ^ mask) for i in range(size)])  17.2 us
    pallas_call x1, Pallas kernels, gathered_body(): kernel_call(own_chunk_kernel, chunk_outs() + (shape((2, 256, 1024)),), 'v...  6.99 us
    pallas_call x1, Pallas kernels, gathered_body(): kernel_call(far_chunk_kernel, chunk_outs(), 'vvvhh', scratch=[pltpu.VMEM(...  5.56 us
    pallas_call x1, Pallas kernels, gathered_body(): kernel_call(weights_kernel, (shape((2, 512, 1024)), shape((2, 1024, 512))...  3.04 us
    pallas_call x1, Pallas kernels, gathered_body(): kernel_call(payload_kernel, (shape((HALF, width)), shape((2 * HALF, width...  2.31 us
    unnamed x6, local copies, waits for them, and re-layouts  2.01 us
  transfers between devices with their start and end apart: 22, of which 8 were waited for; matrix products, arithmetic and copies ran while one was open for 0% of the time, Pallas kernels for 28%

profile of v5, /device:TPU:0, one launch (start us, length us, event | category | flops | bytes accessed | tf_op | source)
XLA Modules:
  0.0 63.8 jit_solution(1965347207772407780)
XLA Ops:
  0.6 2.3 %shard_map.110 = (bf16[64,2176]{1,0:T(8,128)(2,1)}, bf16[128,2176]{1,0:T(8,128)(2,1)}, bf16[2,256,256]{2,1,0:T(8,128)(2,1)}) custom-call(bf16[128,1024]{1,0:T(8,128)(2,1)} %x.1, bf16[128,1024]{1,0:T(8,128)(2,1)} %c.1, f32[2,128]{1,0:T(2,128)} %bitcast.2, s32[2,128]{1,0:T(2,128)} %bitcast.3, bf16[2,256,256]{2,1,0:T(8,128)(2,1)} %pair_in.1), custom_call_target="tpu_custom_call" | custom-call | tf_op jit(solution)/shard_map/pallas_call | solution.py:510
  2.9 3.1 %collective-permute-start.1 = (bf16[64,2176]{1,0:T(8,128)(2,1)}, bf16[64,2176]{1,0:T(8,128)(2,1)S(1)}, u32[]{:S(2)}, u32[]{:S(2)}) collective-permute-start(bf16[64,2176]{1,0:T(8,128)(2,1)} %get-tuple-element.51), channel_id=1, source_target_pairs={{0,4},{4,0},{8,12},{12,8},{1,5},{5,1},{9,13},{13,9},{2,6},{6,2},{1... | collective-permute-start | bytes 835592 | tf_op jit(solution)/shard_map/ppermute | solution.py:458
  6.0 1.5 %collective-permute-start = (bf16[2,256,256]{2,1,0:T(8,128)(2,1)}, bf16[2,256,256]{2,1,0:T(8,128)(2,1)S(1)}, u32[]{:S(2)}, u32[]{:S(2)}) collective-permute-start(bf16[2,256,256]{2,1,0:T(8,128)(2,1)} %get-tuple-element.47.pair), channel_id=1, source_target_pairs={{0,2},{1,3},{2,0},{3,1},{4,6},{5,7},{6,4},{7,5},{8,10},{9,11},{10,... | collective-permute-start | bytes 786440 | tf_op jit(solution)/shard_map/ppermute | solution.py:458
  7.5 2.6 %collective-permute-start.10 = (bf16[64,2176]{1,0:T(8,128)(2,1)}, bf16[64,2176]{1,0:T(8,128)(2,1)S(1)}, u32[]{:S(2)}, u32[]{:S(2)}) collective-permute-start(bf16[64,2176]{1,0:T(8,128)(2,1)} %get-tuple-element.51), channel_id=1, source_target_pairs={{0,8},{4,12},{8,0},{12,4},{1,9},{5,13},{9,1},{13,5},{2,10},{6,14},... | collective-permute-start | bytes 835592 | tf_op jit(solution)/shard_map/ppermute | solution.py:458
  10.1 7.4 %collective-permute-done.1.refs_2_ = bf16[64,2176]{1,0:T(8,128)(2,1)S(1)} collective-permute-done((bf16[64,2176]{1,0:T(8,128)(2,1)}, bf16[64,2176]{1,0:T(8,128)(2,1)S(1)}, u32[]{:S(2)}, u32[]{:S(2)}) %collective-permute-start.1) | collective-permute-done | bytes 278560 | tf_op jit(solution)/shard_map/ppermute | solution.py:458
  17.6 1.1 %copy-done = bf16[128,2176]{1,0:T(8,128)(2,1)S(1)} copy-done((bf16[128,2176]{1,0:T(8,128)(2,1)S(1)}, bf16[128,2176]{1,0:T(8,128)(2,1)}, u32[]{:S(2)}) %copy-start) | copy-done | bytes 557080
  18.6 0.9 %copy-done.1 = bf16[2,256,256]{2,1,0:T(8,128)(2,1)S(1)} copy-done((bf16[2,256,256]{2,1,0:T(8,128)(2,1)S(1)}, bf16[2,256,256]{2,1,0:T(8,128)(2,1)}, u32[]{:S(2)}) %copy-start.1) | copy-done | bytes 262168
  20.3 2.2 %collective-permute-done.10.a = bf16[64,2176]{1,0:T(8,128)(2,1)S(1)} collective-permute-done((bf16[64,2176]{1,0:T(8,128)(2,1)}, bf16[64,2176]{1,0:T(8,128)(2,1)S(1)}, u32[]{:S(2)}, u32[]{:S(2)}) %collective-permute-start.10) | collective-permute-done | bytes 278560 | tf_op jit(solution)/shard_map/ppermute | solution.py:458
  22.5 7.0 %shard_map.112 = (bf16[2,576,256]{2,1,0:T(8,128)(2,1)S(1)}, bf16[576,256]{1,0:T(8,128)(2,1)S(1)}, bf16[320,256]{1,0:T(8,128)(2,1)S(1)}, bf16[256,256]{1,0:T(8,12...) custom-call(bf16[128,2176]{1,0:T(8,128)(2,1)S(1)} %get-tuple-element, ...), custom_call_target="tpu_custom_call" | custom-call | flops 4000000000 | bytes 10000000 | tf_op jit(solution)/shard_map/pallas_call | solution.py:534
  30.2 1.8 %collective-permute-done.7.high = bf16[256,256]{1,0:T(8,128)(2,1)S(1)} collective-permute-done((bf16[256,256]{1,0:T(8,128)(2,1)S(1)}, bf16[256,256]{1,0:T(8,128)(2,1)S(1)}, u32[]{:S(2)}, u32[]{:S(2)}) %collective-permute-start.7) | collective-permute-done | bytes 131104 | tf_op jit(solution)/shard_map/ppermute | solution.py:458
  32.1 2.4 %collective-permute-start.8 = (bf16[576,256]{1,0:T(8,128)(2,1)S(1)}, bf16[576,256]{1,0:T(8,128)(2,1)S(1)}, u32[]{:S(2)}, u32[]{:S(2)}) collective-permute-start(bf16[576,256]{1,0:T(8,128)(2,1)S(1)} %shard_map.113), channel_id=1, source_target_pairs={{0,2},{1,3},{2,0},{3,1},{4,6},{5,7},{6,4},{7,5},{8,10},{9,11},{10,... | collective-permute-start | bytes 884744 | tf_op jit(solution)/shard_map/ppermute | solution.py:458
  34.5 5.6 %shard_map.116 = (bf16[2,576,256]{2,1,0:T(8,128)(2,1)S(1)}, bf16[576,256]{1,0:T(8,128)(2,1)S(1)}, bf16[320,256]{1,0:T(8,128)(2,1)S(1)}, bf16[256,256]{1,0:T(8,12...) custom-call(bf16[128,2176]{1,0:T(8,128)(2,1)S(1)} %shard_map.115.ref, ...), custom_call_target="tpu_custom_call" | custom-call | flops 4000000000 | bytes 10000000 | tf_op jit(solution)/shard_map/pallas_call | solution.py:570
  41.9 1.8 %collective-permute-start.15 = (bf16[320,256]{1,0:T(8,128)(2,1)S(1)}, bf16[320,256]{1,0:T(8,128)(2,1)S(1)}, u32[]{:S(2)}, u32[]{:S(2)}) collective-permute-start(bf16[320,256]{1,0:T(8,128)(2,1)S(1)} %shard_map.117.after), channel_id=1, source_target_pairs={{0,2},{1,3},{2,0},{3,1},{4,6},{5,7},{6,4},{7,5},{8,10},{9,11},{10,... | collective-permute-start | bytes 491528 | tf_op jit(solution)/shard_map/ppermute | solution.py:458
  44.1 3.0 %shard_map.118 = (bf16[2,512,1024]{2,1,0:T(8,128)(2,1)}, bf16[2,1024,512]{2,1,0:T(8,128)(2,1)}, f32[8,128]{1,0:T(8,128)S(1)}) custom-call(bf16[2,128,512]{2,1,0:T(8,128)(2,1)S(1)} %get-tuple-element.66.act0, bf16[2,128,1024]{2,1,0:T(8,128)(2,1)S(1)} %get-tuple-element.67.grad0, bf16[2,128,1024]{2,1,0:T(8,128)(2,1)S(1)} %get-tuple-element.68.cross0, ...), custom_call_target="tpu_custom_call" | custom-call | flops 3000000000 | bytes 8000000 | tf_op jit(solution)/shard_map/pallas_call | solution.py:592
  47.1 1.9 %collective-permute-done.15.theirs = bf16[320,256]{1,0:T(8,128)(2,1)S(1)} collective-permute-done((bf16[320,256]{1,0:T(8,128)(2,1)S(1)}, bf16[320,256]{1,0:T(8,128)(2,1)S(1)}, u32[]{:S(2)}, u32[]{:S(2)}) %collective-permute-start.15) | collective-permute-done | bytes 163872 | tf_op jit(solution)/shard_map/ppermute | solution.py:458
  49.3 1.2 %collective-permute-start.16 = (bf16[160,256]{1,0:T(8,128)(2,1)S(1)}, bf16[160,256]{1,0:T(8,128)(2,1)S(1)}, u32[]{:S(2)}, u32[]{:S(2)}) collective-permute-start(bf16[160,256]{1,0:T(8,128)(2,1)S(1)} %get-tuple-element.76), channel_id=1, source_target_pairs={{0,4},{4,0},{8,12},{12,8},{1,5},{5,1},{9,13},{13,9},{2,6},{6,2},{1... | collective-permute-start | bytes 245768 | tf_op jit(solution)/shard_map/ppermute | solution.py:458
  50.9 1.0 %collective-permute-start.9 = (bf16[288,256]{1,0:T(8,128)(2,1)S(1)}, bf16[288,256]{1,0:T(8,128)(2,1)S(1)}, u32[]{:S(2)}, u32[]{:S(2)}) collective-permute-start(bf16[288,256]{1,0:T(8,128)(2,1)S(1)} %get-tuple-element.60), channel_id=1, source_target_pairs={{0,4},{4,0},{8,12},{12,8},{1,5},{5,1},{9,13},{13,9},{2,6},{6,2},{1... | collective-permute-start | bytes 442376 | tf_op jit(solution)/shard_map/ppermute | solution.py:458
  52.2 1.2 %collective-permute-start.20 = (bf16[128,256]{1,0:T(8,128)(2,1)S(1)}, bf16[128,256]{1,0:T(8,128)(2,1)S(1)}, u32[]{:S(2)}, u32[]{:S(2)}) collective-permute-start(bf16[128,256]{1,0:T(8,128)(2,1)S(1)} %get-tuple-element.80), channel_id=1, source_target_pairs={{0,4},{4,0},{8,12},{12,8},{1,5},{5,1},{9,13},{13,9},{2,6},{6,2},{1... | collective-permute-start | bytes 196616 | tf_op jit(solution)/shard_map/ppermute | solution.py:458
  53.4 0.9 %collective-permute-done.16.b = bf16[160,256]{1,0:T(8,128)(2,1)S(1)} collective-permute-done((bf16[160,256]{1,0:T(8,128)(2,1)S(1)}, bf16[160,256]{1,0:T(8,128)(2,1)S(1)}, u32[]{:S(2)}, u32[]{:S(2)}) %collective-permute-start.16) | collective-permute-done | bytes 81952 | tf_op jit(solution)/shard_map/ppermute | solution.py:458
  54.3 2.7 %collective-permute-start.17 = (bf16[160,256]{1,0:T(8,128)(2,1)S(1)}, bf16[160,256]{1,0:T(8,128)(2,1)S(1)}, u32[]{:S(2)}, u32[]{:S(2)}) collective-permute-start(bf16[160,256]{1,0:T(8,128)(2,1)S(1)} %shard_map.120), channel_id=1, source_target_pairs={{0,8},{4,12},{8,0},{12,4},{1,9},{5,13},{9,1},{13,5},{2,10},{6,14},... | collective-permute-start | bytes 245768 | tf_op jit(solution)/shard_map/ppermute | solution.py:458
  57.6 2.6 %collective-permute-start.21 = (bf16[128,256]{1,0:T(8,128)(2,1)S(1)}, bf16[128,256]{1,0:T(8,128)(2,1)S(1)}, u32[]{:S(2)}, u32[]{:S(2)}) collective-permute-start(bf16[128,256]{1,0:T(8,128)(2,1)S(1)} %shard_map.123), channel_id=1, source_target_pairs={{0,8},{4,12},{8,0},{12,4},{1,9},{5,13},{9,1},{13,5},{2,10},{6,14},... | collective-permute-start | bytes 196616 | tf_op jit(solution)/shard_map/ppermute | solution.py:458
  60.2 1.0 %shard_map.125 = bf16[2,256,256]{2,1,0:T(8,128)(2,1)} custom-call(bf16[2,256,128]{2,1,0:T(8,128)(2,1)S(1)} %get-tuple-element.83.gram0, bf16[2,128,256]{2,1,0:T(8,128)(2,1)S(1)} %get-tuple-element.84.rows0, bf16[2,256,128]{2,1,0:T(8,128)(2,1)S(1)} %get-tuple-element.85.gram1, bf16[2,128,256]{2,1,0:T(8,128)(2,1)S(1)} %get-tuple-element.86.rows1), custom_call_target="tpu_custom_call" | custom-call | flops 300000000 | bytes 2000000 | tf_op jit(solution)/shard_map/pallas_call | solution.py:611
  61.2 1.7 %collective-permute-done.21.far_outs = bf16[128,256]{1,0:T(8,128)(2,1)S(1)} collective-permute-done((bf16[128,256]{1,0:T(8,128)(2,1)S(1)}, bf16[128,256]{1,0:T(8,128)(2,1)S(1)}, u32[]{:S(2)}, u32[]{:S(2)}) %collective-permute-start.21) | collective-permute-done | bytes 65568 | tf_op jit(solution)/shard_map/ppermute | solution.py:458
  62.9 1.0 %shard_map.124 = (bf16[128,256]{1,0:T(8,128)(2,1)}, bf16[128,256]{1,0:T(8,128)(2,1)}) custom-call(bf16[128,2176]{1,0:T(8,128)(2,1)S(1)} %get-tuple-element.49.refs_0_.own, bf16[288,256]{1,0:T(8,128)(2,1)S(1)} %get-tuple-element.59.g0, bf16[288,256]{1,0:T(8,128)(2,1)S(1)} %collective-permute-done.9.g1, ...), custom_call_target="tpu_custom_call" | custom-call | flops 100000000 | bytes 1000000 | tf_op jit(solution)/shard_map/pallas_call | solution.py:614
  (42 shorter events, 5.3 us)
Async XLA Ops:
  2.9 14.6 %collective-permute-start.1 = (bf16[64,2176]{1,0:T(8,128)(2,1)}, bf16[64,2176]{1,0:T(8,128)(2,1)S(1)}, u32[]{:S(2)}, u32[]{:S(2)}) collective-permute-start(bf16[64,2176]{1,0:T(8,128)(2,1)} %get-tuple-element.51), channel_id=1, source_target_pairs={{0,4},{4,0},{8,12},{12,8},{1,5},{5,1},{9,13},{13,9},{2,6},{6,2},{1... | collective-permute-start | bytes 835592 | tf_op jit(solution)/shard_map/ppermute | solution.py:458
  6.0 11.5 %collective-permute-start = (bf16[2,256,256]{2,1,0:T(8,128)(2,1)}, bf16[2,256,256]{2,1,0:T(8,128)(2,1)S(1)}, u32[]{:S(2)}, u32[]{:S(2)}) collective-permute-start(bf16[2,256,256]{2,1,0:T(8,128)(2,1)} %get-tuple-element.47.pair), channel_id=1, source_target_pairs={{0,2},{1,3},{2,0},{3,1},{4,6},{5,7},{6,4},{7,5},{8,10},{9,11},{10,... | collective-permute-start | bytes 786440 | tf_op jit(solution)/shard_map/ppermute | solution.py:458
  7.5 15.0 %collective-permute-start.10 = (bf16[64,2176]{1,0:T(8,128)(2,1)}, bf16[64,2176]{1,0:T(8,128)(2,1)S(1)}, u32[]{:S(2)}, u32[]{:S(2)}) collective-permute-start(bf16[64,2176]{1,0:T(8,128)(2,1)} %get-tuple-element.51), channel_id=1, source_target_pairs={{0,8},{4,12},{8,0},{12,4},{1,9},{5,13},{9,1},{13,5},{2,10},{6,14},... | collective-permute-start | bytes 835592 | tf_op jit(solution)/shard_map/ppermute | solution.py:458
  17.5 5.0 %collective-permute-start.2 = (bf16[64,2176]{1,0:T(8,128)(2,1)S(1)}, bf16[64,2176]{1,0:T(8,128)(2,1)S(1)}, u32[]{:S(2)}, u32[]{:S(2)}) collective-permute-start(bf16[64,2176]{1,0:T(8,128)(2,1)S(1)} %collective-permute-done.1.refs_2_), channel_id=1, source_target_pairs={{0,1},{1,0},{2,3},{3,2},{4,5},{5,4},{6,7},{7,6},{8,9},{9,8},{10,11... | collective-permute-start | bytes 835592 | tf_op jit(solution)/shard_map/ppermute | solution.py:458
  17.6 1.1 %copy-start = (bf16[128,2176]{1,0:T(8,128)(2,1)S(1)}, bf16[128,2176]{1,0:T(8,128)(2,1)}, u32[]{:S(2)}) copy-start(bf16[128,2176]{1,0:T(8,128)(2,1)} %get-tuple-element.48.own) | copy-start | bytes 1671172
  19.6 2.9 %collective-permute-start.3 = (bf16[2,256,256]{2,1,0:T(8,128)(2,1)S(1)}, bf16[2,256,256]{2,1,0:T(8,128)(2,1)S(1)}, u32[]{:S(2)}, u32[]{:S(2)}) collective-permute-start(bf16[2,256,256]{2,1,0:T(8,128)(2,1)S(1)} %get-tuple-element.50.refs_1_), channel_id=1, source_target_pairs={{0,1},{1,0},{2,3},{3,2},{4,5},{5,4},{6,7},{7,6},{8,9},{9,8},{10,11... | collective-permute-start | bytes 786440 | tf_op jit(solution)/shard_map/ppermute | solution.py:458
  20.2 2.3 %collective-permute-start.4 = (bf16[2,256,256]{2,1,0:T(8,128)(2,1)S(1)}, bf16[2,256,256]{2,1,0:T(8,128)(2,1)S(1)}, u32[]{:S(2)}, u32[]{:S(2)}) collective-permute-start(bf16[2,256,256]{2,1,0:T(8,128)(2,1)S(1)} %get-tuple-element.52.refs_5_), channel_id=1, source_target_pairs={{0,1},{1,0},{2,3},{3,2},{4,5},{5,4},{6,7},{7,6},{8,9},{9,8},{10,11... | collective-permute-start | bytes 786440 | tf_op jit(solution)/shard_map/ppermute | solution.py:458
  22.5 7.0 %collective-permute-start.11 = (bf16[64,2176]{1,0:T(8,128)(2,1)S(1)}, bf16[64,2176]{1,0:T(8,128)(2,1)S(1)}, u32[]{:S(2)}, u32[]{:S(2)}) collective-permute-start(bf16[64,2176]{1,0:T(8,128)(2,1)S(1)} %collective-permute-done.10.a), channel_id=1, source_target_pairs={{0,4},{4,0},{8,12},{12,8},{1,5},{5,1},{9,13},{13,9},{2,6},{6,2},{1... | collective-permute-start | bytes 835592 | tf_op jit(solution)/shard_map/ppermute | solution.py:458
  29.5 5.0 %copy-start.2 = (bf16[2,256,1024]{2,1,0:T(8,128)(2,1)S(1)}, bf16[2,256,1024]{2,1,0:T(8,128)(2,1)}, u32[]{:S(2)}) copy-start(bf16[2,256,1024]{2,1,0:T(8,128)(2,1)} %get-tuple-element.61.refs_2_) | copy-start | bytes 3145732
  29.6 5.0 %collective-permute-start.12 = (bf16[128,2176]{1,0:T(8,128)(2,1)S(1)}, bf16[128,2176]{1,0:T(8,128)(2,1)S(1)}, u32[]{:S(2)}, u32[]{:S(2)}) collective-permute-start(bf16[128,2176]{1,0:T(8,128)(2,1)S(1)} %shard_map.115.refs_0_), channel_id=1, source_target_pairs={{0,1},{1,0},{2,3},{3,2},{4,5},{5,4},{6,7},{7,6},{8,9},{9,8},{10,11... | collective-permute-start | bytes 1671176 | tf_op jit(solution)/shard_map/ppermute | solution.py:458
  29.7 2.4 %collective-permute-start.6 = (bf16[320,256]{1,0:T(8,128)(2,1)S(1)}, bf16[320,256]{1,0:T(8,128)(2,1)S(1)}, u32[]{:S(2)}, u32[]{:S(2)}) collective-permute-start(bf16[320,256]{1,0:T(8,128)(2,1)S(1)} %get-tuple-element.55), channel_id=1, source_target_pairs={{0,1},{1,0},{2,3},{3,2},{4,5},{5,4},{6,7},{7,6},{8,9},{9,8},{10,11... | collective-permute-start | bytes 491528 | tf_op jit(solution)/shard_map/ppermute | solution.py:458
  30.2 1.9 %collective-permute-start.7 = (bf16[256,256]{1,0:T(8,128)(2,1)S(1)}, bf16[256,256]{1,0:T(8,128)(2,1)S(1)}, u32[]{:S(2)}, u32[]{:S(2)}) collective-permute-start(bf16[256,256]{1,0:T(8,128)(2,1)S(1)} %get-tuple-element.56), channel_id=1, source_target_pairs={{0,1},{1,0},{2,3},{3,2},{4,5},{5,4},{6,7},{7,6},{8,9},{9,8},{10,11... | collective-permute-start | bytes 393224 | tf_op jit(solution)/shard_map/ppermute | solution.py:458
  32.1 9.7 %collective-permute-start.8 = (bf16[576,256]{1,0:T(8,128)(2,1)S(1)}, bf16[576,256]{1,0:T(8,128)(2,1)S(1)}, u32[]{:S(2)}, u32[]{:S(2)}) collective-permute-start(bf16[576,256]{1,0:T(8,128)(2,1)S(1)} %shard_map.113), channel_id=1, source_target_pairs={{0,2},{1,3},{2,0},{3,1},{4,6},{5,7},{6,4},{7,5},{8,10},{9,11},{10,... | collective-permute-start | bytes 884744 | tf_op jit(solution)/shard_map/ppermute | solution.py:458
  40.1 1.7 %collective-permute-start.14 = (bf16[320,256]{1,0:T(8,128)(2,1)S(1)}, bf16[320,256]{1,0:T(8,128)(2,1)S(1)}, u32[]{:S(2)}, u32[]{:S(2)}) collective-permute-start(bf16[320,256]{1,0:T(8,128)(2,1)S(1)} %get-tuple-element.64), channel_id=1, source_target_pairs={{0,1},{1,0},{2,3},{3,2},{4,5},{5,4},{6,7},{7,6},{8,9},{9,8},{10,11... | collective-permute-start | bytes 491528 | tf_op jit(solution)/shard_map/ppermute | solution.py:458
  40.2 3.5 %collective-permute-start.18 = (bf16[256,256]{1,0:T(8,128)(2,1)S(1)}, bf16[256,256]{1,0:T(8,128)(2,1)S(1)}, u32[]{:S(2)}, u32[]{:S(2)}) collective-permute-start(bf16[256,256]{1,0:T(8,128)(2,1)S(1)} %get-tuple-element.77), channel_id=1, source_target_pairs={{0,1},{1,0},{2,3},{3,2},{4,5},{5,4},{6,7},{7,6},{8,9},{9,8},{10,11... | collective-permute-start | bytes 393224 | tf_op jit(solution)/shard_map/ppermute | solution.py:458
  40.7 6.4 %collective-permute-start.13 = (bf16[576,256]{1,0:T(8,128)(2,1)S(1)}, bf16[576,256]{1,0:T(8,128)(2,1)S(1)}, u32[]{:S(2)}, u32[]{:S(2)}) collective-permute-start(bf16[576,256]{1,0:T(8,128)(2,1)S(1)} %get-tuple-element.63), channel_id=1, source_target_pairs={{0,1},{1,0},{2,3},{3,2},{4,5},{5,4},{6,7},{7,6},{8,9},{9,8},{10,11... | collective-permute-start | bytes 884744 | tf_op jit(solution)/shard_map/ppermute | solution.py:458
  40.8 9.8 %collective-permute-start.5 = (bf16[576,256]{1,0:T(8,128)(2,1)S(1)}, bf16[576,256]{1,0:T(8,128)(2,1)S(1)}, u32[]{:S(2)}, u32[]{:S(2)}) collective-permute-start(bf16[576,256]{1,0:T(8,128)(2,1)S(1)} %get-tuple-element.54), channel_id=1, source_target_pairs={{0,1},{1,0},{2,3},{3,2},{4,5},{5,4},{6,7},{7,6},{8,9},{9,8},{10,11... | collective-permute-start | bytes 884744 | tf_op jit(solution)/shard_map/ppermute | solution.py:458
  41.9 7.1 %collective-permute-start.15 = (bf16[320,256]{1,0:T(8,128)(2,1)S(1)}, bf16[320,256]{1,0:T(8,128)(2,1)S(1)}, u32[]{:S(2)}, u32[]{:S(2)}) collective-permute-start(bf16[320,256]{1,0:T(8,128)(2,1)S(1)} %shard_map.117.after), channel_id=1, source_target_pairs={{0,2},{1,3},{2,0},{3,1},{4,6},{5,7},{6,4},{7,5},{8,10},{9,11},{10,... | collective-permute-start | bytes 491528 | tf_op jit(solution)/shard_map/ppermute | solution.py:458
  43.7 8.2 %collective-permute-start.19 = (bf16[256,256]{1,0:T(8,128)(2,1)S(1)}, bf16[256,256]{1,0:T(8,128)(2,1)S(1)}, u32[]{:S(2)}, u32[]{:S(2)}) collective-permute-start(bf16[256,256]{1,0:T(8,128)(2,1)S(1)} %shard_map.121), channel_id=1, source_target_pairs={{0,2},{1,3},{2,0},{3,1},{4,6},{5,7},{6,4},{7,5},{8,10},{9,11},{10,... | collective-permute-start | bytes 393224 | tf_op jit(solution)/shard_map/ppermute | solution.py:458
  49.3 5.0 %collective-permute-start.16 = (bf16[160,256]{1,0:T(8,128)(2,1)S(1)}, bf16[160,256]{1,0:T(8,128)(2,1)S(1)}, u32[]{:S(2)}, u32[]{:S(2)}) collective-permute-start(bf16[160,256]{1,0:T(8,128)(2,1)S(1)} %get-tuple-element.76), channel_id=1, source_target_pairs={{0,4},{4,0},{8,12},{12,8},{1,5},{5,1},{9,13},{13,9},{2,6},{6,2},{1... | collective-permute-start | bytes 245768 | tf_op jit(solution)/shard_map/ppermute | solution.py:458
  50.9 10.3 %collective-permute-start.9 = (bf16[288,256]{1,0:T(8,128)(2,1)S(1)}, bf16[288,256]{1,0:T(8,128)(2,1)S(1)}, u32[]{:S(2)}, u32[]{:S(2)}) collective-permute-start(bf16[288,256]{1,0:T(8,128)(2,1)S(1)} %get-tuple-element.60), channel_id=1, source_target_pairs={{0,4},{4,0},{8,12},{12,8},{1,5},{5,1},{9,13},{13,9},{2,6},{6,2},{1... | collective-permute-start | bytes 442376 | tf_op jit(solution)/shard_map/ppermute | solution.py:458
  52.2 5.4 %collective-permute-start.20 = (bf16[128,256]{1,0:T(8,128)(2,1)S(1)}, bf16[128,256]{1,0:T(8,128)(2,1)S(1)}, u32[]{:S(2)}, u32[]{:S(2)}) collective-permute-start(bf16[128,256]{1,0:T(8,128)(2,1)S(1)} %get-tuple-element.80), channel_id=1, source_target_pairs={{0,4},{4,0},{8,12},{12,8},{1,5},{5,1},{9,13},{13,9},{2,6},{6,2},{1... | collective-permute-start | bytes 196616 | tf_op jit(solution)/shard_map/ppermute | solution.py:458
  54.3 8.6 %collective-permute-start.17 = (bf16[160,256]{1,0:T(8,128)(2,1)S(1)}, bf16[160,256]{1,0:T(8,128)(2,1)S(1)}, u32[]{:S(2)}, u32[]{:S(2)}) collective-permute-start(bf16[160,256]{1,0:T(8,128)(2,1)S(1)} %shard_map.120), channel_id=1, source_target_pairs={{0,8},{4,12},{8,0},{12,4},{1,9},{5,13},{9,1},{13,5},{2,10},{6,14},... | collective-permute-start | bytes 245768 | tf_op jit(solution)/shard_map/ppermute | solution.py:458
  57.6 5.2 %collective-permute-start.21 = (bf16[128,256]{1,0:T(8,128)(2,1)S(1)}, bf16[128,256]{1,0:T(8,128)(2,1)S(1)}, u32[]{:S(2)}, u32[]{:S(2)}) collective-permute-start(bf16[128,256]{1,0:T(8,128)(2,1)S(1)} %shard_map.123), channel_id=1, source_target_pairs={{0,8},{4,12},{8,0},{12,4},{1,9},{5,13},{9,1},{13,5},{2,10},{6,14},... | collective-permute-start | bytes 196616 | tf_op jit(solution)/shard_map/ppermute | solution.py:458
  (1 other events, 0.9 us)

commit v6 on v5

--- a/solution.py
+++ b/solution.py
@@ -211,6 +211,10 @@
     out_o[:, 2 * WIDTH :] = jnp.where(core == 0, columns[0:HALF], columns[HALF:]).astype(BF16)
     for copy in copies[2:]:
         copy.wait()
+
+
+def after_kernel(value, after, out_o):
+    out_o[...] = value[...]
 
 
 def stage_kernel(pair_x, own, pair, pair_x_o, own_o, pair_o):
@@ -398,7 +402,7 @@
     return mixed.astype(BF16)
 
 
-def combine_kernel(mine, other, theirs, pick, gate, first_o, second_o, rows_o):
+def combine_kernel(mine, other, theirs, pick, gate, after, first_o, second_o, rows_o):
     both = add2(add2(mine[0], other[...]), theirs[...])
     grads, back = combine_grads(both[0:320], pick, rows_o)
     mixed = combine_outs(both[320:576], pick, gate)
@@ -407,7 +411,7 @@
         dst[160:288, :] = mixed[p * 128 : p * 128 + 128]
 
 
-def far_grads_kernel(mine, other, theirs, pick, after, first_o, second_o, rows_o):
+def far_grads_kernel(mine, other, theirs, pick, after, after2, first_o, second_o, rows_o):
     both = add2(add2(mine[0, 0:320], other[0:320]), theirs[...])
     grads, back = combine_grads(both, pick, rows_o)
     for p, dst in enumerate((first_o, second_o)):
@@ -526,8 +530,11 @@
     got.append(swap(got[1], "expert", 1))
     both = shape((2, 256, 256))
     pair_x, own, pair_own = kernel_call(
-        stage_kernel, (both, shape((2 * HALF, width)), both), "vvv"
+        stage_kernel,
+        (both, shape((2 * HALF, width)), both),
+        "vvv",
     )(swap(pair_own, "tensor", 2), own, pair_own)
+    pair_x = kernel_call(after_kernel, both, "va")(pair_x, got[1])
     pair_c = swap(pair_own, "tensor", 1)
     pair_d = swap(pair_x, "tensor", 1)
     near_other = swap(got[0], "tensor", 1)
@@ -554,15 +561,6 @@
     )
     theirs = swap(away, "tensor", 2)
     other = swap(here, "tensor", 1)
-    part = shape((288, 256))
-    combine = kernel_call(
-        combine_kernel,
-        (part, part, shape((2, 128, 256))),
-        "vvvvv",
-        flops=300_000_000,
-        nbytes=2_000_000,
-    )
-    own_part, near_part, rows = combine(keep, other, theirs, pick, gate)
     far_mine = kernel_call(join_kernel, shape((2 * HALF, 2 * WIDTH + 128)), "vva")(
         got[1], got[2], gate
     )
@@ -587,8 +585,12 @@
         fkeep, swap(flast, "tensor", 1), fgrads
     )
     fgrads = swap(fgrads, "tensor", 2)
+    part = shape((288, 256))
+    own_part, near_part, rows = kernel_call(
+        combine_kernel, (part, part, shape((2, 128, 256))), "vvvvva"
+    )(keep, other, theirs, pick, gate, fouts)
+    near_got = swap(near_part, "expert", 1)
     fouts = swap(fouts, "tensor", 2)
-    near_got = swap(near_part, "expert", 1)
     grad_down, grad_up, weights_done = kernel_call(
         weights_kernel,
         (shape((2, 512, 1024)), shape((2, 1024, 512)), shape((8, 128), F32)),
@@ -598,8 +600,8 @@
     )(act, grad, cross, pre, fact, fgrad, fcross, fpre)
     part = shape((160, 256))
     grads2, grads3, frows = kernel_call(
-        far_grads_kernel, (part, part, shape((2, 128, 256))), "vvvva"
-    )(fkeep, fother, fgrads, fpick, weights_done)
+        far_grads_kernel, (part, part, shape((2, 128, 256))), "vvvvaa"
+    )(fkeep, fother, fgrads, fpick, weights_done, near_got)
     grads2 = kernel_call(sum_kernel, part, "vv")(grads2, swap(grads3, "expert", 1))
     far_grads = swap(grads2, "expert", 2)
     part = shape((128, 256))

time: 64.1 us -> 63.1 us (0.984)
  starting transfers between devices: 22.7 us -> 19.6 us
  waiting for transfers between devices: 17.2 us -> 19.5 us
    ppermute x22, starting transfers between devices: 22.7 us -> 19.6 us  [swap(): return lax.ppermute(value, axis, [(i, i ^ mask) for i in range(size)])]
    ppermute x22, waiting for transfers between devices: 17.2 us -> 19.5 us  [swap(): return lax.ppermute(value, axis, [(i, i ^ mask) for i in range(size)])]
  transfers between devices with their start and end apart: 22 -> 22, of which waited for: 8 -> 10; matrix products, arithmetic and copies ran while one was open for 0% -> 0% of each run, Pallas kernels for 28% -> 28%
where the time goes in v6:
time: 63.1 us; the launch traced here: 62.9 us
  Pallas kernels  21.1 us (33%)
  starting transfers between devices  19.6 us (31%)
  waiting for transfers between devices  19.5 us (31%)
  local copies, waits for them, and re-layouts  2.01 us (3%)
  between operations  0.76 us (1%)
    ppermute x22, starting transfers between devices, swap(): return lax.ppermute(value, axis, [(i, i ^ mask) for i in range(size)])  19.6 us
    ppermute x22, waiting for transfers between devices, swap(): return lax.ppermute(value, axis, [(i, i ^ mask) for i in range(size)])  19.5 us
    pallas_call x1, Pallas kernels, gathered_body(): kernel_call(own_chunk_kernel, chunk_outs() + (shape((2, 256, 1024)),), 'v...  6.95 us
    pallas_call x1, Pallas kernels, gathered_body(): kernel_call(far_chunk_kernel, chunk_outs(), 'vvvhh', scratch=[pltpu.VMEM(...  5.55 us
    pallas_call x1, Pallas kernels, gathered_body(): kernel_call(weights_kernel, (shape((2, 512, 1024)), shape((2, 1024, 512))...  3.03 us
    pallas_call x1, Pallas kernels, gathered_body(): kernel_call(payload_kernel, (shape((HALF, width)), shape((2 * HALF, width...  2.31 us
    unnamed x6, local copies, waits for them, and re-layouts  2.01 us
  transfers between devices with their start and end apart: 22, of which 10 were waited for; matrix products, arithmetic and copies ran while one was open for 0% of the time, Pallas kernels for 28%

profile of v6, /device:TPU:0, one launch (start us, length us, event | category | flops | bytes accessed | tf_op | source)
XLA Modules:
  0.0 62.9 jit_solution(14558001144220188538)
XLA Ops:
  0.6 2.3 %shard_map.110 = (bf16[64,2176]{1,0:T(8,128)(2,1)}, bf16[128,2176]{1,0:T(8,128)(2,1)}, bf16[2,256,256]{2,1,0:T(8,128)(2,1)}) custom-call(bf16[128,1024]{1,0:T(8,128)(2,1)} %x.1, bf16[128,1024]{1,0:T(8,128)(2,1)} %c.1, f32[2,128]{1,0:T(2,128)} %bitcast.2, s32[2,128]{1,0:T(2,128)} %bitcast.3, bf16[2,256,256]{2,1,0:T(8,128)(2,1)} %pair_in.1), custom_call_target="tpu_custom_call" | custom-call | tf_op jit(solution)/shard_map/pallas_call | solution.py:514
  2.9 3.1 %collective-permute-start.1 = (bf16[64,2176]{1,0:T(8,128)(2,1)}, bf16[64,2176]{1,0:T(8,128)(2,1)S(1)}, u32[]{:S(2)}, u32[]{:S(2)}) collective-permute-start(bf16[64,2176]{1,0:T(8,128)(2,1)} %get-tuple-element.51), channel_id=1, source_target_pairs={{0,4},{4,0},{8,12},{12,8},{1,5},{5,1},{9,13},{13,9},{2,6},{6,2},{1... | collective-permute-start | bytes 835592 | tf_op jit(solution)/shard_map/ppermute | solution.py:462
  6.0 2.6 %collective-permute-start.4 = (bf16[64,2176]{1,0:T(8,128)(2,1)}, bf16[64,2176]{1,0:T(8,128)(2,1)S(1)}, u32[]{:S(2)}, u32[]{:S(2)}) collective-permute-start(bf16[64,2176]{1,0:T(8,128)(2,1)} %get-tuple-element.51), channel_id=1, source_target_pairs={{0,8},{4,12},{8,0},{12,4},{1,9},{5,13},{9,1},{13,5},{2,10},{6,14},... | collective-permute-start | bytes 835592 | tf_op jit(solution)/shard_map/ppermute | solution.py:462
  8.6 1.5 %collective-permute-start = (bf16[2,256,256]{2,1,0:T(8,128)(2,1)}, bf16[2,256,256]{2,1,0:T(8,128)(2,1)S(1)}, u32[]{:S(2)}, u32[]{:S(2)}) collective-permute-start(bf16[2,256,256]{2,1,0:T(8,128)(2,1)} %get-tuple-element.47.pair), channel_id=1, source_target_pairs={{0,2},{1,3},{2,0},{3,1},{4,6},{5,7},{6,4},{7,5},{8,10},{9,11},{10,... | collective-permute-start | bytes 786440 | tf_op jit(solution)/shard_map/ppermute | solution.py:462
  10.1 8.6 %collective-permute-done.1.refs_2_ = bf16[64,2176]{1,0:T(8,128)(2,1)S(1)} collective-permute-done((bf16[64,2176]{1,0:T(8,128)(2,1)}, bf16[64,2176]{1,0:T(8,128)(2,1)S(1)}, u32[]{:S(2)}, u32[]{:S(2)}) %collective-permute-start.1) | collective-permute-done | bytes 278560 | tf_op jit(solution)/shard_map/ppermute | solution.py:462
  18.8 1.1 %copy-done = bf16[128,2176]{1,0:T(8,128)(2,1)S(1)} copy-done((bf16[128,2176]{1,0:T(8,128)(2,1)S(1)}, bf16[128,2176]{1,0:T(8,128)(2,1)}, u32[]{:S(2)}) %copy-start) | copy-done | bytes 557080
  19.8 0.9 %copy-done.1 = bf16[2,256,256]{2,1,0:T(8,128)(2,1)S(1)} copy-done((bf16[2,256,256]{2,1,0:T(8,128)(2,1)S(1)}, bf16[2,256,256]{2,1,0:T(8,128)(2,1)}, u32[]{:S(2)}) %copy-start.1) | copy-done | bytes 262168
  21.9 0.7 %collective-permute-done.3.refs_4_ = bf16[2,256,256]{2,1,0:T(8,128)(2,1)S(1)} collective-permute-done((bf16[2,256,256]{2,1,0:T(8,128)(2,1)S(1)}, bf16[2,256,256]{2,1,0:T(8,128)(2,1)S(1)}, u32[]{:S(2)}, u32[]{:S(2)}) %collective-permute-start.3) | collective-permute-done | bytes 262176 | tf_op jit(solution)/shard_map/ppermute | solution.py:462
  23.0 6.9 %shard_map.113 = (bf16[2,576,256]{2,1,0:T(8,128)(2,1)S(1)}, bf16[576,256]{1,0:T(8,128)(2,1)S(1)}, bf16[320,256]{1,0:T(8,128)(2,1)S(1)}, bf16[256,256]{1,0:T(8,12...) custom-call(bf16[128,2176]{1,0:T(8,128)(2,1)S(1)} %get-tuple-element, ...), custom_call_target="tpu_custom_call" | custom-call | flops 4000000000 | bytes 10000000 | tf_op jit(solution)/shard_map/pallas_call | solution.py:541
  30.0 0.6 collective-permute-done.10.b
  31.7 1.4 %collective-permute-done.8.high = bf16[256,256]{1,0:T(8,128)(2,1)S(1)} collective-permute-done((bf16[256,256]{1,0:T(8,128)(2,1)S(1)}, bf16[256,256]{1,0:T(8,128)(2,1)S(1)}, u32[]{:S(2)}, u32[]{:S(2)}) %collective-permute-start.8) | collective-permute-done | bytes 131104 | tf_op jit(solution)/shard_map/ppermute | solution.py:462
  33.1 1.7 %collective-permute-start.9 = (bf16[576,256]{1,0:T(8,128)(2,1)S(1)}, bf16[576,256]{1,0:T(8,128)(2,1)S(1)}, u32[]{:S(2)}, u32[]{:S(2)}) collective-permute-start(bf16[576,256]{1,0:T(8,128)(2,1)S(1)} %shard_map.114), channel_id=1, source_target_pairs={{0,2},{1,3},{2,0},{3,1},{4,6},{5,7},{6,4},{7,5},{8,10},{9,11},{10,... | collective-permute-start | bytes 884744 | tf_op jit(solution)/shard_map/ppermute | solution.py:462
  34.9 5.6 %shard_map.116 = (bf16[2,576,256]{2,1,0:T(8,128)(2,1)S(1)}, bf16[576,256]{1,0:T(8,128)(2,1)S(1)}, bf16[320,256]{1,0:T(8,128)(2,1)S(1)}, bf16[256,256]{1,0:T(8,12...) custom-call(bf16[128,2176]{1,0:T(8,128)(2,1)S(1)} %shard_map.115.ref, ...), custom_call_target="tpu_custom_call" | custom-call | flops 4000000000 | bytes 10000000 | tf_op jit(solution)/shard_map/pallas_call | solution.py:568
  41.1 1.2 %collective-permute-done.9.after.theirs = bf16[576,256]{1,0:T(8,128)(2,1)S(1)} collective-permute-done((bf16[576,256]{1,0:T(8,128)(2,1)S(1)}, bf16[576,256]{1,0:T(8,128)(2,1)S(1)}, u32[]{:S(2)}, u32[]{:S(2)}) %collective-permute-start.9) | collective-permute-done | bytes 294944 | tf_op jit(solution)/shard_map/ppermute | solution.py:462
  42.3 1.7 %collective-permute-start.16 = (bf16[320,256]{1,0:T(8,128)(2,1)S(1)}, bf16[320,256]{1,0:T(8,128)(2,1)S(1)}, u32[]{:S(2)}, u32[]{:S(2)}) collective-permute-start(bf16[320,256]{1,0:T(8,128)(2,1)S(1)} %shard_map.117.after), channel_id=1, source_target_pairs={{0,2},{1,3},{2,0},{3,1},{4,6},{5,7},{6,4},{7,5},{8,10},{9,11},{10,... | collective-permute-start | bytes 491528 | tf_op jit(solution)/shard_map/ppermute | solution.py:462
  45.3 3.0 %shard_map.120 = (bf16[2,512,1024]{2,1,0:T(8,128)(2,1)}, bf16[2,1024,512]{2,1,0:T(8,128)(2,1)}, f32[8,128]{1,0:T(8,128)S(1)}) custom-call(bf16[2,128,512]{2,1,0:T(8,128)(2,1)S(1)} %get-tuple-element.67.act0, bf16[2,128,1024]{2,1,0:T(8,128)(2,1)S(1)} %get-tuple-element.68.grad0, bf16[2,128,1024]{2,1,0:T(8,128)(2,1)S(1)} %get-tuple-element.69.cross0, ...), custom_call_target="tpu_custom_call" | custom-call | flops 3000000000 | bytes 8000000 | tf_op jit(solution)/shard_map/pallas_call | solution.py:594
  48.3 1.8 %collective-permute-done.14.after2.g1 = bf16[288,256]{1,0:T(8,128)(2,1)S(1)} collective-permute-done((bf16[288,256]{1,0:T(8,128)(2,1)S(1)}, bf16[288,256]{1,0:T(8,128)(2,1)S(1)}, u32[]{:S(2)}, u32[]{:S(2)}) %collective-permute-start.14) | collective-permute-done | bytes 147488 | tf_op jit(solution)/shard_map/ppermute | solution.py:462
  51.4 1.5 %collective-permute-start.20 = (bf16[128,256]{1,0:T(8,128)(2,1)S(1)}, bf16[128,256]{1,0:T(8,128)(2,1)S(1)}, u32[]{:S(2)}, u32[]{:S(2)}) collective-permute-start(bf16[128,256]{1,0:T(8,128)(2,1)S(1)} %get-tuple-element.80), channel_id=1, source_target_pairs={{0,4},{4,0},{8,12},{12,8},{1,5},{5,1},{9,13},{13,9},{2,6},{6,2},{1... | collective-permute-start | bytes 196616 | tf_op jit(solution)/shard_map/ppermute | solution.py:462
  52.9 2.0 %collective-permute-done.17.b = bf16[160,256]{1,0:T(8,128)(2,1)S(1)} collective-permute-done((bf16[160,256]{1,0:T(8,128)(2,1)S(1)}, bf16[160,256]{1,0:T(8,128)(2,1)S(1)}, u32[]{:S(2)}, u32[]{:S(2)}) %collective-permute-start.17) | collective-permute-done | bytes 81952 | tf_op jit(solution)/shard_map/ppermute | solution.py:462
  54.9 1.7 %collective-permute-start.18 = (bf16[160,256]{1,0:T(8,128)(2,1)S(1)}, bf16[160,256]{1,0:T(8,128)(2,1)S(1)}, u32[]{:S(2)}, u32[]{:S(2)}) collective-permute-start(bf16[160,256]{1,0:T(8,128)(2,1)S(1)} %shard_map.122), channel_id=1, source_target_pairs={{0,8},{4,12},{8,0},{12,4},{1,9},{5,13},{9,1},{13,5},{2,10},{6,14},... | collective-permute-start | bytes 245768 | tf_op jit(solution)/shard_map/ppermute | solution.py:462
  56.7 1.7 %collective-permute-start.21 = (bf16[128,256]{1,0:T(8,128)(2,1)S(1)}, bf16[128,256]{1,0:T(8,128)(2,1)S(1)}, u32[]{:S(2)}, u32[]{:S(2)}) collective-permute-start(bf16[128,256]{1,0:T(8,128)(2,1)S(1)} %shard_map.124), channel_id=1, source_target_pairs={{0,8},{4,12},{8,0},{12,4},{1,9},{5,13},{9,1},{13,5},{2,10},{6,14},... | collective-permute-start | bytes 196616 | tf_op jit(solution)/shard_map/ppermute | solution.py:462
  58.4 1.0 %shard_map.126 = bf16[2,256,256]{2,1,0:T(8,128)(2,1)} custom-call(bf16[2,256,128]{2,1,0:T(8,128)(2,1)S(1)} %get-tuple-element.83.gram0, bf16[2,128,256]{2,1,0:T(8,128)(2,1)S(1)} %get-tuple-element.84.rows0, bf16[2,256,128]{2,1,0:T(8,128)(2,1)S(1)} %get-tuple-element.85.gram1, bf16[2,128,256]{2,1,0:T(8,128)(2,1)S(1)} %get-tuple-element.86.rows1), custom_call_target="tpu_custom_call" | custom-call | flops 300000000 | bytes 2000000 | tf_op jit(solution)/shard_map/pallas_call | solution.py:613
  59.4 2.5 %collective-permute-done.21.far_outs = bf16[128,256]{1,0:T(8,128)(2,1)S(1)} collective-permute-done((bf16[128,256]{1,0:T(8,128)(2,1)S(1)}, bf16[128,256]{1,0:T(8,128)(2,1)S(1)}, u32[]{:S(2)}, u32[]{:S(2)}) %collective-permute-start.21) | collective-permute-done | bytes 65568 | tf_op jit(solution)/shard_map/ppermute | solution.py:462
  61.9 1.0 %shard_map.125 = (bf16[128,256]{1,0:T(8,128)(2,1)}, bf16[128,256]{1,0:T(8,128)(2,1)}) custom-call(bf16[128,2176]{1,0:T(8,128)(2,1)S(1)} %get-tuple-element.49.refs_0_.own, bf16[288,256]{1,0:T(8,128)(2,1)S(1)} %get-tuple-element.63.g0, bf16[288,256]{1,0:T(8,128)(2,1)S(1)} %collective-permute-done.14.after2.g1, ...), custom_call_target="tpu_custom_call" | custom-call | flops 100000000 | bytes 1000000 | tf_op jit(solution)/shard_map/pallas_call | solution.py:616
  (43 shorter events, 6.0 us)
Async XLA Ops:
  2.9 15.8 %collective-permute-start.1 = (bf16[64,2176]{1,0:T(8,128)(2,1)}, bf16[64,2176]{1,0:T(8,128)(2,1)S(1)}, u32[]{:S(2)}, u32[]{:S(2)}) collective-permute-start(bf16[64,2176]{1,0:T(8,128)(2,1)} %get-tuple-element.51), channel_id=1, source_target_pairs={{0,4},{4,0},{8,12},{12,8},{1,5},{5,1},{9,13},{13,9},{2,6},{6,2},{1... | collective-permute-start | bytes 835592 | tf_op jit(solution)/shard_map/ppermute | solution.py:462
  6.0 15.4 %collective-permute-start.4 = (bf16[64,2176]{1,0:T(8,128)(2,1)}, bf16[64,2176]{1,0:T(8,128)(2,1)S(1)}, u32[]{:S(2)}, u32[]{:S(2)}) collective-permute-start(bf16[64,2176]{1,0:T(8,128)(2,1)} %get-tuple-element.51), channel_id=1, source_target_pairs={{0,8},{4,12},{8,0},{12,4},{1,9},{5,13},{9,1},{13,5},{2,10},{6,14},... | collective-permute-start | bytes 835592 | tf_op jit(solution)/shard_map/ppermute | solution.py:462
  8.6 10.1 %collective-permute-start = (bf16[2,256,256]{2,1,0:T(8,128)(2,1)}, bf16[2,256,256]{2,1,0:T(8,128)(2,1)S(1)}, u32[]{:S(2)}, u32[]{:S(2)}) collective-permute-start(bf16[2,256,256]{2,1,0:T(8,128)(2,1)} %get-tuple-element.47.pair), channel_id=1, source_target_pairs={{0,2},{1,3},{2,0},{3,1},{4,6},{5,7},{6,4},{7,5},{8,10},{9,11},{10,... | collective-permute-start | bytes 786440 | tf_op jit(solution)/shard_map/ppermute | solution.py:462
  18.7 4.3 %collective-permute-start.2 = (bf16[64,2176]{1,0:T(8,128)(2,1)S(1)}, bf16[64,2176]{1,0:T(8,128)(2,1)S(1)}, u32[]{:S(2)}, u32[]{:S(2)}) collective-permute-start(bf16[64,2176]{1,0:T(8,128)(2,1)S(1)} %collective-permute-done.1.refs_2_), channel_id=1, source_target_pairs={{0,1},{1,0},{2,3},{3,2},{4,5},{5,4},{6,7},{7,6},{8,9},{9,8},{10,11... | collective-permute-start | bytes 835592 | tf_op jit(solution)/shard_map/ppermute | solution.py:462
  18.7 1.1 %copy-start = (bf16[128,2176]{1,0:T(8,128)(2,1)S(1)}, bf16[128,2176]{1,0:T(8,128)(2,1)}, u32[]{:S(2)}) copy-start(bf16[128,2176]{1,0:T(8,128)(2,1)} %get-tuple-element.48.own) | copy-start | bytes 1671172
  20.8 1.7 %collective-permute-start.3 = (bf16[2,256,256]{2,1,0:T(8,128)(2,1)S(1)}, bf16[2,256,256]{2,1,0:T(8,128)(2,1)S(1)}, u32[]{:S(2)}, u32[]{:S(2)}) collective-permute-start(bf16[2,256,256]{2,1,0:T(8,128)(2,1)S(1)} %get-tuple-element.50.refs_1_), channel_id=1, source_target_pairs={{0,1},{1,0},{2,3},{3,2},{4,5},{5,4},{6,7},{7,6},{8,9},{9,8},{10,11... | collective-permute-start | bytes 786440 | tf_op jit(solution)/shard_map/ppermute | solution.py:462
  21.4 1.6 %collective-permute-start.5 = (bf16[2,256,256]{2,1,0:T(8,128)(2,1)S(1)}, bf16[2,256,256]{2,1,0:T(8,128)(2,1)S(1)}, u32[]{:S(2)}, u32[]{:S(2)}) collective-permute-start(bf16[2,256,256]{2,1,0:T(8,128)(2,1)S(1)} %shard_map.112.refs_5_), channel_id=1, source_target_pairs={{0,1},{1,0},{2,3},{3,2},{4,5},{5,4},{6,7},{7,6},{8,9},{9,8},{10,11... | collective-permute-start | bytes 786440 | tf_op jit(solution)/shard_map/ppermute | solution.py:462
  21.5 9.1 %collective-permute-start.10 = (bf16[64,2176]{1,0:T(8,128)(2,1)S(1)}, bf16[64,2176]{1,0:T(8,128)(2,1)S(1)}, u32[]{:S(2)}, u32[]{:S(2)}) collective-permute-start(bf16[64,2176]{1,0:T(8,128)(2,1)S(1)} %collective-permute-done.4.after.a), channel_id=1, source_target_pairs={{0,4},{4,0},{8,12},{12,8},{1,5},{5,1},{9,13},{13,9},{2,6},{6,2},{1... | collective-permute-start | bytes 835592 | tf_op jit(solution)/shard_map/ppermute | solution.py:462
  30.0 4.9 %copy-start.2 = (bf16[2,256,1024]{2,1,0:T(8,128)(2,1)S(1)}, bf16[2,256,1024]{2,1,0:T(8,128)(2,1)}, u32[]{:S(2)}) copy-start(bf16[2,256,1024]{2,1,0:T(8,128)(2,1)} %get-tuple-element.59.refs_2_) | copy-start | bytes 3145732
  30.6 4.2 %collective-permute-start.11 = (bf16[128,2176]{1,0:T(8,128)(2,1)S(1)}, bf16[128,2176]{1,0:T(8,128)(2,1)S(1)}, u32[]{:S(2)}, u32[]{:S(2)}) collective-permute-start(bf16[128,2176]{1,0:T(8,128)(2,1)S(1)} %shard_map.115.refs_0_), channel_id=1, source_target_pairs={{0,1},{1,0},{2,3},{3,2},{4,5},{5,4},{6,7},{7,6},{8,9},{9,8},{10,11... | collective-permute-start | bytes 1671176 | tf_op jit(solution)/shard_map/ppermute | solution.py:462
  30.7 2.4 %collective-permute-start.7 = (bf16[320,256]{1,0:T(8,128)(2,1)S(1)}, bf16[320,256]{1,0:T(8,128)(2,1)S(1)}, u32[]{:S(2)}, u32[]{:S(2)}) collective-permute-start(bf16[320,256]{1,0:T(8,128)(2,1)S(1)} %get-tuple-element.55), channel_id=1, source_target_pairs={{0,1},{1,0},{2,3},{3,2},{4,5},{5,4},{6,7},{7,6},{8,9},{9,8},{10,11... | collective-permute-start | bytes 491528 | tf_op jit(solution)/shard_map/ppermute | solution.py:462
  31.2 1.9 %collective-permute-start.8 = (bf16[256,256]{1,0:T(8,128)(2,1)S(1)}, bf16[256,256]{1,0:T(8,128)(2,1)S(1)}, u32[]{:S(2)}, u32[]{:S(2)}) collective-permute-start(bf16[256,256]{1,0:T(8,128)(2,1)S(1)} %get-tuple-element.56), channel_id=1, source_target_pairs={{0,1},{1,0},{2,3},{3,2},{4,5},{5,4},{6,7},{7,6},{8,9},{9,8},{10,11... | collective-permute-start | bytes 393224 | tf_op jit(solution)/shard_map/ppermute | solution.py:462
  31.3 13.2 %collective-permute-start.6 = (bf16[576,256]{1,0:T(8,128)(2,1)S(1)}, bf16[576,256]{1,0:T(8,128)(2,1)S(1)}, u32[]{:S(2)}, u32[]{:S(2)}) collective-permute-start(bf16[576,256]{1,0:T(8,128)(2,1)S(1)} %get-tuple-element.54), channel_id=1, source_target_pairs={{0,1},{1,0},{2,3},{3,2},{4,5},{5,4},{6,7},{7,6},{8,9},{9,8},{10,11... | collective-permute-start | bytes 884744 | tf_op jit(solution)/shard_map/ppermute | solution.py:462
  33.1 9.1 %collective-permute-start.9 = (bf16[576,256]{1,0:T(8,128)(2,1)S(1)}, bf16[576,256]{1,0:T(8,128)(2,1)S(1)}, u32[]{:S(2)}, u32[]{:S(2)}) collective-permute-start(bf16[576,256]{1,0:T(8,128)(2,1)S(1)} %shard_map.114), channel_id=1, source_target_pairs={{0,2},{1,3},{2,0},{3,1},{4,6},{5,7},{6,4},{7,5},{8,10},{9,11},{10,... | collective-permute-start | bytes 884744 | tf_op jit(solution)/shard_map/ppermute | solution.py:462
  40.4 1.8 %collective-permute-start.13 = (bf16[320,256]{1,0:T(8,128)(2,1)S(1)}, bf16[320,256]{1,0:T(8,128)(2,1)S(1)}, u32[]{:S(2)}, u32[]{:S(2)}) collective-permute-start(bf16[320,256]{1,0:T(8,128)(2,1)S(1)} %get-tuple-element.62), channel_id=1, source_target_pairs={{0,1},{1,0},{2,3},{3,2},{4,5},{5,4},{6,7},{7,6},{8,9},{9,8},{10,11... | collective-permute-start | bytes 491528 | tf_op jit(solution)/shard_map/ppermute | solution.py:462
  40.5 3.5 %collective-permute-start.12 = (bf16[256,256]{1,0:T(8,128)(2,1)S(1)}, bf16[256,256]{1,0:T(8,128)(2,1)S(1)}, u32[]{:S(2)}, u32[]{:S(2)}) collective-permute-start(bf16[256,256]{1,0:T(8,128)(2,1)S(1)} %get-tuple-element.61), channel_id=1, source_target_pairs={{0,1},{1,0},{2,3},{3,2},{4,5},{5,4},{6,7},{7,6},{8,9},{9,8},{10,11... | collective-permute-start | bytes 393224 | tf_op jit(solution)/shard_map/ppermute | solution.py:462
  41.0 7.3 %collective-permute-start.15 = (bf16[576,256]{1,0:T(8,128)(2,1)S(1)}, bf16[576,256]{1,0:T(8,128)(2,1)S(1)}, u32[]{:S(2)}, u32[]{:S(2)}) collective-permute-start(bf16[576,256]{1,0:T(8,128)(2,1)S(1)} %get-tuple-element.65), channel_id=1, source_target_pairs={{0,1},{1,0},{2,3},{3,2},{4,5},{5,4},{6,7},{7,6},{8,9},{9,8},{10,11... | collective-permute-start | bytes 884744 | tf_op jit(solution)/shard_map/ppermute | solution.py:462
  42.3 7.8 %collective-permute-start.16 = (bf16[320,256]{1,0:T(8,128)(2,1)S(1)}, bf16[320,256]{1,0:T(8,128)(2,1)S(1)}, u32[]{:S(2)}, u32[]{:S(2)}) collective-permute-start(bf16[320,256]{1,0:T(8,128)(2,1)S(1)} %shard_map.117.after), channel_id=1, source_target_pairs={{0,2},{1,3},{2,0},{3,1},{4,6},{5,7},{6,4},{7,5},{8,10},{9,11},{10,... | collective-permute-start | bytes 491528 | tf_op jit(solution)/shard_map/ppermute | solution.py:462
  44.1 7.0 %collective-permute-start.19 = (bf16[256,256]{1,0:T(8,128)(2,1)S(1)}, bf16[256,256]{1,0:T(8,128)(2,1)S(1)}, u32[]{:S(2)}, u32[]{:S(2)}) collective-permute-start(bf16[256,256]{1,0:T(8,128)(2,1)S(1)} %shard_map.118.after), channel_id=1, source_target_pairs={{0,2},{1,3},{2,0},{3,1},{4,6},{5,7},{6,4},{7,5},{8,10},{9,11},{10,... | collective-permute-start | bytes 393224 | tf_op jit(solution)/shard_map/ppermute | solution.py:462
  44.9 5.2 %collective-permute-start.14 = (bf16[288,256]{1,0:T(8,128)(2,1)S(1)}, bf16[288,256]{1,0:T(8,128)(2,1)S(1)}, u32[]{:S(2)}, u32[]{:S(2)}) collective-permute-start(bf16[288,256]{1,0:T(8,128)(2,1)S(1)} %get-tuple-element.64), channel_id=1, source_target_pairs={{0,4},{4,0},{8,12},{12,8},{1,5},{5,1},{9,13},{13,9},{2,6},{6,2},{1... | collective-permute-start | bytes 442376 | tf_op jit(solution)/shard_map/ppermute | solution.py:462
  50.4 4.5 %collective-permute-start.17 = (bf16[160,256]{1,0:T(8,128)(2,1)S(1)}, bf16[160,256]{1,0:T(8,128)(2,1)S(1)}, u32[]{:S(2)}, u32[]{:S(2)}) collective-permute-start(bf16[160,256]{1,0:T(8,128)(2,1)S(1)} %get-tuple-element.77), channel_id=1, source_target_pairs={{0,4},{4,0},{8,12},{12,8},{1,5},{5,1},{9,13},{13,9},{2,6},{6,2},{1... | collective-permute-start | bytes 245768 | tf_op jit(solution)/shard_map/ppermute | solution.py:462
  51.4 5.3 %collective-permute-start.20 = (bf16[128,256]{1,0:T(8,128)(2,1)S(1)}, bf16[128,256]{1,0:T(8,128)(2,1)S(1)}, u32[]{:S(2)}, u32[]{:S(2)}) collective-permute-start(bf16[128,256]{1,0:T(8,128)(2,1)S(1)} %get-tuple-element.80), channel_id=1, source_target_pairs={{0,4},{4,0},{8,12},{12,8},{1,5},{5,1},{9,13},{13,9},{2,6},{6,2},{1... | collective-permute-start | bytes 196616 | tf_op jit(solution)/shard_map/ppermute | solution.py:462
  54.9 7.0 %collective-permute-start.18 = (bf16[160,256]{1,0:T(8,128)(2,1)S(1)}, bf16[160,256]{1,0:T(8,128)(2,1)S(1)}, u32[]{:S(2)}, u32[]{:S(2)}) collective-permute-start(bf16[160,256]{1,0:T(8,128)(2,1)S(1)} %shard_map.122), channel_id=1, source_target_pairs={{0,8},{4,12},{8,0},{12,4},{1,9},{5,13},{9,1},{13,5},{2,10},{6,14},... | collective-permute-start | bytes 245768 | tf_op jit(solution)/shard_map/ppermute | solution.py:462
  56.7 5.2 %collective-permute-start.21 = (bf16[128,256]{1,0:T(8,128)(2,1)S(1)}, bf16[128,256]{1,0:T(8,128)(2,1)S(1)}, u32[]{:S(2)}, u32[]{:S(2)}) collective-permute-start(bf16[128,256]{1,0:T(8,128)(2,1)S(1)} %shard_map.124), channel_id=1, source_target_pairs={{0,8},{4,12},{8,0},{12,4},{1,9},{5,13},{9,1},{13,5},{2,10},{6,14},... | collective-permute-start | bytes 196616 | tf_op jit(solution)/shard_map/ppermute | solution.py:462
  (1 other events, 0.9 us)

commit v7 on v6

--- a/solution.py
+++ b/solution.py
@@ -217,8 +217,7 @@
     out_o[...] = value[...]
 
 
-def stage_kernel(pair_x, own, pair, pair_x_o, own_o, pair_o):
-    pair_x_o[...] = pair_x[...]
+def stage_kernel(own, pair, own_o, pair_o):
     own_o[...] = own[...]
     pair_o[...] = pair[...]
 
@@ -411,14 +410,14 @@
         dst[160:288, :] = mixed[p * 128 : p * 128 + 128]
 
 
-def far_grads_kernel(mine, other, theirs, pick, after, after2, first_o, second_o, rows_o):
+def far_grads_kernel(mine, other, theirs, pick, after, first_o, second_o, rows_o):
     both = add2(add2(mine[0, 0:320], other[0:320]), theirs[...])
     grads, back = combine_grads(both, pick, rows_o)
     for p, dst in enumerate((first_o, second_o)):
         put_grads(dst, grads, back, p)
 
 
-def far_outs_kernel(mine, other, theirs, pick, gate, first_o, second_o):
+def far_outs_kernel(mine, other, theirs, pick, gate, after, first_o, second_o):
     both = add2(add2(mine[0, 320:576], other[320:576]), theirs[...])
     mixed = combine_outs(both, pick, gate)
     first_o[...] = mixed[0:128]
@@ -529,11 +528,10 @@
     got = [swap(payload, "expert", 1), swap(payload, "expert", 2)]
     got.append(swap(got[1], "expert", 1))
     both = shape((2, 256, 256))
-    pair_x, own, pair_own = kernel_call(
-        stage_kernel,
-        (both, shape((2 * HALF, width)), both),
-        "vvv",
-    )(swap(pair_own, "tensor", 2), own, pair_own)
+    own, pair_own = kernel_call(
+        stage_kernel, (shape((2 * HALF, width)), both), "vv"
+    )(own, pair_own)
+    pair_x = swap(pair_own, "tensor", 2)
     pair_x = kernel_call(after_kernel, both, "va")(pair_x, got[1])
     pair_c = swap(pair_own, "tensor", 1)
     pair_d = swap(pair_x, "tensor", 1)
@@ -600,13 +598,13 @@
     )(act, grad, cross, pre, fact, fgrad, fcross, fpre)
     part = shape((160, 256))
     grads2, grads3, frows = kernel_call(
-        far_grads_kernel, (part, part, shape((2, 128, 256))), "vvvvaa"
-    )(fkeep, fother, fgrads, fpick, weights_done, near_got)
+        far_grads_kernel, (part, part, shape((2, 128, 256))), "vvvva"
+    )(fkeep, fother, fgrads, fpick, weights_done)
     grads2 = kernel_call(sum_kernel, part, "vv")(grads2, swap(grads3, "expert", 1))
     far_grads = swap(grads2, "expert", 2)
     part = shape((128, 256))
-    outs2, outs3 = kernel_call(far_outs_kernel, (part, part), "vvvvv")(
-        fkeep, fother, fouts, fpick, fgate
+    outs2, outs3 = kernel_call(far_outs_kernel, (part, part), "vvvvva")(
+        fkeep, fother, fouts, fpick, fgate, near_got
     )
     outs2 = kernel_call(sum_kernel, part, "vv")(outs2, swap(outs3, "expert", 1))
     far_outs = swap(outs2, "expert", 2)

time: 63.1 us -> 62.5 us (level)
  transfers between devices with their start and end apart: 22 -> 22, of which waited for: 10 -> 11; matrix products, arithmetic and copies ran while one was open for 0% -> 0% of each run, Pallas kernels for 28% -> 28%
where the time goes in v7:
time: 62.5 us; the launch traced here: 62.3 us
  Pallas kernels  21.1 us (34%)
  starting transfers between devices  19.3 us (31%)
  waiting for transfers between devices  19.2 us (31%)
  local copies, waits for them, and re-layouts  2.01 us (3%)
  between operations  0.76 us (1%)
    ppermute x22, starting transfers between devices, swap(): return lax.ppermute(value, axis, [(i, i ^ mask) for i in range(size)])  19.3 us
    ppermute x22, waiting for transfers between devices, swap(): return lax.ppermute(value, axis, [(i, i ^ mask) for i in range(size)])  19.2 us
    pallas_call x1, Pallas kernels, gathered_body(): kernel_call(own_chunk_kernel, chunk_outs() + (shape((2, 256, 1024)),), 'v...  6.95 us
    pallas_call x1, Pallas kernels, gathered_body(): kernel_call(far_chunk_kernel, chunk_outs(), 'vvvhh', scratch=[pltpu.VMEM(...  5.55 us
    pallas_call x1, Pallas kernels, gathered_body(): kernel_call(weights_kernel, (shape((2, 512, 1024)), shape((2, 1024, 512))...  3.03 us
    pallas_call x1, Pallas kernels, gathered_body(): kernel_call(payload_kernel, (shape((HALF, width)), shape((2 * HALF, width...  2.31 us
    unnamed x6, local copies, waits for them, and re-layouts  2.01 us
  transfers between devices with their start and end apart: 22, of which 11 were waited for; matrix products, arithmetic and copies ran while one was open for 0% of the time, Pallas kernels for 28%

profile of v7, /device:TPU:0, one launch (start us, length us, event | category | flops | bytes accessed | tf_op | source)
XLA Modules:
  0.0 62.3 jit_solution(15437960080885704303)
XLA Ops:
  0.6 2.3 %shard_map.110 = (bf16[64,2176]{1,0:T(8,128)(2,1)}, bf16[128,2176]{1,0:T(8,128)(2,1)}, bf16[2,256,256]{2,1,0:T(8,128)(2,1)}) custom-call(bf16[128,1024]{1,0:T(8,128)(2,1)} %x.1, bf16[128,1024]{1,0:T(8,128)(2,1)} %c.1, f32[2,128]{1,0:T(2,128)} %bitcast.2, s32[2,128]{1,0:T(2,128)} %bitcast.3, bf16[2,256,256]{2,1,0:T(8,128)(2,1)} %pair_in.1), custom_call_target="tpu_custom_call" | custom-call | tf_op jit(solution)/shard_map/pallas_call | solution.py:513
  2.9 3.1 %collective-permute-start = (bf16[64,2176]{1,0:T(8,128)(2,1)}, bf16[64,2176]{1,0:T(8,128)(2,1)S(1)}, u32[]{:S(2)}, u32[]{:S(2)}) collective-permute-start(bf16[64,2176]{1,0:T(8,128)(2,1)} %get-tuple-element.50), channel_id=1, source_target_pairs={{0,4},{4,0},{8,12},{12,8},{1,5},{5,1},{9,13},{13,9},{2,6},{6,2},{1... | collective-permute-start | bytes 835592 | tf_op jit(solution)/shard_map/ppermute | solution.py:461
  6.0 2.6 %collective-permute-start.4 = (bf16[64,2176]{1,0:T(8,128)(2,1)}, bf16[64,2176]{1,0:T(8,128)(2,1)S(1)}, u32[]{:S(2)}, u32[]{:S(2)}) collective-permute-start(bf16[64,2176]{1,0:T(8,128)(2,1)} %get-tuple-element.50), channel_id=1, source_target_pairs={{0,8},{4,12},{8,0},{12,4},{1,9},{5,13},{9,1},{13,5},{2,10},{6,14},... | collective-permute-start | bytes 835592 | tf_op jit(solution)/shard_map/ppermute | solution.py:461
  8.6 1.1 %copy-done = bf16[128,2176]{1,0:T(8,128)(2,1)S(1)} copy-done((bf16[128,2176]{1,0:T(8,128)(2,1)S(1)}, bf16[128,2176]{1,0:T(8,128)(2,1)}, u32[]{:S(2)}) %copy-start) | copy-done | bytes 557080
  9.7 0.9 %copy-done.1 = bf16[2,256,256]{2,1,0:T(8,128)(2,1)S(1)} copy-done((bf16[2,256,256]{2,1,0:T(8,128)(2,1)S(1)}, bf16[2,256,256]{2,1,0:T(8,128)(2,1)}, u32[]{:S(2)}) %copy-start.1) | copy-done | bytes 262168
  10.7 1.6 %collective-permute-start.3 = (bf16[2,256,256]{2,1,0:T(8,128)(2,1)S(1)}, bf16[2,256,256]{2,1,0:T(8,128)(2,1)S(1)}, u32[]{:S(2)}, u32[]{:S(2)}) collective-permute-start(bf16[2,256,256]{2,1,0:T(8,128)(2,1)S(1)} %get-tuple-element.49.refs_1_), channel_id=1, source_target_pairs={{0,2},{1,3},{2,0},{3,1},{4,6},{5,7},{6,4},{7,5},{8,10},{9,11},{10,... | collective-permute-start | bytes 786440 | tf_op jit(solution)/shard_map/ppermute | solution.py:461
  12.2 6.5 %collective-permute-done.refs_2_ = bf16[64,2176]{1,0:T(8,128)(2,1)S(1)} collective-permute-done((bf16[64,2176]{1,0:T(8,128)(2,1)}, bf16[64,2176]{1,0:T(8,128)(2,1)S(1)}, u32[]{:S(2)}, u32[]{:S(2)}) %collective-permute-start) | collective-permute-done | bytes 278560 | tf_op jit(solution)/shard_map/ppermute | solution.py:461
  19.3 2.0 %collective-permute-done.4.after.a = bf16[64,2176]{1,0:T(8,128)(2,1)S(1)} collective-permute-done((bf16[64,2176]{1,0:T(8,128)(2,1)}, bf16[64,2176]{1,0:T(8,128)(2,1)S(1)}, u32[]{:S(2)}, u32[]{:S(2)}) %collective-permute-start.4) | collective-permute-done | bytes 278560 | tf_op jit(solution)/shard_map/ppermute | solution.py:461
  21.9 1.0 %collective-permute-done.5.refs_6_ = bf16[2,256,256]{2,1,0:T(8,128)(2,1)S(1)} collective-permute-done((bf16[2,256,256]{2,1,0:T(8,128)(2,1)S(1)}, bf16[2,256,256]{2,1,0:T(8,128)(2,1)S(1)}, u32[]{:S(2)}, u32[]{:S(2)}) %collective-permute-start.5) | collective-permute-done | bytes 262176 | tf_op jit(solution)/shard_map/ppermute | solution.py:461
  22.9 6.9 %shard_map.113 = (bf16[2,576,256]{2,1,0:T(8,128)(2,1)S(1)}, bf16[576,256]{1,0:T(8,128)(2,1)S(1)}, bf16[320,256]{1,0:T(8,128)(2,1)S(1)}, bf16[256,256]{1,0:T(8,12...) custom-call(bf16[128,2176]{1,0:T(8,128)(2,1)S(1)} %get-tuple-element, ...), custom_call_target="tpu_custom_call" | custom-call | flops 4000000000 | bytes 10000000 | tf_op jit(solution)/shard_map/pallas_call | solution.py:539
  31.6 1.4 %collective-permute-done.8.high = bf16[256,256]{1,0:T(8,128)(2,1)S(1)} collective-permute-done((bf16[256,256]{1,0:T(8,128)(2,1)S(1)}, bf16[256,256]{1,0:T(8,128)(2,1)S(1)}, u32[]{:S(2)}, u32[]{:S(2)}) %collective-permute-start.8) | collective-permute-done | bytes 131104 | tf_op jit(solution)/shard_map/ppermute | solution.py:461
  33.0 1.6 %collective-permute-start.9 = (bf16[576,256]{1,0:T(8,128)(2,1)S(1)}, bf16[576,256]{1,0:T(8,128)(2,1)S(1)}, u32[]{:S(2)}, u32[]{:S(2)}) collective-permute-start(bf16[576,256]{1,0:T(8,128)(2,1)S(1)} %shard_map.114), channel_id=1, source_target_pairs={{0,2},{1,3},{2,0},{3,1},{4,6},{5,7},{6,4},{7,5},{8,10},{9,11},{10,... | collective-permute-start | bytes 884744 | tf_op jit(solution)/shard_map/ppermute | solution.py:461
  34.6 5.5 %shard_map.116 = (bf16[2,576,256]{2,1,0:T(8,128)(2,1)S(1)}, bf16[576,256]{1,0:T(8,128)(2,1)S(1)}, bf16[320,256]{1,0:T(8,128)(2,1)S(1)}, bf16[256,256]{1,0:T(8,12...) custom-call(bf16[128,2176]{1,0:T(8,128)(2,1)S(1)} %shard_map.115.ref, ...), custom_call_target="tpu_custom_call" | custom-call | flops 4000000000 | bytes 10000000 | tf_op jit(solution)/shard_map/pallas_call | solution.py:566
  40.8 1.3 %collective-permute-done.9.after.theirs = bf16[576,256]{1,0:T(8,128)(2,1)S(1)} collective-permute-done((bf16[576,256]{1,0:T(8,128)(2,1)S(1)}, bf16[576,256]{1,0:T(8,128)(2,1)S(1)}, u32[]{:S(2)}, u32[]{:S(2)}) %collective-permute-start.9) | collective-permute-done | bytes 294944 | tf_op jit(solution)/shard_map/ppermute | solution.py:461
  42.2 1.6 %collective-permute-start.16 = (bf16[320,256]{1,0:T(8,128)(2,1)S(1)}, bf16[320,256]{1,0:T(8,128)(2,1)S(1)}, u32[]{:S(2)}, u32[]{:S(2)}) collective-permute-start(bf16[320,256]{1,0:T(8,128)(2,1)S(1)} %shard_map.117.after), channel_id=1, source_target_pairs={{0,2},{1,3},{2,0},{3,1},{4,6},{5,7},{6,4},{7,5},{8,10},{9,11},{10,... | collective-permute-start | bytes 491528 | tf_op jit(solution)/shard_map/ppermute | solution.py:461
  45.3 3.0 %shard_map.120 = (bf16[2,512,1024]{2,1,0:T(8,128)(2,1)}, bf16[2,1024,512]{2,1,0:T(8,128)(2,1)}, f32[8,128]{1,0:T(8,128)S(1)}) custom-call(bf16[2,128,512]{2,1,0:T(8,128)(2,1)S(1)} %get-tuple-element.65.act0, bf16[2,128,1024]{2,1,0:T(8,128)(2,1)S(1)} %get-tuple-element.66.grad0, bf16[2,128,1024]{2,1,0:T(8,128)(2,1)S(1)} %get-tuple-element.67.cross0, ...), custom_call_target="tpu_custom_call" | custom-call | flops 3000000000 | bytes 8000000 | tf_op jit(solution)/shard_map/pallas_call | solution.py:592
  48.3 1.0 %collective-permute-done.16.theirs = bf16[320,256]{1,0:T(8,128)(2,1)S(1)} collective-permute-done((bf16[320,256]{1,0:T(8,128)(2,1)S(1)}, bf16[320,256]{1,0:T(8,128)(2,1)S(1)}, u32[]{:S(2)}, u32[]{:S(2)}) %collective-permute-start.16) | collective-permute-done | bytes 163872 | tf_op jit(solution)/shard_map/ppermute | solution.py:461
  51.1 1.0 %collective-permute-start.20 = (bf16[128,256]{1,0:T(8,128)(2,1)S(1)}, bf16[128,256]{1,0:T(8,128)(2,1)S(1)}, u32[]{:S(2)}, u32[]{:S(2)}) collective-permute-start(bf16[128,256]{1,0:T(8,128)(2,1)S(1)} %get-tuple-element.78), channel_id=1, source_target_pairs={{0,4},{4,0},{8,12},{12,8},{1,5},{5,1},{9,13},{13,9},{2,6},{6,2},{1... | collective-permute-start | bytes 196616 | tf_op jit(solution)/shard_map/ppermute | solution.py:461
  52.1 2.0 %collective-permute-done.17.b = bf16[160,256]{1,0:T(8,128)(2,1)S(1)} collective-permute-done((bf16[160,256]{1,0:T(8,128)(2,1)S(1)}, bf16[160,256]{1,0:T(8,128)(2,1)S(1)}, u32[]{:S(2)}, u32[]{:S(2)}) %collective-permute-start.17) | collective-permute-done | bytes 81952 | tf_op jit(solution)/shard_map/ppermute | solution.py:461
  54.2 1.6 %collective-permute-start.18 = (bf16[160,256]{1,0:T(8,128)(2,1)S(1)}, bf16[160,256]{1,0:T(8,128)(2,1)S(1)}, u32[]{:S(2)}, u32[]{:S(2)}) collective-permute-start(bf16[160,256]{1,0:T(8,128)(2,1)S(1)} %shard_map.122), channel_id=1, source_target_pairs={{0,8},{4,12},{8,0},{12,4},{1,9},{5,13},{9,1},{13,5},{2,10},{6,14},... | collective-permute-start | bytes 245768 | tf_op jit(solution)/shard_map/ppermute | solution.py:461
  56.1 1.8 %collective-permute-start.21 = (bf16[128,256]{1,0:T(8,128)(2,1)S(1)}, bf16[128,256]{1,0:T(8,128)(2,1)S(1)}, u32[]{:S(2)}, u32[]{:S(2)}) collective-permute-start(bf16[128,256]{1,0:T(8,128)(2,1)S(1)} %shard_map.124), channel_id=1, source_target_pairs={{0,8},{4,12},{8,0},{12,4},{1,9},{5,13},{9,1},{13,5},{2,10},{6,14},... | collective-permute-start | bytes 196616 | tf_op jit(solution)/shard_map/ppermute | solution.py:461
  57.8 1.0 %shard_map.126 = bf16[2,256,256]{2,1,0:T(8,128)(2,1)} custom-call(bf16[2,256,128]{2,1,0:T(8,128)(2,1)S(1)} %get-tuple-element.81.gram0, bf16[2,128,256]{2,1,0:T(8,128)(2,1)S(1)} %get-tuple-element.82.rows0, bf16[2,256,128]{2,1,0:T(8,128)(2,1)S(1)} %get-tuple-element.83.gram1, bf16[2,128,256]{2,1,0:T(8,128)(2,1)S(1)} %get-tuple-element.84.rows1), custom_call_target="tpu_custom_call" | custom-call | flops 300000000 | bytes 2000000 | tf_op jit(solution)/shard_map/pallas_call | solution.py:611
  58.8 2.5 %collective-permute-done.21.far_outs = bf16[128,256]{1,0:T(8,128)(2,1)S(1)} collective-permute-done((bf16[128,256]{1,0:T(8,128)(2,1)S(1)}, bf16[128,256]{1,0:T(8,128)(2,1)S(1)}, u32[]{:S(2)}, u32[]{:S(2)}) %collective-permute-start.21) | collective-permute-done | bytes 65568 | tf_op jit(solution)/shard_map/ppermute | solution.py:461
  61.3 1.0 %shard_map.125 = (bf16[128,256]{1,0:T(8,128)(2,1)}, bf16[128,256]{1,0:T(8,128)(2,1)}) custom-call(bf16[128,2176]{1,0:T(8,128)(2,1)S(1)} %get-tuple-element.48.refs_0_.own, bf16[288,256]{1,0:T(8,128)(2,1)S(1)} %get-tuple-element.61.g0, bf16[288,256]{1,0:T(8,128)(2,1)S(1)} %collective-permute-done.14.after.g1, ...), custom_call_target="tpu_custom_call" | custom-call | flops 100000000 | bytes 1000000 | tf_op jit(solution)/shard_map/pallas_call | solution.py:614
  (43 shorter events, 7.2 us)
Async XLA Ops:
  2.9 15.8 %collective-permute-start = (bf16[64,2176]{1,0:T(8,128)(2,1)}, bf16[64,2176]{1,0:T(8,128)(2,1)S(1)}, u32[]{:S(2)}, u32[]{:S(2)}) collective-permute-start(bf16[64,2176]{1,0:T(8,128)(2,1)} %get-tuple-element.50), channel_id=1, source_target_pairs={{0,4},{4,0},{8,12},{12,8},{1,5},{5,1},{9,13},{13,9},{2,6},{6,2},{1... | collective-permute-start | bytes 835592 | tf_op jit(solution)/shard_map/ppermute | solution.py:461
  6.0 15.3 %collective-permute-start.4 = (bf16[64,2176]{1,0:T(8,128)(2,1)}, bf16[64,2176]{1,0:T(8,128)(2,1)S(1)}, u32[]{:S(2)}, u32[]{:S(2)}) collective-permute-start(bf16[64,2176]{1,0:T(8,128)(2,1)} %get-tuple-element.50), channel_id=1, source_target_pairs={{0,8},{4,12},{8,0},{12,4},{1,9},{5,13},{9,1},{13,5},{2,10},{6,14},... | collective-permute-start | bytes 835592 | tf_op jit(solution)/shard_map/ppermute | solution.py:461
  8.6 1.1 %copy-start = (bf16[128,2176]{1,0:T(8,128)(2,1)S(1)}, bf16[128,2176]{1,0:T(8,128)(2,1)}, u32[]{:S(2)}) copy-start(bf16[128,2176]{1,0:T(8,128)(2,1)} %get-tuple-element.46.own) | copy-start | bytes 1671172
  10.7 8.6 %collective-permute-start.3 = (bf16[2,256,256]{2,1,0:T(8,128)(2,1)S(1)}, bf16[2,256,256]{2,1,0:T(8,128)(2,1)S(1)}, u32[]{:S(2)}, u32[]{:S(2)}) collective-permute-start(bf16[2,256,256]{2,1,0:T(8,128)(2,1)S(1)} %get-tuple-element.49.refs_1_), channel_id=1, source_target_pairs={{0,2},{1,3},{2,0},{3,1},{4,6},{5,7},{6,4},{7,5},{8,10},{9,11},{10,... | collective-permute-start | bytes 786440 | tf_op jit(solution)/shard_map/ppermute | solution.py:461
  18.7 4.2 %collective-permute-start.1 = (bf16[64,2176]{1,0:T(8,128)(2,1)S(1)}, bf16[64,2176]{1,0:T(8,128)(2,1)S(1)}, u32[]{:S(2)}, u32[]{:S(2)}) collective-permute-start(bf16[64,2176]{1,0:T(8,128)(2,1)S(1)} %collective-permute-done.refs_2_), channel_id=1, source_target_pairs={{0,1},{1,0},{2,3},{3,2},{4,5},{5,4},{6,7},{7,6},{8,9},{9,8},{10,11... | collective-permute-start | bytes 835592 | tf_op jit(solution)/shard_map/ppermute | solution.py:461
  18.7 3.2 %collective-permute-start.2 = (bf16[2,256,256]{2,1,0:T(8,128)(2,1)S(1)}, bf16[2,256,256]{2,1,0:T(8,128)(2,1)S(1)}, u32[]{:S(2)}, u32[]{:S(2)}) collective-permute-start(bf16[2,256,256]{2,1,0:T(8,128)(2,1)S(1)} %get-tuple-element.49.refs_1_), channel_id=1, source_target_pairs={{0,1},{1,0},{2,3},{3,2},{4,5},{5,4},{6,7},{7,6},{8,9},{9,8},{10,11... | collective-permute-start | bytes 786440 | tf_op jit(solution)/shard_map/ppermute | solution.py:461
  21.3 1.6 %collective-permute-start.5 = (bf16[2,256,256]{2,1,0:T(8,128)(2,1)S(1)}, bf16[2,256,256]{2,1,0:T(8,128)(2,1)S(1)}, u32[]{:S(2)}, u32[]{:S(2)}) collective-permute-start(bf16[2,256,256]{2,1,0:T(8,128)(2,1)S(1)} %shard_map.112.refs_5_), channel_id=1, source_target_pairs={{0,1},{1,0},{2,3},{3,2},{4,5},{5,4},{6,7},{7,6},{8,9},{9,8},{10,11... | collective-permute-start | bytes 786440 | tf_op jit(solution)/shard_map/ppermute | solution.py:461
  21.4 9.1 %collective-permute-start.10 = (bf16[64,2176]{1,0:T(8,128)(2,1)S(1)}, bf16[64,2176]{1,0:T(8,128)(2,1)S(1)}, u32[]{:S(2)}, u32[]{:S(2)}) collective-permute-start(bf16[64,2176]{1,0:T(8,128)(2,1)S(1)} %collective-permute-done.4.after.a), channel_id=1, source_target_pairs={{0,4},{4,0},{8,12},{12,8},{1,5},{5,1},{9,13},{13,9},{2,6},{6,2},{1... | collective-permute-start | bytes 835592 | tf_op jit(solution)/shard_map/ppermute | solution.py:461
  29.9 4.7 %copy-start.2 = (bf16[2,256,1024]{2,1,0:T(8,128)(2,1)S(1)}, bf16[2,256,1024]{2,1,0:T(8,128)(2,1)}, u32[]{:S(2)}) copy-start(bf16[2,256,1024]{2,1,0:T(8,128)(2,1)} %get-tuple-element.57.refs_2_) | copy-start | bytes 3145732
  30.5 4.1 %collective-permute-start.11 = (bf16[128,2176]{1,0:T(8,128)(2,1)S(1)}, bf16[128,2176]{1,0:T(8,128)(2,1)S(1)}, u32[]{:S(2)}, u32[]{:S(2)}) collective-permute-start(bf16[128,2176]{1,0:T(8,128)(2,1)S(1)} %shard_map.115.refs_0_), channel_id=1, source_target_pairs={{0,1},{1,0},{2,3},{3,2},{4,5},{5,4},{6,7},{7,6},{8,9},{9,8},{10,11... | collective-permute-start | bytes 1671176 | tf_op jit(solution)/shard_map/ppermute | solution.py:461
  30.6 2.4 %collective-permute-start.7 = (bf16[320,256]{1,0:T(8,128)(2,1)S(1)}, bf16[320,256]{1,0:T(8,128)(2,1)S(1)}, u32[]{:S(2)}, u32[]{:S(2)}) collective-permute-start(bf16[320,256]{1,0:T(8,128)(2,1)S(1)} %get-tuple-element.53), channel_id=1, source_target_pairs={{0,1},{1,0},{2,3},{3,2},{4,5},{5,4},{6,7},{7,6},{8,9},{9,8},{10,11... | collective-permute-start | bytes 491528 | tf_op jit(solution)/shard_map/ppermute | solution.py:461
  31.1 1.9 %collective-permute-start.8 = (bf16[256,256]{1,0:T(8,128)(2,1)S(1)}, bf16[256,256]{1,0:T(8,128)(2,1)S(1)}, u32[]{:S(2)}, u32[]{:S(2)}) collective-permute-start(bf16[256,256]{1,0:T(8,128)(2,1)S(1)} %get-tuple-element.54), channel_id=1, source_target_pairs={{0,1},{1,0},{2,3},{3,2},{4,5},{5,4},{6,7},{7,6},{8,9},{9,8},{10,11... | collective-permute-start | bytes 393224 | tf_op jit(solution)/shard_map/ppermute | solution.py:461
  31.2 13.2 %collective-permute-start.6 = (bf16[576,256]{1,0:T(8,128)(2,1)S(1)}, bf16[576,256]{1,0:T(8,128)(2,1)S(1)}, u32[]{:S(2)}, u32[]{:S(2)}) collective-permute-start(bf16[576,256]{1,0:T(8,128)(2,1)S(1)} %get-tuple-element.52), channel_id=1, source_target_pairs={{0,1},{1,0},{2,3},{3,2},{4,5},{5,4},{6,7},{7,6},{8,9},{9,8},{10,11... | collective-permute-start | bytes 884744 | tf_op jit(solution)/shard_map/ppermute | solution.py:461
  33.0 9.1 %collective-permute-start.9 = (bf16[576,256]{1,0:T(8,128)(2,1)S(1)}, bf16[576,256]{1,0:T(8,128)(2,1)S(1)}, u32[]{:S(2)}, u32[]{:S(2)}) collective-permute-start(bf16[576,256]{1,0:T(8,128)(2,1)S(1)} %shard_map.114), channel_id=1, source_target_pairs={{0,2},{1,3},{2,0},{3,1},{4,6},{5,7},{6,4},{7,5},{8,10},{9,11},{10,... | collective-permute-start | bytes 884744 | tf_op jit(solution)/shard_map/ppermute | solution.py:461
  40.2 2.0 %collective-permute-start.13 = (bf16[320,256]{1,0:T(8,128)(2,1)S(1)}, bf16[320,256]{1,0:T(8,128)(2,1)S(1)}, u32[]{:S(2)}, u32[]{:S(2)}) collective-permute-start(bf16[320,256]{1,0:T(8,128)(2,1)S(1)} %get-tuple-element.60), channel_id=1, source_target_pairs={{0,1},{1,0},{2,3},{3,2},{4,5},{5,4},{6,7},{7,6},{8,9},{9,8},{10,11... | collective-permute-start | bytes 491528 | tf_op jit(solution)/shard_map/ppermute | solution.py:461
  40.2 3.5 %collective-permute-start.12 = (bf16[256,256]{1,0:T(8,128)(2,1)S(1)}, bf16[256,256]{1,0:T(8,128)(2,1)S(1)}, u32[]{:S(2)}, u32[]{:S(2)}) collective-permute-start(bf16[256,256]{1,0:T(8,128)(2,1)S(1)} %get-tuple-element.59), channel_id=1, source_target_pairs={{0,1},{1,0},{2,3},{3,2},{4,5},{5,4},{6,7},{7,6},{8,9},{9,8},{10,11... | collective-permute-start | bytes 393224 | tf_op jit(solution)/shard_map/ppermute | solution.py:461
  40.7 7.6 %collective-permute-start.15 = (bf16[576,256]{1,0:T(8,128)(2,1)S(1)}, bf16[576,256]{1,0:T(8,128)(2,1)S(1)}, u32[]{:S(2)}, u32[]{:S(2)}) collective-permute-start(bf16[576,256]{1,0:T(8,128)(2,1)S(1)} %get-tuple-element.63), channel_id=1, source_target_pairs={{0,1},{1,0},{2,3},{3,2},{4,5},{5,4},{6,7},{7,6},{8,9},{9,8},{10,11... | collective-permute-start | bytes 884744 | tf_op jit(solution)/shard_map/ppermute | solution.py:461
  42.2 7.2 %collective-permute-start.16 = (bf16[320,256]{1,0:T(8,128)(2,1)S(1)}, bf16[320,256]{1,0:T(8,128)(2,1)S(1)}, u32[]{:S(2)}, u32[]{:S(2)}) collective-permute-start(bf16[320,256]{1,0:T(8,128)(2,1)S(1)} %shard_map.117.after), channel_id=1, source_target_pairs={{0,2},{1,3},{2,0},{3,1},{4,6},{5,7},{6,4},{7,5},{8,10},{9,11},{10,... | collective-permute-start | bytes 491528 | tf_op jit(solution)/shard_map/ppermute | solution.py:461
  43.8 7.0 %collective-permute-start.19 = (bf16[256,256]{1,0:T(8,128)(2,1)S(1)}, bf16[256,256]{1,0:T(8,128)(2,1)S(1)}, u32[]{:S(2)}, u32[]{:S(2)}) collective-permute-start(bf16[256,256]{1,0:T(8,128)(2,1)S(1)} %shard_map.118.after), channel_id=1, source_target_pairs={{0,2},{1,3},{2,0},{3,1},{4,6},{5,7},{6,4},{7,5},{8,10},{9,11},{10,... | collective-permute-start | bytes 393224 | tf_op jit(solution)/shard_map/ppermute | solution.py:461
  44.8 6.0 %collective-permute-start.14 = (bf16[288,256]{1,0:T(8,128)(2,1)S(1)}, bf16[288,256]{1,0:T(8,128)(2,1)S(1)}, u32[]{:S(2)}, u32[]{:S(2)}) collective-permute-start(bf16[288,256]{1,0:T(8,128)(2,1)S(1)} %get-tuple-element.62), channel_id=1, source_target_pairs={{0,4},{4,0},{8,12},{12,8},{1,5},{5,1},{9,13},{13,9},{2,6},{6,2},{1... | collective-permute-start | bytes 442376 | tf_op jit(solution)/shard_map/ppermute | solution.py:461
  49.7 4.5 %collective-permute-start.17 = (bf16[160,256]{1,0:T(8,128)(2,1)S(1)}, bf16[160,256]{1,0:T(8,128)(2,1)S(1)}, u32[]{:S(2)}, u32[]{:S(2)}) collective-permute-start(bf16[160,256]{1,0:T(8,128)(2,1)S(1)} %get-tuple-element.75), channel_id=1, source_target_pairs={{0,4},{4,0},{8,12},{12,8},{1,5},{5,1},{9,13},{13,9},{2,6},{6,2},{1... | collective-permute-start | bytes 245768 | tf_op jit(solution)/shard_map/ppermute | solution.py:461
  51.1 5.0 %collective-permute-start.20 = (bf16[128,256]{1,0:T(8,128)(2,1)S(1)}, bf16[128,256]{1,0:T(8,128)(2,1)S(1)}, u32[]{:S(2)}, u32[]{:S(2)}) collective-permute-start(bf16[128,256]{1,0:T(8,128)(2,1)S(1)} %get-tuple-element.78), channel_id=1, source_target_pairs={{0,4},{4,0},{8,12},{12,8},{1,5},{5,1},{9,13},{13,9},{2,6},{6,2},{1... | collective-permute-start | bytes 196616 | tf_op jit(solution)/shard_map/ppermute | solution.py:461
  54.2 7.1 %collective-permute-start.18 = (bf16[160,256]{1,0:T(8,128)(2,1)S(1)}, bf16[160,256]{1,0:T(8,128)(2,1)S(1)}, u32[]{:S(2)}, u32[]{:S(2)}) collective-permute-start(bf16[160,256]{1,0:T(8,128)(2,1)S(1)} %shard_map.122), channel_id=1, source_target_pairs={{0,8},{4,12},{8,0},{12,4},{1,9},{5,13},{9,1},{13,5},{2,10},{6,14},... | collective-permute-start | bytes 245768 | tf_op jit(solution)/shard_map/ppermute | solution.py:461
  56.1 5.2 %collective-permute-start.21 = (bf16[128,256]{1,0:T(8,128)(2,1)S(1)}, bf16[128,256]{1,0:T(8,128)(2,1)S(1)}, u32[]{:S(2)}, u32[]{:S(2)}) collective-permute-start(bf16[128,256]{1,0:T(8,128)(2,1)S(1)} %shard_map.124), channel_id=1, source_target_pairs={{0,8},{4,12},{8,0},{12,4},{1,9},{5,13},{9,1},{13,5},{2,10},{6,14},... | collective-permute-start | bytes 196616 | tf_op jit(solution)/shard_map/ppermute | solution.py:461
  (1 other events, 0.9 us)

commit v8 on v7

--- a/solution.py
+++ b/solution.py
@@ -499,11 +499,11 @@
     out_o[320:576, :] = add2(keep[1, 320:576], high[...])
 
 
-def away_grads_kernel(keep, low, after, out_o):
+def away_grads_kernel(keep, low, out_o):
     out_o[...] = add2(keep[1, 0:320], low[...])
 
 
-def away_outs_kernel(keep, high, after, out_o):
+def away_outs_kernel(keep, high, after, after2, out_o):
     out_o[...] = add2(keep[1, 320:576], high[...])
 
 
@@ -532,10 +532,11 @@
         stage_kernel, (shape((2 * HALF, width)), both), "vv"
     )(own, pair_own)
     pair_x = swap(pair_own, "tensor", 2)
-    pair_x = kernel_call(after_kernel, both, "va")(pair_x, got[1])
+    pair_x = kernel_call(after_kernel, both, "va", flops=30_000_000)(pair_x, got[1])
     pair_c = swap(pair_own, "tensor", 1)
     pair_d = swap(pair_x, "tensor", 1)
-    near_other = swap(got[0], "tensor", 1)
+    near = kernel_call(after_kernel, shape((HALF, width)), "va")(got[0], got[1])
+    near_other = swap(near, "tensor", 1)
     chunk = kernel_call(
         own_chunk_kernel,
         chunk_outs() + (shape((2, 256, 1024)),),
@@ -576,11 +577,11 @@
     )(far_mine, far_other, pair_all, up_weight, down_weight)
     fkeep, fhere, faway, flast, fcross, fact, fgrad, fpre, fgram, fpick, fgate = chunk
     fother = swap(fhere, "tensor", 1)
-    fgrads = kernel_call(away_grads_kernel, shape((320, 256)), "vva")(
-        fkeep, swap(faway, "tensor", 1), theirs
-    )
-    fouts = kernel_call(away_outs_kernel, shape((256, 256)), "vva")(
-        fkeep, swap(flast, "tensor", 1), fgrads
+    fgrads = kernel_call(away_grads_kernel, shape((320, 256)), "vv")(
+        fkeep, swap(faway, "tensor", 1)
+    )
+    fouts = kernel_call(away_outs_kernel, shape((256, 256)), "vvaa")(
+        fkeep, swap(flast, "tensor", 1), fgrads, theirs
     )
     fgrads = swap(fgrads, "tensor", 2)
     part = shape((288, 256))

time: 62.5 us -> 62.8 us (level)
  starting transfers between devices: 19.3 us -> 23.4 us
  waiting for transfers between devices: 19.2 us -> 15.3 us
    ppermute x22, starting transfers between devices: 19.3 us -> 23.4 us  [swap(): return lax.ppermute(value, axis, [(i, i ^ mask) for i in range(size)])]
    ppermute x22, waiting for transfers between devices: 19.2 us -> 15.3 us  [swap(): return lax.ppermute(value, axis, [(i, i ^ mask) for i in range(size)])]
  transfers between devices with their start and end apart: 22 -> 22, of which waited for: 11 -> 9; matrix products, arithmetic and copies ran while one was open for 0% -> 0% of each run, Pallas kernels for 28% -> 28%
where the time goes in v8:
time: 62.8 us; the launch traced here: 62.6 us
  starting transfers between devices  23.4 us (37%)
  Pallas kernels  21 us (33%)
  waiting for transfers between devices  15.3 us (24%)
  local copies, waits for them, and re-layouts  2.01 us (3%)
  between operations  0.77 us (1%)
    ppermute x22, starting transfers between devices, swap(): return lax.ppermute(value, axis, [(i, i ^ mask) for i in range(size)])  23.4 us
    ppermute x22, waiting for transfers between devices, swap(): return lax.ppermute(value, axis, [(i, i ^ mask) for i in range(size)])  15.3 us
    pallas_call x1, Pallas kernels, gathered_body(): kernel_call(own_chunk_kernel, chunk_outs() + (shape((2, 256, 1024)),), 'v...  6.95 us
    pallas_call x1, Pallas kernels, gathered_body(): kernel_call(far_chunk_kernel, chunk_outs(), 'vvvhh', scratch=[pltpu.VMEM(...  5.53 us
    pallas_call x1, Pallas kernels, gathered_body(): kernel_call(weights_kernel, (shape((2, 512, 1024)), shape((2, 1024, 512))...  3.02 us
    pallas_call x1, Pallas kernels, gathered_body(): kernel_call(payload_kernel, (shape((HALF, width)), shape((2 * HALF, width...  2.31 us
    unnamed x6, local copies, waits for them, and re-layouts  2.01 us
  transfers between devices with their start and end apart: 22, of which 9 were waited for; matrix products, arithmetic and copies ran while one was open for 0% of the time, Pallas kernels for 28%

profile of v8, /device:TPU:0, one launch (start us, length us, event | category | flops | bytes accessed | tf_op | source)
XLA Modules:
  0.0 62.6 jit_solution(11409789649759041669)
XLA Ops:
  0.6 2.3 %shard_map.110 = (bf16[64,2176]{1,0:T(8,128)(2,1)}, bf16[128,2176]{1,0:T(8,128)(2,1)}, bf16[2,256,256]{2,1,0:T(8,128)(2,1)}) custom-call(bf16[128,1024]{1,0:T(8,128)(2,1)} %x.1, bf16[128,1024]{1,0:T(8,128)(2,1)} %c.1, f32[2,128]{1,0:T(2,128)} %bitcast.2, s32[2,128]{1,0:T(2,128)} %bitcast.3, bf16[2,256,256]{2,1,0:T(8,128)(2,1)} %pair_in.1), custom_call_target="tpu_custom_call" | custom-call | tf_op jit(solution)/shard_map/pallas_call | solution.py:513
  2.9 4.1 %collective-permute-start.1 = (bf16[64,2176]{1,0:T(8,128)(2,1)}, bf16[64,2176]{1,0:T(8,128)(2,1)S(1)}, u32[]{:S(2)}, u32[]{:S(2)}) collective-permute-start(bf16[64,2176]{1,0:T(8,128)(2,1)} %get-tuple-element.50), channel_id=1, source_target_pairs={{0,8},{4,12},{8,0},{12,4},{1,9},{5,13},{9,1},{13,5},{2,10},{6,14},... | collective-permute-start | bytes 835592 | tf_op jit(solution)/shard_map/ppermute | solution.py:461
  7.0 1.6 %collective-permute-start = (bf16[64,2176]{1,0:T(8,128)(2,1)}, bf16[64,2176]{1,0:T(8,128)(2,1)S(1)}, u32[]{:S(2)}, u32[]{:S(2)}) collective-permute-start(bf16[64,2176]{1,0:T(8,128)(2,1)} %get-tuple-element.50), channel_id=1, source_target_pairs={{0,4},{4,0},{8,12},{12,8},{1,5},{5,1},{9,13},{13,9},{2,6},{6,2},{1... | collective-permute-start | bytes 835592 | tf_op jit(solution)/shard_map/ppermute | solution.py:461
  8.6 1.1 %copy-done = bf16[128,2176]{1,0:T(8,128)(2,1)S(1)} copy-done((bf16[128,2176]{1,0:T(8,128)(2,1)S(1)}, bf16[128,2176]{1,0:T(8,128)(2,1)}, u32[]{:S(2)}) %copy-start) | copy-done | bytes 557080
  9.7 0.9 %copy-done.1 = bf16[2,256,256]{2,1,0:T(8,128)(2,1)S(1)} copy-done((bf16[2,256,256]{2,1,0:T(8,128)(2,1)S(1)}, bf16[2,256,256]{2,1,0:T(8,128)(2,1)}, u32[]{:S(2)}) %copy-start.1) | copy-done | bytes 262168
  10.7 1.6 %collective-permute-start.4 = (bf16[2,256,256]{2,1,0:T(8,128)(2,1)S(1)}, bf16[2,256,256]{2,1,0:T(8,128)(2,1)S(1)}, u32[]{:S(2)}, u32[]{:S(2)}) collective-permute-start(bf16[2,256,256]{2,1,0:T(8,128)(2,1)S(1)} %get-tuple-element.49.refs_1_), channel_id=1, source_target_pairs={{0,2},{1,3},{2,0},{3,1},{4,6},{5,7},{6,4},{7,5},{8,10},{9,11},{10,... | collective-permute-start | bytes 786440 | tf_op jit(solution)/shard_map/ppermute | solution.py:461
  12.2 7.7 %collective-permute-done.1.after.a = bf16[64,2176]{1,0:T(8,128)(2,1)S(1)} collective-permute-done((bf16[64,2176]{1,0:T(8,128)(2,1)}, bf16[64,2176]{1,0:T(8,128)(2,1)S(1)}, u32[]{:S(2)}, u32[]{:S(2)}) %collective-permute-start.1) | collective-permute-done | bytes 278560 | tf_op jit(solution)/shard_map/ppermute | solution.py:461
  21.0 1.5 %collective-permute-start.10 = (bf16[64,2176]{1,0:T(8,128)(2,1)S(1)}, bf16[64,2176]{1,0:T(8,128)(2,1)S(1)}, u32[]{:S(2)}, u32[]{:S(2)}) collective-permute-start(bf16[64,2176]{1,0:T(8,128)(2,1)S(1)} %collective-permute-done.1.after.a), channel_id=1, source_target_pairs={{0,4},{4,0},{8,12},{12,8},{1,5},{5,1},{9,13},{13,9},{2,6},{6,2},{1... | collective-permute-start | bytes 835592 | tf_op jit(solution)/shard_map/ppermute | solution.py:461
  22.6 6.9 %shard_map.114 = (bf16[2,576,256]{2,1,0:T(8,128)(2,1)S(1)}, bf16[576,256]{1,0:T(8,128)(2,1)S(1)}, bf16[320,256]{1,0:T(8,128)(2,1)S(1)}, bf16[256,256]{1,0:T(8,12...) custom-call(bf16[128,2176]{1,0:T(8,128)(2,1)S(1)} %get-tuple-element, ...), custom_call_target="tpu_custom_call" | custom-call | flops 4000000000 | bytes 10000000 | tf_op jit(solution)/shard_map/pallas_call | solution.py:540
  31.1 1.4 %collective-permute-done.8.high = bf16[256,256]{1,0:T(8,128)(2,1)S(1)} collective-permute-done((bf16[256,256]{1,0:T(8,128)(2,1)S(1)}, bf16[256,256]{1,0:T(8,128)(2,1)S(1)}, u32[]{:S(2)}, u32[]{:S(2)}) %collective-permute-start.8) | collective-permute-done | bytes 131104 | tf_op jit(solution)/shard_map/ppermute | solution.py:461
  32.5 1.6 %collective-permute-start.9 = (bf16[576,256]{1,0:T(8,128)(2,1)S(1)}, bf16[576,256]{1,0:T(8,128)(2,1)S(1)}, u32[]{:S(2)}, u32[]{:S(2)}) collective-permute-start(bf16[576,256]{1,0:T(8,128)(2,1)S(1)} %shard_map.115), channel_id=1, source_target_pairs={{0,2},{1,3},{2,0},{3,1},{4,6},{5,7},{6,4},{7,5},{8,10},{9,11},{10,... | collective-permute-start | bytes 884744 | tf_op jit(solution)/shard_map/ppermute | solution.py:461
  34.1 5.5 %shard_map.117 = (bf16[2,576,256]{2,1,0:T(8,128)(2,1)S(1)}, bf16[576,256]{1,0:T(8,128)(2,1)S(1)}, bf16[320,256]{1,0:T(8,128)(2,1)S(1)}, bf16[256,256]{1,0:T(8,12...) custom-call(bf16[128,2176]{1,0:T(8,128)(2,1)S(1)} %shard_map.116.ref, ...), custom_call_target="tpu_custom_call" | custom-call | flops 4000000000 | bytes 10000000 | tf_op jit(solution)/shard_map/pallas_call | solution.py:567
  40.3 0.8 %collective-permute-done.13.low = bf16[320,256]{1,0:T(8,128)(2,1)S(1)} collective-permute-done((bf16[320,256]{1,0:T(8,128)(2,1)S(1)}, bf16[320,256]{1,0:T(8,128)(2,1)S(1)}, u32[]{:S(2)}, u32[]{:S(2)}) %collective-permute-start.13) | collective-permute-done | bytes 163872 | tf_op jit(solution)/shard_map/ppermute | solution.py:461
  41.8 1.6 %collective-permute-start.19 = (bf16[256,256]{1,0:T(8,128)(2,1)S(1)}, bf16[256,256]{1,0:T(8,128)(2,1)S(1)}, u32[]{:S(2)}, u32[]{:S(2)}) collective-permute-start(bf16[256,256]{1,0:T(8,128)(2,1)S(1)} %shard_map.119.after), channel_id=1, source_target_pairs={{0,2},{1,3},{2,0},{3,1},{4,6},{5,7},{6,4},{7,5},{8,10},{9,11},{10,... | collective-permute-start | bytes 393224 | tf_op jit(solution)/shard_map/ppermute | solution.py:461
  43.8 1.5 %collective-permute-start.14 = (bf16[288,256]{1,0:T(8,128)(2,1)S(1)}, bf16[288,256]{1,0:T(8,128)(2,1)S(1)}, u32[]{:S(2)}, u32[]{:S(2)}) collective-permute-start(bf16[288,256]{1,0:T(8,128)(2,1)S(1)} %get-tuple-element.62), channel_id=1, source_target_pairs={{0,4},{4,0},{8,12},{12,8},{1,5},{5,1},{9,13},{13,9},{2,6},{6,2},{1... | collective-permute-start | bytes 442376 | tf_op jit(solution)/shard_map/ppermute | solution.py:461
  45.3 3.0 %shard_map.121 = (bf16[2,512,1024]{2,1,0:T(8,128)(2,1)}, bf16[2,1024,512]{2,1,0:T(8,128)(2,1)}, f32[8,128]{1,0:T(8,128)S(1)}) custom-call(bf16[2,128,512]{2,1,0:T(8,128)(2,1)S(1)} %get-tuple-element.65.act0, bf16[2,128,1024]{2,1,0:T(8,128)(2,1)S(1)} %get-tuple-element.66.grad0, bf16[2,128,1024]{2,1,0:T(8,128)(2,1)S(1)} %get-tuple-element.67.cross0, ...), custom_call_target="tpu_custom_call" | custom-call | flops 3000000000 | bytes 8000000 | tf_op jit(solution)/shard_map/pallas_call | solution.py:593
  48.6 1.5 %collective-permute-start.17 = (bf16[160,256]{1,0:T(8,128)(2,1)S(1)}, bf16[160,256]{1,0:T(8,128)(2,1)S(1)}, u32[]{:S(2)}, u32[]{:S(2)}) collective-permute-start(bf16[160,256]{1,0:T(8,128)(2,1)S(1)} %get-tuple-element.75), channel_id=1, source_target_pairs={{0,4},{4,0},{8,12},{12,8},{1,5},{5,1},{9,13},{13,9},{2,6},{6,2},{1... | collective-permute-start | bytes 245768 | tf_op jit(solution)/shard_map/ppermute | solution.py:461
  50.6 1.5 %collective-permute-start.20 = (bf16[128,256]{1,0:T(8,128)(2,1)S(1)}, bf16[128,256]{1,0:T(8,128)(2,1)S(1)}, u32[]{:S(2)}, u32[]{:S(2)}) collective-permute-start(bf16[128,256]{1,0:T(8,128)(2,1)S(1)} %get-tuple-element.78), channel_id=1, source_target_pairs={{0,4},{4,0},{8,12},{12,8},{1,5},{5,1},{9,13},{13,9},{2,6},{6,2},{1... | collective-permute-start | bytes 196616 | tf_op jit(solution)/shard_map/ppermute | solution.py:461
  52.1 1.6 %collective-permute-done.17.b = bf16[160,256]{1,0:T(8,128)(2,1)S(1)} collective-permute-done((bf16[160,256]{1,0:T(8,128)(2,1)S(1)}, bf16[160,256]{1,0:T(8,128)(2,1)S(1)}, u32[]{:S(2)}, u32[]{:S(2)}) %collective-permute-start.17) | collective-permute-done | bytes 81952 | tf_op jit(solution)/shard_map/ppermute | solution.py:461
  53.7 2.6 %collective-permute-start.18 = (bf16[160,256]{1,0:T(8,128)(2,1)S(1)}, bf16[160,256]{1,0:T(8,128)(2,1)S(1)}, u32[]{:S(2)}, u32[]{:S(2)}) collective-permute-start(bf16[160,256]{1,0:T(8,128)(2,1)S(1)} %shard_map.123), channel_id=1, source_target_pairs={{0,8},{4,12},{8,0},{12,4},{1,9},{5,13},{9,1},{13,5},{2,10},{6,14},... | collective-permute-start | bytes 245768 | tf_op jit(solution)/shard_map/ppermute | solution.py:461
  56.4 1.4 %collective-permute-start.21 = (bf16[128,256]{1,0:T(8,128)(2,1)S(1)}, bf16[128,256]{1,0:T(8,128)(2,1)S(1)}, u32[]{:S(2)}, u32[]{:S(2)}) collective-permute-start(bf16[128,256]{1,0:T(8,128)(2,1)S(1)} %shard_map.125), channel_id=1, source_target_pairs={{0,8},{4,12},{8,0},{12,4},{1,9},{5,13},{9,1},{13,5},{2,10},{6,14},... | collective-permute-start | bytes 196616 | tf_op jit(solution)/shard_map/ppermute | solution.py:461
  57.8 1.0 %shard_map.127 = bf16[2,256,256]{2,1,0:T(8,128)(2,1)} custom-call(bf16[2,256,128]{2,1,0:T(8,128)(2,1)S(1)} %get-tuple-element.81.gram0, bf16[2,128,256]{2,1,0:T(8,128)(2,1)S(1)} %get-tuple-element.82.rows0, bf16[2,256,128]{2,1,0:T(8,128)(2,1)S(1)} %get-tuple-element.83.gram1, bf16[2,128,256]{2,1,0:T(8,128)(2,1)S(1)} %get-tuple-element.84.rows1), custom_call_target="tpu_custom_call" | custom-call | flops 300000000 | bytes 2000000 | tf_op jit(solution)/shard_map/pallas_call | solution.py:612
  58.8 2.8 %collective-permute-done.21.far_outs = bf16[128,256]{1,0:T(8,128)(2,1)S(1)} collective-permute-done((bf16[128,256]{1,0:T(8,128)(2,1)S(1)}, bf16[128,256]{1,0:T(8,128)(2,1)S(1)}, u32[]{:S(2)}, u32[]{:S(2)}) %collective-permute-start.21) | collective-permute-done | bytes 65568 | tf_op jit(solution)/shard_map/ppermute | solution.py:461
  61.6 1.0 %shard_map.126 = (bf16[128,256]{1,0:T(8,128)(2,1)}, bf16[128,256]{1,0:T(8,128)(2,1)}) custom-call(bf16[128,2176]{1,0:T(8,128)(2,1)S(1)} %get-tuple-element.48.refs_0_.own, bf16[288,256]{1,0:T(8,128)(2,1)S(1)} %get-tuple-element.61.g0, bf16[288,256]{1,0:T(8,128)(2,1)S(1)} %collective-permute-done.14.after.g1, ...), custom_call_target="tpu_custom_call" | custom-call | flops 100000000 | bytes 1000000 | tf_op jit(solution)/shard_map/pallas_call | solution.py:615
  (44 shorter events, 5.3 us)
Async XLA Ops:
  2.9 17.0 %collective-permute-start.1 = (bf16[64,2176]{1,0:T(8,128)(2,1)}, bf16[64,2176]{1,0:T(8,128)(2,1)S(1)}, u32[]{:S(2)}, u32[]{:S(2)}) collective-permute-start(bf16[64,2176]{1,0:T(8,128)(2,1)} %get-tuple-element.50), channel_id=1, source_target_pairs={{0,8},{4,12},{8,0},{12,4},{1,9},{5,13},{9,1},{13,5},{2,10},{6,14},... | collective-permute-start | bytes 835592 | tf_op jit(solution)/shard_map/ppermute | solution.py:461
  7.0 13.1 %collective-permute-start = (bf16[64,2176]{1,0:T(8,128)(2,1)}, bf16[64,2176]{1,0:T(8,128)(2,1)S(1)}, u32[]{:S(2)}, u32[]{:S(2)}) collective-permute-start(bf16[64,2176]{1,0:T(8,128)(2,1)} %get-tuple-element.50), channel_id=1, source_target_pairs={{0,4},{4,0},{8,12},{12,8},{1,5},{5,1},{9,13},{13,9},{2,6},{6,2},{1... | collective-permute-start | bytes 835592 | tf_op jit(solution)/shard_map/ppermute | solution.py:461
  8.6 1.1 %copy-start = (bf16[128,2176]{1,0:T(8,128)(2,1)S(1)}, bf16[128,2176]{1,0:T(8,128)(2,1)}, u32[]{:S(2)}) copy-start(bf16[128,2176]{1,0:T(8,128)(2,1)} %get-tuple-element.46.own) | copy-start | bytes 1671172
  10.7 10.1 %collective-permute-start.4 = (bf16[2,256,256]{2,1,0:T(8,128)(2,1)S(1)}, bf16[2,256,256]{2,1,0:T(8,128)(2,1)S(1)}, u32[]{:S(2)}, u32[]{:S(2)}) collective-permute-start(bf16[2,256,256]{2,1,0:T(8,128)(2,1)S(1)} %get-tuple-element.49.refs_1_), channel_id=1, source_target_pairs={{0,2},{1,3},{2,0},{3,1},{4,6},{5,7},{6,4},{7,5},{8,10},{9,11},{10,... | collective-permute-start | bytes 786440 | tf_op jit(solution)/shard_map/ppermute | solution.py:461
  20.2 2.4 %collective-permute-start.2 = (bf16[64,2176]{1,0:T(8,128)(2,1)S(1)}, bf16[64,2176]{1,0:T(8,128)(2,1)S(1)}, u32[]{:S(2)}, u32[]{:S(2)}) collective-permute-start(bf16[64,2176]{1,0:T(8,128)(2,1)S(1)} %shard_map.112), channel_id=1, source_target_pairs={{0,1},{1,0},{2,3},{3,2},{4,5},{5,4},{6,7},{7,6},{8,9},{9,8},{10,11... | collective-permute-start | bytes 835592 | tf_op jit(solution)/shard_map/ppermute | solution.py:461
  20.3 2.2 %collective-permute-start.3 = (bf16[2,256,256]{2,1,0:T(8,128)(2,1)S(1)}, bf16[2,256,256]{2,1,0:T(8,128)(2,1)S(1)}, u32[]{:S(2)}, u32[]{:S(2)}) collective-permute-start(bf16[2,256,256]{2,1,0:T(8,128)(2,1)S(1)} %get-tuple-element.49.refs_1_), channel_id=1, source_target_pairs={{0,1},{1,0},{2,3},{3,2},{4,5},{5,4},{6,7},{7,6},{8,9},{9,8},{10,11... | collective-permute-start | bytes 786440 | tf_op jit(solution)/shard_map/ppermute | solution.py:461
  20.8 1.8 %collective-permute-start.5 = (bf16[2,256,256]{2,1,0:T(8,128)(2,1)S(1)}, bf16[2,256,256]{2,1,0:T(8,128)(2,1)S(1)}, u32[]{:S(2)}, u32[]{:S(2)}) collective-permute-start(bf16[2,256,256]{2,1,0:T(8,128)(2,1)S(1)} %shard_map.113.refs_5_), channel_id=1, source_target_pairs={{0,1},{1,0},{2,3},{3,2},{4,5},{5,4},{6,7},{7,6},{8,9},{9,8},{10,11... | collective-permute-start | bytes 786440 | tf_op jit(solution)/shard_map/ppermute | solution.py:461
  21.0 9.0 %collective-permute-start.10 = (bf16[64,2176]{1,0:T(8,128)(2,1)S(1)}, bf16[64,2176]{1,0:T(8,128)(2,1)S(1)}, u32[]{:S(2)}, u32[]{:S(2)}) collective-permute-start(bf16[64,2176]{1,0:T(8,128)(2,1)S(1)} %collective-permute-done.1.after.a), channel_id=1, source_target_pairs={{0,4},{4,0},{8,12},{12,8},{1,5},{5,1},{9,13},{13,9},{2,6},{6,2},{1... | collective-permute-start | bytes 835592 | tf_op jit(solution)/shard_map/ppermute | solution.py:461
  29.5 4.6 %copy-start.2 = (bf16[2,256,1024]{2,1,0:T(8,128)(2,1)S(1)}, bf16[2,256,1024]{2,1,0:T(8,128)(2,1)}, u32[]{:S(2)}) copy-start(bf16[2,256,1024]{2,1,0:T(8,128)(2,1)} %get-tuple-element.57.refs_2_) | copy-start | bytes 3145732
  30.0 4.1 %collective-permute-start.11 = (bf16[128,2176]{1,0:T(8,128)(2,1)S(1)}, bf16[128,2176]{1,0:T(8,128)(2,1)S(1)}, u32[]{:S(2)}, u32[]{:S(2)}) collective-permute-start(bf16[128,2176]{1,0:T(8,128)(2,1)S(1)} %shard_map.116.refs_0_), channel_id=1, source_target_pairs={{0,1},{1,0},{2,3},{3,2},{4,5},{5,4},{6,7},{7,6},{8,9},{9,8},{10,11... | collective-permute-start | bytes 1671176 | tf_op jit(solution)/shard_map/ppermute | solution.py:461
  30.1 2.4 %collective-permute-start.7 = (bf16[320,256]{1,0:T(8,128)(2,1)S(1)}, bf16[320,256]{1,0:T(8,128)(2,1)S(1)}, u32[]{:S(2)}, u32[]{:S(2)}) collective-permute-start(bf16[320,256]{1,0:T(8,128)(2,1)S(1)} %get-tuple-element.53), channel_id=1, source_target_pairs={{0,1},{1,0},{2,3},{3,2},{4,5},{5,4},{6,7},{7,6},{8,9},{9,8},{10,11... | collective-permute-start | bytes 491528 | tf_op jit(solution)/shard_map/ppermute | solution.py:461
  30.6 1.9 %collective-permute-start.8 = (bf16[256,256]{1,0:T(8,128)(2,1)S(1)}, bf16[256,256]{1,0:T(8,128)(2,1)S(1)}, u32[]{:S(2)}, u32[]{:S(2)}) collective-permute-start(bf16[256,256]{1,0:T(8,128)(2,1)S(1)} %get-tuple-element.54), channel_id=1, source_target_pairs={{0,1},{1,0},{2,3},{3,2},{4,5},{5,4},{6,7},{7,6},{8,9},{9,8},{10,11... | collective-permute-start | bytes 393224 | tf_op jit(solution)/shard_map/ppermute | solution.py:461
  30.7 12.7 %collective-permute-start.6 = (bf16[576,256]{1,0:T(8,128)(2,1)S(1)}, bf16[576,256]{1,0:T(8,128)(2,1)S(1)}, u32[]{:S(2)}, u32[]{:S(2)}) collective-permute-start(bf16[576,256]{1,0:T(8,128)(2,1)S(1)} %get-tuple-element.52), channel_id=1, source_target_pairs={{0,1},{1,0},{2,3},{3,2},{4,5},{5,4},{6,7},{7,6},{8,9},{9,8},{10,11... | collective-permute-start | bytes 884744 | tf_op jit(solution)/shard_map/ppermute | solution.py:461
  32.5 9.2 %collective-permute-start.9 = (bf16[576,256]{1,0:T(8,128)(2,1)S(1)}, bf16[576,256]{1,0:T(8,128)(2,1)S(1)}, u32[]{:S(2)}, u32[]{:S(2)}) collective-permute-start(bf16[576,256]{1,0:T(8,128)(2,1)S(1)} %shard_map.115), channel_id=1, source_target_pairs={{0,2},{1,3},{2,0},{3,1},{4,6},{5,7},{6,4},{7,5},{8,10},{9,11},{10,... | collective-permute-start | bytes 884744 | tf_op jit(solution)/shard_map/ppermute | solution.py:461
  39.7 1.5 %collective-permute-start.13 = (bf16[320,256]{1,0:T(8,128)(2,1)S(1)}, bf16[320,256]{1,0:T(8,128)(2,1)S(1)}, u32[]{:S(2)}, u32[]{:S(2)}) collective-permute-start(bf16[320,256]{1,0:T(8,128)(2,1)S(1)} %get-tuple-element.60), channel_id=1, source_target_pairs={{0,1},{1,0},{2,3},{3,2},{4,5},{5,4},{6,7},{7,6},{8,9},{9,8},{10,11... | collective-permute-start | bytes 491528 | tf_op jit(solution)/shard_map/ppermute | solution.py:461
  39.8 2.0 %collective-permute-start.12 = (bf16[256,256]{1,0:T(8,128)(2,1)S(1)}, bf16[256,256]{1,0:T(8,128)(2,1)S(1)}, u32[]{:S(2)}, u32[]{:S(2)}) collective-permute-start(bf16[256,256]{1,0:T(8,128)(2,1)S(1)} %get-tuple-element.59), channel_id=1, source_target_pairs={{0,1},{1,0},{2,3},{3,2},{4,5},{5,4},{6,7},{7,6},{8,9},{9,8},{10,11... | collective-permute-start | bytes 393224 | tf_op jit(solution)/shard_map/ppermute | solution.py:461
  40.2 8.1 %collective-permute-start.15 = (bf16[576,256]{1,0:T(8,128)(2,1)S(1)}, bf16[576,256]{1,0:T(8,128)(2,1)S(1)}, u32[]{:S(2)}, u32[]{:S(2)}) collective-permute-start(bf16[576,256]{1,0:T(8,128)(2,1)S(1)} %get-tuple-element.63), channel_id=1, source_target_pairs={{0,1},{1,0},{2,3},{3,2},{4,5},{5,4},{6,7},{7,6},{8,9},{9,8},{10,11... | collective-permute-start | bytes 884744 | tf_op jit(solution)/shard_map/ppermute | solution.py:461
  41.2 7.1 %collective-permute-start.16 = (bf16[320,256]{1,0:T(8,128)(2,1)S(1)}, bf16[320,256]{1,0:T(8,128)(2,1)S(1)}, u32[]{:S(2)}, u32[]{:S(2)}) collective-permute-start(bf16[320,256]{1,0:T(8,128)(2,1)S(1)} %shard_map.118.after), channel_id=1, source_target_pairs={{0,2},{1,3},{2,0},{3,1},{4,6},{5,7},{6,4},{7,5},{8,10},{9,11},{10,... | collective-permute-start | bytes 491528 | tf_op jit(solution)/shard_map/ppermute | solution.py:461
  41.8 8.5 %collective-permute-start.19 = (bf16[256,256]{1,0:T(8,128)(2,1)S(1)}, bf16[256,256]{1,0:T(8,128)(2,1)S(1)}, u32[]{:S(2)}, u32[]{:S(2)}) collective-permute-start(bf16[256,256]{1,0:T(8,128)(2,1)S(1)} %shard_map.119.after), channel_id=1, source_target_pairs={{0,2},{1,3},{2,0},{3,1},{4,6},{5,7},{6,4},{7,5},{8,10},{9,11},{10,... | collective-permute-start | bytes 393224 | tf_op jit(solution)/shard_map/ppermute | solution.py:461
  43.8 6.5 %collective-permute-start.14 = (bf16[288,256]{1,0:T(8,128)(2,1)S(1)}, bf16[288,256]{1,0:T(8,128)(2,1)S(1)}, u32[]{:S(2)}, u32[]{:S(2)}) collective-permute-start(bf16[288,256]{1,0:T(8,128)(2,1)S(1)} %get-tuple-element.62), channel_id=1, source_target_pairs={{0,4},{4,0},{8,12},{12,8},{1,5},{5,1},{9,13},{13,9},{2,6},{6,2},{1... | collective-permute-start | bytes 442376 | tf_op jit(solution)/shard_map/ppermute | solution.py:461
  48.6 5.1 %collective-permute-start.17 = (bf16[160,256]{1,0:T(8,128)(2,1)S(1)}, bf16[160,256]{1,0:T(8,128)(2,1)S(1)}, u32[]{:S(2)}, u32[]{:S(2)}) collective-permute-start(bf16[160,256]{1,0:T(8,128)(2,1)S(1)} %get-tuple-element.75), channel_id=1, source_target_pairs={{0,4},{4,0},{8,12},{12,8},{1,5},{5,1},{9,13},{13,9},{2,6},{6,2},{1... | collective-permute-start | bytes 245768 | tf_op jit(solution)/shard_map/ppermute | solution.py:461
  50.6 5.7 %collective-permute-start.20 = (bf16[128,256]{1,0:T(8,128)(2,1)S(1)}, bf16[128,256]{1,0:T(8,128)(2,1)S(1)}, u32[]{:S(2)}, u32[]{:S(2)}) collective-permute-start(bf16[128,256]{1,0:T(8,128)(2,1)S(1)} %get-tuple-element.78), channel_id=1, source_target_pairs={{0,4},{4,0},{8,12},{12,8},{1,5},{5,1},{9,13},{13,9},{2,6},{6,2},{1... | collective-permute-start | bytes 196616 | tf_op jit(solution)/shard_map/ppermute | solution.py:461
  53.7 7.9 %collective-permute-start.18 = (bf16[160,256]{1,0:T(8,128)(2,1)S(1)}, bf16[160,256]{1,0:T(8,128)(2,1)S(1)}, u32[]{:S(2)}, u32[]{:S(2)}) collective-permute-start(bf16[160,256]{1,0:T(8,128)(2,1)S(1)} %shard_map.123), channel_id=1, source_target_pairs={{0,8},{4,12},{8,0},{12,4},{1,9},{5,13},{9,1},{13,5},{2,10},{6,14},... | collective-permute-start | bytes 245768 | tf_op jit(solution)/shard_map/ppermute | solution.py:461
  56.4 5.2 %collective-permute-start.21 = (bf16[128,256]{1,0:T(8,128)(2,1)S(1)}, bf16[128,256]{1,0:T(8,128)(2,1)S(1)}, u32[]{:S(2)}, u32[]{:S(2)}) collective-permute-start(bf16[128,256]{1,0:T(8,128)(2,1)S(1)} %shard_map.125), channel_id=1, source_target_pairs={{0,8},{4,12},{8,0},{12,4},{1,9},{5,13},{9,1},{13,5},{2,10},{6,14},... | collective-permute-start | bytes 196616 | tf_op jit(solution)/shard_map/ppermute | solution.py:461
  (1 other events, 0.9 us)

commit v9 on v8

--- a/solution.py
+++ b/solution.py
@@ -360,14 +360,18 @@
     towers(read_meta(info), whole, up, down, copies, pair, outs, refs[21:])
 
 
-def weights_kernel(act0, grad0, cross0, pre0, act1, grad1, cross1, pre1, down_o, up_o, done_o):
+def stack(a, b):
+    return jnp.concatenate([a, b], axis=0)
+
+
+def down_kernel(act0, grad0, act1, grad1, down_o, done_o):
     done_o[...] = jnp.zeros((8, 128), F32)
-
-    def stack(a, b):
-        return jnp.concatenate([a, b], axis=0)
-
     for e in range(2):
         down_o[e] = mm(stack(act0[e], act1[e]), stack(grad0[e], grad1[e]), TN).astype(BF16)
+
+
+def up_kernel(cross0, pre0, cross1, pre1, up_o):
+    for e in range(2):
         up_o[e] = mm(stack(cross0[e], cross1[e]), stack(pre0[e], pre1[e]), TN).astype(BF16)
 
 
@@ -424,8 +428,8 @@
     second_o[...] = mixed[128:256]
 
 
-def sum_kernel(a, b, out_o):
-    out_o[...] = add2(a[...], b[...])
+def sum_kernel(a, b, *rest):
+    rest[-1][...] = add2(a[...], b[...])
 
 
 def pair_kernel(gram0, rows0, gram1, rows1, out_o):
@@ -535,8 +539,7 @@
     pair_x = kernel_call(after_kernel, both, "va", flops=30_000_000)(pair_x, got[1])
     pair_c = swap(pair_own, "tensor", 1)
     pair_d = swap(pair_x, "tensor", 1)
-    near = kernel_call(after_kernel, shape((HALF, width)), "va")(got[0], got[1])
-    near_other = swap(near, "tensor", 1)
+    near_other = swap(got[0], "tensor", 1)
     chunk = kernel_call(
         own_chunk_kernel,
         chunk_outs() + (shape((2, 256, 1024)),),
@@ -590,24 +593,31 @@
     )(keep, other, theirs, pick, gate, fouts)
     near_got = swap(near_part, "expert", 1)
     fouts = swap(fouts, "tensor", 2)
-    grad_down, grad_up, weights_done = kernel_call(
-        weights_kernel,
-        (shape((2, 512, 1024)), shape((2, 1024, 512)), shape((8, 128), F32)),
-        "vvvvvvvv",
-        flops=3_000_000_000,
-        nbytes=8_000_000,
-    )(act, grad, cross, pre, fact, fgrad, fcross, fpre)
+    grad_down, down_done = kernel_call(
+        down_kernel,
+        (shape((2, 512, 1024)), shape((8, 128), F32)),
+        "vvvv",
+        flops=1_500_000_000,
+        nbytes=4_000_000,
+    )(act, grad, fact, fgrad)
+    grad_up = kernel_call(
+        up_kernel,
+        shape((2, 1024, 512)),
+        "vvvv",
+        flops=1_500_000_000,
+        nbytes=4_000_000,
+    )(cross, pre, fcross, fpre)
     part = shape((160, 256))
     grads2, grads3, frows = kernel_call(
         far_grads_kernel, (part, part, shape((2, 128, 256))), "vvvva"
-    )(fkeep, fother, fgrads, fpick, weights_done)
+    )(fkeep, fother, fgrads, fpick, down_done)
     grads2 = kernel_call(sum_kernel, part, "vv")(grads2, swap(grads3, "expert", 1))
     far_grads = swap(grads2, "expert", 2)
     part = shape((128, 256))
     outs2, outs3 = kernel_call(far_outs_kernel, (part, part), "vvvvva")(
         fkeep, fother, fouts, fpick, fgate, near_got
     )
-    outs2 = kernel_call(sum_kernel, part, "vv")(outs2, swap(outs3, "expert", 1))
+    outs2 = kernel_call(sum_kernel, part, "vva")(outs2, swap(outs3, "expert", 1), grads2)
     far_outs = swap(outs2, "expert", 2)
     grad_pair = kernel_call(
         pair_kernel, shape((2, 256, 256)), "vvvv", flops=300_000_000, nbytes=2_000_000

time: 62.8 us -> 63.5 us (1.011)
  starting transfers between devices: 23.4 us -> 17.9 us
  waiting for transfers between devices: 15.3 us -> 20.4 us
  Pallas kernels: 21 us -> 22.1 us
    ppermute x22, starting transfers between devices: 23.4 us -> 17.9 us  [swap(): return lax.ppermute(value, axis, [(i, i ^ mask) for i in range(size)])]
    ppermute x22, waiting for transfers between devices: 15.3 us -> 20.4 us  [swap(): return lax.ppermute(value, axis, [(i, i ^ mask) for i in range(size)])]
    pallas_call x3, Pallas kernels: 3.06 us -> 4.15 us  [the longest x1 2.07 us: gathered_body(): kernel_call(down_kernel, (shape((2, 512, 1024)), shape((8, 128), F32)), '...]
  transfers between devices with their start and end apart: 22 -> 22, of which waited for: 9 -> 11; matrix products, arithmetic and copies ran while one was open for 0% -> 0% of each run, Pallas kernels for 28% -> 30%
where the time goes in v9:
time: 63.5 us; the launch traced here: 63.2 us
  Pallas kernels  22.1 us (35%)
  waiting for transfers between devices  20.4 us (32%)
  starting transfers between devices  17.9 us (28%)
  local copies, waits for them, and re-layouts  2.01 us (3%)
  between operations  0.76 us (1%)
    ppermute x22, waiting for transfers between devices, swap(): return lax.ppermute(value, axis, [(i, i ^ mask) for i in range(size)])  20.4 us
    ppermute x22, starting transfers between devices, swap(): return lax.ppermute(value, axis, [(i, i ^ mask) for i in range(size)])  17.9 us
    pallas_call x1, Pallas kernels, gathered_body(): kernel_call(own_chunk_kernel, chunk_outs() + (shape((2, 256, 1024)),), 'v...  6.97 us
    pallas_call x1, Pallas kernels, gathered_body(): kernel_call(far_chunk_kernel, chunk_outs(), 'vvvhh', scratch=[pltpu.VMEM(...  5.53 us
    pallas_call x1, Pallas kernels, gathered_body(): kernel_call(payload_kernel, (shape((HALF, width)), shape((2 * HALF, width...  2.31 us
    pallas_call x1, Pallas kernels, gathered_body(): kernel_call(down_kernel, (shape((2, 512, 1024)), shape((8, 128), F32)), '...  2.07 us
    pallas_call x1, Pallas kernels, gathered_body(): kernel_call(up_kernel, shape((2, 1024, 512)), 'vvvv', flops=1500000000, n...  2.06 us
    unnamed x6, local copies, waits for them, and re-layouts  2.01 us
  transfers between devices with their start and end apart: 22, of which 11 were waited for; matrix products, arithmetic and copies ran while one was open for 0% of the time, Pallas kernels for 30%

profile of v9, /device:TPU:0, one launch (start us, length us, event | category | flops | bytes accessed | tf_op | source)
XLA Modules:
  0.0 63.2 jit_solution(499586332048992285)
XLA Ops:
  0.6 2.3 %shard_map.110 = (bf16[64,2176]{1,0:T(8,128)(2,1)}, bf16[128,2176]{1,0:T(8,128)(2,1)}, bf16[2,256,256]{2,1,0:T(8,128)(2,1)}) custom-call(bf16[128,1024]{1,0:T(8,128)(2,1)} %x.1, bf16[128,1024]{1,0:T(8,128)(2,1)} %c.1, f32[2,128]{1,0:T(2,128)} %bitcast.2, s32[2,128]{1,0:T(2,128)} %bitcast.3, bf16[2,256,256]{2,1,0:T(8,128)(2,1)} %pair_in.1), custom_call_target="tpu_custom_call" | custom-call | tf_op jit(solution)/shard_map/pallas_call | solution.py:517
  2.9 3.1 %collective-permute-start = (bf16[64,2176]{1,0:T(8,128)(2,1)}, bf16[64,2176]{1,0:T(8,128)(2,1)S(1)}, u32[]{:S(2)}, u32[]{:S(2)}) collective-permute-start(bf16[64,2176]{1,0:T(8,128)(2,1)} %get-tuple-element.49), channel_id=1, source_target_pairs={{0,4},{4,0},{8,12},{12,8},{1,5},{5,1},{9,13},{13,9},{2,6},{6,2},{1... | collective-permute-start | bytes 835592 | tf_op jit(solution)/shard_map/ppermute | solution.py:465
  6.0 2.6 %collective-permute-start.4 = (bf16[64,2176]{1,0:T(8,128)(2,1)}, bf16[64,2176]{1,0:T(8,128)(2,1)S(1)}, u32[]{:S(2)}, u32[]{:S(2)}) collective-permute-start(bf16[64,2176]{1,0:T(8,128)(2,1)} %get-tuple-element.49), channel_id=1, source_target_pairs={{0,8},{4,12},{8,0},{12,4},{1,9},{5,13},{9,1},{13,5},{2,10},{6,14},... | collective-permute-start | bytes 835592 | tf_op jit(solution)/shard_map/ppermute | solution.py:465
  8.6 1.1 %copy-done = bf16[128,2176]{1,0:T(8,128)(2,1)S(1)} copy-done((bf16[128,2176]{1,0:T(8,128)(2,1)S(1)}, bf16[128,2176]{1,0:T(8,128)(2,1)}, u32[]{:S(2)}) %copy-start) | copy-done | bytes 557080
  9.7 0.9 %copy-done.1 = bf16[2,256,256]{2,1,0:T(8,128)(2,1)S(1)} copy-done((bf16[2,256,256]{2,1,0:T(8,128)(2,1)S(1)}, bf16[2,256,256]{2,1,0:T(8,128)(2,1)}, u32[]{:S(2)}) %copy-start.1) | copy-done | bytes 262168
  10.7 1.6 %collective-permute-start.3 = (bf16[2,256,256]{2,1,0:T(8,128)(2,1)S(1)}, bf16[2,256,256]{2,1,0:T(8,128)(2,1)S(1)}, u32[]{:S(2)}, u32[]{:S(2)}) collective-permute-start(bf16[2,256,256]{2,1,0:T(8,128)(2,1)S(1)} %get-tuple-element.48.refs_1_), channel_id=1, source_target_pairs={{0,2},{1,3},{2,0},{3,1},{4,6},{5,7},{6,4},{7,5},{8,10},{9,11},{10,... | collective-permute-start | bytes 786440 | tf_op jit(solution)/shard_map/ppermute | solution.py:465
  12.2 6.5 %collective-permute-done.refs_2_ = bf16[64,2176]{1,0:T(8,128)(2,1)S(1)} collective-permute-done((bf16[64,2176]{1,0:T(8,128)(2,1)}, bf16[64,2176]{1,0:T(8,128)(2,1)S(1)}, u32[]{:S(2)}, u32[]{:S(2)}) %collective-permute-start) | collective-permute-done | bytes 278560 | tf_op jit(solution)/shard_map/ppermute | solution.py:465
  19.3 2.0 %collective-permute-done.4.after.a = bf16[64,2176]{1,0:T(8,128)(2,1)S(1)} collective-permute-done((bf16[64,2176]{1,0:T(8,128)(2,1)}, bf16[64,2176]{1,0:T(8,128)(2,1)S(1)}, u32[]{:S(2)}, u32[]{:S(2)}) %collective-permute-start.4) | collective-permute-done | bytes 278560 | tf_op jit(solution)/shard_map/ppermute | solution.py:465
  21.9 1.0 %collective-permute-done.5.refs_6_ = bf16[2,256,256]{2,1,0:T(8,128)(2,1)S(1)} collective-permute-done((bf16[2,256,256]{2,1,0:T(8,128)(2,1)S(1)}, bf16[2,256,256]{2,1,0:T(8,128)(2,1)S(1)}, u32[]{:S(2)}, u32[]{:S(2)}) %collective-permute-start.5) | collective-permute-done | bytes 262176 | tf_op jit(solution)/shard_map/ppermute | solution.py:465
  22.9 7.0 %shard_map.113 = (bf16[2,576,256]{2,1,0:T(8,128)(2,1)S(1)}, bf16[576,256]{1,0:T(8,128)(2,1)S(1)}, bf16[320,256]{1,0:T(8,128)(2,1)S(1)}, bf16[256,256]{1,0:T(8,12...) custom-call(bf16[128,2176]{1,0:T(8,128)(2,1)S(1)} %get-tuple-element, ...), custom_call_target="tpu_custom_call" | custom-call | flops 4000000000 | bytes 10000000 | tf_op jit(solution)/shard_map/pallas_call | solution.py:543
  31.6 1.4 %collective-permute-done.8.high = bf16[256,256]{1,0:T(8,128)(2,1)S(1)} collective-permute-done((bf16[256,256]{1,0:T(8,128)(2,1)S(1)}, bf16[256,256]{1,0:T(8,128)(2,1)S(1)}, u32[]{:S(2)}, u32[]{:S(2)}) %collective-permute-start.8) | collective-permute-done | bytes 131104 | tf_op jit(solution)/shard_map/ppermute | solution.py:465
  33.0 1.6 %collective-permute-start.9 = (bf16[576,256]{1,0:T(8,128)(2,1)S(1)}, bf16[576,256]{1,0:T(8,128)(2,1)S(1)}, u32[]{:S(2)}, u32[]{:S(2)}) collective-permute-start(bf16[576,256]{1,0:T(8,128)(2,1)S(1)} %shard_map.114), channel_id=1, source_target_pairs={{0,2},{1,3},{2,0},{3,1},{4,6},{5,7},{6,4},{7,5},{8,10},{9,11},{10,... | collective-permute-start | bytes 884744 | tf_op jit(solution)/shard_map/ppermute | solution.py:465
  34.6 5.5 %shard_map.116 = (bf16[2,576,256]{2,1,0:T(8,128)(2,1)S(1)}, bf16[576,256]{1,0:T(8,128)(2,1)S(1)}, bf16[320,256]{1,0:T(8,128)(2,1)S(1)}, bf16[256,256]{1,0:T(8,12...) custom-call(bf16[128,2176]{1,0:T(8,128)(2,1)S(1)} %shard_map.115.ref, ...), custom_call_target="tpu_custom_call" | custom-call | flops 4000000000 | bytes 10000000 | tf_op jit(solution)/shard_map/pallas_call | solution.py:570
  42.3 1.5 %collective-permute-start.19 = (bf16[256,256]{1,0:T(8,128)(2,1)S(1)}, bf16[256,256]{1,0:T(8,128)(2,1)S(1)}, u32[]{:S(2)}, u32[]{:S(2)}) collective-permute-start(bf16[256,256]{1,0:T(8,128)(2,1)S(1)} %shard_map.118.after), channel_id=1, source_target_pairs={{0,2},{1,3},{2,0},{3,1},{4,6},{5,7},{6,4},{7,5},{8,10},{9,11},{10,... | collective-permute-start | bytes 393224 | tf_op jit(solution)/shard_map/ppermute | solution.py:465
  44.7 2.1 %shard_map.120 = (bf16[2,512,1024]{2,1,0:T(8,128)(2,1)}, f32[8,128]{1,0:T(8,128)S(1)}) custom-call(bf16[2,128,512]{2,1,0:T(8,128)(2,1)S(1)} %get-tuple-element.64.act0, bf16[2,128,1024]{2,1,0:T(8,128)(2,1)S(1)} %get-tuple-element.65.grad0, bf16[2,128,512]{2,1,0:T(8,128)(2,1)S(1)} %get-tuple-element.66.act1, bf16[2,128,1024]{2,1,0:T(8,128)(2,1)S(1)} %get-tuple-element.67.grad1), custom_call_target="tpu_custom_call" | custom-call | flops 1500000000 | bytes 4000000 | tf_op jit(solution)/shard_map/pallas_call | solution.py:596
  46.8 1.9 %collective-permute-done.16.theirs = bf16[320,256]{1,0:T(8,128)(2,1)S(1)} collective-permute-done((bf16[320,256]{1,0:T(8,128)(2,1)S(1)}, bf16[320,256]{1,0:T(8,128)(2,1)S(1)}, u32[]{:S(2)}, u32[]{:S(2)}) %collective-permute-start.16) | collective-permute-done | bytes 163872 | tf_op jit(solution)/shard_map/ppermute | solution.py:465
  49.5 1.2 %collective-permute-done.19.theirs = bf16[256,256]{1,0:T(8,128)(2,1)S(1)} collective-permute-done((bf16[256,256]{1,0:T(8,128)(2,1)S(1)}, bf16[256,256]{1,0:T(8,128)(2,1)S(1)}, u32[]{:S(2)}, u32[]{:S(2)}) %collective-permute-start.19) | collective-permute-done | bytes 131104 | tf_op jit(solution)/shard_map/ppermute | solution.py:465
  51.6 2.6 %collective-permute-done.17.b = bf16[160,256]{1,0:T(8,128)(2,1)S(1)} collective-permute-done((bf16[160,256]{1,0:T(8,128)(2,1)S(1)}, bf16[160,256]{1,0:T(8,128)(2,1)S(1)}, u32[]{:S(2)}, u32[]{:S(2)}) %collective-permute-start.17) | collective-permute-done | bytes 81952 | tf_op jit(solution)/shard_map/ppermute | solution.py:465
  54.1 1.3 %collective-permute-start.18 = (bf16[160,256]{1,0:T(8,128)(2,1)S(1)}, bf16[160,256]{1,0:T(8,128)(2,1)S(1)}, u32[]{:S(2)}, u32[]{:S(2)}) collective-permute-start(bf16[160,256]{1,0:T(8,128)(2,1)S(1)} %shard_map.122.rest_0_), channel_id=1, source_target_pairs={{0,8},{4,12},{8,0},{12,4},{1,9},{5,13},{9,1},{13,5},{2,10},{6,14},... | collective-permute-start | bytes 245768 | tf_op jit(solution)/shard_map/ppermute | solution.py:465
  56.1 1.4 %collective-permute-start.21 = (bf16[128,256]{1,0:T(8,128)(2,1)S(1)}, bf16[128,256]{1,0:T(8,128)(2,1)S(1)}, u32[]{:S(2)}, u32[]{:S(2)}) collective-permute-start(bf16[128,256]{1,0:T(8,128)(2,1)S(1)} %shard_map.124), channel_id=1, source_target_pairs={{0,8},{4,12},{8,0},{12,4},{1,9},{5,13},{9,1},{13,5},{2,10},{6,14},... | collective-permute-start | bytes 196616 | tf_op jit(solution)/shard_map/ppermute | solution.py:465
  57.5 2.1 %shard_map.127 = bf16[2,1024,512]{2,1,0:T(8,128)(2,1)} custom-call(bf16[2,128,1024]{2,1,0:T(8,128)(2,1)S(1)} %get-tuple-element.80.cross0, bf16[2,128,512]{2,1,0:T(8,128)(2,1)S(1)} %get-tuple-element.81.pre0, bf16[2,128,1024]{2,1,0:T(8,128)(2,1)S(1)} %get-tuple-element.82.cross1, bf16[2,128,512]{2,1,0:T(8,128)(2,1)S(1)} %get-tuple-element.83.pre1), custom_call_target="tpu_custom_call" | custom-call | flops 1500000000 | bytes 4000000 | tf_op jit(solution)/shard_map/pallas_call | solution.py:603
  59.5 1.0 %shard_map.126 = bf16[2,256,256]{2,1,0:T(8,128)(2,1)} custom-call(bf16[2,256,128]{2,1,0:T(8,128)(2,1)S(1)} %get-tuple-element.76.gram0, bf16[2,128,256]{2,1,0:T(8,128)(2,1)S(1)} %get-tuple-element.77.rows0, bf16[2,256,128]{2,1,0:T(8,128)(2,1)S(1)} %get-tuple-element.78.gram1, bf16[2,128,256]{2,1,0:T(8,128)(2,1)S(1)} %get-tuple-element.79.rows1), custom_call_target="tpu_custom_call" | custom-call | flops 300000000 | bytes 2000000 | tf_op jit(solution)/shard_map/pallas_call | solution.py:622
  60.5 1.7 %collective-permute-done.21.far_outs = bf16[128,256]{1,0:T(8,128)(2,1)S(1)} collective-permute-done((bf16[128,256]{1,0:T(8,128)(2,1)S(1)}, bf16[128,256]{1,0:T(8,128)(2,1)S(1)}, u32[]{:S(2)}, u32[]{:S(2)}) %collective-permute-start.21) | collective-permute-done | bytes 65568 | tf_op jit(solution)/shard_map/ppermute | solution.py:465
  62.3 1.0 %shard_map.125 = (bf16[128,256]{1,0:T(8,128)(2,1)}, bf16[128,256]{1,0:T(8,128)(2,1)}) custom-call(bf16[128,2176]{1,0:T(8,128)(2,1)S(1)} %get-tuple-element.47.refs_0_.own, bf16[288,256]{1,0:T(8,128)(2,1)S(1)} %get-tuple-element.60.g0, bf16[288,256]{1,0:T(8,128)(2,1)S(1)} %collective-permute-done.14.after.g1, ...), custom_call_target="tpu_custom_call" | custom-call | flops 100000000 | bytes 1000000 | tf_op jit(solution)/shard_map/pallas_call | solution.py:625
  (44 shorter events, 8.2 us)
Async XLA Ops:
  2.9 15.8 %collective-permute-start = (bf16[64,2176]{1,0:T(8,128)(2,1)}, bf16[64,2176]{1,0:T(8,128)(2,1)S(1)}, u32[]{:S(2)}, u32[]{:S(2)}) collective-permute-start(bf16[64,2176]{1,0:T(8,128)(2,1)} %get-tuple-element.49), channel_id=1, source_target_pairs={{0,4},{4,0},{8,12},{12,8},{1,5},{5,1},{9,13},{13,9},{2,6},{6,2},{1... | collective-permute-start | bytes 835592 | tf_op jit(solution)/shard_map/ppermute | solution.py:465
  6.0 15.3 %collective-permute-start.4 = (bf16[64,2176]{1,0:T(8,128)(2,1)}, bf16[64,2176]{1,0:T(8,128)(2,1)S(1)}, u32[]{:S(2)}, u32[]{:S(2)}) collective-permute-start(bf16[64,2176]{1,0:T(8,128)(2,1)} %get-tuple-element.49), channel_id=1, source_target_pairs={{0,8},{4,12},{8,0},{12,4},{1,9},{5,13},{9,1},{13,5},{2,10},{6,14},... | collective-permute-start | bytes 835592 | tf_op jit(solution)/shard_map/ppermute | solution.py:465
  8.6 1.1 %copy-start = (bf16[128,2176]{1,0:T(8,128)(2,1)S(1)}, bf16[128,2176]{1,0:T(8,128)(2,1)}, u32[]{:S(2)}) copy-start(bf16[128,2176]{1,0:T(8,128)(2,1)} %get-tuple-element.45.own) | copy-start | bytes 1671172
  10.7 8.6 %collective-permute-start.3 = (bf16[2,256,256]{2,1,0:T(8,128)(2,1)S(1)}, bf16[2,256,256]{2,1,0:T(8,128)(2,1)S(1)}, u32[]{:S(2)}, u32[]{:S(2)}) collective-permute-start(bf16[2,256,256]{2,1,0:T(8,128)(2,1)S(1)} %get-tuple-element.48.refs_1_), channel_id=1, source_target_pairs={{0,2},{1,3},{2,0},{3,1},{4,6},{5,7},{6,4},{7,5},{8,10},{9,11},{10,... | collective-permute-start | bytes 786440 | tf_op jit(solution)/shard_map/ppermute | solution.py:465
  18.7 4.2 %collective-permute-start.1 = (bf16[64,2176]{1,0:T(8,128)(2,1)S(1)}, bf16[64,2176]{1,0:T(8,128)(2,1)S(1)}, u32[]{:S(2)}, u32[]{:S(2)}) collective-permute-start(bf16[64,2176]{1,0:T(8,128)(2,1)S(1)} %collective-permute-done.refs_2_), channel_id=1, source_target_pairs={{0,1},{1,0},{2,3},{3,2},{4,5},{5,4},{6,7},{7,6},{8,9},{9,8},{10,11... | collective-permute-start | bytes 835592 | tf_op jit(solution)/shard_map/ppermute | solution.py:465
  18.7 3.2 %collective-permute-start.2 = (bf16[2,256,256]{2,1,0:T(8,128)(2,1)S(1)}, bf16[2,256,256]{2,1,0:T(8,128)(2,1)S(1)}, u32[]{:S(2)}, u32[]{:S(2)}) collective-permute-start(bf16[2,256,256]{2,1,0:T(8,128)(2,1)S(1)} %get-tuple-element.48.refs_1_), channel_id=1, source_target_pairs={{0,1},{1,0},{2,3},{3,2},{4,5},{5,4},{6,7},{7,6},{8,9},{9,8},{10,11... | collective-permute-start | bytes 786440 | tf_op jit(solution)/shard_map/ppermute | solution.py:465
  21.3 1.6 %collective-permute-start.5 = (bf16[2,256,256]{2,1,0:T(8,128)(2,1)S(1)}, bf16[2,256,256]{2,1,0:T(8,128)(2,1)S(1)}, u32[]{:S(2)}, u32[]{:S(2)}) collective-permute-start(bf16[2,256,256]{2,1,0:T(8,128)(2,1)S(1)} %shard_map.112.refs_5_), channel_id=1, source_target_pairs={{0,1},{1,0},{2,3},{3,2},{4,5},{5,4},{6,7},{7,6},{8,9},{9,8},{10,11... | collective-permute-start | bytes 786440 | tf_op jit(solution)/shard_map/ppermute | solution.py:465
  21.4 9.1 %collective-permute-start.10 = (bf16[64,2176]{1,0:T(8,128)(2,1)S(1)}, bf16[64,2176]{1,0:T(8,128)(2,1)S(1)}, u32[]{:S(2)}, u32[]{:S(2)}) collective-permute-start(bf16[64,2176]{1,0:T(8,128)(2,1)S(1)} %collective-permute-done.4.after.a), channel_id=1, source_target_pairs={{0,4},{4,0},{8,12},{12,8},{1,5},{5,1},{9,13},{13,9},{2,6},{6,2},{1... | collective-permute-start | bytes 835592 | tf_op jit(solution)/shard_map/ppermute | solution.py:465
  29.9 4.7 %copy-start.2 = (bf16[2,256,1024]{2,1,0:T(8,128)(2,1)S(1)}, bf16[2,256,1024]{2,1,0:T(8,128)(2,1)}, u32[]{:S(2)}) copy-start(bf16[2,256,1024]{2,1,0:T(8,128)(2,1)} %get-tuple-element.56.refs_2_) | copy-start | bytes 3145732
  30.5 4.1 %collective-permute-start.11 = (bf16[128,2176]{1,0:T(8,128)(2,1)S(1)}, bf16[128,2176]{1,0:T(8,128)(2,1)S(1)}, u32[]{:S(2)}, u32[]{:S(2)}) collective-permute-start(bf16[128,2176]{1,0:T(8,128)(2,1)S(1)} %shard_map.115.refs_0_), channel_id=1, source_target_pairs={{0,1},{1,0},{2,3},{3,2},{4,5},{5,4},{6,7},{7,6},{8,9},{9,8},{10,11... | collective-permute-start | bytes 1671176 | tf_op jit(solution)/shard_map/ppermute | solution.py:465
  30.6 2.4 %collective-permute-start.7 = (bf16[320,256]{1,0:T(8,128)(2,1)S(1)}, bf16[320,256]{1,0:T(8,128)(2,1)S(1)}, u32[]{:S(2)}, u32[]{:S(2)}) collective-permute-start(bf16[320,256]{1,0:T(8,128)(2,1)S(1)} %get-tuple-element.52), channel_id=1, source_target_pairs={{0,1},{1,0},{2,3},{3,2},{4,5},{5,4},{6,7},{7,6},{8,9},{9,8},{10,11... | collective-permute-start | bytes 491528 | tf_op jit(solution)/shard_map/ppermute | solution.py:465
  31.1 1.9 %collective-permute-start.8 = (bf16[256,256]{1,0:T(8,128)(2,1)S(1)}, bf16[256,256]{1,0:T(8,128)(2,1)S(1)}, u32[]{:S(2)}, u32[]{:S(2)}) collective-permute-start(bf16[256,256]{1,0:T(8,128)(2,1)S(1)} %get-tuple-element.53), channel_id=1, source_target_pairs={{0,1},{1,0},{2,3},{3,2},{4,5},{5,4},{6,7},{7,6},{8,9},{9,8},{10,11... | collective-permute-start | bytes 393224 | tf_op jit(solution)/shard_map/ppermute | solution.py:465
  31.2 12.7 %collective-permute-start.6 = (bf16[576,256]{1,0:T(8,128)(2,1)S(1)}, bf16[576,256]{1,0:T(8,128)(2,1)S(1)}, u32[]{:S(2)}, u32[]{:S(2)}) collective-permute-start(bf16[576,256]{1,0:T(8,128)(2,1)S(1)} %get-tuple-element.51), channel_id=1, source_target_pairs={{0,1},{1,0},{2,3},{3,2},{4,5},{5,4},{6,7},{7,6},{8,9},{9,8},{10,11... | collective-permute-start | bytes 884744 | tf_op jit(solution)/shard_map/ppermute | solution.py:465
  33.0 9.2 %collective-permute-start.9 = (bf16[576,256]{1,0:T(8,128)(2,1)S(1)}, bf16[576,256]{1,0:T(8,128)(2,1)S(1)}, u32[]{:S(2)}, u32[]{:S(2)}) collective-permute-start(bf16[576,256]{1,0:T(8,128)(2,1)S(1)} %shard_map.114), channel_id=1, source_target_pairs={{0,2},{1,3},{2,0},{3,1},{4,6},{5,7},{6,4},{7,5},{8,10},{9,11},{10,... | collective-permute-start | bytes 884744 | tf_op jit(solution)/shard_map/ppermute | solution.py:465
  40.1 1.5 %collective-permute-start.13 = (bf16[320,256]{1,0:T(8,128)(2,1)S(1)}, bf16[320,256]{1,0:T(8,128)(2,1)S(1)}, u32[]{:S(2)}, u32[]{:S(2)}) collective-permute-start(bf16[320,256]{1,0:T(8,128)(2,1)S(1)} %get-tuple-element.59), channel_id=1, source_target_pairs={{0,1},{1,0},{2,3},{3,2},{4,5},{5,4},{6,7},{7,6},{8,9},{9,8},{10,11... | collective-permute-start | bytes 491528 | tf_op jit(solution)/shard_map/ppermute | solution.py:465
  40.2 6.6 %collective-permute-start.15 = (bf16[576,256]{1,0:T(8,128)(2,1)S(1)}, bf16[576,256]{1,0:T(8,128)(2,1)S(1)}, u32[]{:S(2)}, u32[]{:S(2)}) collective-permute-start(bf16[576,256]{1,0:T(8,128)(2,1)S(1)} %get-tuple-element.62), channel_id=1, source_target_pairs={{0,1},{1,0},{2,3},{3,2},{4,5},{5,4},{6,7},{7,6},{8,9},{9,8},{10,11... | collective-permute-start | bytes 884744 | tf_op jit(solution)/shard_map/ppermute | solution.py:465
  40.7 1.5 %collective-permute-start.12 = (bf16[256,256]{1,0:T(8,128)(2,1)S(1)}, bf16[256,256]{1,0:T(8,128)(2,1)S(1)}, u32[]{:S(2)}, u32[]{:S(2)}) collective-permute-start(bf16[256,256]{1,0:T(8,128)(2,1)S(1)} %get-tuple-element.58), channel_id=1, source_target_pairs={{0,1},{1,0},{2,3},{3,2},{4,5},{5,4},{6,7},{7,6},{8,9},{9,8},{10,11... | collective-permute-start | bytes 393224 | tf_op jit(solution)/shard_map/ppermute | solution.py:465
  41.6 7.1 %collective-permute-start.16 = (bf16[320,256]{1,0:T(8,128)(2,1)S(1)}, bf16[320,256]{1,0:T(8,128)(2,1)S(1)}, u32[]{:S(2)}, u32[]{:S(2)}) collective-permute-start(bf16[320,256]{1,0:T(8,128)(2,1)S(1)} %shard_map.117.after), channel_id=1, source_target_pairs={{0,2},{1,3},{2,0},{3,1},{4,6},{5,7},{6,4},{7,5},{8,10},{9,11},{10,... | collective-permute-start | bytes 491528 | tf_op jit(solution)/shard_map/ppermute | solution.py:465
  42.3 8.5 %collective-permute-start.19 = (bf16[256,256]{1,0:T(8,128)(2,1)S(1)}, bf16[256,256]{1,0:T(8,128)(2,1)S(1)}, u32[]{:S(2)}, u32[]{:S(2)}) collective-permute-start(bf16[256,256]{1,0:T(8,128)(2,1)S(1)} %shard_map.118.after), channel_id=1, source_target_pairs={{0,2},{1,3},{2,0},{3,1},{4,6},{5,7},{6,4},{7,5},{8,10},{9,11},{10,... | collective-permute-start | bytes 393224 | tf_op jit(solution)/shard_map/ppermute | solution.py:465
  44.2 6.5 %collective-permute-start.14 = (bf16[288,256]{1,0:T(8,128)(2,1)S(1)}, bf16[288,256]{1,0:T(8,128)(2,1)S(1)}, u32[]{:S(2)}, u32[]{:S(2)}) collective-permute-start(bf16[288,256]{1,0:T(8,128)(2,1)S(1)} %get-tuple-element.61), channel_id=1, source_target_pairs={{0,4},{4,0},{8,12},{12,8},{1,5},{5,1},{9,13},{13,9},{2,6},{6,2},{1... | collective-permute-start | bytes 442376 | tf_op jit(solution)/shard_map/ppermute | solution.py:465
  49.0 5.1 %collective-permute-start.17 = (bf16[160,256]{1,0:T(8,128)(2,1)S(1)}, bf16[160,256]{1,0:T(8,128)(2,1)S(1)}, u32[]{:S(2)}, u32[]{:S(2)}) collective-permute-start(bf16[160,256]{1,0:T(8,128)(2,1)S(1)} %get-tuple-element.70), channel_id=1, source_target_pairs={{0,4},{4,0},{8,12},{12,8},{1,5},{5,1},{9,13},{13,9},{2,6},{6,2},{1... | collective-permute-start | bytes 245768 | tf_op jit(solution)/shard_map/ppermute | solution.py:465
  51.1 5.0 %collective-permute-start.20 = (bf16[128,256]{1,0:T(8,128)(2,1)S(1)}, bf16[128,256]{1,0:T(8,128)(2,1)S(1)}, u32[]{:S(2)}, u32[]{:S(2)}) collective-permute-start(bf16[128,256]{1,0:T(8,128)(2,1)S(1)} %get-tuple-element.73), channel_id=1, source_target_pairs={{0,4},{4,0},{8,12},{12,8},{1,5},{5,1},{9,13},{13,9},{2,6},{6,2},{1... | collective-permute-start | bytes 196616 | tf_op jit(solution)/shard_map/ppermute | solution.py:465
  54.1 8.1 %collective-permute-start.18 = (bf16[160,256]{1,0:T(8,128)(2,1)S(1)}, bf16[160,256]{1,0:T(8,128)(2,1)S(1)}, u32[]{:S(2)}, u32[]{:S(2)}) collective-permute-start(bf16[160,256]{1,0:T(8,128)(2,1)S(1)} %shard_map.122.rest_0_), channel_id=1, source_target_pairs={{0,8},{4,12},{8,0},{12,4},{1,9},{5,13},{9,1},{13,5},{2,10},{6,14},... | collective-permute-start | bytes 245768 | tf_op jit(solution)/shard_map/ppermute | solution.py:465
  56.1 6.2 %collective-permute-start.21 = (bf16[128,256]{1,0:T(8,128)(2,1)S(1)}, bf16[128,256]{1,0:T(8,128)(2,1)S(1)}, u32[]{:S(2)}, u32[]{:S(2)}) collective-permute-start(bf16[128,256]{1,0:T(8,128)(2,1)S(1)} %shard_map.124), channel_id=1, source_target_pairs={{0,8},{4,12},{8,0},{12,4},{1,9},{5,13},{9,1},{13,5},{2,10},{6,14},... | collective-permute-start | bytes 196616 | tf_op jit(solution)/shard_map/ppermute | solution.py:465
  (1 other events, 0.9 us)

commit v10 on v8

--- a/solution.py
+++ b/solution.py
@@ -184,7 +184,7 @@
     return copies
 
 
-def payload_kernel(x, c, gates_in, routes_in, pair_in, out_o, own_o, pair_o, gates, routes, sems):
+def payload_kernel(x, c, gates_in, routes_in, out_o, meta_o, gates, routes, sems):
     core = lax.rem(lax.axis_index("tensor"), 2)
     mine = pl.ds(pl.multiple_of(core * HALF, HALF), HALF)
     copies = load(
@@ -193,9 +193,6 @@
             (routes_in, routes),
             (x.at[mine, :], out_o.at[:, 0:WIDTH]),
             (c.at[mine, :], out_o.at[:, WIDTH : 2 * WIDTH]),
-            (x, own_o.at[:, 0:WIDTH]),
-            (c, own_o.at[:, WIDTH : 2 * WIDTH]),
-            (pair_in, pair_o),
         ],
         sems,
     )
@@ -207,7 +204,7 @@
         [routes[...].astype(F32), high, low, jnp.zeros((122, 128), F32)], axis=0
     )
     columns = meta.T
-    own_o[:, 2 * WIDTH :] = columns.astype(BF16)
+    meta_o[...] = columns.astype(BF16)
     out_o[:, 2 * WIDTH :] = jnp.where(core == 0, columns[0:HALF], columns[HALF:]).astype(BF16)
     for copy in copies[2:]:
         copy.wait()
@@ -217,8 +214,10 @@
     out_o[...] = value[...]
 
 
-def stage_kernel(own, pair, own_o, pair_o):
-    own_o[...] = own[...]
+def stage_kernel(x, c, meta, pair, own_o, pair_o):
+    own_o[:, 0:WIDTH] = x[...]
+    own_o[:, WIDTH : 2 * WIDTH] = c[...]
+    own_o[:, 2 * WIDTH :] = meta[...]
     pair_o[...] = pair[...]
 
 
@@ -332,32 +331,38 @@
     return jnp.concatenate([rows[0:2], rows[2:4] + rows[4:6]], axis=0)
 
 
+def place_pairs(pair, pieces):
+    j = lax.axis_index("tensor")
+    for k, piece in enumerate(pieces):
+        cols = pl.ds(pl.multiple_of((j ^ k) * 256, 256), 256)
+        for e in range(2):
+            pair[e, :, cols] = piece[e]
+
+
 def own_chunk_kernel(*refs):
-    own, p0, near, far, p1, p2, p3, up_in, down_in = refs[:9]
-    outs, pair_o = refs[9:20], refs[20]
-    whole, info, up, down, sems = refs[21:26]
-    j = lax.axis_index("tensor")
+    own, near, far, p0, p1, p2, p3, up_in, down_in = refs[:9]
+    outs = refs[9:20]
+    whole, info, pair, up, down, sems = refs[20:26]
+    core = lax.rem(lax.axis_index("tensor"), 2)
     copies = load([(up_in, up), (down_in, down)], sems)
     whole[0:128, :] = own[:, 0 : 2 * WIDTH]
     info[0:128, :] = own[:, 2 * WIDTH :]
-    place_rows(whole, info, 1, lax.rem(j, 2), near, far)
-    for k, piece in enumerate((p0, p1, p2, p3)):
-        cols = pl.ds(pl.multiple_of((j ^ k) * 256, 256), 256)
-        for e in range(2):
-            pair_o[e, :, cols] = piece[e]
-    towers(read_meta(info), whole, up, down, copies, pair_o, outs, refs[26:])
+    place_rows(whole, info, 1, core, near, far)
+    place_pairs(pair, (p0, p1, p2, p3))
+    towers(read_meta(info), whole, up, down, copies, pair, outs, refs[26:])
 
 
 def far_chunk_kernel(*refs):
-    near, far, pair, up_in, down_in = refs[:5]
-    outs = refs[5:16]
-    whole, info, up, down, sems = refs[16:21]
+    near, far, p0, p1, p2, p3, up_in, down_in = refs[:8]
+    outs = refs[8:19]
+    whole, info, pair, up, down, sems = refs[19:25]
     core = lax.rem(lax.axis_index("tensor"), 2)
     copies = load([(up_in, up), (down_in, down)], sems)
     for r in range(2):
         rows = slice(r * HALF, r * HALF + HALF)
         place_rows(whole, info, r, core, near.at[rows, :], far.at[rows, :])
-    towers(read_meta(info), whole, up, down, copies, pair, outs, refs[21:])
+    place_pairs(pair, (p0, p1, p2, p3))
+    towers(read_meta(info), whole, up, down, copies, pair, outs, refs[25:])
 
 
 def weights_kernel(act0, grad0, cross0, pre0, act1, grad1, cross1, pre1, down_o, up_o, done_o):
@@ -510,51 +515,46 @@
 def gathered_body(inputs, cotangent, gate_values, routes, pair_weight, up_weight, down_weight):
     gates, choices = gate_values.T, routes.T
     width = 2 * WIDTH + 128
-    payload, own, pair_own = kernel_call(
+    payload, meta = kernel_call(
         payload_kernel,
-        (
-            shape((HALF, width)),
-            shape((2 * HALF, width)),
-            shape((2, 256, 256)),
-        ),
-        "hhhhh",
+        (shape((HALF, width)), shape((2 * HALF, 128))),
+        "hhhh",
         scratch=[
             pltpu.VMEM((2, 128), F32),
             pltpu.VMEM((2, 128), jnp.int32),
-            pltpu.SemaphoreType.DMA((7,)),
+            pltpu.SemaphoreType.DMA((4,)),
         ],
         vmem=60,
-    )(inputs, cotangent, gates, choices, pair_weight)
+    )(inputs, cotangent, gates, choices)
     got = [swap(payload, "expert", 1), swap(payload, "expert", 2)]
     got.append(swap(got[1], "expert", 1))
     both = shape((2, 256, 256))
     own, pair_own = kernel_call(
-        stage_kernel, (shape((2 * HALF, width)), both), "vv"
-    )(own, pair_own)
+        stage_kernel, (shape((2 * HALF, width)), both), "vvvv"
+    )(inputs, cotangent, meta, pair_weight)
     pair_x = swap(pair_own, "tensor", 2)
     pair_x = kernel_call(after_kernel, both, "va", flops=30_000_000)(pair_x, got[1])
     pair_c = swap(pair_own, "tensor", 1)
     pair_d = swap(pair_x, "tensor", 1)
-    near = kernel_call(after_kernel, shape((HALF, width)), "va")(got[0], got[1])
-    near_other = swap(near, "tensor", 1)
+    near_other = swap(got[0], "tensor", 1)
+    pairs = (pair_own, pair_c, pair_x, pair_d)
+    chunk_spaces = [
+        pltpu.VMEM((256, 2048), BF16),
+        pltpu.VMEM((256, 128), BF16),
+        pltpu.VMEM((2, 256, 1024), BF16),
+        *weight_scratch(),
+        pltpu.SemaphoreType.DMA((2,)),
+        *chunk_scratch(),
+    ]
     chunk = kernel_call(
         own_chunk_kernel,
-        chunk_outs() + (shape((2, 256, 1024)),),
+        chunk_outs(),
         "vvvvvvvhh",
-        scratch=[
-            pltpu.VMEM((256, 2048), BF16),
-            pltpu.VMEM((256, 128), BF16),
-        ]
-        + weight_scratch()
-        + [pltpu.SemaphoreType.DMA((2,))]
-        + chunk_scratch(),
+        scratch=chunk_spaces,
         flops=4_000_000_000,
         nbytes=10_000_000,
-    )(
-        own, pair_own, got[0], near_other,
-        pair_c, pair_x, pair_d, up_weight, down_weight,
-    )
-    keep, here, away, last, cross, act, grad, pre, gram, pick, gate, pair_all = chunk
+    )(own, got[0], near_other, *pairs, up_weight, down_weight)
+    keep, here, away, last, cross, act, grad, pre, gram, pick, gate = chunk
     away = kernel_call(away_kernel, shape((576, 256)), "vvv")(
         keep, swap(away, "tensor", 1), swap(last, "tensor", 1)
     )
@@ -567,14 +567,11 @@
     chunk = kernel_call(
         far_chunk_kernel,
         chunk_outs(),
-        "vvvhh",
-        scratch=[pltpu.VMEM((256, 2048), BF16), pltpu.VMEM((256, 128), BF16)]
-        + weight_scratch()
-        + [pltpu.SemaphoreType.DMA((2,))]
-        + chunk_scratch(),
+        "vvvvvvhh",
+        scratch=chunk_spaces,
         flops=4_000_000_000,
         nbytes=10_000_000,
-    )(far_mine, far_other, pair_all, up_weight, down_weight)
+    )(far_mine, far_other, *pairs, up_weight, down_weight)
     fkeep, fhere, faway, flast, fcross, fact, fgrad, fpre, fgram, fpick, fgate = chunk
     fother = swap(fhere, "tensor", 1)
     fgrads = kernel_call(away_grads_kernel, shape((320, 256)), "vv")(

time: 62.8 us -> 64.8 us (1.032)
  starting transfers between devices: 23.4 us -> 18.7 us
  waiting for transfers between devices: 15.3 us -> 19.2 us
  local copies, waits for them, and re-layouts: 2.01 us -> 3.61 us
  Pallas kernels: 21 us -> 22.2 us
    ppermute x22, starting transfers between devices: 23.4 us -> 18.7 us  [swap(): return lax.ppermute(value, axis, [(i, i ^ mask) for i in range(size)])]
    ppermute x22, waiting for transfers between devices: 15.3 us -> 19.2 us  [swap(): return lax.ppermute(value, axis, [(i, i ^ mask) for i in range(size)])]
    unnamed x6 -> x8, local copies, waits for them, and re-layouts: 2.01 us -> 3.61 us
    pallas_call x5 -> x4, Pallas kernels: 14.9 us -> 16 us  [the longest x1 7.17 us: gathered_body(): kernel_call(far_chunk_kernel, chunk_outs(), 'vvvvvvhh', scratch=chunk_spa...]
  transfers between devices with their start and end apart: 22 -> 22, of which waited for: 9 -> 12; matrix products, arithmetic and copies ran while one was open for 0% -> 0% of each run, Pallas kernels for 28% -> 30%
where the time goes in v10:
time: 64.8 us; the launch traced here: 64.4 us
  Pallas kernels  22.2 us (34%)
  waiting for transfers between devices  19.2 us (30%)
  starting transfers between devices  18.7 us (29%)
  local copies, waits for them, and re-layouts  3.61 us (6%)
  between operations  0.76 us (1%)
    ppermute x22, waiting for transfers between devices, swap(): return lax.ppermute(value, axis, [(i, i ^ mask) for i in range(size)])  19.2 us
    ppermute x22, starting transfers between devices, swap(): return lax.ppermute(value, axis, [(i, i ^ mask) for i in range(size)])  18.7 us
    pallas_call x1, Pallas kernels, gathered_body(): kernel_call(far_chunk_kernel, chunk_outs(), 'vvvvvvhh', scratch=chunk_spa...  7.17 us
    pallas_call x1, Pallas kernels, gathered_body(): kernel_call(own_chunk_kernel, chunk_outs(), 'vvvvvvvhh', scratch=chunk_sp...  7.03 us
    unnamed x8, local copies, waits for them, and re-layouts  3.61 us
    pallas_call x1, Pallas kernels, gathered_body(): kernel_call(weights_kernel, (shape((2, 512, 1024)), shape((2, 1024, 512))...  3.02 us
    pallas_call x1, Pallas kernels, gathered_body(): kernel_call(payload_kernel, (shape((HALF, width)), shape((2 * HALF, 128))...  1.75 us
  transfers between devices with their start and end apart: 22, of which 12 were waited for; matrix products, arithmetic and copies ran while one was open for 0% of the time, Pallas kernels for 30%

profile of v10, /device:TPU:0, one launch (start us, length us, event | category | flops | bytes accessed | tf_op | source)
XLA Modules:
  0.0 64.4 jit_solution(14282318520383449345)
XLA Ops:
  0.6 1.7 %shard_map.110 = (bf16[64,2176]{1,0:T(8,128)(2,1)}, bf16[128,128]{1,0:T(8,128)(2,1)}) custom-call(bf16[128,1024]{1,0:T(8,128)(2,1)} %x.3, bf16[128,1024]{1,0:T(8,128)(2,1)} %c.3, f32[2,128]{1,0:T(2,128)} %bitcast.2, s32[2,128]{1,0:T(2,128)} %bitcast.3), custom_call_target="tpu_custom_call" | custom-call | tf_op jit(solution)/shard_map/pallas_call | solution.py:518
  2.4 3.1 %collective-permute-start = (bf16[64,2176]{1,0:T(8,128)(2,1)}, bf16[64,2176]{1,0:T(8,128)(2,1)S(1)}, u32[]{:S(2)}, u32[]{:S(2)}) collective-permute-start(bf16[64,2176]{1,0:T(8,128)(2,1)} %get-tuple-element.46), channel_id=1, source_target_pairs={{0,4},{4,0},{8,12},{12,8},{1,5},{5,1},{9,13},{13,9},{2,6},{6,2},{1... | collective-permute-start | bytes 835592 | tf_op jit(solution)/shard_map/ppermute | solution.py:466
  5.5 2.6 %collective-permute-start.4 = (bf16[64,2176]{1,0:T(8,128)(2,1)}, bf16[64,2176]{1,0:T(8,128)(2,1)S(1)}, u32[]{:S(2)}, u32[]{:S(2)}) collective-permute-start(bf16[64,2176]{1,0:T(8,128)(2,1)} %get-tuple-element.46), channel_id=1, source_target_pairs={{0,8},{4,12},{8,0},{12,4},{1,9},{5,13},{9,1},{13,5},{2,10},{6,14},... | collective-permute-start | bytes 835592 | tf_op jit(solution)/shard_map/ppermute | solution.py:466
  8.1 0.9 %copy-done = bf16[128,1024]{1,0:T(8,128)(2,1)S(1)} copy-done((bf16[128,1024]{1,0:T(8,128)(2,1)S(1)}, bf16[128,1024]{1,0:T(8,128)(2,1)}, u32[]{:S(2)}) %copy-start) | copy-done | bytes 262168
  9.0 0.9 %copy-done.1 = bf16[128,1024]{1,0:T(8,128)(2,1)S(1)} copy-done((bf16[128,1024]{1,0:T(8,128)(2,1)S(1)}, bf16[128,1024]{1,0:T(8,128)(2,1)}, u32[]{:S(2)}) %copy-start.1) | copy-done | bytes 262168
  10.0 0.9 %copy-done.2 = bf16[2,256,256]{2,1,0:T(8,128)(2,1)S(1)} copy-done((bf16[2,256,256]{2,1,0:T(8,128)(2,1)S(1)}, bf16[2,256,256]{2,1,0:T(8,128)(2,1)}, u32[]{:S(2)}) %copy-start.2) | copy-done | bytes 262168
  11.7 1.6 %collective-permute-start.3 = (bf16[2,256,256]{2,1,0:T(8,128)(2,1)S(1)}, bf16[2,256,256]{2,1,0:T(8,128)(2,1)S(1)}, u32[]{:S(2)}, u32[]{:S(2)}) collective-permute-start(bf16[2,256,256]{2,1,0:T(8,128)(2,1)S(1)} %get-tuple-element.47.refs_3_.refs_2_), channel_id=1, source_target_pairs={{0,2},{1,3},{2,0},{3,1},{4,6},{5,7},{6,4},{7,5},{8,10},{9,11},{10,... | collective-permute-start | bytes 786440 | tf_op jit(solution)/shard_map/ppermute | solution.py:466
  13.3 4.9 %collective-permute-done.refs_1_ = bf16[64,2176]{1,0:T(8,128)(2,1)S(1)} collective-permute-done((bf16[64,2176]{1,0:T(8,128)(2,1)}, bf16[64,2176]{1,0:T(8,128)(2,1)S(1)}, u32[]{:S(2)}, u32[]{:S(2)}) %collective-permute-start) | collective-permute-done | bytes 278560 | tf_op jit(solution)/shard_map/ppermute | solution.py:466
  19.3 1.4 %collective-permute-done.4.after.a = bf16[64,2176]{1,0:T(8,128)(2,1)S(1)} collective-permute-done((bf16[64,2176]{1,0:T(8,128)(2,1)}, bf16[64,2176]{1,0:T(8,128)(2,1)S(1)}, u32[]{:S(2)}, u32[]{:S(2)}) %collective-permute-start.4) | collective-permute-done | bytes 278560 | tf_op jit(solution)/shard_map/ppermute | solution.py:466
  21.3 1.0 %collective-permute-done.5.refs_6_.refs_5_ = bf16[2,256,256]{2,1,0:T(8,128)(2,1)S(1)} collective-permute-done((bf16[2,256,256]{2,1,0:T(8,128)(2,1)S(1)}, bf16[2,256,256]{2,1,0:T(8,128)(2,1)S(1)}, u32[]{:S(2)}, u32[]{:S(2)}) %collective-permute-start.5) | collective-permute-done | bytes 262176 | tf_op jit(solution)/shard_map/ppermute | solution.py:466
  22.4 7.0 %shard_map.113 = (bf16[2,576,256]{2,1,0:T(8,128)(2,1)S(1)}, bf16[576,256]{1,0:T(8,128)(2,1)S(1)}, bf16[320,256]{1,0:T(8,128)(2,1)S(1)}, bf16[256,256]{1,0:T(8,12...) custom-call(bf16[128,2176]{1,0:T(8,128)(2,1)S(1)} %get-tuple-element, ...), custom_call_target="tpu_custom_call" | custom-call | flops 4000000000 | bytes 10000000 | tf_op jit(solution)/shard_map/pallas_call | solution.py:549
  31.0 1.4 %collective-permute-done.8.high = bf16[256,256]{1,0:T(8,128)(2,1)S(1)} collective-permute-done((bf16[256,256]{1,0:T(8,128)(2,1)S(1)}, bf16[256,256]{1,0:T(8,128)(2,1)S(1)}, u32[]{:S(2)}, u32[]{:S(2)}) %collective-permute-start.8) | collective-permute-done | bytes 131104 | tf_op jit(solution)/shard_map/ppermute | solution.py:466
  32.5 1.6 %collective-permute-start.9 = (bf16[576,256]{1,0:T(8,128)(2,1)S(1)}, bf16[576,256]{1,0:T(8,128)(2,1)S(1)}, u32[]{:S(2)}, u32[]{:S(2)}) collective-permute-start(bf16[576,256]{1,0:T(8,128)(2,1)S(1)} %shard_map.114), channel_id=1, source_target_pairs={{0,2},{1,3},{2,0},{3,1},{4,6},{5,7},{6,4},{7,5},{8,10},{9,11},{10,... | collective-permute-start | bytes 884744 | tf_op jit(solution)/shard_map/ppermute | solution.py:466
  34.0 7.2 %shard_map.116 = (bf16[2,576,256]{2,1,0:T(8,128)(2,1)S(1)}, bf16[576,256]{1,0:T(8,128)(2,1)S(1)}, bf16[320,256]{1,0:T(8,128)(2,1)S(1)}, bf16[256,256]{1,0:T(8,12...) custom-call(bf16[128,2176]{1,0:T(8,128)(2,1)S(1)} %shard_map.115.ref, ...), custom_call_target="tpu_custom_call" | custom-call | flops 4000000000 | bytes 10000000 | tf_op jit(solution)/shard_map/pallas_call | solution.py:567
  43.4 1.6 %collective-permute-start.19 = (bf16[256,256]{1,0:T(8,128)(2,1)S(1)}, bf16[256,256]{1,0:T(8,128)(2,1)S(1)}, u32[]{:S(2)}, u32[]{:S(2)}) collective-permute-start(bf16[256,256]{1,0:T(8,128)(2,1)S(1)} %shard_map.118.after), channel_id=1, source_target_pairs={{0,2},{1,3},{2,0},{3,1},{4,6},{5,7},{6,4},{7,5},{8,10},{9,11},{10,... | collective-permute-start | bytes 393224 | tf_op jit(solution)/shard_map/ppermute | solution.py:466
  45.8 3.0 %shard_map.120 = (bf16[2,512,1024]{2,1,0:T(8,128)(2,1)}, bf16[2,1024,512]{2,1,0:T(8,128)(2,1)}, f32[8,128]{1,0:T(8,128)S(1)}) custom-call(bf16[2,128,512]{2,1,0:T(8,128)(2,1)S(1)} %get-tuple-element.61.act0, bf16[2,128,1024]{2,1,0:T(8,128)(2,1)S(1)} %get-tuple-element.62.grad0, bf16[2,128,1024]{2,1,0:T(8,128)(2,1)S(1)} %get-tuple-element.63.cross0, ...), custom_call_target="tpu_custom_call" | custom-call | flops 3000000000 | bytes 8000000 | tf_op jit(solution)/shard_map/pallas_call | solution.py:590
  48.8 1.0 %collective-permute-done.16.theirs = bf16[320,256]{1,0:T(8,128)(2,1)S(1)} collective-permute-done((bf16[320,256]{1,0:T(8,128)(2,1)S(1)}, bf16[320,256]{1,0:T(8,128)(2,1)S(1)}, u32[]{:S(2)}, u32[]{:S(2)}) %collective-permute-start.16) | collective-permute-done | bytes 163872 | tf_op jit(solution)/shard_map/ppermute | solution.py:466
  50.8 1.0 %collective-permute-done.19.theirs = bf16[256,256]{1,0:T(8,128)(2,1)S(1)} collective-permute-done((bf16[256,256]{1,0:T(8,128)(2,1)S(1)}, bf16[256,256]{1,0:T(8,128)(2,1)S(1)}, u32[]{:S(2)}, u32[]{:S(2)}) %collective-permute-start.19) | collective-permute-done | bytes 131104 | tf_op jit(solution)/shard_map/ppermute | solution.py:466
  52.6 2.6 %collective-permute-done.17.b = bf16[160,256]{1,0:T(8,128)(2,1)S(1)} collective-permute-done((bf16[160,256]{1,0:T(8,128)(2,1)S(1)}, bf16[160,256]{1,0:T(8,128)(2,1)S(1)}, u32[]{:S(2)}, u32[]{:S(2)}) %collective-permute-start.17) | collective-permute-done | bytes 81952 | tf_op jit(solution)/shard_map/ppermute | solution.py:466
  55.2 1.8 %collective-permute-start.18 = (bf16[160,256]{1,0:T(8,128)(2,1)S(1)}, bf16[160,256]{1,0:T(8,128)(2,1)S(1)}, u32[]{:S(2)}, u32[]{:S(2)}) collective-permute-start(bf16[160,256]{1,0:T(8,128)(2,1)S(1)} %shard_map.122), channel_id=1, source_target_pairs={{0,8},{4,12},{8,0},{12,4},{1,9},{5,13},{9,1},{13,5},{2,10},{6,14},... | collective-permute-start | bytes 245768 | tf_op jit(solution)/shard_map/ppermute | solution.py:466
  57.2 1.5 %collective-permute-start.21 = (bf16[128,256]{1,0:T(8,128)(2,1)S(1)}, bf16[128,256]{1,0:T(8,128)(2,1)S(1)}, u32[]{:S(2)}, u32[]{:S(2)}) collective-permute-start(bf16[128,256]{1,0:T(8,128)(2,1)S(1)} %shard_map.124), channel_id=1, source_target_pairs={{0,8},{4,12},{8,0},{12,4},{1,9},{5,13},{9,1},{13,5},{2,10},{6,14},... | collective-permute-start | bytes 196616 | tf_op jit(solution)/shard_map/ppermute | solution.py:466
  58.6 1.0 %shard_map.126 = bf16[2,256,256]{2,1,0:T(8,128)(2,1)} custom-call(bf16[2,256,128]{2,1,0:T(8,128)(2,1)S(1)} %get-tuple-element.77.gram0, bf16[2,128,256]{2,1,0:T(8,128)(2,1)S(1)} %get-tuple-element.78.rows0, bf16[2,256,128]{2,1,0:T(8,128)(2,1)S(1)} %get-tuple-element.79.gram1, bf16[2,128,256]{2,1,0:T(8,128)(2,1)S(1)} %get-tuple-element.80.rows1), custom_call_target="tpu_custom_call" | custom-call | flops 300000000 | bytes 2000000 | tf_op jit(solution)/shard_map/pallas_call | solution.py:609
  59.6 3.8 %collective-permute-done.21.far_outs = bf16[128,256]{1,0:T(8,128)(2,1)S(1)} collective-permute-done((bf16[128,256]{1,0:T(8,128)(2,1)S(1)}, bf16[128,256]{1,0:T(8,128)(2,1)S(1)}, u32[]{:S(2)}, u32[]{:S(2)}) %collective-permute-start.21) | collective-permute-done | bytes 65568 | tf_op jit(solution)/shard_map/ppermute | solution.py:466
  63.5 1.0 %shard_map.125 = (bf16[128,256]{1,0:T(8,128)(2,1)}, bf16[128,256]{1,0:T(8,128)(2,1)}) custom-call(bf16[128,2176]{1,0:T(8,128)(2,1)S(1)} %get-tuple-element.45.refs_0_.own, bf16[288,256]{1,0:T(8,128)(2,1)S(1)} %get-tuple-element.57.g0, bf16[288,256]{1,0:T(8,128)(2,1)S(1)} %collective-permute-done.14.after.g1, ...), custom_call_target="tpu_custom_call" | custom-call | flops 100000000 | bytes 1000000 | tf_op jit(solution)/shard_map/pallas_call | solution.py:612
  (45 shorter events, 9.2 us)
Async XLA Ops:
  2.4 15.8 %collective-permute-start = (bf16[64,2176]{1,0:T(8,128)(2,1)}, bf16[64,2176]{1,0:T(8,128)(2,1)S(1)}, u32[]{:S(2)}, u32[]{:S(2)}) collective-permute-start(bf16[64,2176]{1,0:T(8,128)(2,1)} %get-tuple-element.46), channel_id=1, source_target_pairs={{0,4},{4,0},{8,12},{12,8},{1,5},{5,1},{9,13},{13,9},{2,6},{6,2},{1... | collective-permute-start | bytes 835592 | tf_op jit(solution)/shard_map/ppermute | solution.py:466
  5.5 15.3 %collective-permute-start.4 = (bf16[64,2176]{1,0:T(8,128)(2,1)}, bf16[64,2176]{1,0:T(8,128)(2,1)S(1)}, u32[]{:S(2)}, u32[]{:S(2)}) collective-permute-start(bf16[64,2176]{1,0:T(8,128)(2,1)} %get-tuple-element.46), channel_id=1, source_target_pairs={{0,8},{4,12},{8,0},{12,4},{1,9},{5,13},{9,1},{13,5},{2,10},{6,14},... | collective-permute-start | bytes 835592 | tf_op jit(solution)/shard_map/ppermute | solution.py:466
  8.1 0.9 %copy-start = (bf16[128,1024]{1,0:T(8,128)(2,1)S(1)}, bf16[128,1024]{1,0:T(8,128)(2,1)}, u32[]{:S(2)}) copy-start(bf16[128,1024]{1,0:T(8,128)(2,1)} %x.3) | copy-start | bytes 786436
  9.0 0.9 %copy-start.1 = (bf16[128,1024]{1,0:T(8,128)(2,1)S(1)}, bf16[128,1024]{1,0:T(8,128)(2,1)}, u32[]{:S(2)}) copy-start(bf16[128,1024]{1,0:T(8,128)(2,1)} %c.3) | copy-start | bytes 786436
  11.7 7.6 %collective-permute-start.3 = (bf16[2,256,256]{2,1,0:T(8,128)(2,1)S(1)}, bf16[2,256,256]{2,1,0:T(8,128)(2,1)S(1)}, u32[]{:S(2)}, u32[]{:S(2)}) collective-permute-start(bf16[2,256,256]{2,1,0:T(8,128)(2,1)S(1)} %get-tuple-element.47.refs_3_.refs_2_), channel_id=1, source_target_pairs={{0,2},{1,3},{2,0},{3,1},{4,6},{5,7},{6,4},{7,5},{8,10},{9,11},{10,... | collective-permute-start | bytes 786440 | tf_op jit(solution)/shard_map/ppermute | solution.py:466
  18.2 4.2 %collective-permute-start.1 = (bf16[64,2176]{1,0:T(8,128)(2,1)S(1)}, bf16[64,2176]{1,0:T(8,128)(2,1)S(1)}, u32[]{:S(2)}, u32[]{:S(2)}) collective-permute-start(bf16[64,2176]{1,0:T(8,128)(2,1)S(1)} %collective-permute-done.refs_1_), channel_id=1, source_target_pairs={{0,1},{1,0},{2,3},{3,2},{4,5},{5,4},{6,7},{7,6},{8,9},{9,8},{10,11... | collective-permute-start | bytes 835592 | tf_op jit(solution)/shard_map/ppermute | solution.py:466
  18.2 3.2 %collective-permute-start.2 = (bf16[2,256,256]{2,1,0:T(8,128)(2,1)S(1)}, bf16[2,256,256]{2,1,0:T(8,128)(2,1)S(1)}, u32[]{:S(2)}, u32[]{:S(2)}) collective-permute-start(bf16[2,256,256]{2,1,0:T(8,128)(2,1)S(1)} %get-tuple-element.47.refs_3_.refs_2_), channel_id=1, source_target_pairs={{0,1},{1,0},{2,3},{3,2},{4,5},{5,4},{6,7},{7,6},{8,9},{9,8},{10,11... | collective-permute-start | bytes 786440 | tf_op jit(solution)/shard_map/ppermute | solution.py:466
  20.8 1.6 %collective-permute-start.5 = (bf16[2,256,256]{2,1,0:T(8,128)(2,1)S(1)}, bf16[2,256,256]{2,1,0:T(8,128)(2,1)S(1)}, u32[]{:S(2)}, u32[]{:S(2)}) collective-permute-start(bf16[2,256,256]{2,1,0:T(8,128)(2,1)S(1)} %shard_map.112.refs_5_.refs_4_), channel_id=1, source_target_pairs={{0,1},{1,0},{2,3},{3,2},{4,5},{5,4},{6,7},{7,6},{8,9},{9,8},{10,11... | collective-permute-start | bytes 786440 | tf_op jit(solution)/shard_map/ppermute | solution.py:466
  20.8 9.1 %collective-permute-start.10 = (bf16[64,2176]{1,0:T(8,128)(2,1)S(1)}, bf16[64,2176]{1,0:T(8,128)(2,1)S(1)}, u32[]{:S(2)}, u32[]{:S(2)}) collective-permute-start(bf16[64,2176]{1,0:T(8,128)(2,1)S(1)} %collective-permute-done.4.after.a), channel_id=1, source_target_pairs={{0,4},{4,0},{8,12},{12,8},{1,5},{5,1},{9,13},{13,9},{2,6},{6,2},{1... | collective-permute-start | bytes 835592 | tf_op jit(solution)/shard_map/ppermute | solution.py:466
  30.0 4.1 %collective-permute-start.11 = (bf16[128,2176]{1,0:T(8,128)(2,1)S(1)}, bf16[128,2176]{1,0:T(8,128)(2,1)S(1)}, u32[]{:S(2)}, u32[]{:S(2)}) collective-permute-start(bf16[128,2176]{1,0:T(8,128)(2,1)S(1)} %shard_map.115.refs_0_), channel_id=1, source_target_pairs={{0,1},{1,0},{2,3},{3,2},{4,5},{5,4},{6,7},{7,6},{8,9},{9,8},{10,11... | collective-permute-start | bytes 1671176 | tf_op jit(solution)/shard_map/ppermute | solution.py:466
  30.0 2.4 %collective-permute-start.7 = (bf16[320,256]{1,0:T(8,128)(2,1)S(1)}, bf16[320,256]{1,0:T(8,128)(2,1)S(1)}, u32[]{:S(2)}, u32[]{:S(2)}) collective-permute-start(bf16[320,256]{1,0:T(8,128)(2,1)S(1)} %get-tuple-element.50), channel_id=1, source_target_pairs={{0,1},{1,0},{2,3},{3,2},{4,5},{5,4},{6,7},{7,6},{8,9},{9,8},{10,11... | collective-permute-start | bytes 491528 | tf_op jit(solution)/shard_map/ppermute | solution.py:466
  30.5 1.9 %collective-permute-start.8 = (bf16[256,256]{1,0:T(8,128)(2,1)S(1)}, bf16[256,256]{1,0:T(8,128)(2,1)S(1)}, u32[]{:S(2)}, u32[]{:S(2)}) collective-permute-start(bf16[256,256]{1,0:T(8,128)(2,1)S(1)} %get-tuple-element.51), channel_id=1, source_target_pairs={{0,1},{1,0},{2,3},{3,2},{4,5},{5,4},{6,7},{7,6},{8,9},{9,8},{10,11... | collective-permute-start | bytes 393224 | tf_op jit(solution)/shard_map/ppermute | solution.py:466
  30.6 14.3 %collective-permute-start.6 = (bf16[576,256]{1,0:T(8,128)(2,1)S(1)}, bf16[576,256]{1,0:T(8,128)(2,1)S(1)}, u32[]{:S(2)}, u32[]{:S(2)}) collective-permute-start(bf16[576,256]{1,0:T(8,128)(2,1)S(1)} %get-tuple-element.49), channel_id=1, source_target_pairs={{0,1},{1,0},{2,3},{3,2},{4,5},{5,4},{6,7},{7,6},{8,9},{9,8},{10,11... | collective-permute-start | bytes 884744 | tf_op jit(solution)/shard_map/ppermute | solution.py:466
  32.5 10.8 %collective-permute-start.9 = (bf16[576,256]{1,0:T(8,128)(2,1)S(1)}, bf16[576,256]{1,0:T(8,128)(2,1)S(1)}, u32[]{:S(2)}, u32[]{:S(2)}) collective-permute-start(bf16[576,256]{1,0:T(8,128)(2,1)S(1)} %shard_map.114), channel_id=1, source_target_pairs={{0,2},{1,3},{2,0},{3,1},{4,6},{5,7},{6,4},{7,5},{8,10},{9,11},{10,... | collective-permute-start | bytes 884744 | tf_op jit(solution)/shard_map/ppermute | solution.py:466
  41.2 1.5 %collective-permute-start.13 = (bf16[320,256]{1,0:T(8,128)(2,1)S(1)}, bf16[320,256]{1,0:T(8,128)(2,1)S(1)}, u32[]{:S(2)}, u32[]{:S(2)}) collective-permute-start(bf16[320,256]{1,0:T(8,128)(2,1)S(1)} %get-tuple-element.56), channel_id=1, source_target_pairs={{0,1},{1,0},{2,3},{3,2},{4,5},{5,4},{6,7},{7,6},{8,9},{9,8},{10,11... | collective-permute-start | bytes 491528 | tf_op jit(solution)/shard_map/ppermute | solution.py:466
  41.3 2.0 %collective-permute-start.12 = (bf16[256,256]{1,0:T(8,128)(2,1)S(1)}, bf16[256,256]{1,0:T(8,128)(2,1)S(1)}, u32[]{:S(2)}, u32[]{:S(2)}) collective-permute-start(bf16[256,256]{1,0:T(8,128)(2,1)S(1)} %get-tuple-element.55), channel_id=1, source_target_pairs={{0,1},{1,0},{2,3},{3,2},{4,5},{5,4},{6,7},{7,6},{8,9},{9,8},{10,11... | collective-permute-start | bytes 393224 | tf_op jit(solution)/shard_map/ppermute | solution.py:466
  41.8 7.1 %collective-permute-start.15 = (bf16[576,256]{1,0:T(8,128)(2,1)S(1)}, bf16[576,256]{1,0:T(8,128)(2,1)S(1)}, u32[]{:S(2)}, u32[]{:S(2)}) collective-permute-start(bf16[576,256]{1,0:T(8,128)(2,1)S(1)} %get-tuple-element.59), channel_id=1, source_target_pairs={{0,1},{1,0},{2,3},{3,2},{4,5},{5,4},{6,7},{7,6},{8,9},{9,8},{10,11... | collective-permute-start | bytes 884744 | tf_op jit(solution)/shard_map/ppermute | solution.py:466
  42.7 7.1 %collective-permute-start.16 = (bf16[320,256]{1,0:T(8,128)(2,1)S(1)}, bf16[320,256]{1,0:T(8,128)(2,1)S(1)}, u32[]{:S(2)}, u32[]{:S(2)}) collective-permute-start(bf16[320,256]{1,0:T(8,128)(2,1)S(1)} %shard_map.117.after), channel_id=1, source_target_pairs={{0,2},{1,3},{2,0},{3,1},{4,6},{5,7},{6,4},{7,5},{8,10},{9,11},{10,... | collective-permute-start | bytes 491528 | tf_op jit(solution)/shard_map/ppermute | solution.py:466
  43.4 8.5 %collective-permute-start.19 = (bf16[256,256]{1,0:T(8,128)(2,1)S(1)}, bf16[256,256]{1,0:T(8,128)(2,1)S(1)}, u32[]{:S(2)}, u32[]{:S(2)}) collective-permute-start(bf16[256,256]{1,0:T(8,128)(2,1)S(1)} %shard_map.118.after), channel_id=1, source_target_pairs={{0,2},{1,3},{2,0},{3,1},{4,6},{5,7},{6,4},{7,5},{8,10},{9,11},{10,... | collective-permute-start | bytes 393224 | tf_op jit(solution)/shard_map/ppermute | solution.py:466
  45.3 6.5 %collective-permute-start.14 = (bf16[288,256]{1,0:T(8,128)(2,1)S(1)}, bf16[288,256]{1,0:T(8,128)(2,1)S(1)}, u32[]{:S(2)}, u32[]{:S(2)}) collective-permute-start(bf16[288,256]{1,0:T(8,128)(2,1)S(1)} %get-tuple-element.58), channel_id=1, source_target_pairs={{0,4},{4,0},{8,12},{12,8},{1,5},{5,1},{9,13},{13,9},{2,6},{6,2},{1... | collective-permute-start | bytes 442376 | tf_op jit(solution)/shard_map/ppermute | solution.py:466
  50.1 5.1 %collective-permute-start.17 = (bf16[160,256]{1,0:T(8,128)(2,1)S(1)}, bf16[160,256]{1,0:T(8,128)(2,1)S(1)}, u32[]{:S(2)}, u32[]{:S(2)}) collective-permute-start(bf16[160,256]{1,0:T(8,128)(2,1)S(1)} %get-tuple-element.71), channel_id=1, source_target_pairs={{0,4},{4,0},{8,12},{12,8},{1,5},{5,1},{9,13},{13,9},{2,6},{6,2},{1... | collective-permute-start | bytes 245768 | tf_op jit(solution)/shard_map/ppermute | solution.py:466
  52.1 5.0 %collective-permute-start.20 = (bf16[128,256]{1,0:T(8,128)(2,1)S(1)}, bf16[128,256]{1,0:T(8,128)(2,1)S(1)}, u32[]{:S(2)}, u32[]{:S(2)}) collective-permute-start(bf16[128,256]{1,0:T(8,128)(2,1)S(1)} %get-tuple-element.74), channel_id=1, source_target_pairs={{0,4},{4,0},{8,12},{12,8},{1,5},{5,1},{9,13},{13,9},{2,6},{6,2},{1... | collective-permute-start | bytes 196616 | tf_op jit(solution)/shard_map/ppermute | solution.py:466
  55.2 8.2 %collective-permute-start.18 = (bf16[160,256]{1,0:T(8,128)(2,1)S(1)}, bf16[160,256]{1,0:T(8,128)(2,1)S(1)}, u32[]{:S(2)}, u32[]{:S(2)}) collective-permute-start(bf16[160,256]{1,0:T(8,128)(2,1)S(1)} %shard_map.122), channel_id=1, source_target_pairs={{0,8},{4,12},{8,0},{12,4},{1,9},{5,13},{9,1},{13,5},{2,10},{6,14},... | collective-permute-start | bytes 245768 | tf_op jit(solution)/shard_map/ppermute | solution.py:466
  57.2 6.3 %collective-permute-start.21 = (bf16[128,256]{1,0:T(8,128)(2,1)S(1)}, bf16[128,256]{1,0:T(8,128)(2,1)S(1)}, u32[]{:S(2)}, u32[]{:S(2)}) collective-permute-start(bf16[128,256]{1,0:T(8,128)(2,1)S(1)} %shard_map.124), channel_id=1, source_target_pairs={{0,8},{4,12},{8,0},{12,4},{1,9},{5,13},{9,1},{13,5},{2,10},{6,14},... | collective-permute-start | bytes 196616 | tf_op jit(solution)/shard_map/ppermute | solution.py:466
  (2 other events, 1.7 us)

commit v11 on v8

--- a/solution.py
+++ b/solution.py
@@ -184,7 +184,7 @@
     return copies
 
 
-def payload_kernel(x, c, gates_in, routes_in, pair_in, out_o, own_o, pair_o, gates, routes, sems):
+def payload_kernel(x, c, gates_in, routes_in, out_o, meta_o, gates, routes, sems):
     core = lax.rem(lax.axis_index("tensor"), 2)
     mine = pl.ds(pl.multiple_of(core * HALF, HALF), HALF)
     copies = load(
@@ -193,9 +193,6 @@
             (routes_in, routes),
             (x.at[mine, :], out_o.at[:, 0:WIDTH]),
             (c.at[mine, :], out_o.at[:, WIDTH : 2 * WIDTH]),
-            (x, own_o.at[:, 0:WIDTH]),
-            (c, own_o.at[:, WIDTH : 2 * WIDTH]),
-            (pair_in, pair_o),
         ],
         sems,
     )
@@ -207,7 +204,7 @@
         [routes[...].astype(F32), high, low, jnp.zeros((122, 128), F32)], axis=0
     )
     columns = meta.T
-    own_o[:, 2 * WIDTH :] = columns.astype(BF16)
+    meta_o[...] = columns.astype(BF16)
     out_o[:, 2 * WIDTH :] = jnp.where(core == 0, columns[0:HALF], columns[HALF:]).astype(BF16)
     for copy in copies[2:]:
         copy.wait()
@@ -217,8 +214,10 @@
     out_o[...] = value[...]
 
 
-def stage_kernel(own, pair, own_o, pair_o):
-    own_o[...] = own[...]
+def stage_kernel(x, c, meta, pair, own_o, pair_o):
+    own_o[:, 0:WIDTH] = x[...]
+    own_o[:, WIDTH : 2 * WIDTH] = c[...]
+    own_o[:, 2 * WIDTH :] = meta[...]
     pair_o[...] = pair[...]
 
 
@@ -291,9 +290,11 @@
                 acc = acc + partial[e, pl.ds(g * 64 + q, 8, stride=8), :]
             half_gram[e, g * 8 : g * 8 + 8, :] = acc * (1.0 / DE)
         gram_o[e] = mm(spread, half_gram[e].astype(BF16)).astype(BF16)
+    for copy in ready[2:]:
+        copy.wait()
     for e in both_e:
         cross_o[e] = (rows[e] + mm(gram_o[e], pair[e], TN)).astype(BF16)
-    for copy in ready:
+    for copy in ready[:2]:
         copy.wait()
     for e in both_e:
         slope[e] = mm(grad_o[e], down[e], NT)
@@ -337,14 +338,14 @@
     outs, pair_o = refs[9:20], refs[20]
     whole, info, up, down, sems = refs[21:26]
     j = lax.axis_index("tensor")
-    copies = load([(up_in, up), (down_in, down)], sems)
+    pairs = []
+    for k, piece in enumerate((p0, p1, p2, p3)):
+        cols = pl.ds(pl.multiple_of((j ^ k) * 256, 256), 256)
+        pairs.append((piece, pair_o.at[:, :, cols]))
+    copies = load([(up_in, up), (down_in, down), *pairs], sems)
     whole[0:128, :] = own[:, 0 : 2 * WIDTH]
     info[0:128, :] = own[:, 2 * WIDTH :]
     place_rows(whole, info, 1, lax.rem(j, 2), near, far)
-    for k, piece in enumerate((p0, p1, p2, p3)):
-        cols = pl.ds(pl.multiple_of((j ^ k) * 256, 256), 256)
-        for e in range(2):
-            pair_o[e, :, cols] = piece[e]
     towers(read_meta(info), whole, up, down, copies, pair_o, outs, refs[26:])
 
 
@@ -510,33 +511,28 @@
 def gathered_body(inputs, cotangent, gate_values, routes, pair_weight, up_weight, down_weight):
     gates, choices = gate_values.T, routes.T
     width = 2 * WIDTH + 128
-    payload, own, pair_own = kernel_call(
+    payload, meta = kernel_call(
         payload_kernel,
-        (
-            shape((HALF, width)),
-            shape((2 * HALF, width)),
-            shape((2, 256, 256)),
-        ),
-        "hhhhh",
+        (shape((HALF, width)), shape((2 * HALF, 128))),
+        "hhhh",
         scratch=[
             pltpu.VMEM((2, 128), F32),
             pltpu.VMEM((2, 128), jnp.int32),
-            pltpu.SemaphoreType.DMA((7,)),
+            pltpu.SemaphoreType.DMA((4,)),
         ],
         vmem=60,
-    )(inputs, cotangent, gates, choices, pair_weight)
+    )(inputs, cotangent, gates, choices)
     got = [swap(payload, "expert", 1), swap(payload, "expert", 2)]
     got.append(swap(got[1], "expert", 1))
     both = shape((2, 256, 256))
     own, pair_own = kernel_call(
-        stage_kernel, (shape((2 * HALF, width)), both), "vv"
-    )(own, pair_own)
+        stage_kernel, (shape((2 * HALF, width)), both), "vvvv"
+    )(inputs, cotangent, meta, pair_weight)
     pair_x = swap(pair_own, "tensor", 2)
     pair_x = kernel_call(after_kernel, both, "va", flops=30_000_000)(pair_x, got[1])
     pair_c = swap(pair_own, "tensor", 1)
     pair_d = swap(pair_x, "tensor", 1)
-    near = kernel_call(after_kernel, shape((HALF, width)), "va")(got[0], got[1])
-    near_other = swap(near, "tensor", 1)
+    near_other = swap(got[0], "tensor", 1)
     chunk = kernel_call(
         own_chunk_kernel,
         chunk_outs() + (shape((2, 256, 1024)),),
@@ -546,7 +542,7 @@
             pltpu.VMEM((256, 128), BF16),
         ]
         + weight_scratch()
-        + [pltpu.SemaphoreType.DMA((2,))]
+        + [pltpu.SemaphoreType.DMA((6,))]
         + chunk_scratch(),
         flops=4_000_000_000,
         nbytes=10_000_000,
@@ -561,7 +557,7 @@
     theirs = swap(away, "tensor", 2)
     other = swap(here, "tensor", 1)
     far_mine = kernel_call(join_kernel, shape((2 * HALF, 2 * WIDTH + 128)), "vva")(
-        got[1], got[2], gate
+        got[1], got[2], away
     )
     far_other = swap(far_mine, "tensor", 1)
     chunk = kernel_call(

time: 62.8 us -> 61.1 us (0.973)
  starting transfers between devices: 23.4 us -> 18.7 us
  waiting for transfers between devices: 15.3 us -> 18.7 us
  Pallas kernels: 21 us -> 19 us
  local copies, waits for them, and re-layouts: 2.01 us -> 3.61 us
    ppermute x22, starting transfers between devices: 23.4 us -> 18.7 us  [swap(): return lax.ppermute(value, axis, [(i, i ^ mask) for i in range(size)])]
    ppermute x22, waiting for transfers between devices: 15.3 us -> 18.7 us  [swap(): return lax.ppermute(value, axis, [(i, i ^ mask) for i in range(size)])]
    unnamed x6 -> x10, local copies, waits for them, and re-layouts: 2.01 us -> 3.61 us
    pallas_call x1, Pallas kernels: 6.95 us -> 5.47 us  [gathered_body(): kernel_call(own_chunk_kernel, chunk_outs() + (shape((2, 256, 1024)),), 'v...]
    pallas_call x3 -> x2, Pallas kernels: 2.38 us -> 1.8 us  [the longest x1 1.75 us: gathered_body(): kernel_call(payload_kernel, (shape((HALF, width)), shape((2 * HALF, 128))...]
  transfers between devices with their start and end apart: 22 -> 22, of which waited for: 9 -> 12; matrix products, arithmetic and copies ran while one was open for 0% -> 0% of each run, Pallas kernels for 28% -> 27%
where the time goes in v11:
time: 61.1 us; the launch traced here: 60.8 us
  Pallas kernels  19 us (31%)
  starting transfers between devices  18.7 us (31%)
  waiting for transfers between devices  18.7 us (31%)
  local copies, waits for them, and re-layouts  3.61 us (6%)
  between operations  0.75 us (1%)
    ppermute x22, waiting for transfers between devices, swap(): return lax.ppermute(value, axis, [(i, i ^ mask) for i in range(size)])  18.7 us
    ppermute x22, starting transfers between devices, swap(): return lax.ppermute(value, axis, [(i, i ^ mask) for i in range(size)])  18.7 us
    pallas_call x1, Pallas kernels, gathered_body(): kernel_call(far_chunk_kernel, chunk_outs(), 'vvvhh', scratch=[pltpu.VMEM(...  5.54 us
    pallas_call x1, Pallas kernels, gathered_body(): kernel_call(own_chunk_kernel, chunk_outs() + (shape((2, 256, 1024)),), 'v...  5.47 us
    unnamed x10, local copies, waits for them, and re-layouts  3.61 us
    pallas_call x1, Pallas kernels, gathered_body(): kernel_call(weights_kernel, (shape((2, 512, 1024)), shape((2, 1024, 512))...  3.03 us
    pallas_call x1, Pallas kernels, gathered_body(): kernel_call(payload_kernel, (shape((HALF, width)), shape((2 * HALF, 128))...  1.75 us
  transfers between devices with their start and end apart: 22, of which 12 were waited for; matrix products, arithmetic and copies ran while one was open for 0% of the time, Pallas kernels for 27%

profile of v11, /device:TPU:0, one launch (start us, length us, event | category | flops | bytes accessed | tf_op | source)
XLA Modules:
  0.0 60.8 jit_solution(2532982235610263970)
XLA Ops:
  0.6 1.7 %shard_map.110 = (bf16[64,2176]{1,0:T(8,128)(2,1)}, bf16[128,128]{1,0:T(8,128)(2,1)}) custom-call(bf16[128,1024]{1,0:T(8,128)(2,1)} %x.3, bf16[128,1024]{1,0:T(8,128)(2,1)} %c.3, f32[2,128]{1,0:T(2,128)} %bitcast.2, s32[2,128]{1,0:T(2,128)} %bitcast.3), custom_call_target="tpu_custom_call" | custom-call | tf_op jit(solution)/shard_map/pallas_call | solution.py:514
  2.4 3.1 %collective-permute-start = (bf16[64,2176]{1,0:T(8,128)(2,1)}, bf16[64,2176]{1,0:T(8,128)(2,1)S(1)}, u32[]{:S(2)}, u32[]{:S(2)}) collective-permute-start(bf16[64,2176]{1,0:T(8,128)(2,1)} %get-tuple-element.48), channel_id=1, source_target_pairs={{0,4},{4,0},{8,12},{12,8},{1,5},{5,1},{9,13},{13,9},{2,6},{6,2},{1... | collective-permute-start | bytes 835592 | tf_op jit(solution)/shard_map/ppermute | solution.py:462
  5.5 2.6 %collective-permute-start.4 = (bf16[64,2176]{1,0:T(8,128)(2,1)}, bf16[64,2176]{1,0:T(8,128)(2,1)S(1)}, u32[]{:S(2)}, u32[]{:S(2)}) collective-permute-start(bf16[64,2176]{1,0:T(8,128)(2,1)} %get-tuple-element.48), channel_id=1, source_target_pairs={{0,8},{4,12},{8,0},{12,4},{1,9},{5,13},{9,1},{13,5},{2,10},{6,14},... | collective-permute-start | bytes 835592 | tf_op jit(solution)/shard_map/ppermute | solution.py:462
  8.1 0.9 %copy-done = bf16[128,1024]{1,0:T(8,128)(2,1)S(1)} copy-done((bf16[128,1024]{1,0:T(8,128)(2,1)S(1)}, bf16[128,1024]{1,0:T(8,128)(2,1)}, u32[]{:S(2)}) %copy-start) | copy-done | bytes 262168
  9.0 0.9 %copy-done.1 = bf16[128,1024]{1,0:T(8,128)(2,1)S(1)} copy-done((bf16[128,1024]{1,0:T(8,128)(2,1)S(1)}, bf16[128,1024]{1,0:T(8,128)(2,1)}, u32[]{:S(2)}) %copy-start.1) | copy-done | bytes 262168
  10.0 0.9 %copy-done.2 = bf16[2,256,256]{2,1,0:T(8,128)(2,1)S(1)} copy-done((bf16[2,256,256]{2,1,0:T(8,128)(2,1)S(1)}, bf16[2,256,256]{2,1,0:T(8,128)(2,1)}, u32[]{:S(2)}) %copy-start.2) | copy-done | bytes 262168
  11.7 1.6 %collective-permute-start.3 = (bf16[2,256,256]{2,1,0:T(8,128)(2,1)S(1)}, bf16[2,256,256]{2,1,0:T(8,128)(2,1)S(1)}, u32[]{:S(2)}, u32[]{:S(2)}) collective-permute-start(bf16[2,256,256]{2,1,0:T(8,128)(2,1)S(1)} %get-tuple-element.47.refs_1_), channel_id=1, source_target_pairs={{0,2},{1,3},{2,0},{3,1},{4,6},{5,7},{6,4},{7,5},{8,10},{9,11},{10,... | collective-permute-start | bytes 786440 | tf_op jit(solution)/shard_map/ppermute | solution.py:462
  13.3 4.9 %collective-permute-done.refs_2_ = bf16[64,2176]{1,0:T(8,128)(2,1)S(1)} collective-permute-done((bf16[64,2176]{1,0:T(8,128)(2,1)}, bf16[64,2176]{1,0:T(8,128)(2,1)S(1)}, u32[]{:S(2)}, u32[]{:S(2)}) %collective-permute-start) | collective-permute-done | bytes 278560 | tf_op jit(solution)/shard_map/ppermute | solution.py:462
  19.3 1.4 %collective-permute-done.4.after.a = bf16[64,2176]{1,0:T(8,128)(2,1)S(1)} collective-permute-done((bf16[64,2176]{1,0:T(8,128)(2,1)}, bf16[64,2176]{1,0:T(8,128)(2,1)S(1)}, u32[]{:S(2)}, u32[]{:S(2)}) %collective-permute-start.4) | collective-permute-done | bytes 278560 | tf_op jit(solution)/shard_map/ppermute | solution.py:462
  21.3 1.0 %collective-permute-done.5.refs_6_ = bf16[2,256,256]{2,1,0:T(8,128)(2,1)S(1)} collective-permute-done((bf16[2,256,256]{2,1,0:T(8,128)(2,1)S(1)}, bf16[2,256,256]{2,1,0:T(8,128)(2,1)S(1)}, u32[]{:S(2)}, u32[]{:S(2)}) %collective-permute-start.5) | collective-permute-done | bytes 262176 | tf_op jit(solution)/shard_map/ppermute | solution.py:462
  22.4 5.5 %shard_map.113 = (bf16[2,576,256]{2,1,0:T(8,128)(2,1)S(1)}, bf16[576,256]{1,0:T(8,128)(2,1)S(1)}, bf16[320,256]{1,0:T(8,128)(2,1)S(1)}, bf16[256,256]{1,0:T(8,12...) custom-call(bf16[128,2176]{1,0:T(8,128)(2,1)S(1)} %get-tuple-element, ...), custom_call_target="tpu_custom_call" | custom-call | flops 4000000000 | bytes 10000000 | tf_op jit(solution)/shard_map/pallas_call | solution.py:536
  28.4 1.1 %collective-permute-done.8.high = bf16[256,256]{1,0:T(8,128)(2,1)S(1)} collective-permute-done((bf16[256,256]{1,0:T(8,128)(2,1)S(1)}, bf16[256,256]{1,0:T(8,128)(2,1)S(1)}, u32[]{:S(2)}, u32[]{:S(2)}) %collective-permute-start.8) | collective-permute-done | bytes 131104 | tf_op jit(solution)/shard_map/ppermute | solution.py:462
  30.5 1.5 %collective-permute-start.9 = (bf16[576,256]{1,0:T(8,128)(2,1)S(1)}, bf16[576,256]{1,0:T(8,128)(2,1)S(1)}, u32[]{:S(2)}, u32[]{:S(2)}) collective-permute-start(bf16[576,256]{1,0:T(8,128)(2,1)S(1)} %shard_map.114.after), channel_id=1, source_target_pairs={{0,2},{1,3},{2,0},{3,1},{4,6},{5,7},{6,4},{7,5},{8,10},{9,11},{10,... | collective-permute-start | bytes 884744 | tf_op jit(solution)/shard_map/ppermute | solution.py:462
  32.0 5.5 %shard_map.116 = (bf16[2,576,256]{2,1,0:T(8,128)(2,1)S(1)}, bf16[576,256]{1,0:T(8,128)(2,1)S(1)}, bf16[320,256]{1,0:T(8,128)(2,1)S(1)}, bf16[256,256]{1,0:T(8,12...) custom-call(bf16[128,2176]{1,0:T(8,128)(2,1)S(1)} %shard_map.115.ref, ...), custom_call_target="tpu_custom_call" | custom-call | flops 4000000000 | bytes 10000000 | tf_op jit(solution)/shard_map/pallas_call | solution.py:563
  39.1 1.5 %collective-permute-start.16 = (bf16[320,256]{1,0:T(8,128)(2,1)S(1)}, bf16[320,256]{1,0:T(8,128)(2,1)S(1)}, u32[]{:S(2)}, u32[]{:S(2)}) collective-permute-start(bf16[320,256]{1,0:T(8,128)(2,1)S(1)} %shard_map.117.after), channel_id=1, source_target_pairs={{0,2},{1,3},{2,0},{3,1},{4,6},{5,7},{6,4},{7,5},{8,10},{9,11},{10,... | collective-permute-start | bytes 491528 | tf_op jit(solution)/shard_map/ppermute | solution.py:462
  42.2 3.0 %shard_map.120 = (bf16[2,512,1024]{2,1,0:T(8,128)(2,1)}, bf16[2,1024,512]{2,1,0:T(8,128)(2,1)}, f32[8,128]{1,0:T(8,128)S(1)}) custom-call(bf16[2,128,512]{2,1,0:T(8,128)(2,1)S(1)} %get-tuple-element.63.act0, bf16[2,128,1024]{2,1,0:T(8,128)(2,1)S(1)} %get-tuple-element.64.grad0, bf16[2,128,1024]{2,1,0:T(8,128)(2,1)S(1)} %get-tuple-element.65.cross0, ...), custom_call_target="tpu_custom_call" | custom-call | flops 3000000000 | bytes 8000000 | tf_op jit(solution)/shard_map/pallas_call | solution.py:589
  45.2 1.0 %collective-permute-done.16.theirs = bf16[320,256]{1,0:T(8,128)(2,1)S(1)} collective-permute-done((bf16[320,256]{1,0:T(8,128)(2,1)S(1)}, bf16[320,256]{1,0:T(8,128)(2,1)S(1)}, u32[]{:S(2)}, u32[]{:S(2)}) %collective-permute-start.16) | collective-permute-done | bytes 163872 | tf_op jit(solution)/shard_map/ppermute | solution.py:462
  47.2 1.0 %collective-permute-done.19.theirs = bf16[256,256]{1,0:T(8,128)(2,1)S(1)} collective-permute-done((bf16[256,256]{1,0:T(8,128)(2,1)S(1)}, bf16[256,256]{1,0:T(8,128)(2,1)S(1)}, u32[]{:S(2)}, u32[]{:S(2)}) %collective-permute-start.19) | collective-permute-done | bytes 131104 | tf_op jit(solution)/shard_map/ppermute | solution.py:462
  49.0 2.6 %collective-permute-done.17.b = bf16[160,256]{1,0:T(8,128)(2,1)S(1)} collective-permute-done((bf16[160,256]{1,0:T(8,128)(2,1)S(1)}, bf16[160,256]{1,0:T(8,128)(2,1)S(1)}, u32[]{:S(2)}, u32[]{:S(2)}) %collective-permute-start.17) | collective-permute-done | bytes 81952 | tf_op jit(solution)/shard_map/ppermute | solution.py:462
  51.6 1.8 %collective-permute-start.18 = (bf16[160,256]{1,0:T(8,128)(2,1)S(1)}, bf16[160,256]{1,0:T(8,128)(2,1)S(1)}, u32[]{:S(2)}, u32[]{:S(2)}) collective-permute-start(bf16[160,256]{1,0:T(8,128)(2,1)S(1)} %shard_map.122), channel_id=1, source_target_pairs={{0,8},{4,12},{8,0},{12,4},{1,9},{5,13},{9,1},{13,5},{2,10},{6,14},... | collective-permute-start | bytes 245768 | tf_op jit(solution)/shard_map/ppermute | solution.py:462
  53.5 1.5 %collective-permute-start.21 = (bf16[128,256]{1,0:T(8,128)(2,1)S(1)}, bf16[128,256]{1,0:T(8,128)(2,1)S(1)}, u32[]{:S(2)}, u32[]{:S(2)}) collective-permute-start(bf16[128,256]{1,0:T(8,128)(2,1)S(1)} %shard_map.124), channel_id=1, source_target_pairs={{0,8},{4,12},{8,0},{12,4},{1,9},{5,13},{9,1},{13,5},{2,10},{6,14},... | collective-permute-start | bytes 196616 | tf_op jit(solution)/shard_map/ppermute | solution.py:462
  55.0 1.0 %shard_map.126 = bf16[2,256,256]{2,1,0:T(8,128)(2,1)} custom-call(bf16[2,256,128]{2,1,0:T(8,128)(2,1)S(1)} %get-tuple-element.79.gram0, bf16[2,128,256]{2,1,0:T(8,128)(2,1)S(1)} %get-tuple-element.80.rows0, bf16[2,256,128]{2,1,0:T(8,128)(2,1)S(1)} %get-tuple-element.81.gram1, bf16[2,128,256]{2,1,0:T(8,128)(2,1)S(1)} %get-tuple-element.82.rows1), custom_call_target="tpu_custom_call" | custom-call | flops 300000000 | bytes 2000000 | tf_op jit(solution)/shard_map/pallas_call | solution.py:608
  56.0 3.8 %collective-permute-done.21.far_outs = bf16[128,256]{1,0:T(8,128)(2,1)S(1)} collective-permute-done((bf16[128,256]{1,0:T(8,128)(2,1)S(1)}, bf16[128,256]{1,0:T(8,128)(2,1)S(1)}, u32[]{:S(2)}, u32[]{:S(2)}) %collective-permute-start.21) | collective-permute-done | bytes 65568 | tf_op jit(solution)/shard_map/ppermute | solution.py:462
  59.8 1.0 %shard_map.125 = (bf16[128,256]{1,0:T(8,128)(2,1)}, bf16[128,256]{1,0:T(8,128)(2,1)}) custom-call(bf16[128,2176]{1,0:T(8,128)(2,1)S(1)} %get-tuple-element.46.refs_0_.own, bf16[288,256]{1,0:T(8,128)(2,1)S(1)} %get-tuple-element.59.g0, bf16[288,256]{1,0:T(8,128)(2,1)S(1)} %collective-permute-done.14.after.g1, ...), custom_call_target="tpu_custom_call" | custom-call | flops 100000000 | bytes 1000000 | tf_op jit(solution)/shard_map/pallas_call | solution.py:611
  (47 shorter events, 9.1 us)
Async XLA Ops:
  2.4 15.8 %collective-permute-start = (bf16[64,2176]{1,0:T(8,128)(2,1)}, bf16[64,2176]{1,0:T(8,128)(2,1)S(1)}, u32[]{:S(2)}, u32[]{:S(2)}) collective-permute-start(bf16[64,2176]{1,0:T(8,128)(2,1)} %get-tuple-element.48), channel_id=1, source_target_pairs={{0,4},{4,0},{8,12},{12,8},{1,5},{5,1},{9,13},{13,9},{2,6},{6,2},{1... | collective-permute-start | bytes 835592 | tf_op jit(solution)/shard_map/ppermute | solution.py:462
  5.5 15.3 %collective-permute-start.4 = (bf16[64,2176]{1,0:T(8,128)(2,1)}, bf16[64,2176]{1,0:T(8,128)(2,1)S(1)}, u32[]{:S(2)}, u32[]{:S(2)}) collective-permute-start(bf16[64,2176]{1,0:T(8,128)(2,1)} %get-tuple-element.48), channel_id=1, source_target_pairs={{0,8},{4,12},{8,0},{12,4},{1,9},{5,13},{9,1},{13,5},{2,10},{6,14},... | collective-permute-start | bytes 835592 | tf_op jit(solution)/shard_map/ppermute | solution.py:462
  8.1 0.9 %copy-start = (bf16[128,1024]{1,0:T(8,128)(2,1)S(1)}, bf16[128,1024]{1,0:T(8,128)(2,1)}, u32[]{:S(2)}) copy-start(bf16[128,1024]{1,0:T(8,128)(2,1)} %x.3) | copy-start | bytes 786436
  11.7 7.6 %collective-permute-start.3 = (bf16[2,256,256]{2,1,0:T(8,128)(2,1)S(1)}, bf16[2,256,256]{2,1,0:T(8,128)(2,1)S(1)}, u32[]{:S(2)}, u32[]{:S(2)}) collective-permute-start(bf16[2,256,256]{2,1,0:T(8,128)(2,1)S(1)} %get-tuple-element.47.refs_1_), channel_id=1, source_target_pairs={{0,2},{1,3},{2,0},{3,1},{4,6},{5,7},{6,4},{7,5},{8,10},{9,11},{10,... | collective-permute-start | bytes 786440 | tf_op jit(solution)/shard_map/ppermute | solution.py:462
  18.2 4.2 %collective-permute-start.1 = (bf16[64,2176]{1,0:T(8,128)(2,1)S(1)}, bf16[64,2176]{1,0:T(8,128)(2,1)S(1)}, u32[]{:S(2)}, u32[]{:S(2)}) collective-permute-start(bf16[64,2176]{1,0:T(8,128)(2,1)S(1)} %collective-permute-done.refs_2_), channel_id=1, source_target_pairs={{0,1},{1,0},{2,3},{3,2},{4,5},{5,4},{6,7},{7,6},{8,9},{9,8},{10,11... | collective-permute-start | bytes 835592 | tf_op jit(solution)/shard_map/ppermute | solution.py:462
  18.2 3.2 %collective-permute-start.2 = (bf16[2,256,256]{2,1,0:T(8,128)(2,1)S(1)}, bf16[2,256,256]{2,1,0:T(8,128)(2,1)S(1)}, u32[]{:S(2)}, u32[]{:S(2)}) collective-permute-start(bf16[2,256,256]{2,1,0:T(8,128)(2,1)S(1)} %get-tuple-element.47.refs_1_), channel_id=1, source_target_pairs={{0,1},{1,0},{2,3},{3,2},{4,5},{5,4},{6,7},{7,6},{8,9},{9,8},{10,11... | collective-permute-start | bytes 786440 | tf_op jit(solution)/shard_map/ppermute | solution.py:462
  20.8 1.6 %collective-permute-start.5 = (bf16[2,256,256]{2,1,0:T(8,128)(2,1)S(1)}, bf16[2,256,256]{2,1,0:T(8,128)(2,1)S(1)}, u32[]{:S(2)}, u32[]{:S(2)}) collective-permute-start(bf16[2,256,256]{2,1,0:T(8,128)(2,1)S(1)} %shard_map.112.refs_5_), channel_id=1, source_target_pairs={{0,1},{1,0},{2,3},{3,2},{4,5},{5,4},{6,7},{7,6},{8,9},{9,8},{10,11... | collective-permute-start | bytes 786440 | tf_op jit(solution)/shard_map/ppermute | solution.py:462
  20.8 9.1 %collective-permute-start.10 = (bf16[64,2176]{1,0:T(8,128)(2,1)S(1)}, bf16[64,2176]{1,0:T(8,128)(2,1)S(1)}, u32[]{:S(2)}, u32[]{:S(2)}) collective-permute-start(bf16[64,2176]{1,0:T(8,128)(2,1)S(1)} %collective-permute-done.4.after.a), channel_id=1, source_target_pairs={{0,4},{4,0},{8,12},{12,8},{1,5},{5,1},{9,13},{13,9},{2,6},{6,2},{1... | collective-permute-start | bytes 835592 | tf_op jit(solution)/shard_map/ppermute | solution.py:462
  27.8 4.2 %copy-start.4 = (bf16[2,256,1024]{2,1,0:T(8,128)(2,1)S(1)}, bf16[2,256,1024]{2,1,0:T(8,128)(2,1)}, u32[]{:S(2)}) copy-start(bf16[2,256,1024]{2,1,0:T(8,128)(2,1)} %get-tuple-element.55.refs_2_) | copy-start | bytes 3145732
  27.9 1.7 %collective-permute-start.7 = (bf16[320,256]{1,0:T(8,128)(2,1)S(1)}, bf16[320,256]{1,0:T(8,128)(2,1)S(1)}, u32[]{:S(2)}, u32[]{:S(2)}) collective-permute-start(bf16[320,256]{1,0:T(8,128)(2,1)S(1)} %get-tuple-element.51), channel_id=1, source_target_pairs={{0,1},{1,0},{2,3},{3,2},{4,5},{5,4},{6,7},{7,6},{8,9},{9,8},{10,11... | collective-permute-start | bytes 491528 | tf_op jit(solution)/shard_map/ppermute | solution.py:462
  28.1 1.4 %collective-permute-start.8 = (bf16[256,256]{1,0:T(8,128)(2,1)S(1)}, bf16[256,256]{1,0:T(8,128)(2,1)S(1)}, u32[]{:S(2)}, u32[]{:S(2)}) collective-permute-start(bf16[256,256]{1,0:T(8,128)(2,1)S(1)} %get-tuple-element.52), channel_id=1, source_target_pairs={{0,1},{1,0},{2,3},{3,2},{4,5},{5,4},{6,7},{7,6},{8,9},{9,8},{10,11... | collective-permute-start | bytes 393224 | tf_op jit(solution)/shard_map/ppermute | solution.py:462
  30.0 2.1 %collective-permute-start.11 = (bf16[128,2176]{1,0:T(8,128)(2,1)S(1)}, bf16[128,2176]{1,0:T(8,128)(2,1)S(1)}, u32[]{:S(2)}, u32[]{:S(2)}) collective-permute-start(bf16[128,2176]{1,0:T(8,128)(2,1)S(1)} %shard_map.115.refs_0_), channel_id=1, source_target_pairs={{0,1},{1,0},{2,3},{3,2},{4,5},{5,4},{6,7},{7,6},{8,9},{9,8},{10,11... | collective-permute-start | bytes 1671176 | tf_op jit(solution)/shard_map/ppermute | solution.py:462
  30.0 11.3 %collective-permute-start.6 = (bf16[576,256]{1,0:T(8,128)(2,1)S(1)}, bf16[576,256]{1,0:T(8,128)(2,1)S(1)}, u32[]{:S(2)}, u32[]{:S(2)}) collective-permute-start(bf16[576,256]{1,0:T(8,128)(2,1)S(1)} %get-tuple-element.50), channel_id=1, source_target_pairs={{0,1},{1,0},{2,3},{3,2},{4,5},{5,4},{6,7},{7,6},{8,9},{9,8},{10,11... | collective-permute-start | bytes 884744 | tf_op jit(solution)/shard_map/ppermute | solution.py:462
  30.5 10.1 %collective-permute-start.9 = (bf16[576,256]{1,0:T(8,128)(2,1)S(1)}, bf16[576,256]{1,0:T(8,128)(2,1)S(1)}, u32[]{:S(2)}, u32[]{:S(2)}) collective-permute-start(bf16[576,256]{1,0:T(8,128)(2,1)S(1)} %shard_map.114.after), channel_id=1, source_target_pairs={{0,2},{1,3},{2,0},{3,1},{4,6},{5,7},{6,4},{7,5},{8,10},{9,11},{10,... | collective-permute-start | bytes 884744 | tf_op jit(solution)/shard_map/ppermute | solution.py:462
  37.6 1.5 %collective-permute-start.13 = (bf16[320,256]{1,0:T(8,128)(2,1)S(1)}, bf16[320,256]{1,0:T(8,128)(2,1)S(1)}, u32[]{:S(2)}, u32[]{:S(2)}) collective-permute-start(bf16[320,256]{1,0:T(8,128)(2,1)S(1)} %get-tuple-element.58), channel_id=1, source_target_pairs={{0,1},{1,0},{2,3},{3,2},{4,5},{5,4},{6,7},{7,6},{8,9},{9,8},{10,11... | collective-permute-start | bytes 491528 | tf_op jit(solution)/shard_map/ppermute | solution.py:462
  37.7 2.9 %collective-permute-start.12 = (bf16[256,256]{1,0:T(8,128)(2,1)S(1)}, bf16[256,256]{1,0:T(8,128)(2,1)S(1)}, u32[]{:S(2)}, u32[]{:S(2)}) collective-permute-start(bf16[256,256]{1,0:T(8,128)(2,1)S(1)} %get-tuple-element.57), channel_id=1, source_target_pairs={{0,1},{1,0},{2,3},{3,2},{4,5},{5,4},{6,7},{7,6},{8,9},{9,8},{10,11... | collective-permute-start | bytes 393224 | tf_op jit(solution)/shard_map/ppermute | solution.py:462
  38.2 7.1 %collective-permute-start.15 = (bf16[576,256]{1,0:T(8,128)(2,1)S(1)}, bf16[576,256]{1,0:T(8,128)(2,1)S(1)}, u32[]{:S(2)}, u32[]{:S(2)}) collective-permute-start(bf16[576,256]{1,0:T(8,128)(2,1)S(1)} %get-tuple-element.61), channel_id=1, source_target_pairs={{0,1},{1,0},{2,3},{3,2},{4,5},{5,4},{6,7},{7,6},{8,9},{9,8},{10,11... | collective-permute-start | bytes 884744 | tf_op jit(solution)/shard_map/ppermute | solution.py:462
  39.1 7.1 %collective-permute-start.16 = (bf16[320,256]{1,0:T(8,128)(2,1)S(1)}, bf16[320,256]{1,0:T(8,128)(2,1)S(1)}, u32[]{:S(2)}, u32[]{:S(2)}) collective-permute-start(bf16[320,256]{1,0:T(8,128)(2,1)S(1)} %shard_map.117.after), channel_id=1, source_target_pairs={{0,2},{1,3},{2,0},{3,1},{4,6},{5,7},{6,4},{7,5},{8,10},{9,11},{10,... | collective-permute-start | bytes 491528 | tf_op jit(solution)/shard_map/ppermute | solution.py:462
  40.6 7.6 %collective-permute-start.19 = (bf16[256,256]{1,0:T(8,128)(2,1)S(1)}, bf16[256,256]{1,0:T(8,128)(2,1)S(1)}, u32[]{:S(2)}, u32[]{:S(2)}) collective-permute-start(bf16[256,256]{1,0:T(8,128)(2,1)S(1)} %shard_map.118.after), channel_id=1, source_target_pairs={{0,2},{1,3},{2,0},{3,1},{4,6},{5,7},{6,4},{7,5},{8,10},{9,11},{10,... | collective-permute-start | bytes 393224 | tf_op jit(solution)/shard_map/ppermute | solution.py:462
  41.7 6.5 %collective-permute-start.14 = (bf16[288,256]{1,0:T(8,128)(2,1)S(1)}, bf16[288,256]{1,0:T(8,128)(2,1)S(1)}, u32[]{:S(2)}, u32[]{:S(2)}) collective-permute-start(bf16[288,256]{1,0:T(8,128)(2,1)S(1)} %get-tuple-element.60), channel_id=1, source_target_pairs={{0,4},{4,0},{8,12},{12,8},{1,5},{5,1},{9,13},{13,9},{2,6},{6,2},{1... | collective-permute-start | bytes 442376 | tf_op jit(solution)/shard_map/ppermute | solution.py:462
  46.5 5.1 %collective-permute-start.17 = (bf16[160,256]{1,0:T(8,128)(2,1)S(1)}, bf16[160,256]{1,0:T(8,128)(2,1)S(1)}, u32[]{:S(2)}, u32[]{:S(2)}) collective-permute-start(bf16[160,256]{1,0:T(8,128)(2,1)S(1)} %get-tuple-element.73), channel_id=1, source_target_pairs={{0,4},{4,0},{8,12},{12,8},{1,5},{5,1},{9,13},{13,9},{2,6},{6,2},{1... | collective-permute-start | bytes 245768 | tf_op jit(solution)/shard_map/ppermute | solution.py:462
  48.5 5.0 %collective-permute-start.20 = (bf16[128,256]{1,0:T(8,128)(2,1)S(1)}, bf16[128,256]{1,0:T(8,128)(2,1)S(1)}, u32[]{:S(2)}, u32[]{:S(2)}) collective-permute-start(bf16[128,256]{1,0:T(8,128)(2,1)S(1)} %get-tuple-element.76), channel_id=1, source_target_pairs={{0,4},{4,0},{8,12},{12,8},{1,5},{5,1},{9,13},{13,9},{2,6},{6,2},{1... | collective-permute-start | bytes 196616 | tf_op jit(solution)/shard_map/ppermute | solution.py:462
  51.6 8.2 %collective-permute-start.18 = (bf16[160,256]{1,0:T(8,128)(2,1)S(1)}, bf16[160,256]{1,0:T(8,128)(2,1)S(1)}, u32[]{:S(2)}, u32[]{:S(2)}) collective-permute-start(bf16[160,256]{1,0:T(8,128)(2,1)S(1)} %shard_map.122), channel_id=1, source_target_pairs={{0,8},{4,12},{8,0},{12,4},{1,9},{5,13},{9,1},{13,5},{2,10},{6,14},... | collective-permute-start | bytes 245768 | tf_op jit(solution)/shard_map/ppermute | solution.py:462
  53.5 6.3 %collective-permute-start.21 = (bf16[128,256]{1,0:T(8,128)(2,1)S(1)}, bf16[128,256]{1,0:T(8,128)(2,1)S(1)}, u32[]{:S(2)}, u32[]{:S(2)}) collective-permute-start(bf16[128,256]{1,0:T(8,128)(2,1)S(1)} %shard_map.124), channel_id=1, source_target_pairs={{0,8},{4,12},{8,0},{12,4},{1,9},{5,13},{9,1},{13,5},{2,10},{6,14},... | collective-permute-start | bytes 196616 | tf_op jit(solution)/shard_map/ppermute | solution.py:462
  (3 other events, 2.7 us)

commit v12 on v11

--- a/solution.py
+++ b/solution.py
@@ -555,7 +555,6 @@
         keep, swap(away, "tensor", 1), swap(last, "tensor", 1)
     )
     theirs = swap(away, "tensor", 2)
-    other = swap(here, "tensor", 1)
     far_mine = kernel_call(join_kernel, shape((2 * HALF, 2 * WIDTH + 128)), "vva")(
         got[1], got[2], away
     )
@@ -579,7 +578,10 @@
     fouts = kernel_call(away_outs_kernel, shape((256, 256)), "vvaa")(
         fkeep, swap(flast, "tensor", 1), fgrads, theirs
     )
+    fgrads_away = fgrads
     fgrads = swap(fgrads, "tensor", 2)
+    here = kernel_call(after_kernel, shape((576, 256)), "va")(here, fgrads_away)
+    other = swap(here, "tensor", 1)
     part = shape((288, 256))
     own_part, near_part, rows = kernel_call(
         combine_kernel, (part, part, shape((2, 128, 256))), "vvvvva"

time: 61.1 us -> 67.7 us (1.11)
  waiting for transfers between devices: 18.7 us -> 22.9 us
  starting transfers between devices: 18.7 us -> 21.1 us
    ppermute x22, waiting for transfers between devices: 18.7 us -> 22.9 us  [swap(): return lax.ppermute(value, axis, [(i, i ^ mask) for i in range(size)])]
    ppermute x22, starting transfers between devices: 18.7 us -> 21.1 us  [swap(): return lax.ppermute(value, axis, [(i, i ^ mask) for i in range(size)])]
  transfers between devices with their start and end apart: 22 -> 22, of which waited for: 12 -> 11; matrix products, arithmetic and copies ran while one was open for 0% -> 0% of each run, Pallas kernels for 27% -> 16%
where the time goes in v12:
time: 67.7 us; the launch traced here: 67.4 us
  waiting for transfers between devices  22.9 us (34%)
  starting transfers between devices  21.1 us (31%)
  Pallas kernels  19 us (28%)
  local copies, waits for them, and re-layouts  3.61 us (5%)
  between operations  0.77 us (1%)
    ppermute x22, waiting for transfers between devices, swap(): return lax.ppermute(value, axis, [(i, i ^ mask) for i in range(size)])  22.9 us
    ppermute x22, starting transfers between devices, swap(): return lax.ppermute(value, axis, [(i, i ^ mask) for i in range(size)])  21.1 us
    pallas_call x1, Pallas kernels, gathered_body(): kernel_call(far_chunk_kernel, chunk_outs(), 'vvvhh', scratch=[pltpu.VMEM(...  5.55 us
    pallas_call x1, Pallas kernels, gathered_body(): kernel_call(own_chunk_kernel, chunk_outs() + (shape((2, 256, 1024)),), 'v...  5.47 us
    unnamed x10, local copies, waits for them, and re-layouts  3.61 us
    pallas_call x1, Pallas kernels, gathered_body(): kernel_call(weights_kernel, (shape((2, 512, 1024)), shape((2, 1024, 512))...  3.03 us
    pallas_call x1, Pallas kernels, gathered_body(): kernel_call(payload_kernel, (shape((HALF, width)), shape((2 * HALF, 128))...  1.75 us
  transfers between devices with their start and end apart: 22, of which 11 were waited for; matrix products, arithmetic and copies ran while one was open for 0% of the time, Pallas kernels for 16%

profile of v12, /device:TPU:0, one launch (start us, length us, event | category | flops | bytes accessed | tf_op | source)
XLA Modules:
  0.0 67.4 jit_solution(3729633418016684640)
XLA Ops:
  0.6 1.7 %shard_map.110 = (bf16[64,2176]{1,0:T(8,128)(2,1)}, bf16[128,128]{1,0:T(8,128)(2,1)}) custom-call(bf16[128,1024]{1,0:T(8,128)(2,1)} %x.3, bf16[128,1024]{1,0:T(8,128)(2,1)} %c.3, f32[2,128]{1,0:T(2,128)} %bitcast.2, s32[2,128]{1,0:T(2,128)} %bitcast.3), custom_call_target="tpu_custom_call" | custom-call | tf_op jit(solution)/shard_map/pallas_call | solution.py:514
  2.4 3.1 %collective-permute-start = (bf16[64,2176]{1,0:T(8,128)(2,1)}, bf16[64,2176]{1,0:T(8,128)(2,1)S(1)}, u32[]{:S(2)}, u32[]{:S(2)}) collective-permute-start(bf16[64,2176]{1,0:T(8,128)(2,1)} %get-tuple-element.48), channel_id=1, source_target_pairs={{0,4},{4,0},{8,12},{12,8},{1,5},{5,1},{9,13},{13,9},{2,6},{6,2},{1... | collective-permute-start | bytes 835592 | tf_op jit(solution)/shard_map/ppermute | solution.py:462
  5.5 2.6 %collective-permute-start.4 = (bf16[64,2176]{1,0:T(8,128)(2,1)}, bf16[64,2176]{1,0:T(8,128)(2,1)S(1)}, u32[]{:S(2)}, u32[]{:S(2)}) collective-permute-start(bf16[64,2176]{1,0:T(8,128)(2,1)} %get-tuple-element.48), channel_id=1, source_target_pairs={{0,8},{4,12},{8,0},{12,4},{1,9},{5,13},{9,1},{13,5},{2,10},{6,14},... | collective-permute-start | bytes 835592 | tf_op jit(solution)/shard_map/ppermute | solution.py:462
  11.7 1.6 %collective-permute-start.3 = (bf16[2,256,256]{2,1,0:T(8,128)(2,1)S(1)}, bf16[2,256,256]{2,1,0:T(8,128)(2,1)S(1)}, u32[]{:S(2)}, u32[]{:S(2)}) collective-permute-start(bf16[2,256,256]{2,1,0:T(8,128)(2,1)S(1)} %get-tuple-element.47.refs_1_), channel_id=1, source_target_pairs={{0,2},{1,3},{2,0},{3,1},{4,6},{5,7},{6,4},{7,5},{8,10},{9,11},{10,... | collective-permute-start | bytes 786440 | tf_op jit(solution)/shard_map/ppermute | solution.py:462
  13.3 4.9 %collective-permute-done.refs_2_ = bf16[64,2176]{1,0:T(8,128)(2,1)S(1)} collective-permute-done((bf16[64,2176]{1,0:T(8,128)(2,1)}, bf16[64,2176]{1,0:T(8,128)(2,1)S(1)}, u32[]{:S(2)}, u32[]{:S(2)}) %collective-permute-start) | collective-permute-done | bytes 278560 | tf_op jit(solution)/shard_map/ppermute | solution.py:462
  19.3 1.4 %collective-permute-done.4.after.a = bf16[64,2176]{1,0:T(8,128)(2,1)S(1)} collective-permute-done((bf16[64,2176]{1,0:T(8,128)(2,1)}, bf16[64,2176]{1,0:T(8,128)(2,1)S(1)}, u32[]{:S(2)}, u32[]{:S(2)}) %collective-permute-start.4) | collective-permute-done | bytes 278560 | tf_op jit(solution)/shard_map/ppermute | solution.py:462
  21.3 1.0 %collective-permute-done.5.refs_6_ = bf16[2,256,256]{2,1,0:T(8,128)(2,1)S(1)} collective-permute-done((bf16[2,256,256]{2,1,0:T(8,128)(2,1)S(1)}, bf16[2,256,256]{2,1,0:T(8,128)(2,1)S(1)}, u32[]{:S(2)}, u32[]{:S(2)}) %collective-permute-start.5) | collective-permute-done | bytes 262176 | tf_op jit(solution)/shard_map/ppermute | solution.py:462
  22.4 5.5 %shard_map.113 = (bf16[2,576,256]{2,1,0:T(8,128)(2,1)S(1)}, bf16[576,256]{1,0:T(8,128)(2,1)S(1)}, bf16[320,256]{1,0:T(8,128)(2,1)S(1)}, bf16[256,256]{1,0:T(8,12...) custom-call(bf16[128,2176]{1,0:T(8,128)(2,1)S(1)} %get-tuple-element, ...), custom_call_target="tpu_custom_call" | custom-call | flops 4000000000 | bytes 10000000 | tf_op jit(solution)/shard_map/pallas_call | solution.py:536
  28.4 1.1 %collective-permute-done.8.high = bf16[256,256]{1,0:T(8,128)(2,1)S(1)} collective-permute-done((bf16[256,256]{1,0:T(8,128)(2,1)S(1)}, bf16[256,256]{1,0:T(8,128)(2,1)S(1)}, u32[]{:S(2)}, u32[]{:S(2)}) %collective-permute-start.8) | collective-permute-done | bytes 131104 | tf_op jit(solution)/shard_map/ppermute | solution.py:462
  30.0 1.9 %collective-permute-done.9.refs_1_ = bf16[128,2176]{1,0:T(8,128)(2,1)S(1)} collective-permute-done((bf16[128,2176]{1,0:T(8,128)(2,1)S(1)}, bf16[128,2176]{1,0:T(8,128)(2,1)S(1)}, u32[]{:S(2)}, u32[]{:S(2)}) %collective-permute-start.9) | collective-permute-done | bytes 557088 | tf_op jit(solution)/shard_map/ppermute | solution.py:462
  32.0 5.5 %shard_map.116 = (bf16[2,576,256]{2,1,0:T(8,128)(2,1)S(1)}, bf16[576,256]{1,0:T(8,128)(2,1)S(1)}, bf16[320,256]{1,0:T(8,128)(2,1)S(1)}, bf16[256,256]{1,0:T(8,12...) custom-call(bf16[128,2176]{1,0:T(8,128)(2,1)S(1)} %shard_map.115.ref, ...), custom_call_target="tpu_custom_call" | custom-call | flops 4000000000 | bytes 10000000 | tf_op jit(solution)/shard_map/pallas_call | solution.py:562
  37.7 1.5 %collective-permute-start.12 = (bf16[576,256]{1,0:T(8,128)(2,1)S(1)}, bf16[576,256]{1,0:T(8,128)(2,1)S(1)}, u32[]{:S(2)}, u32[]{:S(2)}) collective-permute-start(bf16[576,256]{1,0:T(8,128)(2,1)S(1)} %shard_map.114.after), channel_id=1, source_target_pairs={{0,2},{1,3},{2,0},{3,1},{4,6},{5,7},{6,4},{7,5},{8,10},{9,11},{10,... | collective-permute-start | bytes 884744 | tf_op jit(solution)/shard_map/ppermute | solution.py:462
  40.0 1.3 %collective-permute-start.16 = (bf16[320,256]{1,0:T(8,128)(2,1)S(1)}, bf16[320,256]{1,0:T(8,128)(2,1)S(1)}, u32[]{:S(2)}, u32[]{:S(2)}) collective-permute-start(bf16[320,256]{1,0:T(8,128)(2,1)S(1)} %shard_map.117.after), channel_id=1, source_target_pairs={{0,2},{1,3},{2,0},{3,1},{4,6},{5,7},{6,4},{7,5},{8,10},{9,11},{10,... | collective-permute-start | bytes 491528 | tf_op jit(solution)/shard_map/ppermute | solution.py:462
  41.3 6.3 %collective-permute-done.12.after2.theirs = bf16[576,256]{1,0:T(8,128)(2,1)S(1)} collective-permute-done((bf16[576,256]{1,0:T(8,128)(2,1)S(1)}, bf16[576,256]{1,0:T(8,128)(2,1)S(1)}, u32[]{:S(2)}, u32[]{:S(2)}) %collective-permute-start.12) | collective-permute-done | bytes 294944 | tf_op jit(solution)/shard_map/ppermute | solution.py:462
  47.6 1.6 %collective-permute-start.19 = (bf16[256,256]{1,0:T(8,128)(2,1)S(1)}, bf16[256,256]{1,0:T(8,128)(2,1)S(1)}, u32[]{:S(2)}, u32[]{:S(2)}) collective-permute-start(bf16[256,256]{1,0:T(8,128)(2,1)S(1)} %shard_map.119.after), channel_id=1, source_target_pairs={{0,2},{1,3},{2,0},{3,1},{4,6},{5,7},{6,4},{7,5},{8,10},{9,11},{10,... | collective-permute-start | bytes 393224 | tf_op jit(solution)/shard_map/ppermute | solution.py:462
  50.1 3.0 %shard_map.121 = (bf16[2,512,1024]{2,1,0:T(8,128)(2,1)}, bf16[2,1024,512]{2,1,0:T(8,128)(2,1)}, f32[8,128]{1,0:T(8,128)S(1)}) custom-call(bf16[2,128,512]{2,1,0:T(8,128)(2,1)S(1)} %get-tuple-element.63.act0, bf16[2,128,1024]{2,1,0:T(8,128)(2,1)S(1)} %get-tuple-element.64.grad0, bf16[2,128,1024]{2,1,0:T(8,128)(2,1)S(1)} %get-tuple-element.65.cross0, ...), custom_call_target="tpu_custom_call" | custom-call | flops 3000000000 | bytes 8000000 | tf_op jit(solution)/shard_map/pallas_call | solution.py:591
  53.4 1.7 %collective-permute-start.17 = (bf16[160,256]{1,0:T(8,128)(2,1)S(1)}, bf16[160,256]{1,0:T(8,128)(2,1)S(1)}, u32[]{:S(2)}, u32[]{:S(2)}) collective-permute-start(bf16[160,256]{1,0:T(8,128)(2,1)S(1)} %get-tuple-element.73), channel_id=1, source_target_pairs={{0,4},{4,0},{8,12},{12,8},{1,5},{5,1},{9,13},{13,9},{2,6},{6,2},{1... | collective-permute-start | bytes 245768 | tf_op jit(solution)/shard_map/ppermute | solution.py:462
  55.9 2.0 %collective-permute-done.17.b = bf16[160,256]{1,0:T(8,128)(2,1)S(1)} collective-permute-done((bf16[160,256]{1,0:T(8,128)(2,1)S(1)}, bf16[160,256]{1,0:T(8,128)(2,1)S(1)}, u32[]{:S(2)}, u32[]{:S(2)}) %collective-permute-start.17) | collective-permute-done | bytes 81952 | tf_op jit(solution)/shard_map/ppermute | solution.py:462
  57.9 2.8 %collective-permute-start.18 = (bf16[160,256]{1,0:T(8,128)(2,1)S(1)}, bf16[160,256]{1,0:T(8,128)(2,1)S(1)}, u32[]{:S(2)}, u32[]{:S(2)}) collective-permute-start(bf16[160,256]{1,0:T(8,128)(2,1)S(1)} %shard_map.123), channel_id=1, source_target_pairs={{0,8},{4,12},{8,0},{12,4},{1,9},{5,13},{9,1},{13,5},{2,10},{6,14},... | collective-permute-start | bytes 245768 | tf_op jit(solution)/shard_map/ppermute | solution.py:462
  60.8 1.4 %collective-permute-start.21 = (bf16[128,256]{1,0:T(8,128)(2,1)S(1)}, bf16[128,256]{1,0:T(8,128)(2,1)S(1)}, u32[]{:S(2)}, u32[]{:S(2)}) collective-permute-start(bf16[128,256]{1,0:T(8,128)(2,1)S(1)} %shard_map.125), channel_id=1, source_target_pairs={{0,8},{4,12},{8,0},{12,4},{1,9},{5,13},{9,1},{13,5},{2,10},{6,14},... | collective-permute-start | bytes 196616 | tf_op jit(solution)/shard_map/ppermute | solution.py:462
  62.1 1.0 %shard_map.127 = bf16[2,256,256]{2,1,0:T(8,128)(2,1)} custom-call(bf16[2,256,128]{2,1,0:T(8,128)(2,1)S(1)} %get-tuple-element.79.gram0, bf16[2,128,256]{2,1,0:T(8,128)(2,1)S(1)} %get-tuple-element.80.rows0, bf16[2,256,128]{2,1,0:T(8,128)(2,1)S(1)} %get-tuple-element.81.gram1, bf16[2,128,256]{2,1,0:T(8,128)(2,1)S(1)} %get-tuple-element.82.rows1), custom_call_target="tpu_custom_call" | custom-call | flops 300000000 | bytes 2000000 | tf_op jit(solution)/shard_map/pallas_call | solution.py:610
  63.1 1.4 %collective-permute-done.18.far_grads = bf16[160,256]{1,0:T(8,128)(2,1)S(1)} collective-permute-done((bf16[160,256]{1,0:T(8,128)(2,1)S(1)}, bf16[160,256]{1,0:T(8,128)(2,1)S(1)}, u32[]{:S(2)}, u32[]{:S(2)}) %collective-permute-start.18) | collective-permute-done | bytes 81952 | tf_op jit(solution)/shard_map/ppermute | solution.py:462
  64.5 1.9 %collective-permute-done.21.far_outs = bf16[128,256]{1,0:T(8,128)(2,1)S(1)} collective-permute-done((bf16[128,256]{1,0:T(8,128)(2,1)S(1)}, bf16[128,256]{1,0:T(8,128)(2,1)S(1)}, u32[]{:S(2)}, u32[]{:S(2)}) %collective-permute-start.21) | collective-permute-done | bytes 65568 | tf_op jit(solution)/shard_map/ppermute | solution.py:462
  66.4 1.0 %shard_map.126 = (bf16[128,256]{1,0:T(8,128)(2,1)}, bf16[128,256]{1,0:T(8,128)(2,1)}) custom-call(bf16[128,2176]{1,0:T(8,128)(2,1)S(1)} %get-tuple-element.46.refs_0_.own, bf16[288,256]{1,0:T(8,128)(2,1)S(1)} %get-tuple-element.59.g0, bf16[288,256]{1,0:T(8,128)(2,1)S(1)} %collective-permute-done.14.after.g1, ...), custom_call_target="tpu_custom_call" | custom-call | flops 100000000 | bytes 1000000 | tf_op jit(solution)/shard_map/pallas_call | solution.py:613
  (48 shorter events, 9.4 us)
Async XLA Ops:
  2.4 15.8 %collective-permute-start = (bf16[64,2176]{1,0:T(8,128)(2,1)}, bf16[64,2176]{1,0:T(8,128)(2,1)S(1)}, u32[]{:S(2)}, u32[]{:S(2)}) collective-permute-start(bf16[64,2176]{1,0:T(8,128)(2,1)} %get-tuple-element.48), channel_id=1, source_target_pairs={{0,4},{4,0},{8,12},{12,8},{1,5},{5,1},{9,13},{13,9},{2,6},{6,2},{1... | collective-permute-start | bytes 835592 | tf_op jit(solution)/shard_map/ppermute | solution.py:462
  5.5 15.3 %collective-permute-start.4 = (bf16[64,2176]{1,0:T(8,128)(2,1)}, bf16[64,2176]{1,0:T(8,128)(2,1)S(1)}, u32[]{:S(2)}, u32[]{:S(2)}) collective-permute-start(bf16[64,2176]{1,0:T(8,128)(2,1)} %get-tuple-element.48), channel_id=1, source_target_pairs={{0,8},{4,12},{8,0},{12,4},{1,9},{5,13},{9,1},{13,5},{2,10},{6,14},... | collective-permute-start | bytes 835592 | tf_op jit(solution)/shard_map/ppermute | solution.py:462
  8.1 0.9 %copy-start = (bf16[128,1024]{1,0:T(8,128)(2,1)S(1)}, bf16[128,1024]{1,0:T(8,128)(2,1)}, u32[]{:S(2)}) copy-start(bf16[128,1024]{1,0:T(8,128)(2,1)} %x.3) | copy-start | bytes 786436
  11.7 7.6 %collective-permute-start.3 = (bf16[2,256,256]{2,1,0:T(8,128)(2,1)S(1)}, bf16[2,256,256]{2,1,0:T(8,128)(2,1)S(1)}, u32[]{:S(2)}, u32[]{:S(2)}) collective-permute-start(bf16[2,256,256]{2,1,0:T(8,128)(2,1)S(1)} %get-tuple-element.47.refs_1_), channel_id=1, source_target_pairs={{0,2},{1,3},{2,0},{3,1},{4,6},{5,7},{6,4},{7,5},{8,10},{9,11},{10,... | collective-permute-start | bytes 786440 | tf_op jit(solution)/shard_map/ppermute | solution.py:462
  18.2 4.2 %collective-permute-start.1 = (bf16[64,2176]{1,0:T(8,128)(2,1)S(1)}, bf16[64,2176]{1,0:T(8,128)(2,1)S(1)}, u32[]{:S(2)}, u32[]{:S(2)}) collective-permute-start(bf16[64,2176]{1,0:T(8,128)(2,1)S(1)} %collective-permute-done.refs_2_), channel_id=1, source_target_pairs={{0,1},{1,0},{2,3},{3,2},{4,5},{5,4},{6,7},{7,6},{8,9},{9,8},{10,11... | collective-permute-start | bytes 835592 | tf_op jit(solution)/shard_map/ppermute | solution.py:462
  18.2 3.2 %collective-permute-start.2 = (bf16[2,256,256]{2,1,0:T(8,128)(2,1)S(1)}, bf16[2,256,256]{2,1,0:T(8,128)(2,1)S(1)}, u32[]{:S(2)}, u32[]{:S(2)}) collective-permute-start(bf16[2,256,256]{2,1,0:T(8,128)(2,1)S(1)} %get-tuple-element.47.refs_1_), channel_id=1, source_target_pairs={{0,1},{1,0},{2,3},{3,2},{4,5},{5,4},{6,7},{7,6},{8,9},{9,8},{10,11... | collective-permute-start | bytes 786440 | tf_op jit(solution)/shard_map/ppermute | solution.py:462
  20.8 1.6 %collective-permute-start.5 = (bf16[2,256,256]{2,1,0:T(8,128)(2,1)S(1)}, bf16[2,256,256]{2,1,0:T(8,128)(2,1)S(1)}, u32[]{:S(2)}, u32[]{:S(2)}) collective-permute-start(bf16[2,256,256]{2,1,0:T(8,128)(2,1)S(1)} %shard_map.112.refs_5_), channel_id=1, source_target_pairs={{0,1},{1,0},{2,3},{3,2},{4,5},{5,4},{6,7},{7,6},{8,9},{9,8},{10,11... | collective-permute-start | bytes 786440 | tf_op jit(solution)/shard_map/ppermute | solution.py:462
  20.8 9.1 %collective-permute-start.6 = (bf16[64,2176]{1,0:T(8,128)(2,1)S(1)}, bf16[64,2176]{1,0:T(8,128)(2,1)S(1)}, u32[]{:S(2)}, u32[]{:S(2)}) collective-permute-start(bf16[64,2176]{1,0:T(8,128)(2,1)S(1)} %collective-permute-done.4.after.a), channel_id=1, source_target_pairs={{0,4},{4,0},{8,12},{12,8},{1,5},{5,1},{9,13},{13,9},{2,6},{6,2},{1... | collective-permute-start | bytes 835592 | tf_op jit(solution)/shard_map/ppermute | solution.py:462
  27.8 4.1 %copy-start.4 = (bf16[2,256,1024]{2,1,0:T(8,128)(2,1)S(1)}, bf16[2,256,1024]{2,1,0:T(8,128)(2,1)}, u32[]{:S(2)}) copy-start(bf16[2,256,1024]{2,1,0:T(8,128)(2,1)} %get-tuple-element.53.refs_2_) | copy-start | bytes 3145732
  27.9 1.7 %collective-permute-start.7 = (bf16[320,256]{1,0:T(8,128)(2,1)S(1)}, bf16[320,256]{1,0:T(8,128)(2,1)S(1)}, u32[]{:S(2)}, u32[]{:S(2)}) collective-permute-start(bf16[320,256]{1,0:T(8,128)(2,1)S(1)} %get-tuple-element.51), channel_id=1, source_target_pairs={{0,1},{1,0},{2,3},{3,2},{4,5},{5,4},{6,7},{7,6},{8,9},{9,8},{10,11... | collective-permute-start | bytes 491528 | tf_op jit(solution)/shard_map/ppermute | solution.py:462
  28.1 1.4 %collective-permute-start.8 = (bf16[256,256]{1,0:T(8,128)(2,1)S(1)}, bf16[256,256]{1,0:T(8,128)(2,1)S(1)}, u32[]{:S(2)}, u32[]{:S(2)}) collective-permute-start(bf16[256,256]{1,0:T(8,128)(2,1)S(1)} %get-tuple-element.52), channel_id=1, source_target_pairs={{0,1},{1,0},{2,3},{3,2},{4,5},{5,4},{6,7},{7,6},{8,9},{9,8},{10,11... | collective-permute-start | bytes 393224 | tf_op jit(solution)/shard_map/ppermute | solution.py:462
  30.0 2.0 %collective-permute-start.9 = (bf16[128,2176]{1,0:T(8,128)(2,1)S(1)}, bf16[128,2176]{1,0:T(8,128)(2,1)S(1)}, u32[]{:S(2)}, u32[]{:S(2)}) collective-permute-start(bf16[128,2176]{1,0:T(8,128)(2,1)S(1)} %shard_map.115.refs_0_), channel_id=1, source_target_pairs={{0,1},{1,0},{2,3},{3,2},{4,5},{5,4},{6,7},{7,6},{8,9},{9,8},{10,11... | collective-permute-start | bytes 1671176 | tf_op jit(solution)/shard_map/ppermute | solution.py:462
  37.5 1.7 %collective-permute-start.10 = (bf16[320,256]{1,0:T(8,128)(2,1)S(1)}, bf16[320,256]{1,0:T(8,128)(2,1)S(1)}, u32[]{:S(2)}, u32[]{:S(2)}) collective-permute-start(bf16[320,256]{1,0:T(8,128)(2,1)S(1)} %get-tuple-element.55), channel_id=1, source_target_pairs={{0,1},{1,0},{2,3},{3,2},{4,5},{5,4},{6,7},{7,6},{8,9},{9,8},{10,11... | collective-permute-start | bytes 491528 | tf_op jit(solution)/shard_map/ppermute | solution.py:462
  37.7 9.8 %collective-permute-start.12 = (bf16[576,256]{1,0:T(8,128)(2,1)S(1)}, bf16[576,256]{1,0:T(8,128)(2,1)S(1)}, u32[]{:S(2)}, u32[]{:S(2)}) collective-permute-start(bf16[576,256]{1,0:T(8,128)(2,1)S(1)} %shard_map.114.after), channel_id=1, source_target_pairs={{0,2},{1,3},{2,0},{3,1},{4,6},{5,7},{6,4},{7,5},{8,10},{9,11},{10,... | collective-permute-start | bytes 884744 | tf_op jit(solution)/shard_map/ppermute | solution.py:462
  39.3 9.9 %collective-permute-start.11 = (bf16[576,256]{1,0:T(8,128)(2,1)S(1)}, bf16[576,256]{1,0:T(8,128)(2,1)S(1)}, u32[]{:S(2)}, u32[]{:S(2)}) collective-permute-start(bf16[576,256]{1,0:T(8,128)(2,1)S(1)} %shard_map.118), channel_id=1, source_target_pairs={{0,1},{1,0},{2,3},{3,2},{4,5},{5,4},{6,7},{7,6},{8,9},{9,8},{10,11... | collective-permute-start | bytes 884744 | tf_op jit(solution)/shard_map/ppermute | solution.py:462
  39.5 8.1 %collective-permute-start.13 = (bf16[256,256]{1,0:T(8,128)(2,1)S(1)}, bf16[256,256]{1,0:T(8,128)(2,1)S(1)}, u32[]{:S(2)}, u32[]{:S(2)}) collective-permute-start(bf16[256,256]{1,0:T(8,128)(2,1)S(1)} %get-tuple-element.58), channel_id=1, source_target_pairs={{0,1},{1,0},{2,3},{3,2},{4,5},{5,4},{6,7},{7,6},{8,9},{9,8},{10,11... | collective-permute-start | bytes 393224 | tf_op jit(solution)/shard_map/ppermute | solution.py:462
  39.9 13.2 %collective-permute-start.15 = (bf16[576,256]{1,0:T(8,128)(2,1)S(1)}, bf16[576,256]{1,0:T(8,128)(2,1)S(1)}, u32[]{:S(2)}, u32[]{:S(2)}) collective-permute-start(bf16[576,256]{1,0:T(8,128)(2,1)S(1)} %get-tuple-element.61), channel_id=1, source_target_pairs={{0,1},{1,0},{2,3},{3,2},{4,5},{5,4},{6,7},{7,6},{8,9},{9,8},{10,11... | collective-permute-start | bytes 884744 | tf_op jit(solution)/shard_map/ppermute | solution.py:462
  40.0 13.1 %collective-permute-start.16 = (bf16[320,256]{1,0:T(8,128)(2,1)S(1)}, bf16[320,256]{1,0:T(8,128)(2,1)S(1)}, u32[]{:S(2)}, u32[]{:S(2)}) collective-permute-start(bf16[320,256]{1,0:T(8,128)(2,1)S(1)} %shard_map.117.after), channel_id=1, source_target_pairs={{0,2},{1,3},{2,0},{3,1},{4,6},{5,7},{6,4},{7,5},{8,10},{9,11},{10,... | collective-permute-start | bytes 491528 | tf_op jit(solution)/shard_map/ppermute | solution.py:462
  47.6 7.5 %collective-permute-start.19 = (bf16[256,256]{1,0:T(8,128)(2,1)S(1)}, bf16[256,256]{1,0:T(8,128)(2,1)S(1)}, u32[]{:S(2)}, u32[]{:S(2)}) collective-permute-start(bf16[256,256]{1,0:T(8,128)(2,1)S(1)} %shard_map.119.after), channel_id=1, source_target_pairs={{0,2},{1,3},{2,0},{3,1},{4,6},{5,7},{6,4},{7,5},{8,10},{9,11},{10,... | collective-permute-start | bytes 393224 | tf_op jit(solution)/shard_map/ppermute | solution.py:462
  49.6 5.5 %collective-permute-start.14 = (bf16[288,256]{1,0:T(8,128)(2,1)S(1)}, bf16[288,256]{1,0:T(8,128)(2,1)S(1)}, u32[]{:S(2)}, u32[]{:S(2)}) collective-permute-start(bf16[288,256]{1,0:T(8,128)(2,1)S(1)} %get-tuple-element.60), channel_id=1, source_target_pairs={{0,4},{4,0},{8,12},{12,8},{1,5},{5,1},{9,13},{13,9},{2,6},{6,2},{1... | collective-permute-start | bytes 442376 | tf_op jit(solution)/shard_map/ppermute | solution.py:462
  53.4 4.5 %collective-permute-start.17 = (bf16[160,256]{1,0:T(8,128)(2,1)S(1)}, bf16[160,256]{1,0:T(8,128)(2,1)S(1)}, u32[]{:S(2)}, u32[]{:S(2)}) collective-permute-start(bf16[160,256]{1,0:T(8,128)(2,1)S(1)} %get-tuple-element.73), channel_id=1, source_target_pairs={{0,4},{4,0},{8,12},{12,8},{1,5},{5,1},{9,13},{13,9},{2,6},{6,2},{1... | collective-permute-start | bytes 245768 | tf_op jit(solution)/shard_map/ppermute | solution.py:462
  55.4 5.4 %collective-permute-start.20 = (bf16[128,256]{1,0:T(8,128)(2,1)S(1)}, bf16[128,256]{1,0:T(8,128)(2,1)S(1)}, u32[]{:S(2)}, u32[]{:S(2)}) collective-permute-start(bf16[128,256]{1,0:T(8,128)(2,1)S(1)} %get-tuple-element.76), channel_id=1, source_target_pairs={{0,4},{4,0},{8,12},{12,8},{1,5},{5,1},{9,13},{13,9},{2,6},{6,2},{1... | collective-permute-start | bytes 196616 | tf_op jit(solution)/shard_map/ppermute | solution.py:462
  57.9 6.6 %collective-permute-start.18 = (bf16[160,256]{1,0:T(8,128)(2,1)S(1)}, bf16[160,256]{1,0:T(8,128)(2,1)S(1)}, u32[]{:S(2)}, u32[]{:S(2)}) collective-permute-start(bf16[160,256]{1,0:T(8,128)(2,1)S(1)} %shard_map.123), channel_id=1, source_target_pairs={{0,8},{4,12},{8,0},{12,4},{1,9},{5,13},{9,1},{13,5},{2,10},{6,14},... | collective-permute-start | bytes 245768 | tf_op jit(solution)/shard_map/ppermute | solution.py:462
  60.8 5.6 %collective-permute-start.21 = (bf16[128,256]{1,0:T(8,128)(2,1)S(1)}, bf16[128,256]{1,0:T(8,128)(2,1)S(1)}, u32[]{:S(2)}, u32[]{:S(2)}) collective-permute-start(bf16[128,256]{1,0:T(8,128)(2,1)S(1)} %shard_map.125), channel_id=1, source_target_pairs={{0,8},{4,12},{8,0},{12,4},{1,9},{5,13},{9,1},{13,5},{2,10},{6,14},... | collective-permute-start | bytes 196616 | tf_op jit(solution)/shard_map/ppermute | solution.py:462
  (3 other events, 2.7 us)
